TPU v7x, 32 devices: a whole 2x2x4 slice. The times are simulated.
32 devices in a mesh: weight: 4 (over z), context: 2 (over x), tensor: 4 (over y, core).
Axes of the slice: x: 2, y: 2, z: 4, core: 2. Of those that a mesh axis runs over, the one named last changes fastest.
Arguments:
- tokens: bfloat16 [4, 32, 32, 2240], P('weight', 'context'), may hold values from -6 to 6
- caption: bfloat16 [4, 300, 2240], P('weight', 'context'), may hold values from -6 to 6
- caption_lengths: int32 [4], P('weight'), may hold values from 37 to 300, as said below
- adapter_index: int32 [4], P('weight'), may hold values from 0 to 7
- modulation: float32 [4, 6, 2240], P('weight'), may hold values from -1 to 1
- cotangent: bfloat16 [4, 32, 32, 2240], P('weight', 'context'), may hold values from -6 to 6
- qkv_weight: bfloat16 [2240, 3, 2240], P('weight'), may hold values from -1 to 1
- proj_weight: bfloat16 [2240, 2240], P(None, 'weight'), may hold values from -1 to 1
- cross_q_weight: bfloat16 [2240, 2240], P('weight'), may hold values from -0.125 to 0.125
- cross_kv_weight: bfloat16 [2240, 2, 2240], P('weight'), may hold values from -0.125 to 0.125
- cross_out_weight: bfloat16 [2240, 2240], P(None, 'weight'), may hold values from -0.5 to 0.5
- inverted_weight: bfloat16 [2240, 2, 5600], P('weight', None, 'tensor'), may hold values from -0.125 to 0.125
- depth_weight: bfloat16 [3, 3, 2, 5600], P(None, None, None, 'tensor'), may hold values from -2 to 2
- point_weight: bfloat16 [5600, 2240], P('tensor', 'weight'), may hold values from -0.078125 to 0.078125
- qkv_down: bfloat16 [8, 2240, 16], replicated, may hold values from -0.125 to 0.125
- qkv_up: bfloat16 [8, 16, 3, 2240], replicated, may hold values from -0.75 to 0.75
- proj_down: bfloat16 [8, 2240, 16], replicated, may hold values from -1 to 1
- proj_up: bfloat16 [8, 16, 2240], replicated, may hold values from -0.75 to 0.75
- query_down: bfloat16 [8, 2240, 16], replicated, may hold values from -0.125 to 0.125
- query_up: bfloat16 [8, 16, 2240], replicated, may hold values from -0.75 to 0.75
- kv_down: bfloat16 [8, 2240, 16], replicated, may hold values from -0.125 to 0.125
- kv_up: bfloat16 [8, 16, 2, 2240], replicated, may hold values from -0.75 to 0.75
- cross_down: bfloat16 [8, 2240, 16], replicated, may hold values from -0.5 to 0.5
- cross_up: bfloat16 [8, 16, 2240], replicated, may hold values from -0.75 to 0.75
- inverted_down: bfloat16 [8, 2240, 16], replicated, may hold values from -0.125 to 0.125
- inverted_up: bfloat16 [8, 16, 2, 5600], replicated, may hold values from -0.75 to 0.75
- point_down: bfloat16 [8, 5600, 16], replicated, may hold values from -0.078125 to 0.078125
- point_up: bfloat16 [8, 16, 2240], replicated, may hold values from -0.75 to 0.75
Outputs:
- output: float32 [4, 32, 32, 2240], P('weight', 'context')
- input_grad: float32 [4, 32, 32, 2240], P('weight', 'context')
- qkv_down_sum: float32 [8, 2240, 16], P(None, ('weight', 'context'), 'tensor')
- qkv_up_sum: float32 [8, 16, 3, 2240], P(None, 'tensor', None, ('weight', 'context'))
- proj_down_sum: float32 [8, 2240, 16], P(None, ('weight', 'context'), 'tensor')
- proj_up_sum: float32 [8, 16, 2240], P(None, 'tensor', ('weight', 'context'))
- query_down_sum: float32 [8, 2240, 16], P(None, ('weight', 'context'), 'tensor')
- query_up_sum: float32 [8, 16, 2240], P(None, 'tensor', ('weight', 'context'))
- kv_down_sum: float32 [8, 2240, 16], P(None, ('weight', 'context'), 'tensor')
- kv_up_sum: float32 [8, 16, 2, 2240], P(None, 'tensor', None, ('weight', 'context'))
- cross_down_sum: float32 [8, 2240, 16], P(None, ('weight', 'context'), 'tensor')
- cross_up_sum: float32 [8, 16, 2240], P(None, 'tensor', ('weight', 'context'))
- inverted_down_sum: float32 [8, 2240, 16], P(None, ('weight', 'context'), 'tensor')
- inverted_up_sum: float32 [8, 16, 2, 5600], P(None, 'tensor', None, ('weight', 'context'))
- point_down_sum: float32 [8, 5600, 16], P(None, ('weight', 'context'), 'tensor')
- point_up_sum: float32 [8, 16, 2240], P(None, 'tensor', ('weight', 'context'))
Inputs may be any that keep to these rules, and one draw needn't show every extreme that they name: Sequence b attends to its first caption_lengths[b] caption tokens; in every draw some sequence has all 300 and another has 37.
All inputs are finite; a program needn't handle non-finite values.
Results may differ from a plain program's by a relative error of at most 0.035.
The roundings to bfloat16 on the way count: a program that leaves them out, or rounds other values in their place, can miss the bound.
Values may be sent and summed in bfloat16 or wider, within the bound.
No kernel may reach another device: no remote copies, remote signals or barrier semaphores. Data moves between devices by JAX's collectives and lax.ppermute only.
A program may use at most 448 MiB of HBM per device.

v0:
```python
import jax
import jax.numpy as jnp
from jax import lax
from jax.sharding import PartitionSpec as P

W, C, T = "weight", "context", "tensor"
HD = 32
bf16, f32 = jnp.bfloat16, jnp.float32
full_precision = lax.Precision.HIGHEST
norm_eps = 1e-06
attention_epsilon = 1e-06
masked_score = -1000000000.0


def ring_order(n):
    return list(range(0, n, 2)) + list(range(n - 1 - n % 2, 0, -2))


def ring_pairs(n):
    order = ring_order(n)
    return [(order[i], order[(i + 1) % n]) for i in range(n)]


def ring_source(n, step):
    z = lax.axis_index(W)
    place = jnp.where(z % 2 == 0, z // 2, n - 1 - z // 2)
    from_place = (place - step + n) % n
    return jnp.where(2 * from_place < n, 2 * from_place, 2 * (n - 1 - from_place) + 1)


def swap_pairs(n, distance):
    return [(i, i ^ distance) for i in range(n)]


def gather_pair(first, second, tie):
    n = lax.axis_size(W)
    c = lax.axis_index(C)
    rows, cols = first.shape
    buf = jnp.zeros((2, n * rows, cols), bf16)
    buf = lax.dynamic_update_slice(buf, jnp.stack([first, second]), (0, lax.axis_index(W) * rows, 0))
    moving = jnp.where(c == 0, first, second)
    if tie is not None:
        moving, tie = lax.optimization_barrier((moving, tie))
    for step in range(1, n):
        moving = lax.ppermute(moving, W, ring_pairs(n))
        other = lax.ppermute(moving, C, swap_pairs(2, 1))
        at = ring_source(n, step) * rows
        buf = lax.dynamic_update_slice(buf, moving[None], (c, at, 0))
        buf = lax.dynamic_update_slice(buf, other[None], (1 - c, at, 0))
    return buf, moving[:16, :128]


def sum_halves(partial):
    groups = lax.axis_size(T)
    b = lax.axis_index(T) % 2
    half = partial.shape[0] // 2
    away = lax.dynamic_slice_in_dim(partial, (1 - b) * half, half, 0).astype(bf16)
    mine = lax.dynamic_slice_in_dim(partial, b * half, half, 0)
    total = mine + lax.ppermute(away, T, swap_pairs(groups, 1)).astype(f32)
    distance = 2
    while distance < groups:
        low = total.astype(bf16)
        total = low.astype(f32) + lax.ppermute(low, T, swap_pairs(groups, distance)).astype(f32)
        distance *= 2
    return total


def share_halves(mine):
    b = lax.axis_index(T) % 2
    other = lax.ppermute(mine, T, swap_pairs(lax.axis_size(T), 1))
    return jnp.where(b == 0, jnp.concatenate([mine, other]), jnp.concatenate([other, mine]))


def add_context(values):
    return values + lax.ppermute(values, C, swap_pairs(2, 1))


def layer_stats(values):
    center = values - jnp.mean(values, axis=-1, keepdims=True)
    inverse = lax.rsqrt(jnp.mean(center * center, axis=-1, keepdims=True) + norm_eps)
    return center * inverse, inverse


def norm_back(normed, inverse, grad):
    return inverse * (
        grad
        - jnp.mean(grad, axis=-1, keepdims=True)
        - normed * jnp.mean(grad * normed, axis=-1, keepdims=True)
    )


def dot(a, b, ca=1, cb=0):
    return lax.dot_general(a, b, (((ca,), (cb,)), ((), ())), preferred_element_type=f32)


def two_parts(values, axis):
    high = lax.reduce_precision(values, 8, 7)
    return jnp.concatenate([high.astype(bf16), (values - high).astype(bf16)], axis=axis)


def twice(table, axis=0):
    return jnp.concatenate([table, table], axis=axis)


def thin_dot(latent, table):
    return dot(two_parts(latent, 1), twice(table))


def outer_sum(latent, values):
    both = dot(two_parts(latent, 1), values, 0, 0)
    half = both.shape[0] // 2
    return both[:half] + both[half:]


def shifted(rows_of, kernel, flip):
    height = rows_of.shape[0] - 2
    width = rows_of.shape[1]
    padded = jnp.pad(rows_of, ((0, 0), (1, 1), (0, 0)))
    total = jnp.zeros((height, width, rows_of.shape[2]), f32)
    for i in range(3):
        for j in range(3):
            tap = kernel[2 - i, 2 - j] if flip else kernel[i, j]
            total = total + padded[i : i + height, j : j + width] * tap
    return total


def with_halo(blocks):
    c = lax.axis_index(C)
    edge = jnp.stack([jnp.where(c == 0, v[-1], v[0]) for v in blocks])
    got = lax.ppermute(edge, C, swap_pairs(2, 1))
    zero = jnp.zeros_like(got)
    above = jnp.where(c == 0, zero, got)
    below = jnp.where(c == 0, got, zero)
    return [
        jnp.concatenate([above[i][None], v, below[i][None]]) for i, v in enumerate(blocks)
    ]


def silu_slope(values):
    sig = jax.nn.sigmoid(values)
    return sig * (1.0 + values * (1.0 - sig))


def slot_layout(groups, rank, heads):
    per, left = heads // groups, heads % groups
    slots = per + (1 if left else 0)
    own_first = rank * per + jnp.minimum(rank, left)
    own_count = per + jnp.where(rank < left, 1, 0)
    first = jnp.minimum(own_first, heads - slots)
    slot = first + jnp.arange(slots, dtype=jnp.int32)
    owned = ((slot >= own_first) & (slot < own_first + own_count)).astype(f32)
    return slots, first, owned


def slot_ranges(groups, heads):
    per, left = heads // groups, heads % groups
    slots = per + (1 if left else 0)
    out = []
    for rank in range(groups):
        own_first = rank * per + min(rank, left)
        count = per + (1 if rank < left else 0)
        skip = own_first - min(own_first, heads - slots)
        out.append((skip, count))
    return out


def shards(
    tokens, caption, caption_lengths, adapter_index, modulation, cotangent,
    qkv_weight, proj_weight, cross_q_weight, cross_kv_weight, cross_out_weight,
    inverted_weight, depth_weight, point_weight,
    qkv_down, qkv_up, proj_down, proj_up, query_down, query_up, kv_down, kv_up,
    cross_down, cross_up, inverted_down, inverted_up, point_down, point_up,
):
    grid_rows, grid_cols, D = tokens.shape[1:]
    n = grid_rows * grid_cols
    heads = D // HD
    groups = lax.axis_size(T)
    rank = lax.axis_index(T)
    c = lax.axis_index(C)
    b = rank % 2
    half = n // 2
    adapters, R = qkv_up.shape[:2]
    slots, slot_first, owned = slot_layout(groups, rank, heads)
    width = slots * HD
    col = slot_first * HD
    owned_cols = jnp.repeat(owned, HD)
    hid = inverted_weight.shape[2]
    hh = hid // 2
    hid_first = rank * hid
    index = adapter_index[0]

    def cut(table, start, size, axis):
        return lax.dynamic_slice_in_dim(table, start, size, axis)

    def pick(table):
        return lax.dynamic_index_in_dim(table, index, 0, keepdims=False)

    qkv_cut = cut(qkv_weight, col, width, 2)
    kv_cut = cut(cross_kv_weight, col, width, 2)
    proj_t = cut(proj_weight, col, width, 0).T
    out_t = cut(cross_out_weight, col, width, 0).T
    query_cut = cut(cross_q_weight, col, width, 1)
    point_t = point_weight.T
    w_a, t_a = gather_pair(qkv_cut[:, 0], qkv_cut[:, 1], None)
    w_b, t_b = gather_pair(qkv_cut[:, 2], proj_t, None)
    w_c, t_c = gather_pair(query_cut, kv_cut[:, 0], t_a)
    w_d, t_d = gather_pair(kv_cut[:, 1], out_t, t_b)
    w_v, t_v = gather_pair(inverted_weight[:, 0, :hh], inverted_weight[:, 0, hh:], t_c)
    w_g, t_g = gather_pair(inverted_weight[:, 1, :hh], inverted_weight[:, 1, hh:], t_d)
    w_p, t_p = gather_pair(point_t[:, :hh], point_t[:, hh:], t_v)

    qkv_d, qkv_u = pick(qkv_down), cut(pick(qkv_up), col, width, 2)
    proj_d, proj_u = cut(pick(proj_down), col, width, 0), pick(proj_up)
    query_d, query_u = pick(query_down), cut(pick(query_up), col, width, 1)
    kv_d, kv_u = pick(kv_down), cut(pick(kv_up), col, width, 2)
    cross_d, cross_u = cut(pick(cross_down), col, width, 0), pick(cross_up)
    inv_d, inv_u = pick(inverted_down), cut(pick(inverted_up), hid_first, hid, 2)
    point_d, point_u = cut(pick(point_down), hid_first, hid, 0), pick(point_up)

    mods = modulation[0]
    shift_a, scale_a, gate_a, shift_f, scale_f, gate_f = (mods[i : i + 1] for i in range(6))
    low_tokens = tokens.reshape(n, D)
    x_all = low_tokens.astype(f32)
    x_half = cut(low_tokens, b * half, half, 0).astype(f32)
    cot_all = cotangent.reshape(n, D)
    cot_half = cut(cot_all, b * half, half, 0).astype(f32)

    def per_head(values):
        return values.reshape(values.shape[0], slots, HD)

    normed, unused = layer_stats(x_all)
    attn_in = (normed * (1.0 + scale_a) + shift_a).astype(bf16)
    qkv_lat = dot(attn_in, qkv_d)
    q_raw, k_raw, v_raw = (
        dot(attn_in, w) + thin_dot(qkv_lat, qkv_u[:, i])
        for i, w in enumerate((w_a[0], w_a[1], w_b[0]))
    )
    q_h, k_h, v_h = per_head(jax.nn.relu(q_raw)), per_head(jax.nn.relu(k_raw)), per_head(v_raw)
    state = jnp.einsum("pha,phb->hab", k_h, v_h, precision=full_precision)
    keys = jnp.sum(k_h, axis=0)
    state_keys = add_context(jnp.concatenate([state, keys[:, None]], axis=1))
    state, keys = state_keys[:, :HD], state_keys[:, HD]
    numer = jnp.einsum("pha,hab->phb", q_h, state, precision=full_precision)
    denom = jnp.sum(q_h * keys, axis=-1, keepdims=True) + attention_epsilon
    ratio = numer / denom
    mixed = (ratio * owned[:, None]).reshape(n, width).astype(bf16)
    proj_lat = dot(mixed, proj_d)
    attn_part = dot(mixed, w_b[1], 1, 1) + thin_dot(proj_lat, proj_u)
    after_attn = x_half + gate_a * sum_halves(attn_part)
    cross_in = share_halves(after_attn.astype(bf16))

    text_here = caption.shape[1]
    kv_lat = dot(caption[0], kv_d)
    key_rows = dot(caption[0], w_c[1]) + thin_dot(kv_lat, kv_u[:, 0])
    value_rows = dot(caption[0], w_d[0]) + thin_dot(kv_lat, kv_u[:, 1])
    kv_own = jnp.concatenate([key_rows, value_rows], axis=1).astype(bf16)
    kv_other = lax.ppermute(kv_own, C, swap_pairs(2, 1))
    kv_all = jnp.concatenate([kv_own, kv_other])
    key_all, value_all = per_head(kv_all[:, :width]), per_head(kv_all[:, width:])
    places = jnp.arange(text_here)
    places = jnp.concatenate([c * text_here + places, (1 - c) * text_here + places])
    live = places < caption_lengths[0]
    query_lat = dot(cross_in, query_d)
    query = (dot(cross_in, w_c[0]) + thin_dot(query_lat, query_u)).astype(bf16)
    query_h = per_head(query)

    def raw_scores():
        s = jnp.einsum("phd,thd->hpt", query_h, key_all, preferred_element_type=f32)
        return jnp.where(live, s * HD ** (-0.5), masked_score)

    scores = raw_scores()
    row_max = jnp.max(scores, axis=-1, keepdims=True)
    exps = jnp.exp(scores - row_max)
    row_sum = jnp.sum(exps, axis=-1, keepdims=True)
    log_total = row_max + jnp.log(row_sum)
    probs = (exps / row_sum).astype(bf16)
    mix = jnp.einsum("hpt,thd->phd", probs, value_all, preferred_element_type=f32)
    mix = (mix * owned[:, None]).reshape(n, width).astype(bf16)
    cross_lat = dot(mix, cross_d)
    cross_part = dot(mix, w_d[1], 1, 1) + thin_dot(cross_lat, cross_u)
    after_cross = after_attn + sum_halves(cross_part)

    normed_f, inverse_f = layer_stats(after_cross)
    ffn_in = share_halves((normed_f * (1.0 + scale_f) + shift_f).astype(bf16))
    inv_lat = dot(ffn_in, inv_d)
    pre = []
    for part, w in enumerate((w_v, w_g)):
        for h in range(2):
            pre.append(dot(ffn_in, w[h]) + thin_dot(inv_lat, inv_u[:, part, h * hh : (h + 1) * hh]))
    grid = (grid_rows, grid_cols, hh)
    hidden = [jax.nn.silu(v).astype(bf16).reshape(grid) for v in pre]
    taps = depth_weight.astype(f32)
    taps = [taps[:, :, p, h * hh : (h + 1) * hh] for p in range(2) for h in range(2)]
    conv = [shifted(v, t, False).reshape(n, hh) for v, t in zip(with_halo(hidden), taps)]
    conv_v, conv_g = conv[:2], conv[2:]
    acts = [jax.nn.silu(g) for g in conv_g]
    gated = [(v * a).astype(bf16) for v, a in zip(conv_v, acts)]
    point_lat = dot(gated[0], point_d[:hh]) + dot(gated[1], point_d[hh:])
    ffn_part = (
        dot(gated[0], w_p[0], 1, 1) + dot(gated[1], w_p[1], 1, 1) + thin_dot(point_lat, point_u)
    )
    output = after_cross + gate_f * sum_halves(ffn_part)
    output = share_halves(output)

    grad_ffn = (gate_f * cot_all.astype(f32)).astype(bf16)
    point_gl = dot(grad_ffn, point_u, 1, 1)
    grad_conv = []
    for h in range(2):
        grad_gated = dot(grad_ffn, w_p[h]) + dot(
            two_parts(point_gl, 1), twice(point_d[h * hh : (h + 1) * hh], 1), 1, 1
        )
        grad_conv.append((grad_gated * acts[h], grad_gated * conv_v[h] * silu_slope(conv_g[h])))
    grad_conv = [grad_conv[h][p].astype(bf16).reshape(grid) for p in range(2) for h in range(2)]
    grad_pre = []
    for v, t, s in zip(with_halo(grad_conv), taps, pre):
        grad_pre.append((shifted(v, t, True).reshape(n, hh) * silu_slope(s)).astype(bf16))
    inv_ups = [inv_u[:, p, h * hh : (h + 1) * hh] for p in range(2) for h in range(2)]
    inv_ws = [w_v[0], w_v[1], w_g[0], w_g[1]]
    inv_gl = sum(dot(g, u, 1, 1) for g, u in zip(grad_pre, inv_ups))
    ffn_in_part = sum(dot(g, w, 1, 1) for g, w in zip(grad_pre, inv_ws)) + dot(
        two_parts(inv_gl, 1), twice(inv_d, 1), 1, 1
    )
    grad_cross = cot_half + norm_back(
        normed_f, inverse_f, sum_halves(ffn_in_part) * (1.0 + scale_f)
    )
    grad_cross_low = share_halves(grad_cross.astype(bf16))

    cross_gl = dot(grad_cross_low, cross_u, 1, 1)
    grad_mix = dot(grad_cross_low, w_d[1]) + dot(
        two_parts(cross_gl, 1), twice(cross_d, 1), 1, 1
    )
    grad_mix = per_head((grad_mix * owned_cols).astype(bf16))
    probs_wide = jnp.exp(raw_scores() - log_total)
    grad_probs = jnp.einsum("phd,thd->hpt", grad_mix, value_all, preferred_element_type=f32)
    grad_value = jnp.einsum(
        "hpt,phd->thd", probs_wide.astype(bf16), grad_mix, preferred_element_type=f32
    )
    inner = jnp.sum(probs_wide * grad_probs, axis=-1, keepdims=True)
    grad_scores = (probs_wide * (grad_probs - inner)).astype(bf16)
    grad_query = jnp.einsum("hpt,thd->phd", grad_scores, key_all, preferred_element_type=f32)
    grad_key = jnp.einsum("hpt,phd->thd", grad_scores, query_h, preferred_element_type=f32)
    grad_query = (grad_query * HD ** (-0.5)).reshape(n, width).astype(bf16)
    kv_terms = jnp.concatenate(
        [
            (grad_key * HD ** (-0.5)).reshape(2 * text_here, width),
            grad_value.reshape(2 * text_here, width),
        ],
        axis=1,
    )
    kv_got = lax.ppermute(kv_terms[text_here:], C, swap_pairs(2, 1))
    grad_kv = (kv_terms[:text_here] + kv_got).astype(bf16)
    query_gl = dot(grad_query, query_u, 1, 1)
    cross_in_part = dot(grad_query, w_c[0], 1, 1) + dot(
        two_parts(query_gl, 1), twice(query_d, 1), 1, 1
    )
    kv_gl = dot(grad_kv[:, :width], kv_u[:, 0], 1, 1) + dot(grad_kv[:, width:], kv_u[:, 1], 1, 1)
    grad_after = grad_cross + sum_halves(cross_in_part)

    grad_attn = share_halves((gate_a * grad_after).astype(bf16))
    proj_gl = dot(grad_attn, proj_u, 1, 1)
    grad_heads = dot(grad_attn, w_b[1]) + dot(two_parts(proj_gl, 1), twice(proj_d, 1), 1, 1)
    grad_heads = per_head(grad_heads * owned_cols)
    grad_numer = grad_heads / denom
    grad_den = -jnp.sum(grad_heads * ratio, axis=-1, keepdims=True) / denom
    grad_q = (
        jnp.einsum("phb,hab->pha", grad_numer, state, precision=full_precision) + grad_den * keys
    )
    state_grad = jnp.einsum("pha,phb->hab", q_h, grad_numer, precision=full_precision)
    keys_grad = jnp.sum(grad_den * q_h, axis=0)
    both_grad = add_context(jnp.concatenate([state_grad, keys_grad[:, None]], axis=1))
    state_grad, keys_grad = both_grad[:, :HD], both_grad[:, HD]
    grad_k = (
        jnp.einsum("phb,hab->pha", v_h, state_grad, precision=full_precision) + keys_grad
    )
    grad_v = jnp.einsum("pha,hab->phb", k_h, state_grad, precision=full_precision)
    grad_q = (grad_q.reshape(n, width) * (q_raw > 0)).astype(bf16)
    grad_k = (grad_k.reshape(n, width) * (k_raw > 0)).astype(bf16)
    grad_v = grad_v.reshape(n, width).astype(bf16)
    qkv_gl = sum(dot(g, qkv_u[:, i], 1, 1) for i, g in enumerate((grad_q, grad_k, grad_v)))
    attn_in_part = (
        dot(grad_q, w_a[0], 1, 1)
        + dot(grad_k, w_a[1], 1, 1)
        + dot(grad_v, w_b[0], 1, 1)
        + dot(two_parts(qkv_gl, 1), twice(qkv_d, 1), 1, 1)
    )
    normed_half, inverse_half = layer_stats(x_half)
    input_grad = grad_after + norm_back(
        normed_half, inverse_half, sum_halves(attn_in_part) * (1.0 + scale_a)
    )
    input_grad = share_halves(input_grad)

    part_r = R // groups
    blocks = lax.axis_size(W) * lax.axis_size(C)
    ranges = slot_ranges(groups, heads)

    def by_rank(*values):
        joined = jnp.concatenate(values, axis=1)
        sent = joined.reshape(groups, part_r, joined.shape[1])
        return lax.all_to_all(sent, T, 0, 0, tiled=True)

    def slots_to_heads(got):
        return jnp.concatenate(
            [got[t][:, s * HD : (s + m) * HD] for t, (s, m) in enumerate(ranges)], axis=1
        )

    def hidden_to_full(got):
        return jnp.concatenate([got[t] for t in range(groups)], axis=1)

    def finish(values):
        sizes = [v.shape[1] // blocks for v in values]
        payload = jnp.concatenate([v.reshape(part_r, blocks, -1) for v in values], axis=2)
        payload = payload.transpose(1, 0, 2)
        mark = jnp.full((blocks, part_r, 1), 0.0, f32) + index.astype(f32)
        got = lax.all_to_all(jnp.concatenate([payload, mark], axis=2), (W, C), 0, 0, tiled=True)
        owner = got[:, 0, -1]
        chosen = (owner[None, :] == jnp.arange(adapters, dtype=f32)[:, None]).astype(f32)
        table = jnp.einsum("as,srk->ark", chosen, got[:, :, :-1], precision=full_precision)
        out, at = [], 0
        for size in sizes:
            out.append(table[:, :, at : at + size])
            at += size
        return out

    lat_cols = [proj_lat.T, cross_lat.T, point_lat.T, inv_gl.T, query_gl.T, kv_gl.T]
    got = jnp.sum(by_rank(*lat_cols), axis=0)
    proj_s, cross_s, point_s, inv_s, query_s, kv_s = (
        got[:, i * n : (i + 1) * n] if i < 5 else got[:, 5 * n :] for i in range(6)
    )
    qkv_s = jnp.sum(by_rank(qkv_gl.T), axis=0)

    def thin_sum(latent, values):
        return outer_sum(latent.T, values)

    low_caption = caption[0]
    early = [
        outer_sum(cross_gl, mix),
        outer_sum(query_lat, grad_query),
        outer_sum(kv_lat, grad_kv[:, :width]),
        outer_sum(kv_lat, grad_kv[:, width:]),
        outer_sum(point_gl, gated[0]),
        outer_sum(point_gl, gated[1]),
    ] + [outer_sum(inv_lat, g) for g in grad_pre]
    got = by_rank(*early)
    pieces, at = [], 0
    for v in early:
        pieces.append(got[:, :, at : at + v.shape[1]])
        at += v.shape[1]
    cross_down_g, query_up_g, key_up_g, value_up_g = (slots_to_heads(p) for p in pieces[:4])
    point_down_g = hidden_to_full(jnp.concatenate(pieces[4:6], axis=2))
    inv_up_g = [hidden_to_full(jnp.concatenate(pieces[i : i + 2], axis=2)) for i in (6, 8)]
    first = finish(
        [
            thin_sum(cross_s, grad_cross_low),
            thin_sum(point_s, grad_ffn),
            thin_sum(inv_s, ffn_in),
            thin_sum(query_s, cross_in),
            thin_sum(kv_s, low_caption),
            cross_down_g,
            query_up_g,
            key_up_g,
            value_up_g,
            point_down_g,
        ]
        + inv_up_g
    )
    late = [outer_sum(proj_gl, mixed)] + [
        outer_sum(qkv_lat, g) for g in (grad_q, grad_k, grad_v)
    ]
    got = by_rank(*late)
    late = [slots_to_heads(got[:, :, i * width : (i + 1) * width]) for i in range(4)]
    second = finish([thin_sum(proj_s, grad_attn), thin_sum(qkv_s, attn_in)] + late)

    def down_of(t):
        return t.transpose(0, 2, 1)

    return (
        output.reshape(tokens.shape),
        input_grad.reshape(tokens.shape),
        down_of(second[1]),
        jnp.stack(second[3:6], axis=2),
        down_of(second[2]),
        second[0],
        down_of(first[3]),
        first[6],
        down_of(first[4]),
        jnp.stack(first[7:9], axis=2),
        down_of(first[5]),
        first[0],
        down_of(first[2]),
        jnp.stack(first[10:12], axis=2),
        down_of(first[9]),
        first[1],
    )


def solution(mesh):
    down = P(None, (W, C), T)
    up3 = P(None, T, (W, C))
    up4 = P(None, T, None, (W, C))
    rows = P(W, C)
    return jax.shard_map(
        shards,
        mesh=mesh,
        in_specs=(
            rows, rows, P(W), P(W), P(W), rows,
            P(W), P(None, W), P(W), P(W), P(None, W),
            P(W, None, T), P(None, None, None, T), P(T, W),
        )
        + (P(),) * 14,
        out_specs=(
            rows, rows, down, up4, down, up3, down, up3, down, up4, down, up3, down, up4, down, up3,
        ),
        check_vma=False,
    )
```

profile of v0, /device:TPU:0, one launch (start us, length us, event | category | flops | bytes accessed | tf_op | source)
XLA Modules:
  0.0 1025.3 jit_solution(10912514719082224136)
XLA Ops:
  25.9 9.7 fusion.317
  154.8 14.8 %collective-permute-done.45 = bf16[560,700]{1,0:T(8,128)(2,1)} collective-permute-done((bf16[560,700]{1,0:T(8,128)(2,1)S(1)}, bf16[560,700]{1,0:T(8,128)(2,1)}, u32[]{:S(2)}, u32[]{:S(2)}) %collective-permute-start.45) | collective-permute-done | bytes 784032 | tf_op jit(solution)/shard_map/ppermute | solution.py:45
  174.3 10.6 %collective-permute-done.2 = bf16[560,576]{1,0:T(8,128)(2,1)S(1)} collective-permute-done((bf16[560,576]{1,0:T(8,128)(2,1)}, bf16[560,576]{1,0:T(8,128)(2,1)S(1)}, u32[]{:S(2)}, u32[]{:S(2)}) %collective-permute-start.2) | collective-permute-done | bytes 645152 | tf_op jit(solution)/shard_map/ppermute | solution.py:45
  190.6 9.8 collective-permute-done.8
  201.9 13.8 %collective-permute-done.23 = bf16[560,576]{1,0:T(8,128)(2,1)S(1)} collective-permute-done((bf16[560,576]{1,0:T(8,128)(2,1)}, bf16[560,576]{1,0:T(8,128)(2,1)S(1)}, u32[]{:S(2)}, u32[]{:S(2)}) %collective-permute-start.23) | collective-permute-done | bytes 645152 | tf_op jit(solution)/shard_map/ppermute | solution.py:45
  218.1 12.9 %collective-permute-done.4 = bf16[560,576]{1,0:T(8,128)(2,1)S(1)} collective-permute-done((bf16[560,576]{1,0:T(8,128)(2,1)S(1)}, bf16[560,576]{1,0:T(8,128)(2,1)S(1)}, u32[]{:S(2)}, u32[]{:S(2)}) %collective-permute-start.4) | collective-permute-done | bytes 645152 | tf_op jit(solution)/shard_map/ppermute | solution.py:45
  236.7 9.6 collective-permute-done.10
  258.0 25.9 %collective-permute-done.9 = bf16[560,576]{1,0:T(8,128)(2,1)} collective-permute-done((bf16[560,576]{1,0:T(8,128)(2,1)}, bf16[560,576]{1,0:T(8,128)(2,1)}, u32[]{:S(2)}, u32[]{:S(2)}) %collective-permute-start.9) | collective-permute-done | bytes 645152 | tf_op jit(solution)/shard_map/ppermute | solution.py:46
  329.8 11.6 %collective-permute-done.25 = bf16[560,576]{1,0:T(8,128)(2,1)S(1)} collective-permute-done((bf16[560,576]{1,0:T(8,128)(2,1)S(1)}, bf16[560,576]{1,0:T(8,128)(2,1)S(1)}, u32[]{:S(2)}, u32[]{:S(2)}) %collective-permute-start.25) | collective-permute-done | bytes 645152 | tf_op jit(solution)/shard_map/ppermute | solution.py:45
  342.8 13.5 %collective-permute-done.19 = bf16[560,576]{1,0:T(8,128)(2,1)S(1)} collective-permute-done((bf16[560,576]{1,0:T(8,128)(2,1)}, bf16[560,576]{1,0:T(8,128)(2,1)S(1)}, u32[]{:S(2)}, u32[]{:S(2)}) %collective-permute-start.19) | collective-permute-done | bytes 645152 | tf_op jit(solution)/shard_map/ppermute | solution.py:45
  358.8 7.0 collective-permute-done.18
  367.0 14.1 %collective-permute-done.26 = bf16[560,576]{1,0:T(8,128)(2,1)S(1)} collective-permute-done((bf16[560,576]{1,0:T(8,128)(2,1)S(1)}, bf16[560,576]{1,0:T(8,128)(2,1)S(1)}, u32[]{:S(2)}, u32[]{:S(2)}) %collective-permute-start.26) | collective-permute-done | bytes 645152 | tf_op jit(solution)/shard_map/ppermute | solution.py:46
  382.3 13.5 %collective-permute-done.20 = bf16[560,576]{1,0:T(8,128)(2,1)S(1)} collective-permute-done((bf16[560,576]{1,0:T(8,128)(2,1)S(1)}, bf16[560,576]{1,0:T(8,128)(2,1)S(1)}, u32[]{:S(2)}, u32[]{:S(2)}) %collective-permute-start.20) | collective-permute-done | bytes 645152 | tf_op jit(solution)/shard_map/ppermute | solution.py:46
  397.2 9.8 collective-permute-done.14
  415.4 8.5 collective-permute-done.27
  466.2 8.6 collective-permute-done.42
  476.2 16.8 %collective-permute-done.49 = bf16[560,700]{1,0:T(8,128)(2,1)S(1)} collective-permute-done((bf16[560,700]{1,0:T(8,128)(2,1)}, bf16[560,700]{1,0:T(8,128)(2,1)S(1)}, u32[]{:S(2)}, u32[]{:S(2)}) %collective-permute-start.49) | collective-permute-done | bytes 784032 | tf_op jit(solution)/shard_map/ppermute | solution.py:45
  503.7 18.4 %collective-permute-done.30 = bf16[256,2240]{0,1:T(8,128)(2,1)S(1)} collective-permute-done((bf16[256,2240]{0,1:T(8,128)(2,1)S(1)}, bf16[256,2240]{0,1:T(8,128)(2,1)S(1)}, u32[]{:S(2)}, u32[]{:S(2)}) %collective-permute-start.30) | collective-permute-done | bytes 1146912 | tf_op jit(solution)/shard_map/ppermute | solution.py:63
  527.7 10.9 %collective-permute-done.43 = bf16[560,700]{1,0:T(8,128)(2,1)S(1)} collective-permute-done((bf16[560,700]{1,0:T(8,128)(2,1)S(1)}, bf16[560,700]{1,0:T(8,128)(2,1)S(1)}, u32[]{:S(2)}, u32[]{:S(2)}) %collective-permute-start.43) | collective-permute-done | bytes 784032 | tf_op jit(solution)/shard_map/ppermute | solution.py:46
  539.6 16.4 %collective-permute-done.50 = bf16[560,700]{1,0:T(8,128)(2,1)S(1)} collective-permute-done((bf16[560,700]{1,0:T(8,128)(2,1)S(1)}, bf16[560,700]{1,0:T(8,128)(2,1)S(1)}, u32[]{:S(2)}, u32[]{:S(2)}) %collective-permute-start.50) | collective-permute-done | bytes 784032 | tf_op jit(solution)/shard_map/ppermute | solution.py:46
  567.0 5.9 multiply_convert_fusion.19
  586.1 6.0 multiply_convert_fusion.17
  620.4 7.2 multiply_convert_fusion.13
  644.8 7.1 multiply_convert_fusion.16
  741.1 22.6 %collective-permute-done.56 = bf16[256,2240]{0,1:T(8,128)(2,1)S(1)} collective-permute-done((bf16[256,2240]{0,1:T(8,128)(2,1)S(1)}, bf16[256,2240]{0,1:T(8,128)(2,1)S(1)}, u32[]{:S(2)}, u32[]{:S(2)}) %collective-permute-start.56) | collective-permute-done | bytes 1146912 | tf_op jit(solution)/shard_map/ppermute | solution.py:63
  764.4 23.1 %collective-permute-done.52 = bf16[256,2240]{0,1:T(8,128)(2,1)S(1)} collective-permute-done((bf16[256,2240]{0,1:T(8,128)(2,1)S(1)}, bf16[256,2240]{0,1:T(8,128)(2,1)S(1)}, u32[]{:S(2)}, u32[]{:S(2)}) %collective-permute-start.52) | collective-permute-done | bytes 1146912 | tf_op jit(solution)/shard_map/ppermute | solution.py:63
  823.2 8.8 collective-permute-done.65
  875.8 6.8 collective-permute-done.59
  885.4 6.8 maximum_select_fusion
  892.3 6.3 copy.279
  966.7 16.6 %collective-permute-done.63 = bf16[256,2240]{0,1:T(8,128)(2,1)} collective-permute-done((bf16[256,2240]{0,1:T(8,128)(2,1)}, bf16[256,2240]{0,1:T(8,128)(2,1)}, u32[]{:S(2)}, u32[]{:S(2)}) %collective-permute-start.63) | collective-permute-done | bytes 1146912 | tf_op jit(solution)/shard_map/ppermute | solution.py:63
  1019.0 6.1 copy.304
  (1161 shorter events, 638.8 us)
Async XLA Ops:
  5.5 123.3 %collective-permute-start = (bf16[560,576]{1,0:T(8,128)(2,1)}, bf16[560,576]{1,0:T(8,128)(2,1)}, u32[]{:S(2)}, u32[]{:S(2)}) collective-permute-start(bf16[560,576]{1,0:T(8,128)(2,1)} %get-tuple-element.137), channel_id=1, source_target_pairs={{0,16},{16,24},{24,8},{8,0},{1,17},{17,25},{25,9},{9,1},{2,18},{18... | collective-permute-start | bytes 1935368 | tf_op jit(solution)/shard_map/ppermute | solution.py:45
  12.4 120.0 %collective-permute-start.6 = (bf16[560,576]{1,0:T(8,128)(2,1)}, bf16[560,576]{1,0:T(8,128)(2,1)}, u32[]{:S(2)}, u32[]{:S(2)}) collective-permute-start(bf16[560,576]{1,0:T(8,128)(2,1)} %bitcast_select_fusion.4), channel_id=1, source_target_pairs={{0,16},{16,24},{24,8},{8,0},{1,17},{17,25},{25,9},{9,1},{2,18},{18... | collective-permute-start | bytes 1935368 | tf_op jit(solution)/shard_map/ppermute | solution.py:45
  23.1 111.8 %collective-permute-start.15 = (bf16[560,576]{1,0:T(8,128)(2,1)}, bf16[560,576]{1,0:T(8,128)(2,1)}, u32[]{:S(2)}, u32[]{:S(2)}) collective-permute-start(bf16[560,576]{1,0:T(8,128)(2,1)} %get-tuple-element.150), channel_id=1, source_target_pairs={{0,16},{16,24},{24,8},{8,0},{1,17},{17,25},{25,9},{9,1},{2,18},{18... | collective-permute-start | bytes 1935368 | tf_op jit(solution)/shard_map/ppermute | solution.py:45
  25.8 112.5 %collective-permute-start.21 = (bf16[560,576]{1,0:T(8,128)(2,1)}, bf16[560,576]{1,0:T(8,128)(2,1)}, u32[]{:S(2)}, u32[]{:S(2)}) collective-permute-start(bf16[560,576]{1,0:T(8,128)(2,1)} %bitcast_select_fusion.2), channel_id=1, source_target_pairs={{0,16},{16,24},{24,8},{8,0},{1,17},{17,25},{25,9},{9,1},{2,18},{18... | collective-permute-start | bytes 1935368 | tf_op jit(solution)/shard_map/ppermute | solution.py:45
  38.0 103.0 %collective-permute-start.32 = (bf16[560,700]{1,0:T(8,128)(2,1)}, bf16[560,700]{1,0:T(8,128)(2,1)}, u32[]{:S(2)}, u32[]{:S(2)}) collective-permute-start(bf16[560,700]{1,0:T(8,128)(2,1)} %get-tuple-element.335), channel_id=1, source_target_pairs={{0,16},{16,24},{24,8},{8,0},{1,17},{17,25},{25,9},{9,1},{2,18},{18... | collective-permute-start | bytes 2352008 | tf_op jit(solution)/shard_map/ppermute | solution.py:45
  134.9 51.5 %collective-permute-start.1 = (bf16[560,576]{1,0:T(8,128)(2,1)}, bf16[560,576]{1,0:T(8,128)(2,1)S(1)}, u32[]{:S(2)}, u32[]{:S(2)}) collective-permute-start(bf16[560,576]{1,0:T(8,128)(2,1)} %collective-permute-done), channel_id=1, source_target_pairs={{0,4},{4,0},{1,5},{5,1},{2,6},{6,2},{3,7},{7,3},{8,12},{12,8},{9,1... | collective-permute-start | bytes 1935368 | tf_op jit(solution)/shard_map/ppermute | solution.py:46
  138.4 46.5 %collective-permute-start.2 = (bf16[560,576]{1,0:T(8,128)(2,1)}, bf16[560,576]{1,0:T(8,128)(2,1)S(1)}, u32[]{:S(2)}, u32[]{:S(2)}) collective-permute-start(bf16[560,576]{1,0:T(8,128)(2,1)} %collective-permute-done), channel_id=1, source_target_pairs={{0,16},{16,24},{24,8},{8,0},{1,17},{17,25},{25,9},{9,1},{2,18},{18... | collective-permute-start | bytes 1935368 | tf_op jit(solution)/shard_map/ppermute | solution.py:45
  141.0 59.4 %collective-permute-start.8 = (bf16[560,576]{1,0:T(8,128)(2,1)}, bf16[560,576]{1,0:T(8,128)(2,1)}, u32[]{:S(2)}, u32[]{:S(2)}) collective-permute-start(bf16[560,576]{1,0:T(8,128)(2,1)} %collective-permute-done.6), channel_id=1, source_target_pairs={{0,16},{16,24},{24,8},{8,0},{1,17},{17,25},{25,9},{9,1},{2,18},{18... | collective-permute-start | bytes 1935368 | tf_op jit(solution)/shard_map/ppermute | solution.py:45
  151.2 37.9 %collective-permute-start.22 = (bf16[560,576]{1,0:T(8,128)(2,1)}, bf16[560,576]{1,0:T(8,128)(2,1)S(1)}, u32[]{:S(2)}, u32[]{:S(2)}) collective-permute-start(bf16[560,576]{1,0:T(8,128)(2,1)} %collective-permute-done.21), channel_id=1, source_target_pairs={{0,4},{4,0},{1,5},{5,1},{2,6},{6,2},{3,7},{7,3},{8,12},{12,8},{9,1... | collective-permute-start | bytes 1935368 | tf_op jit(solution)/shard_map/ppermute | solution.py:46
  169.6 46.0 %collective-permute-start.23 = (bf16[560,576]{1,0:T(8,128)(2,1)}, bf16[560,576]{1,0:T(8,128)(2,1)S(1)}, u32[]{:S(2)}, u32[]{:S(2)}) collective-permute-start(bf16[560,576]{1,0:T(8,128)(2,1)} %collective-permute-done.21), channel_id=1, source_target_pairs={{0,16},{16,24},{24,8},{8,0},{1,17},{17,25},{25,9},{9,1},{2,18},{18... | collective-permute-start | bytes 1935368 | tf_op jit(solution)/shard_map/ppermute | solution.py:45
  184.9 48.5 %collective-permute-start.3 = (bf16[560,576]{1,0:T(8,128)(2,1)S(1)}, bf16[560,576]{1,0:T(8,128)(2,1)S(1)}, u32[]{:S(2)}, u32[]{:S(2)}) collective-permute-start(bf16[560,576]{1,0:T(8,128)(2,1)S(1)} %collective-permute-done.2), channel_id=1, source_target_pairs={{0,4},{4,0},{1,5},{5,1},{2,6},{6,2},{3,7},{7,3},{8,12},{12,8},{9,1... | collective-permute-start | bytes 1935368 | tf_op jit(solution)/shard_map/ppermute | solution.py:46
  186.4 44.6 %collective-permute-start.4 = (bf16[560,576]{1,0:T(8,128)(2,1)S(1)}, bf16[560,576]{1,0:T(8,128)(2,1)S(1)}, u32[]{:S(2)}, u32[]{:S(2)}) collective-permute-start(bf16[560,576]{1,0:T(8,128)(2,1)S(1)} %collective-permute-done.2), channel_id=1, source_target_pairs={{0,16},{16,24},{24,8},{8,0},{1,17},{17,25},{25,9},{9,1},{2,18},{18... | collective-permute-start | bytes 1935368 | tf_op jit(solution)/shard_map/ppermute | solution.py:45
  189.1 47.1 %collective-permute-start.7 = (bf16[560,576]{1,0:T(8,128)(2,1)}, bf16[560,576]{1,0:T(8,128)(2,1)S(1)}, u32[]{:S(2)}, u32[]{:S(2)}) collective-permute-start(bf16[560,576]{1,0:T(8,128)(2,1)} %collective-permute-done.6), channel_id=1, source_target_pairs={{0,4},{4,0},{1,5},{5,1},{2,6},{6,2},{3,7},{7,3},{8,12},{12,8},{9,1... | collective-permute-start | bytes 1935368 | tf_op jit(solution)/shard_map/ppermute | solution.py:46
  200.4 120.8 %collective-permute-start.16 = (bf16[560,576]{1,0:T(8,128)(2,1)}, bf16[560,576]{1,0:T(8,128)(2,1)}, u32[]{:S(2)}, u32[]{:S(2)}) collective-permute-start(bf16[560,576]{1,0:T(8,128)(2,1)} %collective-permute-done.15), channel_id=1, source_target_pairs={{0,4},{4,0},{1,5},{5,1},{2,6},{6,2},{3,7},{7,3},{8,12},{12,8},{9,1... | collective-permute-start | bytes 1935368 | tf_op jit(solution)/shard_map/ppermute | solution.py:46
  233.4 89.1 %collective-permute-start.17 = (bf16[560,576]{1,0:T(8,128)(2,1)}, bf16[560,576]{1,0:T(8,128)(2,1)}, u32[]{:S(2)}, u32[]{:S(2)}) collective-permute-start(bf16[560,576]{1,0:T(8,128)(2,1)} %collective-permute-done.15), channel_id=1, source_target_pairs={{0,16},{16,24},{24,8},{8,0},{1,17},{17,25},{25,9},{9,1},{2,18},{18... | collective-permute-start | bytes 1935368 | tf_op jit(solution)/shard_map/ppermute | solution.py:45
  236.2 89.9 %collective-permute-start.33 = (bf16[560,700]{1,0:T(8,128)(2,1)}, bf16[560,700]{1,0:T(8,128)(2,1)}, u32[]{:S(2)}, u32[]{:S(2)}) collective-permute-start(bf16[560,700]{1,0:T(8,128)(2,1)} %collective-permute-done.32), channel_id=1, source_target_pairs={{0,4},{4,0},{1,5},{5,1},{2,6},{6,2},{3,7},{7,3},{8,12},{12,8},{9,1... | collective-permute-start | bytes 2352008 | tf_op jit(solution)/shard_map/ppermute | solution.py:46
  246.3 37.5 %collective-permute-start.9 = (bf16[560,576]{1,0:T(8,128)(2,1)}, bf16[560,576]{1,0:T(8,128)(2,1)}, u32[]{:S(2)}, u32[]{:S(2)}) collective-permute-start(bf16[560,576]{1,0:T(8,128)(2,1)} %collective-permute-done.8), channel_id=1, source_target_pairs={{0,4},{4,0},{1,5},{5,1},{2,6},{6,2},{3,7},{7,3},{8,12},{12,8},{9,1... | collective-permute-start | bytes 1935368 | tf_op jit(solution)/shard_map/ppermute | solution.py:46
  250.0 43.2 %collective-permute-start.11 = (bf16[560,576]{1,0:T(8,128)(2,1)S(1)}, bf16[560,576]{1,0:T(8,128)(2,1)}, u32[]{:S(2)}, u32[]{:S(2)}) collective-permute-start(bf16[560,576]{1,0:T(8,128)(2,1)S(1)} %collective-permute-done.10), channel_id=1, source_target_pairs={{0,4},{4,0},{1,5},{5,1},{2,6},{6,2},{3,7},{7,3},{8,12},{12,8},{9,1... | collective-permute-start | bytes 1935368 | tf_op jit(solution)/shard_map/ppermute | solution.py:46
  283.9 127.5 %collective-permute-start.34 = (bf16[560,700]{1,0:T(8,128)(2,1)}, bf16[560,700]{1,0:T(8,128)(2,1)}, u32[]{:S(2)}, u32[]{:S(2)}) collective-permute-start(bf16[560,700]{1,0:T(8,128)(2,1)} %collective-permute-done.32), channel_id=1, source_target_pairs={{0,16},{16,24},{24,8},{8,0},{1,17},{17,25},{25,9},{9,1},{2,18},{18... | collective-permute-start | bytes 2352008 | tf_op jit(solution)/shard_map/ppermute | solution.py:45
  328.3 85.9 %collective-permute-start.39 = (bf16[560,700]{1,0:T(8,128)(2,1)}, bf16[560,700]{1,0:T(8,128)(2,1)S(1)}, u32[]{:S(2)}, u32[]{:S(2)}) collective-permute-start(bf16[560,700]{1,0:T(8,128)(2,1)} %collective-permute-done.38), channel_id=1, source_target_pairs={{0,4},{4,0},{1,5},{5,1},{2,6},{6,2},{3,7},{7,3},{8,12},{12,8},{9,1... | collective-permute-start | bytes 2352008 | tf_op jit(solution)/shard_map/ppermute | solution.py:46
  356.9 38.9 %collective-permute-start.20 = (bf16[560,576]{1,0:T(8,128)(2,1)S(1)}, bf16[560,576]{1,0:T(8,128)(2,1)S(1)}, u32[]{:S(2)}, u32[]{:S(2)}) collective-permute-start(bf16[560,576]{1,0:T(8,128)(2,1)S(1)} %collective-permute-done.19), channel_id=1, source_target_pairs={{0,4},{4,0},{1,5},{5,1},{2,6},{6,2},{3,7},{7,3},{8,12},{12,8},{9,1... | collective-permute-start | bytes 1935368 | tf_op jit(solution)/shard_map/ppermute | solution.py:46
  365.8 84.6 %collective-permute-start.40 = (bf16[560,700]{1,0:T(8,128)(2,1)}, bf16[560,700]{1,0:T(8,128)(2,1)}, u32[]{:S(2)}, u32[]{:S(2)}) collective-permute-start(bf16[560,700]{1,0:T(8,128)(2,1)} %collective-permute-done.38), channel_id=1, source_target_pairs={{0,16},{16,24},{24,8},{8,0},{1,17},{17,25},{25,9},{9,1},{2,18},{18... | collective-permute-start | bytes 2352008 | tf_op jit(solution)/shard_map/ppermute | solution.py:45
  395.8 56.8 %collective-permute-start.46 = (bf16[560,700]{1,0:T(8,128)(2,1)}, bf16[560,700]{1,0:T(8,128)(2,1)}, u32[]{:S(2)}, u32[]{:S(2)}) collective-permute-start(bf16[560,700]{1,0:T(8,128)(2,1)} %collective-permute-done.45), channel_id=1, source_target_pairs={{0,4},{4,0},{1,5},{5,1},{2,6},{6,2},{3,7},{7,3},{8,12},{12,8},{9,1... | collective-permute-start | bytes 2352008 | tf_op jit(solution)/shard_map/ppermute | solution.py:46
  414.2 40.1 %collective-permute-start.47 = (bf16[560,700]{1,0:T(8,128)(2,1)}, bf16[560,700]{1,0:T(8,128)(2,1)}, u32[]{:S(2)}, u32[]{:S(2)}) collective-permute-start(bf16[560,700]{1,0:T(8,128)(2,1)} %collective-permute-done.45), channel_id=1, source_target_pairs={{0,16},{16,24},{24,8},{8,0},{1,17},{17,25},{25,9},{9,1},{2,18},{18... | collective-permute-start | bytes 2352008 | tf_op jit(solution)/shard_map/ppermute | solution.py:45
  450.4 44.1 %collective-permute-start.29 = (bf16[256,2240]{0,1:T(8,128)(2,1)S(1)}, bf16[256,2240]{0,1:T(8,128)(2,1)S(1)}, u32[]{:S(2)}, u32[]{:S(2)}) collective-permute-start(bf16[256,2240]{0,1:T(8,128)(2,1)S(1)} %dynamic-slice_convert_fusion.4), channel_id=1, source_target_pairs={{0,1},{1,0},{2,3},{3,2},{4,5},{5,4},{6,7},{7,6},{8,9},{9,8},{10,11... | collective-permute-start | bytes 3440648 | tf_op jit(solution)/shard_map/ppermute | solution.py:59
  454.3 38.7 %collective-permute-start.49 = (bf16[560,700]{1,0:T(8,128)(2,1)}, bf16[560,700]{1,0:T(8,128)(2,1)S(1)}, u32[]{:S(2)}, u32[]{:S(2)}) collective-permute-start(bf16[560,700]{1,0:T(8,128)(2,1)} %collective-permute-done.47), channel_id=1, source_target_pairs={{0,16},{16,24},{24,8},{8,0},{1,17},{17,25},{25,9},{9,1},{2,18},{18... | collective-permute-start | bytes 2352008 | tf_op jit(solution)/shard_map/ppermute | solution.py:45
  474.8 51.9 %collective-permute-start.37 = (bf16[560,700]{1,0:T(8,128)(2,1)S(1)}, bf16[560,700]{1,0:T(8,128)(2,1)S(1)}, u32[]{:S(2)}, u32[]{:S(2)}) collective-permute-start(bf16[560,700]{1,0:T(8,128)(2,1)S(1)} %collective-permute-done.36), channel_id=1, source_target_pairs={{0,4},{4,0},{1,5},{5,1},{2,6},{6,2},{3,7},{7,3},{8,12},{12,8},{9,1... | collective-permute-start | bytes 2352008 | tf_op jit(solution)/shard_map/ppermute | solution.py:46
  493.0 45.5 %collective-permute-start.43 = (bf16[560,700]{1,0:T(8,128)(2,1)S(1)}, bf16[560,700]{1,0:T(8,128)(2,1)S(1)}, u32[]{:S(2)}, u32[]{:S(2)}) collective-permute-start(bf16[560,700]{1,0:T(8,128)(2,1)S(1)} %collective-permute-done.42), channel_id=1, source_target_pairs={{0,4},{4,0},{1,5},{5,1},{2,6},{6,2},{3,7},{7,3},{8,12},{12,8},{9,1... | collective-permute-start | bytes 2352008 | tf_op jit(solution)/shard_map/ppermute | solution.py:46
  494.5 61.5 %collective-permute-start.50 = (bf16[560,700]{1,0:T(8,128)(2,1)S(1)}, bf16[560,700]{1,0:T(8,128)(2,1)S(1)}, u32[]{:S(2)}, u32[]{:S(2)}) collective-permute-start(bf16[560,700]{1,0:T(8,128)(2,1)S(1)} %collective-permute-done.49), channel_id=1, source_target_pairs={{0,4},{4,0},{1,5},{5,1},{2,6},{6,2},{3,7},{7,3},{8,12},{12,8},{9,1... | collective-permute-start | bytes 2352008 | tf_op jit(solution)/shard_map/ppermute | solution.py:46
  682.5 53.1 %collective-permute-start.51 = (bf16[256,2240]{0,1:T(8,128)(2,1)}, bf16[256,2240]{0,1:T(8,128)(2,1)}, u32[]{:S(2)}, u32[]{:S(2)}) collective-permute-start(bf16[256,2240]{0,1:T(8,128)(2,1)} %dynamic-slice_convert_fusion.3), channel_id=1, source_target_pairs={{0,1},{1,0},{2,3},{3,2},{4,5},{5,4},{6,7},{7,6},{8,9},{9,8},{10,11... | collective-permute-start | bytes 3440648 | tf_op jit(solution)/shard_map/ppermute | solution.py:59
  737.7 49.8 %collective-permute-start.52 = (bf16[256,2240]{0,1:T(8,128)(2,1)S(1)}, bf16[256,2240]{0,1:T(8,128)(2,1)S(1)}, u32[]{:S(2)}, u32[]{:S(2)}) collective-permute-start(bf16[256,2240]{0,1:T(8,128)(2,1)S(1)} %add_convert_fusion.5), channel_id=1, source_target_pairs={{0,2},{1,3},{2,0},{3,1},{4,6},{5,7},{6,4},{7,5},{8,10},{9,11},{10,... | collective-permute-start | bytes 3440648 | tf_op jit(solution)/shard_map/ppermute | solution.py:63
  793.2 92.2 %collective-permute-start.53 = (f32[256,2240]{0,1:T(8,128)}, f32[256,2240]{0,1:T(8,128)}, u32[]{:S(2)}, u32[]{:S(2)}) collective-permute-start(f32[256,2240]{0,1:T(8,128)} %get-tuple-element.152), channel_id=1, source_target_pairs={{0,1},{1,0},{2,3},{3,2},{4,5},{5,4},{6,7},{7,6},{8,9},{9,8},{10,11... | collective-permute-start | bytes 6881288 | tf_op jit(solution)/shard_map/ppermute | solution.py:70
  (339 other events, 4569.0 us)
where the time goes:
time: 1040 us; the launch traced here: 1030 us
  waiting for transfers between devices  354 us (34%)
  local copies, waits for them, and re-layouts  255 us (25%)
  matrix products  180 us (17%)
  other arithmetic  134 us (13%)
  starting transfers between devices  95 us (9%)
    dot_general x88, matrix products, dot(): lax.dot_general(a, b, (((ca,), (cb,)), ((), ())), preferred_element_type=...  157 us
    ppermute x21, waiting for transfers between devices, gather_pair(): moving = lax.ppermute(moving, W, ring_pairs(n))  127 us
    ppermute x21, waiting for transfers between devices, gather_pair(): other = lax.ppermute(moving, C, swap_pairs(2, 1))  97.9 us
    ppermute x6, waiting for transfers between devices, sum_halves(): lax.ppermute(low, T, swap_pairs(groups, distance)).astype(f32)  97.4 us
    unnamed x625, local copies, waits for them, and re-layouts  43.3 us
    ppermute x21, starting transfers between devices, gather_pair(): moving = lax.ppermute(moving, W, ring_pairs(n))  35 us
    dynamic_update_slice x21, local copies, waits for them, and re-layouts, gather_pair(): buf = lax.dynamic_update_slice(buf, moving[None], (c, at, 0))  30.9 us
    ppermute x21, starting transfers between devices, gather_pair(): other = lax.ppermute(moving, C, swap_pairs(2, 1))  22.9 us
  transfers between devices with their start and end apart: 72, of which 33 were waited for; matrix products, arithmetic and copies ran while one was open for 39% of the time, Pallas kernels for 0%

commit v1 on v0

v1 whole, which is shorter than its diff:
```python
import functools
import jax
import jax.numpy as jnp
from jax import lax
from jax.experimental import pallas as pl
from jax.experimental.pallas import tpu as pltpu
from jax.sharding import PartitionSpec as P

W, C, T = "weight", "context", "tensor"
HD = 32
LANES = 128
bf16, f32 = jnp.bfloat16, jnp.float32
full_precision = lax.Precision.HIGHEST
norm_eps = 1e-06
attention_epsilon = 1e-06
masked_score = -1000000000.0
big = pltpu.CompilerParams(vmem_limit_bytes=58 * 1024 * 1024)


def shape(dims, dtype):
    return jax.ShapeDtypeStruct(dims, dtype)


def mm(a, b, ca=1, cb=0):
    return lax.dot_general(a, b, (((ca,), (cb,)), ((), ())), preferred_element_type=f32)


def two(pair):
    high = pair.astype(bf16)
    rest = (pair - high.astype(f32)).astype(bf16)
    lane = lax.broadcasted_iota(jnp.int32, pair.shape, 1)
    return jnp.where(lane < pair.shape[1] // 2, high.astype(f32), rest.astype(f32)).astype(bf16)


def split(values):
    high = values.astype(bf16)
    return high, (values - high.astype(f32)).astype(bf16)


def mm3(a, b, ca=1, cb=0):
    ah, al = split(a)
    bh, bl = split(b)
    return mm(ah, bh, ca, cb) + mm(ah, bl, ca, cb) + mm(al, bh, ca, cb)


def head_mask(width):
    row = lax.broadcasted_iota(jnp.int32, (width, width), 0) // HD
    col = lax.broadcasted_iota(jnp.int32, (width, width), 1) // HD
    return (row == col).astype(f32)


def head_total(values, mask):
    high, low = split(values)
    low_mask = mask.astype(bf16)
    return mm(high, low_mask) + mm(low, low_mask)


def squeeze_heads(square, mask):
    kept = square * mask
    total = kept[:HD]
    for h in range(1, kept.shape[0] // HD):
        total = total + kept[h * HD : (h + 1) * HD]
    return total


def spread_heads(state, width, mask):
    return jnp.concatenate([state] * (width // HD), axis=0) * mask


def sigmoid(values):
    return 1.0 / (1.0 + jnp.exp(-values))


def row_stats(values):
    center = values - jnp.mean(values, axis=-1, keepdims=True)
    inverse = lax.rsqrt(jnp.mean(center * center, axis=-1, keepdims=True) + norm_eps)
    return center * inverse, inverse


def put(out, rows, values):
    width = values.shape[1]
    out[rows, :width] = values.astype(out.dtype)
    if width < out.shape[1]:
        out[rows, width:] = jnp.zeros((values.shape[0], out.shape[1] - width), out.dtype)


everything = slice(None)


def attn_front(w, x, mods, d2, u2, a_out, q_out, k_out, v_out, lat_out, st_out):
    n = x.shape[0]
    step = 64

    def norm(i, carry):
        at = pl.ds(pl.multiple_of(i * step, step), step)
        normed, unused = row_stats(x[at, :].astype(f32))
        a_out[at, :] = (normed * (1.0 + mods[1:2, :]) + mods[0:1, :]).astype(bf16)
        return carry

    lax.fori_loop(0, n // step, norm, 0)
    a = a_out[...]
    lat = mm(a, d2[...])
    lat_out[...] = lat
    pair = two(lat)
    for i, (out, weight, j) in enumerate(((q_out, w[0], 0), (k_out, w[0], 1), (v_out, w[1], 0))):
        out[...] = mm(a, weight.take(j)) + mm(pair, u2[i])
    keys = jnp.maximum(k_out[...], 0.0)
    width = keys.shape[1]
    st_out[:HD, :] = squeeze_heads(mm3(v_out[...], keys, 0, 0), head_mask(width))
    st_out[HD:, :] = jnp.broadcast_to(jnp.sum(keys, axis=0, keepdims=True), (8, width))


def put_partial(low, lat_pair, w, u2, mine, away):
    half = mine.shape[0]
    put(mine, everything, mm(low[:half], w, 1, 1) + mm(lat_pair[:half], u2))
    put(away, everything, mm(low[half:], w, 1, 1) + mm(lat_pair[half:], u2))


def attn_back(w, q, st1, st2, owned, d2, u2, ratio_out, den_out, mixed_out, lat_out, mine, away):
    st = st1[...] + st2[...]
    width = q.shape[1]
    mask = head_mask(width)
    queries = jnp.maximum(q[...], 0.0)
    numer = mm3(queries, spread_heads(st[:HD], width, mask), 1, 1)
    den = head_total(queries * st[HD : HD + 1], mask) + attention_epsilon
    ratio = numer / den
    ratio_out[...] = ratio
    den_out[...] = den
    mixed = (ratio * owned[...]).astype(bf16)
    mixed_out[...] = mixed
    lat = mm(mixed, d2[...])
    lat_out[...] = lat
    put_partial(mixed, two(lat), w[0].take(0), u2[...], mine, away)


def caption_rows(w, cap, d2, u2, kv_out, lat_out):
    lat = mm(cap[...], d2[...])
    lat_out[...] = lat
    pair = two(lat)
    kv_out[0] = (mm(cap[...], w[0].take(0)) + mm(pair, u2[0])).astype(bf16)
    kv_out[1] = (mm(cap[...], w[1].take(0)) + mm(pair, u2[1])).astype(bf16)


def lane_groups(width):
    return [(at, min(LANES, width - at)) for at in range(0, width, LANES)]


def only_head(values, j):
    lane = lax.broadcasted_iota(jnp.int32, values.shape, 1) // HD
    return jnp.where(lane == j, values.astype(f32), 0.0).astype(values.dtype)


def cross_fwd(
    w, xo, xt, kv1, kv2, live, owned, qd2, qu2, cd2, cu2,
    q_out, mix_out, qlat_out, clat_out, lse_out, mine, away, keys, vals,
):
    half = xo.shape[0]
    width = q_out.shape[1]
    here = kv1.shape[1]
    for buf, i in ((keys, 0), (vals, 1)):
        buf[:here, :] = kv1[i]
        buf[here:, :] = kv2[i]
    depth = qd2.shape[0]
    weight = w[0].take(0)
    for i, rows in enumerate((xo, xt)):
        at = pl.ds(i * half, half)
        lat = mm(rows[:, :depth], qd2[...])
        qlat_out[at, :] = lat
        q_out[at, :] = (mm(rows[:, :depth], weight) + mm(two(lat), qu2[...])).astype(bf16)

    def block(i, carry):
        at = pl.ds(pl.multiple_of(i * half, half), half)
        for first, size in lane_groups(width):
            cols = slice(first, first + size)
            query = q_out[at, cols]
            total = jnp.zeros((half, size), f32)
            for j in range(size // HD):
                scores = mm(query, only_head(keys[:, cols], j), 1, 1) * HD ** (-0.5)
                scores = jnp.where(live[...] > 0.0, scores, masked_score)
                top = jnp.max(scores, axis=-1, keepdims=True)
                exps = jnp.exp(scores - top)
                tot = jnp.sum(exps, axis=-1, keepdims=True)
                h = first // HD + j
                lse_out[at, h : h + 1] = top + jnp.log(tot)
                probs = (exps * (1.0 / tot)).astype(bf16)
                total = total + mm(probs, only_head(vals[:, cols], j))
            mix_out[at, cols] = (total * owned[:, cols]).astype(bf16)
        return carry

    lax.fori_loop(0, 2, block, 0)
    mix = mix_out[...]
    lat = mm(mix, cd2[...])
    clat_out[...] = lat
    put_partial(mix, two(lat), w[1].take(0), cu2[...], mine, away)


def ffn_front(w, xo, xt, d2, uv, ug, pv, pg, hv, hg, lat_out, u):
    half = xo.shape[0]
    depth = d2.shape[0]
    h = pl.program_id(0)

    @pl.when(h == 0)
    def first():
        u[:half, :] = xo[:, :depth]
        u[half:, :] = xt[:, :depth]
        lat_out[...] = mm(u[...], d2[...])

    pair = two(lat_out[...])
    for weight, up, pre, hid in ((w[0], uv, pv, hv), (w[1], ug, pg, hg)):
        s = mm(u[...], weight.take(h)) + mm(pair, up[0])
        pre[0] = s
        hid[0] = (s * sigmoid(s)).astype(bf16)


def fill_grid(buf, rows, halo, b, c):
    half = rows.shape[0] // 2
    edge = halo.shape[0]
    buf[pl.ds(pl.multiple_of(edge + b * half, edge), half), :] = rows[:half, :].astype(f32)
    buf[pl.ds(pl.multiple_of(edge + (1 - b) * half, edge), half), :] = rows[half:, :].astype(f32)
    zero = jnp.zeros(halo.shape, f32)
    got = halo.astype(f32)
    buf[:edge, :] = jnp.where(c == 0, zero, got)
    buf[buf.shape[0] - edge :, :] = jnp.where(c == 0, got, zero)


def conv_row(buf, taps, r, edge, flip):
    sums = []
    rows = [buf[pl.ds(pl.multiple_of((r + i) * edge, edge), edge), :] for i in range(3)]
    for j in range(3):
        total = None
        for i in range(3):
            k = (2 - i) * 3 + 2 - j if flip else i * 3 + j
            term = rows[i] * taps[k : k + 1, :]
            total = term if total is None else total + term
        sums.append(total)
    cell = lax.broadcasted_iota(jnp.int32, sums[0].shape, 0)
    left = jnp.where(cell == 0, 0.0, pltpu.roll(sums[0], 1, 0))
    right = jnp.where(cell == edge - 1, 0.0, pltpu.roll(sums[2], edge - 1, 0))
    return left + sums[1] + right


def own_first(r, edge, half, b):
    per = half // edge
    return pl.multiple_of(jnp.where(r // per == b, 0, half) + (r % per) * edge, edge)


def ffn_mid(
    w, where, hv, hg, halo, taps, cot, gate, d2, u2,
    gated_out, gcv_out, gcg_out, gffn_out, gl_out, lat_out, mine, away, bv, bg, gg, acc,
):
    h = pl.program_id(0)
    b, c = where[0], where[1]
    n = hv.shape[1]
    half = n // 2
    edge = halo.shape[2]

    @pl.when(h == 0)
    def first():
        gffn_out[...] = (gate[...] * cot[...].astype(f32)).astype(bf16)
        gl_out[...] = mm(gffn_out[...], u2[...], 1, 1)

    fill_grid(bv, hv[0], halo[0, 0], b, c)
    fill_grid(bg, hg[0], halo[0, 1], b, c)
    weight = w[0].take(h)
    gg[...] = mm(gffn_out[...], weight) + mm(two(gl_out[...]), d2[0], 1, 1)

    def row(r, carry):
        v = conv_row(bv, taps[0, 0], r, edge, False)
        g = conv_row(bg, taps[0, 1], r, edge, False)
        sig = sigmoid(g)
        act = g * sig
        at = pl.ds(own_first(r, edge, half, b), edge)
        gated_out[0, at, :] = (v * act).astype(bf16)
        grad = gg[at, :]
        gcv_out[0, at, :] = (grad * act).astype(bf16)
        gcg_out[0, at, :] = (grad * v * (sig * (1.0 + g * (1.0 - sig)))).astype(bf16)
        return carry

    lax.fori_loop(0, n // edge, row, 0)
    gated = gated_out[0]
    part = mm(gated, weight, 1, 1)
    lat = mm(gated, d2[0])

    @pl.when(h == 0)
    def start():
        acc[...] = part
        lat_out[...] = lat

    @pl.when(h == 1)
    def end():
        total = lat_out[...] + lat
        lat_out[...] = total
        full = acc[...] + part + mm(two(total), u2[...])
        put(mine, everything, full[:half])
        put(away, everything, full[half:])


def ffn_back(
    w, where, gcv, gcg, halo, taps, pv, pg, lat, d2, uv, ug,
    gpv_out, gpg_out, up_out, gl_out, mine, away, bv, bg, acc,
):
    h = pl.program_id(0)
    b, c = where[0], where[1]
    n = gcv.shape[1]
    half = n // 2
    edge = halo.shape[2]
    fill_grid(bv, gcv[0], halo[0, 0], b, c)
    fill_grid(bg, gcg[0], halo[0, 1], b, c)

    def row(r, carry):
        at = pl.ds(own_first(r, edge, half, b), edge)
        for i, (buf, pre, out) in enumerate(((bv, pv, gpv_out), (bg, pg, gpg_out))):
            grad = conv_row(buf, taps[0, i], r, edge, True)
            s = pre[0, at, :]
            sig = sigmoid(s)
            out[0, at, :] = (grad * (sig * (1.0 + s * (1.0 - sig)))).astype(bf16)
        return carry

    lax.fori_loop(0, n // edge, row, 0)
    gpv, gpg = gpv_out[0], gpg_out[0]
    part = mm(gpv, w[0].take(h), 1, 1) + mm(gpg, w[1].take(h), 1, 1)
    gl = mm(gpv, uv[0], 1, 1) + mm(gpg, ug[0], 1, 1)
    pair = two(lat[...])
    up_out[0, 0] = mm(pair, gpv, 0, 0)
    up_out[0, 1] = mm(pair, gpg, 0, 0)

    @pl.when(h == 0)
    def start():
        acc[...] = part
        gl_out[...] = gl

    @pl.when(h == 1)
    def end():
        total = gl_out[...] + gl
        gl_out[...] = total
        full = acc[...] + part + mm(two(total), d2[...], 1, 1)
        put(mine, everything, full[:half])
        put(away, everything, full[half:])


def cross_bwd(
    w, go, gt, kv1, kv2, live, owned, qd2, qu2, cd2, cu2, query, lse,
    gq_out, gkv_out, qgl_out, cgl_out, mine, away, keys, vals, gm, gqs,
):
    half = go.shape[0]
    width = query.shape[1]
    here = kv1.shape[1]
    for buf, i in ((keys, 0), (vals, 1)):
        buf[:here, :] = kv1[i]
        buf[here:, :] = kv2[i]
    depth = cu2.shape[1]
    weight = w[1].take(0)
    for i, rows in enumerate((go, gt)):
        at = pl.ds(i * half, half)
        gl = mm(rows[:, :depth], cu2[...], 1, 1)
        cgl_out[at, :] = gl
        grad = mm(rows[:, :depth], weight) + mm(two(gl), cd2[...], 1, 1)
        gm[at, :] = (grad * owned[...]).astype(bf16)
    scale = HD ** (-0.5)

    def block(i, carry):
        at = pl.ds(pl.multiple_of(i * half, half), half)
        for first, size in lane_groups(width):
            cols = slice(first, first + size)
            q_all, g_all = query[at, cols], gm[at, cols]
            grad_q = jnp.zeros((half, size), f32)
            grad_k = jnp.zeros((2 * here, size), f32)
            grad_v = jnp.zeros((2 * here, size), f32)
            for j in range(size // HD):
                key, val = only_head(keys[:, cols], j), only_head(vals[:, cols], j)
                h = first // HD + j
                scores = mm(q_all, key, 1, 1) * scale
                scores = jnp.where(live[...] > 0.0, scores, masked_score)
                probs = jnp.exp(scores - lse[at, h : h + 1])
                grad_p = mm(g_all, val, 1, 1)
                grad_v = grad_v + mm(probs.astype(bf16), only_head(g_all, j), 0, 0)
                inner = jnp.sum(probs * grad_p, axis=-1, keepdims=True)
                grad_s = (probs * (grad_p - inner)).astype(bf16)
                grad_q = grad_q + mm(grad_s, key)
                grad_k = grad_k + mm(grad_s, only_head(q_all, j), 0, 0)
            gqs[at, cols] = grad_q
            for side, new in ((0, grad_k * scale), (1, grad_v)):
                old = jnp.where(i == 0, 0.0, gkv_out[side, :, cols])
                gkv_out[side, :, cols] = old + new
        return carry

    lax.fori_loop(0, 2, block, 0)
    gq = (gqs[...] * scale).astype(bf16)
    gq_out[...] = gq
    gl = mm(gq, qu2[...], 1, 1)
    qgl_out[...] = gl
    pair = two(gl)
    weight = w[0].take(0)
    put(mine, everything, mm(gq[:half], weight, 1, 1) + mm(pair[:half], qd2[...], 1, 1))
    put(away, everything, mm(gq[half:], weight, 1, 1) + mm(pair[half:], qd2[...], 1, 1))


def linear_bwd(
    w, go, gt, q, st1, st2, ratio, den, owned, d2, u2, gq_out, gl_out, st_out, gh,
):
    half = go.shape[0]
    width = q.shape[1]
    depth = u2.shape[1]
    weight = w[0].take(0)
    for i, rows in enumerate((go, gt)):
        at = pl.ds(i * half, half)
        gl = mm(rows[:, :depth], u2[...], 1, 1)
        gl_out[at, :] = gl
        gh[at, :] = (mm(rows[:, :depth], weight) + mm(two(gl), d2[...], 1, 1)) * owned[...]
    st = st1[...] + st2[...]
    mask = head_mask(width)
    grad = gh[...]
    inverse = 1.0 / den[...]
    numer = grad * inverse
    grad_den = -head_total(grad * ratio[...], mask) * inverse
    raw = q[...]
    queries = jnp.maximum(raw, 0.0)
    grad_q = mm3(numer, spread_heads(st[:HD], width, mask)) + grad_den * st[HD : HD + 1]
    gq_out[...] = jnp.where(raw > 0.0, grad_q, 0.0).astype(bf16)
    st_out[:HD, :] = squeeze_heads(mm3(numer, queries, 0, 0), mask)
    total = jnp.sum(grad_den * queries, axis=0, keepdims=True)
    st_out[HD:, :] = jnp.broadcast_to(total, (8, width))


def linear_end(
    w, gq, k, v, st1, st2, d2, u2, gk_out, gv_out, gl_out, mine, away,
):
    width = k.shape[1]
    half = mine.shape[0]
    st = st1[...] + st2[...]
    mask = head_mask(width)
    wide = spread_heads(st[:HD], width, mask)
    raw = k[...]
    grad_k = mm3(v[...], wide) + st[HD : HD + 1]
    gk_out[...] = jnp.where(raw > 0.0, grad_k, 0.0).astype(bf16)
    gv_out[...] = mm3(jnp.maximum(raw, 0.0), wide, 1, 1).astype(bf16)
    grads = (gq, gk_out, gv_out)
    gl = sum(mm(g[...], u2[i], 1, 1) for i, g in enumerate(grads))
    gl_out[...] = gl
    pair = two(gl)
    weights = (w[0].take(0), w[0].take(1), w[1].take(0))

    def part(rows):
        total = mm(pair[rows], d2[...], 1, 1)
        for g, weight in zip(grads, weights):
            total = total + mm(g[rows, :], weight, 1, 1)
        return total

    put(mine, everything, part(slice(0, half)))
    put(away, everything, part(slice(half, 2 * half)))


def in_steps(rows, body, step=32):
    def one(i, carry):
        body(pl.ds(pl.multiple_of(i * step, step), step))
        return carry

    lax.fori_loop(0, rows // step, one, 0)


def slope_of_norm(values, grad):
    normed, inverse = row_stats(values)
    return inverse * (
        grad
        - jnp.mean(grad, axis=-1, keepdims=True)
        - normed * jnp.mean(grad * normed, axis=-1, keepdims=True)
    )


def total_of(low, got, at, width):
    return low[at, :width].astype(f32) + got[at, :width].astype(f32)


def end_attn(low, got, x, mods, after_out, own_out):
    def body(at):
        after = x[at, :].astype(f32) + mods[2:3, :] * total_of(low, got, at, x.shape[1])
        after_out[at, :] = after
        put(own_out, at, after)

    in_steps(x.shape[0], body)


def end_cross(low, got, before, mods, after_out, own_out):
    def body(at):
        after = before[at, :] + total_of(low, got, at, before.shape[1])
        after_out[at, :] = after
        normed, unused = row_stats(after)
        put(own_out, at, normed * (1.0 + mods[4:5, :]) + mods[3:4, :])

    in_steps(before.shape[0], body)


def end_output(low, got, before, mods, out):
    def body(at):
        put(out, at, before[at, :] + mods[5:6, :] * total_of(low, got, at, before.shape[1]))

    in_steps(before.shape[0], body)


def end_ffn_back(low, got, after, cot, mods, grad_out, own_out):
    def body(at):
        grad = total_of(low, got, at, after.shape[1]) * (1.0 + mods[4:5, :])
        grad = cot[at, :].astype(f32) + slope_of_norm(after[at, :], grad)
        grad_out[at, :] = grad
        put(own_out, at, grad)

    in_steps(after.shape[0], body)


def end_cross_back(low, got, before, mods, grad_out, own_out):
    def body(at):
        grad = before[at, :] + total_of(low, got, at, before.shape[1])
        grad_out[at, :] = grad
        put(own_out, at, mods[2:3, :] * grad)

    in_steps(before.shape[0], body)


def end_attn_back(low, got, before, x, mods, out):
    def body(at):
        grad = total_of(low, got, at, before.shape[1]) * (1.0 + mods[1:2, :])
        put(out, at, before[at, :] + slope_of_norm(x[at, :].astype(f32), grad))

    in_steps(before.shape[0], body)


def place_rows(where, own, other, out):
    half = own.shape[0]
    width = out.shape[1]
    out[pl.ds(pl.multiple_of(where[0] * half, half), half), :] = own[:, :width]
    out[pl.ds(pl.multiple_of((1 - where[0]) * half, half), half), :] = other[:, :width]


def ring_order(n):
    return list(range(0, n, 2)) + list(range(n - 1 - n % 2, 0, -2))


def ring_pairs(n):
    order = ring_order(n)
    return [(order[i], order[(i + 1) % n]) for i in range(n)]


def ring_source(n, step):
    z = lax.axis_index(W)
    place = jnp.where(z % 2 == 0, z // 2, n - 1 - z // 2)
    from_place = (place - step + n) % n
    return jnp.where(2 * from_place < n, 2 * from_place, 2 * (n - 1 - from_place) + 1)


def swap_pairs(n, distance):
    return [(i, i ^ distance) for i in range(n)]


def across(values, axis, distance=1):
    return lax.ppermute(values, axis, swap_pairs(lax.axis_size(axis), distance))


class Stream:
    def __init__(self, makers, order):
        self.n = lax.axis_size(W)
        self.makers, self.order = makers, list(order)
        self.own, self.got, self.crossed = {}, {}, {}
        self.flying, self.crossing = [], []

    def launch(self, name, step):
        if step == 1:
            self.own[name] = self.makers[name]()
            moving = self.own[name][0]
        else:
            moving = self.got[name, step - 1]
        self.flying.append((name, step, lax.ppermute(moving, W, ring_pairs(self.n))))

    def settle(self, done, crossed, values):
        leaves, tree = jax.tree.flatten((values, [d[2] for d in done], [d[2] for d in crossed]))
        values, arrived, over = jax.tree.unflatten(tree, lax.optimization_barrier(leaves))
        for (name, step, unused), v in zip(crossed, over):
            self.crossed[name, step] = v
        for (name, step, unused), v in zip(done, arrived):
            self.got[name, step] = v
            self.crossing.append((name, step, across(v, C)))
        return values

    def tick(self, values):
        done = [self.flying.pop(0)] if self.flying else []
        crossed = [self.crossing.pop(0)] if self.crossing and (len(self.crossing) > 1 or not done) else []
        values = self.settle(done, crossed, values)
        while len(self.flying) < 2 and self.order:
            name, step = self.order[0]
            if step > 1 and (name, step - 1) not in self.got:
                break
            self.order.pop(0)
            self.launch(name, step)
        return values

    def ready(self, names, values):
        last = [(name, self.n - 1) for name in names]
        while not all(key in self.got for key in last):
            values = self.tick(values)
        if self.flying:
            values = self.tick(values)
        left = [d for d in self.crossing if d[0] in names]
        self.crossing = [d for d in self.crossing if d[0] not in names]
        return self.settle([], left, values)

    def pieces(self, name):
        steps = range(1, self.n)
        mine = [self.own[name][0]] + [self.got[name, s] for s in steps]
        other = [self.own[name][1]] + [self.crossed[name, s] for s in steps]
        rows = mine[0].shape[0]
        if rows % 16 == 0:
            return mine + other
        c = lax.axis_index(C)
        buf = jnp.zeros((2, self.n * rows, mine[0].shape[1]), bf16)
        for s in range(self.n):
            at = ring_source(self.n, s) * rows
            buf = lax.dynamic_update_slice(buf, mine[s][None], (c, at, 0))
            buf = lax.dynamic_update_slice(buf, other[s][None], (1 - c, at, 0))
        return [buf]


class Weight:
    def __init__(self, meta, pieces, buf, sems, halves):
        self.meta, self.pieces, self.buf, self.sems, self.halves = meta, pieces, buf, sems, halves

    def copies(self, j, pieces):
        rows = pieces[0].shape[0]
        return [
            pltpu.make_async_copy(
                piece,
                self.buf.at[j, pl.ds(pl.multiple_of(self.meta[1 + k] * rows, rows), rows), :],
                self.sems.at[j, k],
            )
            for k, piece in enumerate(pieces)
        ]

    def start(self):
        count = len(self.pieces) // 2
        for j, half in enumerate(self.halves):
            if not count:
                pltpu.make_async_copy(self.pieces[0].at[half], self.buf.at[j], self.sems.at[j, 0]).start()
                continue

            @pl.when(self.meta[0] == half)
            def mine():
                for copy in self.copies(j, self.pieces[:count]):
                    copy.start()

            @pl.when(self.meta[0] != half)
            def other():
                for copy in self.copies(j, self.pieces[count:]):
                    copy.start()

    def take(self, j):
        count = len(self.pieces) // 2
        if not count:
            pltpu.make_async_copy(self.pieces[0].at[0], self.buf.at[j], self.sems.at[j, 0]).wait()
        else:
            for copy in self.copies(j, self.pieces[:count]):
                copy.wait()
        return self.buf[j]


def per_step(a):
    zeros = (0,) * (a.ndim - 1)
    return pl.BlockSpec((1,) + tuple(a.shape[1:]), lambda h: (h,) + zeros)


def all_of(a):
    zeros = (0,) * len(a.shape)
    return pl.BlockSpec(tuple(a.shape), lambda *g: zeros)


def scalars(a):
    return pl.BlockSpec(memory_space=pltpu.SMEM)


def anywhere(a):
    return pl.BlockSpec(memory_space=pl.ANY)


def run(kernel, ins, outs, scratch=(), steps=1, weights=(), meta=None):
    args, specs = [], []
    if weights:
        args.append(meta)
        specs.append(scalars(meta))
    counts, extra = [], []
    for pieces, halves in weights:
        counts.append((len(pieces), halves))
        args += pieces
        specs += [anywhere(p) for p in pieces]
        rows = pieces[0].shape[0] * len(pieces) // 2 if len(pieces) > 1 else pieces[0].shape[1]
        extra.append(pltpu.VMEM((len(halves), rows, pieces[0].shape[-1]), bf16))
        extra.append(pltpu.SemaphoreType.DMA((len(halves), max(len(pieces) // 2, 1))))
    first = len(args)
    for item in ins:
        a, spec = item if isinstance(item, tuple) else (item, all_of)
        args.append(a)
        specs.append(spec(a))
    shapes, out_specs = [], []
    for item in outs:
        dims, dtype, spec = item if len(item) == 3 else item + (all_of,)
        shapes.append(shape(dims, dtype))
        out_specs.append(spec(shapes[-1]))

    def body(*refs):
        if not weights:
            return kernel(*refs)
        at, loaders = 1, []
        tail = refs[len(refs) - len(extra) :]
        for i, (count, halves) in enumerate(counts):
            loaders.append(Weight(refs[0], refs[at : at + count], tail[2 * i], tail[2 * i + 1], halves))
            at += count

        @pl.when(pl.program_id(0) == 0)
        def begin():
            for loader in loaders:
                loader.start()

        kernel(loaders, *refs[first : len(refs) - len(extra)])

    return pl.pallas_call(
        body,
        grid=(steps,),
        in_specs=specs,
        out_specs=out_specs,
        out_shape=shapes,
        scratch_shapes=list(scratch) + extra,
        compiler_params=big,
    )(*args)


def twice(table, axis):
    return jnp.concatenate([table, table], axis=axis)


def two_parts(values, axis):
    high = lax.reduce_precision(values, 8, 7)
    return jnp.concatenate([high.astype(bf16), (values - high).astype(bf16)], axis=axis)


def fold(both):
    half = both.shape[0] // 2
    return both[:half] + both[half:]


def outer_sum(latent, values, axis=0):
    return fold(mm(two_parts(latent, 1 - axis), values, axis, 0))


def slot_layout(groups, rank, heads):
    per, left = heads // groups, heads % groups
    slots = per + (1 if left else 0)
    own_start = rank * per + jnp.minimum(rank, left)
    own_count = per + jnp.where(rank < left, 1, 0)
    first = jnp.minimum(own_start, heads - slots)
    slot = first + jnp.arange(slots, dtype=jnp.int32)
    owned = ((slot >= own_start) & (slot < own_start + own_count)).astype(f32)
    return slots, first, owned


def slot_ranges(groups, heads):
    per, left = heads // groups, heads % groups
    slots = per + (1 if left else 0)
    out = []
    for rank in range(groups):
        own_start = rank * per + min(rank, left)
        count = per + (1 if rank < left else 0)
        out.append((own_start - min(own_start, heads - slots), count))
    return out


def shards(
    tokens, caption, caption_lengths, adapter_index, modulation, cotangent,
    qkv_weight, proj_weight, cross_q_weight, cross_kv_weight, cross_out_weight,
    inverted_weight, depth_weight, point_weight,
    qkv_down, qkv_up, proj_down, proj_up, query_down, query_up, kv_down, kv_up,
    cross_down, cross_up, inverted_down, inverted_up, point_down, point_up,
):
    grid_rows, grid_cols, D = tokens.shape[1:]
    n = grid_rows * grid_cols
    half = n // 2
    heads = D // HD
    groups = lax.axis_size(T)
    rank = lax.axis_index(T)
    c = lax.axis_index(C)
    b = rank % 2
    adapters, R = qkv_up.shape[:2]
    slots, slot_first, owned = slot_layout(groups, rank, heads)
    width = slots * HD
    col = slot_first * HD
    owned = jnp.repeat(owned, HD)[None]
    hid = inverted_weight.shape[2]
    hh = hid // 2
    hid_first = rank * hid
    index = adapter_index[0]
    where = jnp.stack([b, c]).astype(jnp.int32)

    def cut(table, start, size, axis):
        return lax.dynamic_slice_in_dim(table, start, size, axis)

    def pick(table):
        return lax.dynamic_index_in_dim(table, index, 0, keepdims=False)

    def own_rows(rows):
        own = cut(rows, b * half, half, 0)
        return own, jnp.concatenate([own, cut(rows, (1 - b) * half, half, 0)])

    late = {}
    def pair_of(first, second):
        return [jnp.where(c == 0, first, second), jnp.where(c == 0, second, first)]

    def taken(table, middle, start, size):
        return lax.dynamic_slice(table, (0, middle, start), (table.shape[0], 1, size))[:, 0]

    def sides(make):
        return [make(c), make(1 - c)]

    makers = dict(
        a=lambda: sides(lambda i: taken(qkv_weight, i, col, width)),
        b=lambda: pair_of(taken(qkv_weight, 2, col, width), cut(proj_weight, col, width, 0).T),
        c=lambda: pair_of(cut(late["q"], col, width, 1), taken(late["kv"], 0, col, width)),
        d=lambda: pair_of(taken(late["kv"], 1, col, width), cut(late["o"], col, width, 0).T),
        v=lambda: sides(lambda i: taken(late["i"], 0, i * hh, hh)),
        g=lambda: sides(lambda i: taken(late["i"], 1, i * hh, hh)),
        p=lambda: sides(lambda i: cut(late["p"], i * hh, hh, 0).T),
    )
    size = lax.axis_size(W)
    order = []
    for pair in (("a", "b"), ("c", "d"), ("v", "g"), ("p",)):
        order += [(name, step) for step in range(1, size) for name in pair]
    if size == 4:
        order[-4:] = [("p", 1), ("g", 3), ("p", 2), ("p", 3)]
    stream = Stream(makers, order)
    tick = stream.tick

    def spread(first, last):
        return range(len(order) * first // 21, len(order) * last // 21)

    tick(())
    mods = modulation[0]
    low_tokens = tokens.reshape(n, D)
    x_low, x_rows = own_rows(low_tokens)
    qd2, qu2 = twice(pick(qkv_down), 1), twice(cut(pick(qkv_up), col, width, 2), 0).transpose(1, 0, 2)
    pd2, pu2 = twice(cut(pick(proj_down), col, width, 0), 1), twice(pick(proj_up), 0)
    raw = dict(q=cross_q_weight, kv=cross_kv_weight, o=cross_out_weight, i=inverted_weight, p=point_weight)
    tables = [query_down, query_up, kv_down, kv_up, cross_down, cross_up]
    tables_f = [inverted_down, inverted_up, point_down, point_up, depth_weight]
    for i in spread(0, 3):
        raw, tables, tables_f, caption, cotangent = tick((raw, tables, tables_f, caption, cotangent))
    late["q"], late["kv"], late["o"] = raw["q"], raw["kv"], raw["o"]
    query_down, query_up, kv_down, kv_up, cross_down, cross_up = tables
    cd2 = twice(cut(pick(cross_down), col, width, 0), 1)
    cu2 = twice(pick(cross_up), 0)
    xd2, xu2 = twice(pick(query_down), 1), twice(cut(pick(query_up), col, width, 1), 0)
    kd2, ku2 = twice(pick(kv_down), 1), twice(cut(pick(kv_up), col, width, 2), 0).transpose(1, 0, 2)
    text_here = caption.shape[1]
    text_rows = -(-text_here // 16) * 16
    cap = jnp.pad(caption[0], ((0, text_rows - text_here), (0, 0)))
    for i in spread(3, 6):
        raw, tables_f, cotangent = tick((raw, tables_f, cotangent))
    late["i"], late["p"] = raw["i"], raw["p"]
    inverted_down, inverted_up, point_down, point_up, depth_weight = tables_f
    x_rows = stream.ready("ab", x_rows)

    w_a, w_b = stream.pieces("a"), stream.pieces("b")
    meta = jnp.stack([c] + [ring_source(size, s) for s in range(size)]).astype(jnp.int32)
    padded = -(-D // LANES) * LANES
    rows_bf = ((n, D), bf16)
    thin = ((n, 2 * R), f32)
    wide = ((n, width), f32)
    wide_bf = ((n, width), bf16)
    pair = [((half, padded), f32), ((half, padded), bf16)]
    ended = [((half, D), f32), ((half, padded), bf16)]
    state_of = ((HD + 8, width), f32)
    attn_in, q_raw, k_raw, v_raw, qkv_lat, st_own = run(
        attn_front, [x_rows, mods, qd2, qu2], [rows_bf, wide, wide, wide, thin, state_of],
        weights=[(w_a, (0, 1)), (w_b, (0,))], meta=meta,
    )
    st_other = across(st_own, C)
    for i in spread(7, 8):
        st_own, st_other = tick((st_own, st_other))
    ratio, denom, mixed, proj_lat, mine, away = run(
        attn_back, [q_raw, st_own, st_other, owned, pd2, pu2], [wide, wide, wide_bf, thin] + pair,
        weights=[(w_b, (1,))], meta=meta,
    )

    def core_sum(mine, away):
        return (mine + across(away, T).astype(f32)).astype(bf16)

    def summed(mine, away, span):
        low, distance = core_sum(mine, away), 2
        while True:
            got = across(low, T, distance)
            for i in span:
                low = tick(low)
            distance, span = distance * 2, ()
            if distance >= groups:
                return low, got
            low = (low.astype(f32) + got.astype(f32)).astype(bf16)

    low, got = summed(mine, away, spread(8, 10))
    after_attn, cross_own = run(end_attn, [low, got, x_low, mods], ended)
    cross_other = across(cross_own, T)

    cross_own, cross_other, after_attn = stream.ready("cd", (cross_own, cross_other, after_attn))
    w_c, w_d = stream.pieces("c"), stream.pieces("d")
    kv_own, kv_lat = run(
        caption_rows, [cap, kd2, ku2], [((2, text_rows, width), bf16), ((text_rows, 2 * R), f32)],
        weights=[(w_c, (1,)), (w_d, (0,))], meta=meta,
    )
    kv_other = across(kv_own, C)
    places = jnp.arange(text_rows)
    live = jnp.concatenate([c * text_here + places, (1 - c) * text_here + places])
    live = (live < caption_lengths[0]) & (jnp.concatenate([places, places]) < text_here)
    live = live.astype(f32)[None]
    for i in spread(13, 14):
        kv_own, kv_other = tick((kv_own, kv_other))
    key_buf = pltpu.VMEM((2 * text_rows, width), bf16)
    query, mix, query_lat, cross_lat, lse, mine, away = run(
        cross_fwd,
        [cross_own, cross_other, kv_own, kv_other, live, owned, xd2, xu2, cd2, cu2],
        [wide_bf, wide_bf, thin, thin, ((n, LANES), f32)] + pair,
        [key_buf, key_buf],
        weights=[(w_c, (0,)), (w_d, (1,))], meta=meta,
    )
    low, got = summed(mine, away, spread(14, 16))
    after_cross, ffn_own = run(end_cross, [low, got, after_attn, mods], ended)
    ffn_other = across(ffn_own, T)

    fd2, fu2 = twice(pick(inverted_down), 1), twice(cut(pick(inverted_up), hid_first, hid, 2), 0)
    fu2 = fu2.reshape(2 * R, 2, 2, hh).transpose(1, 2, 0, 3)
    od2 = twice(cut(pick(point_down), hid_first, hid, 0), 1).reshape(2, hh, 2 * R)
    ou2 = twice(pick(point_up), 0)
    taps = depth_weight.astype(f32).reshape(9, 2, 2, hh).transpose(2, 1, 0, 3)
    cot = cotangent.reshape(n, D)
    cot_low, cot = own_rows(cot)
    ffn_own, ffn_other, after_cross = stream.ready("vg", (ffn_own, ffn_other, after_cross))
    w_v, w_g = stream.pieces("v"), stream.pieces("g")
    hid_f, hid_bf = ((2, n, hh), f32, per_step), ((2, n, hh), bf16, per_step)
    pre_v, pre_g, hid_v, hid_g, inv_lat = run(
        ffn_front,
        [ffn_own, ffn_other, fd2, (fu2[0], per_step), (fu2[1], per_step)],
        [hid_f, hid_f, hid_bf, hid_bf, thin],
        [pltpu.VMEM((n, D), bf16)],
        2,
        weights=[(w_v, (0, 1)), (w_g, (0, 1))], meta=meta,
    )

    def edge_rows(v, g):
        row = jnp.where(c == 0, grid_rows - 1, 0)
        at = jnp.where(c == 0, jnp.where(b == 1, half, 2 * half) - grid_cols, jnp.where(b == 0, 0, half))
        edge = jnp.stack([cut(v, at, grid_cols, 1), cut(g, at, grid_cols, 1)], axis=1)
        return across(edge, C)

    halo = edge_rows(hid_v, hid_g)
    hid_v, halo = stream.ready("p", (hid_v, halo))
    w_p = stream.pieces("p")
    grid_buf = pltpu.VMEM((n + 2 * grid_cols, hh), f32)
    row_acc = pltpu.VMEM((n, D), f32)
    gated, gcv, gcg, grad_ffn, point_gl, point_lat, mine, away = run(
        ffn_mid,
        [
            (where, scalars), (hid_v, per_step), (hid_g, per_step), (halo, per_step), (taps, per_step),
            cot, mods[5:6], (od2, per_step), ou2,
        ],
        [hid_bf, hid_bf, hid_bf, rows_bf, thin, thin] + pair,
        [grid_buf, grid_buf, pltpu.VMEM((n, hh), f32), row_acc],
        2,
        weights=[(w_p, (0, 1))], meta=meta,
    )
    halo = edge_rows(gcv, gcg)
    low, got = summed(mine, away, ())
    (output,) = run(end_output, [low, got, after_cross, mods], [((half, padded), f32)])
    output_other = across(output, T)

    gpv, gpg, inv_up_g, inv_gl, mine, away = run(
        ffn_back,
        [
            (where, scalars), (gcv, per_step), (gcg, per_step), (halo, per_step), (taps, per_step),
            (pre_v, per_step), (pre_g, per_step), inv_lat, fd2,
            (fu2[0], per_step), (fu2[1], per_step),
        ],
        [hid_bf, hid_bf, ((2, 2, 2 * R, hh), f32, per_step), thin] + pair,
        [grid_buf, grid_buf, row_acc],
        2,
        weights=[(w_v, (0, 1)), (w_g, (0, 1))], meta=meta,
    )
    low, got = summed(mine, away, ())
    grad_cross, gc_own = run(end_ffn_back, [low, got, after_cross, cot_low, mods], ended)
    gc_other = across(gc_own, T)

    grad_query, gkv, query_gl, cross_gl, mine, away = run(
        cross_bwd,
        [
            gc_own, gc_other, kv_own, kv_other, live, owned,
            xd2, xu2, cd2, cu2, query, lse,
        ],
        [wide_bf, ((2, 2 * text_rows, width), f32), thin, thin] + pair,
        [key_buf, key_buf, pltpu.VMEM((n, width), bf16), pltpu.VMEM((n, width), f32)],
        weights=[(w_c, (0,)), (w_d, (1,))], meta=meta,
    )
    gkv_got = across(gkv[:, text_rows:], C)
    low, got = summed(mine, away, ())
    grad_after, ga_own = run(end_cross_back, [low, got, grad_cross, mods], ended)
    ga_other = across(ga_own, T)
    grad_kv = (gkv[:, :text_rows] + gkv_got).astype(bf16)
    kv_gl = mm(grad_kv[0], ku2[0], 1, 1) + mm(grad_kv[1], ku2[1], 1, 1)

    grad_q, proj_gl, sg_own = run(
        linear_bwd,
        [ga_own, ga_other, q_raw, st_own, st_other, ratio, denom, owned, pd2, pu2],
        [wide_bf, thin, state_of],
        [pltpu.VMEM((n, width), f32)],
        weights=[(w_b, (1,))], meta=meta,
    )
    sg_other = across(sg_own, C)
    grad_k, grad_v, qkv_gl, mine, away = run(
        linear_end,
        [grad_q, k_raw, v_raw, sg_own, sg_other, qd2, qu2],
        [wide_bf, wide_bf, thin] + pair,
        weights=[(w_a, (0, 1)), (w_b, (0,))], meta=meta,
    )
    low, got = summed(mine, away, ())
    (input_grad,) = run(end_attn_back, [low, got, grad_after, x_low, mods], [((half, padded), f32)])
    input_other = across(input_grad, T)

    def in_order(own, other):
        return run(place_rows, [(where, scalars), own, other], [((n, D), f32)])[0]

    part_r = R // groups
    blocks = lax.axis_size(W) * lax.axis_size(C)
    ranges = slot_ranges(groups, heads)

    def by_rank(*values):
        joined = jnp.concatenate(values, axis=1)
        sent = joined.reshape(groups, part_r, joined.shape[1])
        return lax.all_to_all(sent, T, 0, 0, tiled=True)

    def slots_to_heads(got):
        return jnp.concatenate(
            [got[t][:, s * HD : (s + m) * HD] for t, (s, m) in enumerate(ranges)], axis=1
        )

    def hidden_to_full(got):
        return jnp.concatenate([got[t] for t in range(groups)], axis=1)

    def finish(values):
        sizes = [v.shape[1] // blocks for v in values]
        payload = jnp.concatenate([v.reshape(part_r, blocks, -1) for v in values], axis=2)
        payload = payload.transpose(1, 0, 2)
        mark = jnp.full((blocks, part_r, 1), 0.0, f32) + index.astype(f32)
        got = lax.all_to_all(jnp.concatenate([payload, mark], axis=2), (W, C), 0, 0, tiled=True)
        owner = got[:, 0, -1]
        chosen = (owner[None, :] == jnp.arange(adapters, dtype=f32)[:, None]).astype(f32)
        table = jnp.einsum("as,srk->ark", chosen, got[:, :, :-1], precision=full_precision)
        out, at = [], 0
        for size in sizes:
            out.append(table[:, :, at : at + size])
            at += size
        return out

    def lat(v):
        return v[:, :R]

    def turned(v):
        return jnp.where(b == 0, v, jnp.concatenate([v[:, half:], v[:, :half]], axis=1))

    lat_cols = [turned(lat(v).T) for v in (proj_lat, cross_lat, point_lat, inv_gl, query_gl)]
    got = jnp.sum(by_rank(*lat_cols, lat(kv_gl).T), axis=0)
    proj_s, cross_s, point_s, inv_s, query_s = (
        turned(got[:, i * n : (i + 1) * n]) for i in range(5)
    )
    kv_s = got[:, 5 * n :]

    def thin_sum(latent, values):
        return outer_sum(latent, values, 1)

    early = [
        outer_sum(lat(cross_gl), mix),
        outer_sum(lat(query_lat), grad_query),
        outer_sum(lat(kv_lat), grad_kv[0]),
        outer_sum(lat(kv_lat), grad_kv[1]),
        outer_sum(lat(point_gl), gated[0]),
        outer_sum(lat(point_gl), gated[1]),
    ] + [fold(inv_up_g[h, p]) for p in range(2) for h in range(2)]
    got = by_rank(*early)
    pieces, at = [], 0
    for v in early:
        pieces.append(got[:, :, at : at + v.shape[1]])
        at += v.shape[1]
    cross_down_g, query_up_g, key_up_g, value_up_g = (slots_to_heads(p) for p in pieces[:4])
    point_down_g = hidden_to_full(jnp.concatenate(pieces[4:6], axis=2))
    inv_up_full = [hidden_to_full(jnp.concatenate(pieces[i : i + 2], axis=2)) for i in (6, 8)]

    def joint(latent, own, other):
        both = thin_sum(latent[:, :half], own) + thin_sum(latent[:, half:], other)
        return both[:, :D]

    first = finish(
        [
            joint(cross_s, gc_own, gc_other),
            thin_sum(point_s, grad_ffn),
            joint(inv_s, ffn_own, ffn_other),
            joint(query_s, cross_own, cross_other),
            thin_sum(kv_s, cap),
            cross_down_g,
            query_up_g,
            key_up_g,
            value_up_g,
            point_down_g,
        ]
        + inv_up_full
    )
    qkv_s = turned(jnp.sum(by_rank(turned(lat(qkv_gl).T)), axis=0))
    last = [outer_sum(lat(proj_gl), mixed)] + [
        outer_sum(lat(qkv_lat), g) for g in (grad_q, grad_k, grad_v)
    ]
    got = by_rank(*last)
    last = [slots_to_heads(got[:, :, i * width : (i + 1) * width]) for i in range(4)]
    second = finish([joint(proj_s, ga_own, ga_other), thin_sum(qkv_s, attn_in)] + last)

    def down_of(t):
        return t.transpose(0, 2, 1)

    return (
        in_order(output, output_other).reshape(tokens.shape),
        in_order(input_grad, input_other).reshape(tokens.shape),
        down_of(second[1]),
        jnp.stack(second[3:6], axis=2),
        down_of(second[2]),
        second[0],
        down_of(first[3]),
        first[6],
        down_of(first[4]),
        jnp.stack(first[7:9], axis=2),
        down_of(first[5]),
        first[0],
        down_of(first[2]),
        jnp.stack(first[10:12], axis=2),
        down_of(first[9]),
        first[1],
    )


def solution(mesh):
    down = P(None, (W, C), T)
    up3 = P(None, T, (W, C))
    up4 = P(None, T, None, (W, C))
    rows = P(W, C)
    return jax.shard_map(
        shards,
        mesh=mesh,
        in_specs=(
            rows, rows, P(W), P(W), P(W), rows,
            P(W), P(None, W), P(W), P(W), P(None, W),
            P(W, None, T), P(None, None, None, T), P(T, W),
        )
        + (P(),) * 14,
        out_specs=(
            rows, rows, down, up4, down, up3, down, up3, down, up4, down, up3, down, up4, down, up3,
        ),
        check_vma=False,
    )
```

time: 1040 us -> 891 us (0.86)
  Pallas kernels: 0 us -> 234 us
  local copies, waits for them, and re-layouts: 255 us -> 89.4 us
  matrix products: 180 us -> 16.2 us
  other arithmetic: 134 us -> 45.1 us
  waiting for transfers between devices: 354 us -> 393 us
    pallas_call x0 -> x18, Pallas kernels: none -> 234 us  [run(): pl.pallas_call(body, grid=(steps,), in_specs=specs, out_specs=out_specs,...]
    dot_general x100 -> x23, matrix products: 179 us -> 14.4 us  [mm(): lax.dot_general(a, b, (((ca,), (cb,)), ((), ())), preferred_element_type=...]
    dynamic_update_slice x40 -> x0, local copies, waits for them, and re-layouts: 52.9 us -> none  [the longest x21 30.9 us: gather_pair(): buf = lax.dynamic_update_slice(buf, moving[None], (c, at, 0))]
    reshape x10 -> x0, local copies, waits for them, and re-layouts: 25.8 us -> none  [the longest x4 12.1 us: shards(): shifted(v, t, True).reshape(n, hh) * silu_slope(s)]
    select_n x17 -> x9, other arithmetic: 34.2 us -> 8.49 us  [the longest x2 8.25 us: pair_of(): return [jnp.where(c == 0, first, second), jnp.where(c == 0, second, first)]]
    convert_element_type x22 -> x9, other arithmetic: 38.2 us -> 14.7 us  [the longest x6 12.8 us: core_sum(): return (mine + across(away, T).astype(f32)).astype(bf16)]
    slice x16 -> x18, local copies, waits for them, and re-layouts: 22.4 us -> 1.67 us  [the longest x1 1.3 us: shards(): mods[5:6]]
    convert_element_type x14 -> x7, local copies, waits for them, and re-layouts: 21.6 us -> 1.13 us  [the longest x6 1.05 us: two_parts(): high.astype(bf16)]
  transfers between devices with their start and end apart: 72 -> 72, of which waited for: 33 -> 44; matrix products, arithmetic and copies ran while one was open for 39% -> 14% of each run, Pallas kernels for 0% -> 12%
where the time goes in v1:
time: 891 us; the launch traced here: 884 us
  waiting for transfers between devices  393 us (44%)
  Pallas kernels  234 us (26%)
  starting transfers between devices  102 us (11%)
  local copies, waits for them, and re-layouts  89.4 us (10%)
  other arithmetic  45.1 us (5%)
  matrix products  16.2 us (2%)
    ppermute x45, waiting for transfers between devices, across(): return lax.ppermute(values, axis, swap_pairs(lax.axis_size(axis), distance))  257 us
    pallas_call x18, Pallas kernels, run(): pl.pallas_call(body, grid=(steps,), in_specs=specs, out_specs=out_specs,...  234 us
    ppermute x21, waiting for transfers between devices, launch(): lax.ppermute(moving, W, ring_pairs(self.n))  99.7 us
    ppermute x21, starting transfers between devices, launch(): lax.ppermute(moving, W, ring_pairs(self.n))  46.2 us
    ppermute x45, starting transfers between devices, across(): return lax.ppermute(values, axis, swap_pairs(lax.axis_size(axis), distance))  34.4 us
    unnamed x172, local copies, waits for them, and re-layouts  24.6 us
    all_to_all x4, waiting for transfers between devices, by_rank(): return lax.all_to_all(sent, T, 0, 0, tiled=True)  22.3 us
  transfers between devices with their start and end apart: 72, of which 44 were waited for; matrix products, arithmetic and copies ran while one was open for 14% of the time, Pallas kernels for 12%

profile of v1, /device:TPU:0, one launch (start us, length us, event | category | flops | bytes accessed | tf_op | source)
XLA Modules:
  0.0 883.6 jit_solution(17058146361110002768)
XLA Ops:
  15.4 9.5 %collective-permute-done.refs_2_ = bf16[560,576]{1,0:T(8,128)(2,1)} collective-permute-done((bf16[560,576]{1,0:T(8,128)(2,1)}, bf16[560,576]{1,0:T(8,128)(2,1)}, u32[]{:S(2)}, u32[]{:S(2)}) %collective-permute-start) | collective-permute-done | bytes 645152 | tf_op jit(solution)/shard_map/ppermute | solution.py:571
  29.7 10.5 %collective-permute-done.1.refs_10_.refs_2_ = bf16[560,576]{1,0:T(8,128)(2,1)} collective-permute-done((bf16[560,576]{1,0:T(8,128)(2,1)}, bf16[560,576]{1,0:T(8,128)(2,1)}, u32[]{:S(2)}, u32[]{:S(2)}) %collective-permute-start.1) | collective-permute-done | bytes 645152 | tf_op jit(solution)/shard_map/ppermute | solution.py:571
  60.4 10.5 %collective-permute-done.4.refs_11_.refs_3_ = bf16[560,576]{1,0:T(8,128)(2,1)} collective-permute-done((bf16[560,576]{1,0:T(8,128)(2,1)}, bf16[560,576]{1,0:T(8,128)(2,1)}, u32[]{:S(2)}, u32[]{:S(2)}) %collective-permute-start.4) | collective-permute-done | bytes 645152 | tf_op jit(solution)/shard_map/ppermute | solution.py:571
  90.6 11.0 %collective-permute-done.8.refs_12_.refs_4_ = bf16[560,576]{1,0:T(8,128)(2,1)} collective-permute-done((bf16[560,576]{1,0:T(8,128)(2,1)}, bf16[560,576]{1,0:T(8,128)(2,1)}, u32[]{:S(2)}, u32[]{:S(2)}) %collective-permute-start.8) | collective-permute-done | bytes 645152 | tf_op jit(solution)/shard_map/ppermute | solution.py:571
  120.7 17.0 %shard_map.387 = (bf16[512,2240]{1,0:T(8,128)(2,1)}, f32[512,576]{1,0:T(8,128)}, f32[512,576]{1,0:T(8,128)}, f32[512,576]{1,0:T(8,128)}, f32[512,32]{1,0:T(8,128)}, /*index=5*/f32[40,576]{1,0:T(8,128)}) custom-call(s32[5]{0:T(128)} %stack.80.refs_0_, bf16[560,576]{1,0:T(8,128)(2,1)} %get-tuple-element.561.refs_1_, ...), custom_call_target="tpu_custom_call" | custom-call | tf_op jit(solution)/shard_map/pallas_call | solution.py:721
  143.3 9.0 %shard_map.388 = (f32[512,576]{1,0:T(8,128)}, f32[512,576]{1,0:T(8,128)}, bf16[512,576]{1,0:T(8,128)(2,1)}, f32[512,32]{1,0:T(8,128)}, f32[256,2304]{1,0:T(8,128)}, /*index=5*/bf16[256,2304]{1,0:T(8,128)(2,1)}) custom-call(s32[5]{0:T(128)} %stack.80.refs_0_, bf16[560,576]{1,0:T(8,128)(2,1)} %get-tuple-element.555.refs_9_.refs_1_, ...), custom_call_target="tpu_custom_call" | custom-call | tf_op jit(solution)/shard_map/pallas_call | solution.py:721
  164.6 14.3 %collective-permute-done.17.refs_6_ = bf16[560,576]{1,0:T(8,128)(2,1)} collective-permute-done((bf16[560,576]{1,0:T(8,128)(2,1)}, bf16[560,576]{1,0:T(8,128)(2,1)}, u32[]{:S(2)}, u32[]{:S(2)}) %collective-permute-start.17) | collective-permute-done | bytes 645152 | tf_op jit(solution)/shard_map/ppermute | solution.py:555
  179.5 13.7 %collective-permute-done.19.refs_14_ = bf16[560,576]{1,0:T(8,128)(2,1)} collective-permute-done((bf16[560,576]{1,0:T(8,128)(2,1)}, bf16[560,576]{1,0:T(8,128)(2,1)}, u32[]{:S(2)}, u32[]{:S(2)}) %collective-permute-start.19) | collective-permute-done | bytes 645152 | tf_op jit(solution)/shard_map/ppermute | solution.py:555
  221.7 17.9 %collective-permute-done.22.refs_4_ = bf16[560,576]{1,0:T(8,128)(2,1)S(1)} collective-permute-done((bf16[560,576]{1,0:T(8,128)(2,1)}, bf16[560,576]{1,0:T(8,128)(2,1)S(1)}, u32[]{:S(2)}, u32[]{:S(2)}) %collective-permute-start.22) | collective-permute-done | bytes 645152 | tf_op jit(solution)/shard_map/ppermute | solution.py:571
  245.6 12.4 %collective-permute-done.26.refs_2_ = bf16[560,700]{1,0:T(8,128)(2,1)} collective-permute-done((bf16[560,700]{1,0:T(8,128)(2,1)S(1)}, bf16[560,700]{1,0:T(8,128)(2,1)}, u32[]{:S(2)}, u32[]{:S(2)}) %collective-permute-start.26) | collective-permute-done | bytes 784032 | tf_op jit(solution)/shard_map/ppermute | solution.py:571
  258.1 13.6 %collective-permute-done.27.refs_8_ = bf16[560,576]{1,0:T(8,128)(2,1)S(1)} collective-permute-done((bf16[560,576]{1,0:T(8,128)(2,1)S(1)}, bf16[560,576]{1,0:T(8,128)(2,1)S(1)}, u32[]{:S(2)}, u32[]{:S(2)}) %collective-permute-start.27) | collective-permute-done | bytes 645152 | tf_op jit(solution)/shard_map/ppermute | solution.py:555
  290.2 22.8 %shard_map.391 = (bf16[512,576]{1,0:T(8,128)(2,1)}, bf16[512,576]{1,0:T(8,128)(2,1)}, f32[512,32]{1,0:T(8,128)}, f32[512,32]{1,0:T(8,128)}, f32[512,128]{1,0:T(8...) custom-call(s32[5]{0:T(128)} %stack.80.refs_0_, bf16[560,576]{1,0:T(8,128)(2,1)} %get-tuple-element.562.refs_1_, ...), custom_call_target="tpu_custom_call" | custom-call | tf_op jit(solution)/shard_map/pallas_call | solution.py:721
  331.2 11.5 %collective-permute-done.33.refs_6_ = bf16[560,700]{1,0:T(8,128)(2,1)} collective-permute-done((bf16[560,700]{1,0:T(8,128)(2,1)}, bf16[560,700]{1,0:T(8,128)(2,1)}, u32[]{:S(2)}, u32[]{:S(2)}) %collective-permute-start.33) | collective-permute-done | bytes 784032 | tf_op jit(solution)/shard_map/ppermute | solution.py:555
  344.3 15.7 %collective-permute-done.35.refs_14_ = bf16[560,700]{1,0:T(8,128)(2,1)} collective-permute-done((bf16[560,700]{1,0:T(8,128)(2,1)}, bf16[560,700]{1,0:T(8,128)(2,1)}, u32[]{:S(2)}, u32[]{:S(2)}) %collective-permute-start.35) | collective-permute-done | bytes 784032 | tf_op jit(solution)/shard_map/ppermute | solution.py:555
  380.9 10.4 %collective-permute-done.39.refs_7_ = bf16[560,700]{1,0:T(8,128)(2,1)S(1)} collective-permute-done((bf16[560,700]{1,0:T(8,128)(2,1)}, bf16[560,700]{1,0:T(8,128)(2,1)S(1)}, u32[]{:S(2)}, u32[]{:S(2)}) %collective-permute-start.39) | collective-permute-done | bytes 784032 | tf_op jit(solution)/shard_map/ppermute | solution.py:555
  400.7 9.2 %collective-permute-done.41.refs_15_ = bf16[560,700]{1,0:T(8,128)(2,1)S(1)} collective-permute-done((bf16[560,700]{1,0:T(8,128)(2,1)}, bf16[560,700]{1,0:T(8,128)(2,1)S(1)}, u32[]{:S(2)}, u32[]{:S(2)}) %collective-permute-start.41) | collective-permute-done | bytes 784032 | tf_op jit(solution)/shard_map/ppermute | solution.py:555
  418.0 10.3 %collective-permute-done.43.refs_8_ = bf16[560,700]{1,0:T(8,128)(2,1)S(1)} collective-permute-done((bf16[560,700]{1,0:T(8,128)(2,1)S(1)}, bf16[560,700]{1,0:T(8,128)(2,1)S(1)}, u32[]{:S(2)}, u32[]{:S(2)}) %collective-permute-start.43) | collective-permute-done | bytes 784032 | tf_op jit(solution)/shard_map/ppermute | solution.py:555
  430.0 16.8 %collective-permute-done.45.refs_6_ = bf16[560,700]{1,0:T(8,128)(2,1)} collective-permute-done((bf16[560,700]{1,0:T(8,128)(2,1)}, bf16[560,700]{1,0:T(8,128)(2,1)}, u32[]{:S(2)}, u32[]{:S(2)}) %collective-permute-start.45) | collective-permute-done | bytes 784032 | tf_op jit(solution)/shard_map/ppermute | solution.py:555
  450.1 14.7 %collective-permute-done.46.refs_16_ = bf16[560,700]{1,0:T(8,128)(2,1)} collective-permute-done((bf16[560,700]{1,0:T(8,128)(2,1)}, bf16[560,700]{1,0:T(8,128)(2,1)}, u32[]{:S(2)}, u32[]{:S(2)}) %collective-permute-start.46) | collective-permute-done | bytes 784032 | tf_op jit(solution)/shard_map/ppermute | solution.py:555
  464.9 23.8 %shard_map.393 = (f32[2,512,700]{2,1,0:T(8,128)}, f32[2,512,700]{2,1,0:T(8,128)}, bf16[2,512,700]{2,1,0:T(8,128)(2,1)}, bf16[2,512,700]{2,1,0:T(8,128)(2,1)}, f32[512,32]{1,0:T(8,128)}) custom-call(s32[5]{0:T(128)} %stack.80.refs_0_, bf16[560,700]{1,0:T(8,128)(2,1)} %copy-done.2, bf16[560,700]{1,0:T(8,128)(2,1)} %collective-permute-done.26.refs_2_, ...), custom_call_target="tpu_custom_call" | custom-call | tf_op jit(solution)/shard_map/pallas_call | solution.py:721
  499.1 17.7 %collective-permute-done.49.refs_7_ = bf16[560,700]{1,0:T(8,128)(2,1)S(1)} collective-permute-done((bf16[560,700]{1,0:T(8,128)(2,1)}, bf16[560,700]{1,0:T(8,128)(2,1)S(1)}, u32[]{:S(2)}, u32[]{:S(2)}) %collective-permute-start.49) | collective-permute-done | bytes 784032 | tf_op jit(solution)/shard_map/ppermute | solution.py:555
  516.8 17.2 %collective-permute-done.50.refs_8_ = bf16[560,700]{1,0:T(8,128)(2,1)S(1)} collective-permute-done((bf16[560,700]{1,0:T(8,128)(2,1)}, bf16[560,700]{1,0:T(8,128)(2,1)S(1)}, u32[]{:S(2)}, u32[]{:S(2)}) %collective-permute-start.50) | collective-permute-done | bytes 784032 | tf_op jit(solution)/shard_map/ppermute | solution.py:555
  534.8 29.0 %shard_map.394 = (bf16[2,512,700]{2,1,0:T(8,128)(2,1)}, bf16[2,512,700]{2,1,0:T(8,128)(2,1)}, bf16[2,512,700]{2,1,0:T(8,128)(2,1)}, bf16[512,2240]{1,0:T(8,128)(...) custom-call(s32[5]{0:T(128)} %stack.80.refs_0_, ...), custom_call_target="tpu_custom_call" | custom-call | tf_op jit(solution)/shard_map/pallas_call | solution.py:721
  572.1 24.8 %shard_map.397 = (bf16[2,512,700]{2,1,0:T(8,128)(2,1)}, bf16[2,512,700]{2,1,0:T(8,128)(2,1)}, f32[2,2,32,700]{3,2,1,0:T(8,128)}, f32[512,32]{1,0:T(8,128)}, f32[...) custom-call(s32[5]{0:T(128)} %stack.80.refs_0_, bf16[560,700]{1,0:T(8,128)(2,1)} %copy-done.2, ...), custom_call_target="tpu_custom_call" | custom-call | tf_op jit(solution)/shard_map/pallas_call | solution.py:721
  606.6 25.6 %collective-permute-done.56.refs_1_ = bf16[256,2304]{1,0:T(8,128)(2,1)S(1)} collective-permute-done((bf16[256,2304]{1,0:T(8,128)(2,1)S(1)}, bf16[256,2304]{1,0:T(8,128)(2,1)S(1)}, u32[]{:S(2)}, u32[]{:S(2)}) %collective-permute-start.56) | collective-permute-done | bytes 1179680 | tf_op jit(solution)/shard_map/ppermute | solution.py:555
  644.6 12.2 %collective-permute-done.52.refs_1_ = bf16[256,2304]{1,0:T(8,128)(2,1)} collective-permute-done((bf16[256,2304]{1,0:T(8,128)(2,1)S(1)}, bf16[256,2304]{1,0:T(8,128)(2,1)}, u32[]{:S(2)}, u32[]{:S(2)}) %collective-permute-start.52) | collective-permute-done | bytes 1179680 | tf_op jit(solution)/shard_map/ppermute | solution.py:555
  662.1 28.4 %shard_map.399 = (bf16[512,576]{1,0:T(8,128)(2,1)}, f32[2,320,576]{2,1,0:T(8,128)}, f32[512,32]{1,0:T(8,128)}, f32[512,32]{1,0:T(8,128)}, f32[256,2304]{1,0:T(8,128)}, /*index=5*/bf16[256,2304]{1,0:T(8,128)(2,1)}) custom-call(s32[5]{0:T(128)} %stack.80.refs_0_, bf16[560,576]{1,0:T(8,128)(2,1)} %get-tuple-element.562.refs_1_, ...), custom_call_target="tpu_custom_call" | custom-call | tf_op jit(solution)/shard_map/pallas_call | solution.py:721
  696.8 17.9 %collective-permute-done.65 = f32[2,160,576]{2,1,0:T(8,128)} collective-permute-done((f32[2,160,576]{2,1,0:T(8,128)S(1)}, f32[2,160,576]{2,1,0:T(8,128)}, u32[]{:S(2)}, u32[]{:S(2)}) %collective-permute-start.65) | collective-permute-done | bytes 737312 | tf_op jit(solution)/shard_map/ppermute | solution.py:555
  755.1 11.1 %all-to-all-done.5 = f32[8,4,4621]{2,1,0:T(4,128)S(1)} async-done(((f32[8,4,4621]{2,1,0:T(4,128)}), f32[8,4,4621]{2,1,0:T(4,128)S(1)}, u32[]{:S(2)}, u32[]{:S(2)}) %all-to-all-start.5) | async-done | bytes 591520 | tf_op jit(solution)/shard_map/all_to_all | solution.py:1052
  779.0 13.3 %shard_map.401 = (bf16[512,576]{1,0:T(8,128)(2,1)}, f32[512,32]{1,0:T(8,128)}, f32[40,576]{1,0:T(8,128)}) custom-call(s32[5]{0:T(128)} %stack.80.refs_0_, bf16[560,576]{1,0:T(8,128)(2,1)} %get-tuple-element.555.refs_9_.refs_1_, bf16[560,576]{1,0:T(8,128)(2,1)} %collective-permute-done.1.refs_10_.refs_2_, ...), custom_call_target="tpu_custom_call" | custom-call | tf_op jit(solution)/shard_map/pallas_call | solution.py:721
  798.4 15.8 %shard_map.402 = (bf16[512,576]{1,0:T(8,128)(2,1)}, bf16[512,576]{1,0:T(8,128)(2,1)}, f32[512,32]{1,0:T(8,128)}, f32[256,2304]{1,0:T(8,128)}, bf16[256,2304]{1,0:T(8,128)(2,1)}) custom-call(s32[5]{0:T(128)} %stack.80.refs_0_, bf16[560,576]{1,0:T(8,128)(2,1)} %get-tuple-element.561.refs_1_, bf16[560,576]{1,0:T(8,128)(2,1)} %collective-permute-done.refs_2_, ...), custom_call_target="tpu_custom_call" | custom-call | tf_op jit(solution)/shard_map/pallas_call | solution.py:721
  829.3 18.4 %all-to-all-done.1 = f32[4,4,512]{2,1,0:T(4,128)S(1)} async-done(((f32[4,4,512]{2,1,0:T(4,128)}), f32[4,4,512]{2,1,0:T(4,128)S(1)}, u32[]{:S(2)}, u32[]{:S(2)}) %all-to-all-start.1) | async-done | bytes 32800 | tf_op jit(solution)/shard_map/all_to_all | solution.py:1037
  (556 shorter events, 374.0 us)
Async XLA Ops:
  41.7 29.2 %collective-permute-start.4 = (bf16[560,576]{1,0:T(8,128)(2,1)}, bf16[560,576]{1,0:T(8,128)(2,1)}, u32[]{:S(2)}, u32[]{:S(2)}) collective-permute-start(bf16[560,576]{1,0:T(8,128)(2,1)} %collective-permute-done.1.refs_10_.refs_2_), channel_id=1, source_target_pairs={{0,16},{16,24},{24,8},{8,0},{1,17},{17,25},{25,9},{9,1},{2,18},{18... | collective-permute-start | bytes 1935368 | tf_op jit(solution)/shard_map/ppermute | solution.py:571
  55.5 34.5 %collective-permute-start.7 = (bf16[560,576]{1,0:T(8,128)(2,1)}, bf16[560,576]{1,0:T(8,128)(2,1)}, u32[]{:S(2)}, u32[]{:S(2)}) collective-permute-start(bf16[560,576]{1,0:T(8,128)(2,1)} %collective-permute-done.2.refs_3_), channel_id=1, source_target_pairs={{0,4},{4,0},{1,5},{5,1},{2,6},{6,2},{3,7},{7,3},{8,12},{12,8},{9,1... | collective-permute-start | bytes 1935368 | tf_op jit(solution)/shard_map/ppermute | solution.py:555
  57.0 33.0 %collective-permute-start.6 = (bf16[560,576]{1,0:T(8,128)(2,1)}, bf16[560,576]{1,0:T(8,128)(2,1)}, u32[]{:S(2)}, u32[]{:S(2)}) collective-permute-start(bf16[560,576]{1,0:T(8,128)(2,1)} %collective-permute-done.2.refs_3_), channel_id=1, source_target_pairs={{0,16},{16,24},{24,8},{8,0},{1,17},{17,25},{25,9},{9,1},{2,18},{18... | collective-permute-start | bytes 1935368 | tf_op jit(solution)/shard_map/ppermute | solution.py:571
  72.4 29.2 %collective-permute-start.8 = (bf16[560,576]{1,0:T(8,128)(2,1)}, bf16[560,576]{1,0:T(8,128)(2,1)}, u32[]{:S(2)}, u32[]{:S(2)}) collective-permute-start(bf16[560,576]{1,0:T(8,128)(2,1)} %collective-permute-done.4.refs_11_.refs_3_), channel_id=1, source_target_pairs={{0,16},{16,24},{24,8},{8,0},{1,17},{17,25},{25,9},{9,1},{2,18},{18... | collective-permute-start | bytes 1935368 | tf_op jit(solution)/shard_map/ppermute | solution.py:571
  104.7 34.5 %collective-permute-start.14 = (bf16[560,576]{1,0:T(8,128)(2,1)}, bf16[560,576]{1,0:T(8,128)(2,1)}, u32[]{:S(2)}, u32[]{:S(2)}) collective-permute-start(bf16[560,576]{1,0:T(8,128)(2,1)} %get-tuple-element.557.refs_9_), channel_id=1, source_target_pairs={{0,16},{16,24},{24,8},{8,0},{1,17},{17,25},{25,9},{9,1},{2,18},{18... | collective-permute-start | bytes 1935368 | tf_op jit(solution)/shard_map/ppermute | solution.py:571
  158.4 35.0 %collective-permute-start.20 = (bf16[256,2304]{1,0:T(8,128)(2,1)}, bf16[256,2304]{1,0:T(8,128)(2,1)}, u32[]{:S(2)}, u32[]{:S(2)}) collective-permute-start(bf16[256,2304]{1,0:T(8,128)(2,1)} %add_convert_fusion.5.refs_0_), channel_id=1, source_target_pairs={{0,2},{1,3},{2,0},{3,1},{4,6},{5,7},{6,4},{7,5},{8,10},{9,11},{10,... | collective-permute-start | bytes 3538952 | tf_op jit(solution)/shard_map/ppermute | solution.py:555
  161.6 31.5 %collective-permute-start.19 = (bf16[560,576]{1,0:T(8,128)(2,1)}, bf16[560,576]{1,0:T(8,128)(2,1)}, u32[]{:S(2)}, u32[]{:S(2)}) collective-permute-start(bf16[560,576]{1,0:T(8,128)(2,1)} %collective-permute-done.14.refs_10_), channel_id=1, source_target_pairs={{0,4},{4,0},{1,5},{5,1},{2,6},{6,2},{3,7},{7,3},{8,12},{12,8},{9,1... | collective-permute-start | bytes 1935368 | tf_op jit(solution)/shard_map/ppermute | solution.py:555
  162.9 30.5 %collective-permute-start.18 = (bf16[560,576]{1,0:T(8,128)(2,1)}, bf16[560,576]{1,0:T(8,128)(2,1)}, u32[]{:S(2)}, u32[]{:S(2)}) collective-permute-start(bf16[560,576]{1,0:T(8,128)(2,1)} %collective-permute-done.14.refs_10_), channel_id=1, source_target_pairs={{0,16},{16,24},{24,8},{8,0},{1,17},{17,25},{25,9},{9,1},{2,18},{18... | collective-permute-start | bytes 1935368 | tf_op jit(solution)/shard_map/ppermute | solution.py:571
  197.7 41.8 %collective-permute-start.21 = (bf16[256,2304]{1,0:T(8,128)(2,1)}, bf16[256,2304]{1,0:T(8,128)(2,1)}, u32[]{:S(2)}, u32[]{:S(2)}) collective-permute-start(bf16[256,2304]{1,0:T(8,128)(2,1)} %get-tuple-element.347.refs_17_), channel_id=1, source_target_pairs={{0,1},{1,0},{2,3},{3,2},{4,5},{5,4},{6,7},{7,6},{8,9},{9,8},{10,11... | collective-permute-start | bytes 3538952 | tf_op jit(solution)/shard_map/ppermute | solution.py:555
  204.3 35.3 %collective-permute-start.25 = (bf16[560,576]{1,0:T(8,128)(2,1)}, bf16[560,576]{1,0:T(8,128)(2,1)S(1)}, u32[]{:S(2)}, u32[]{:S(2)}) collective-permute-start(bf16[560,576]{1,0:T(8,128)(2,1)} %collective-permute-done.18.refs_11_), channel_id=1, source_target_pairs={{0,4},{4,0},{1,5},{5,1},{2,6},{6,2},{3,7},{7,3},{8,12},{12,8},{9,1... | collective-permute-start | bytes 1935368 | tf_op jit(solution)/shard_map/ppermute | solution.py:555
  204.8 34.7 %collective-permute-start.24 = (bf16[560,576]{1,0:T(8,128)(2,1)}, bf16[560,576]{1,0:T(8,128)(2,1)S(1)}, u32[]{:S(2)}, u32[]{:S(2)}) collective-permute-start(bf16[560,576]{1,0:T(8,128)(2,1)} %collective-permute-done.18.refs_11_), channel_id=1, source_target_pairs={{0,16},{16,24},{24,8},{8,0},{1,17},{17,25},{25,9},{9,1},{2,18},{18... | collective-permute-start | bytes 1935368 | tf_op jit(solution)/shard_map/ppermute | solution.py:571
  207.2 32.4 %collective-permute-start.22 = (bf16[560,576]{1,0:T(8,128)(2,1)}, bf16[560,576]{1,0:T(8,128)(2,1)S(1)}, u32[]{:S(2)}, u32[]{:S(2)}) collective-permute-start(bf16[560,576]{1,0:T(8,128)(2,1)} %collective-permute-done.16.refs_3_), channel_id=1, source_target_pairs={{0,16},{16,24},{24,8},{8,0},{1,17},{17,25},{25,9},{9,1},{2,18},{18... | collective-permute-start | bytes 1935368 | tf_op jit(solution)/shard_map/ppermute | solution.py:571
  217.9 40.1 %collective-permute-start.26 = (bf16[560,700]{1,0:T(8,128)(2,1)S(1)}, bf16[560,700]{1,0:T(8,128)(2,1)}, u32[]{:S(2)}, u32[]{:S(2)}) collective-permute-start(bf16[560,700]{1,0:T(8,128)(2,1)S(1)} %get-tuple-element.567.refs_1_), channel_id=1, source_target_pairs={{0,16},{16,24},{24,8},{8,0},{1,17},{17,25},{25,9},{9,1},{2,18},{18... | collective-permute-start | bytes 2352008 | tf_op jit(solution)/shard_map/ppermute | solution.py:571
  239.6 32.1 %collective-permute-start.28 = (bf16[560,576]{1,0:T(8,128)(2,1)S(1)}, bf16[560,576]{1,0:T(8,128)(2,1)S(1)}, u32[]{:S(2)}, u32[]{:S(2)}) collective-permute-start(bf16[560,576]{1,0:T(8,128)(2,1)S(1)} %collective-permute-done.24.refs_12_), channel_id=1, source_target_pairs={{0,4},{4,0},{1,5},{5,1},{2,6},{6,2},{3,7},{7,3},{8,12},{12,8},{9,1... | collective-permute-start | bytes 1935368 | tf_op jit(solution)/shard_map/ppermute | solution.py:555
  241.1 30.5 %collective-permute-start.27 = (bf16[560,576]{1,0:T(8,128)(2,1)S(1)}, bf16[560,576]{1,0:T(8,128)(2,1)S(1)}, u32[]{:S(2)}, u32[]{:S(2)}) collective-permute-start(bf16[560,576]{1,0:T(8,128)(2,1)S(1)} %collective-permute-done.22.refs_4_), channel_id=1, source_target_pairs={{0,4},{4,0},{1,5},{5,1},{2,6},{6,2},{3,7},{7,3},{8,12},{12,8},{9,1... | collective-permute-start | bytes 1935368 | tf_op jit(solution)/shard_map/ppermute | solution.py:555
  241.7 42.2 %collective-permute-start.30 = (bf16[560,700]{1,0:T(8,128)(2,1)}, bf16[560,700]{1,0:T(8,128)(2,1)}, u32[]{:S(2)}, u32[]{:S(2)}) collective-permute-start(bf16[560,700]{1,0:T(8,128)(2,1)} %get-tuple-element.566.refs_9_), channel_id=1, source_target_pairs={{0,16},{16,24},{24,8},{8,0},{1,17},{17,25},{25,9},{9,1},{2,18},{18... | collective-permute-start | bytes 2352008 | tf_op jit(solution)/shard_map/ppermute | solution.py:571
  319.6 43.1 %collective-permute-start.36 = (bf16[256,2304]{1,0:T(8,128)(2,1)}, bf16[256,2304]{1,0:T(8,128)(2,1)}, u32[]{:S(2)}, u32[]{:S(2)}) collective-permute-start(bf16[256,2304]{1,0:T(8,128)(2,1)} %add_convert_fusion.4.refs_0_), channel_id=1, source_target_pairs={{0,2},{1,3},{2,0},{3,1},{4,6},{5,7},{6,4},{7,5},{8,10},{9,11},{10,... | collective-permute-start | bytes 3538952 | tf_op jit(solution)/shard_map/ppermute | solution.py:555
  323.4 36.6 %collective-permute-start.35 = (bf16[560,700]{1,0:T(8,128)(2,1)}, bf16[560,700]{1,0:T(8,128)(2,1)}, u32[]{:S(2)}, u32[]{:S(2)}) collective-permute-start(bf16[560,700]{1,0:T(8,128)(2,1)} %collective-permute-done.30.refs_10_), channel_id=1, source_target_pairs={{0,4},{4,0},{1,5},{5,1},{2,6},{6,2},{3,7},{7,3},{8,12},{12,8},{9,1... | collective-permute-start | bytes 2352008 | tf_op jit(solution)/shard_map/ppermute | solution.py:555
  324.0 38.6 %collective-permute-start.34 = (bf16[560,700]{1,0:T(8,128)(2,1)}, bf16[560,700]{1,0:T(8,128)(2,1)}, u32[]{:S(2)}, u32[]{:S(2)}) collective-permute-start(bf16[560,700]{1,0:T(8,128)(2,1)} %collective-permute-done.30.refs_10_), channel_id=1, source_target_pairs={{0,16},{16,24},{24,8},{8,0},{1,17},{17,25},{25,9},{9,1},{2,18},{18... | collective-permute-start | bytes 2352008 | tf_op jit(solution)/shard_map/ppermute | solution.py:571
  342.7 58.0 %collective-permute-start.40 = (bf16[560,700]{1,0:T(8,128)(2,1)}, bf16[560,700]{1,0:T(8,128)(2,1)}, u32[]{:S(2)}, u32[]{:S(2)}) collective-permute-start(bf16[560,700]{1,0:T(8,128)(2,1)} %get-tuple-element.573.refs_1_), channel_id=1, source_target_pairs={{0,16},{16,24},{24,8},{8,0},{1,17},{17,25},{25,9},{9,1},{2,18},{18... | collective-permute-start | bytes 2352008 | tf_op jit(solution)/shard_map/ppermute | solution.py:571
  368.8 30.6 %collective-permute-start.37 = (bf16[256,2304]{1,0:T(8,128)(2,1)}, bf16[256,2304]{1,0:T(8,128)(2,1)}, u32[]{:S(2)}, u32[]{:S(2)}) collective-permute-start(bf16[256,2304]{1,0:T(8,128)(2,1)} %get-tuple-element.392.refs_17_), channel_id=1, source_target_pairs={{0,1},{1,0},{2,3},{3,2},{4,5},{5,4},{6,7},{7,6},{8,9},{9,8},{10,11... | collective-permute-start | bytes 3538952 | tf_op jit(solution)/shard_map/ppermute | solution.py:555
  369.8 29.6 %collective-permute-start.38 = (bf16[560,700]{1,0:T(8,128)(2,1)}, bf16[560,700]{1,0:T(8,128)(2,1)S(1)}, u32[]{:S(2)}, u32[]{:S(2)}) collective-permute-start(bf16[560,700]{1,0:T(8,128)(2,1)} %collective-permute-done.32.refs_3_), channel_id=1, source_target_pairs={{0,16},{16,24},{24,8},{8,0},{1,17},{17,25},{25,9},{9,1},{2,18},{18... | collective-permute-start | bytes 2352008 | tf_op jit(solution)/shard_map/ppermute | solution.py:571
  378.9 31.0 %collective-permute-start.41 = (bf16[560,700]{1,0:T(8,128)(2,1)}, bf16[560,700]{1,0:T(8,128)(2,1)S(1)}, u32[]{:S(2)}, u32[]{:S(2)}) collective-permute-start(bf16[560,700]{1,0:T(8,128)(2,1)} %collective-permute-done.34.refs_11_), channel_id=1, source_target_pairs={{0,4},{4,0},{1,5},{5,1},{2,6},{6,2},{3,7},{7,3},{8,12},{12,8},{9,1... | collective-permute-start | bytes 2352008 | tf_op jit(solution)/shard_map/ppermute | solution.py:555
  409.8 37.0 %collective-permute-start.45 = (bf16[560,700]{1,0:T(8,128)(2,1)}, bf16[560,700]{1,0:T(8,128)(2,1)}, u32[]{:S(2)}, u32[]{:S(2)}) collective-permute-start(bf16[560,700]{1,0:T(8,128)(2,1)} %collective-permute-done.40.refs_2_), channel_id=1, source_target_pairs={{0,4},{4,0},{1,5},{5,1},{2,6},{6,2},{3,7},{7,3},{8,12},{12,8},{9,1... | collective-permute-start | bytes 2352008 | tf_op jit(solution)/shard_map/ppermute | solution.py:555
  410.4 36.4 %collective-permute-start.44 = (bf16[560,700]{1,0:T(8,128)(2,1)}, bf16[560,700]{1,0:T(8,128)(2,1)}, u32[]{:S(2)}, u32[]{:S(2)}) collective-permute-start(bf16[560,700]{1,0:T(8,128)(2,1)} %collective-permute-done.40.refs_2_), channel_id=1, source_target_pairs={{0,16},{16,24},{24,8},{8,0},{1,17},{17,25},{25,9},{9,1},{2,18},{18... | collective-permute-start | bytes 2352008 | tf_op jit(solution)/shard_map/ppermute | solution.py:571
  429.2 35.7 %collective-permute-start.46 = (bf16[560,700]{1,0:T(8,128)(2,1)}, bf16[560,700]{1,0:T(8,128)(2,1)}, u32[]{:S(2)}, u32[]{:S(2)}) collective-permute-start(bf16[560,700]{1,0:T(8,128)(2,1)} %collective-permute-done.42.refs_12_), channel_id=1, source_target_pairs={{0,4},{4,0},{1,5},{5,1},{2,6},{6,2},{3,7},{7,3},{8,12},{12,8},{9,1... | collective-permute-start | bytes 2352008 | tf_op jit(solution)/shard_map/ppermute | solution.py:555
  446.8 46.5 %collective-permute-start.48 = (bf16[560,700]{1,0:T(8,128)(2,1)}, bf16[560,700]{1,0:T(8,128)(2,1)}, u32[]{:S(2)}, u32[]{:S(2)}) collective-permute-start(bf16[560,700]{1,0:T(8,128)(2,1)} %collective-permute-done.44.refs_3_), channel_id=1, source_target_pairs={{0,16},{16,24},{24,8},{8,0},{1,17},{17,25},{25,9},{9,1},{2,18},{18... | collective-permute-start | bytes 2352008 | tf_op jit(solution)/shard_map/ppermute | solution.py:571
  498.3 35.6 %collective-permute-start.50 = (bf16[560,700]{1,0:T(8,128)(2,1)}, bf16[560,700]{1,0:T(8,128)(2,1)S(1)}, u32[]{:S(2)}, u32[]{:S(2)}) collective-permute-start(bf16[560,700]{1,0:T(8,128)(2,1)} %collective-permute-done.48.refs_4_), channel_id=1, source_target_pairs={{0,4},{4,0},{1,5},{5,1},{2,6},{6,2},{3,7},{7,3},{8,12},{12,8},{9,1... | collective-permute-start | bytes 2352008 | tf_op jit(solution)/shard_map/ppermute | solution.py:555
  605.8 51.0 %collective-permute-start.52 = (bf16[256,2304]{1,0:T(8,128)(2,1)S(1)}, bf16[256,2304]{1,0:T(8,128)(2,1)}, u32[]{:S(2)}, u32[]{:S(2)}) collective-permute-start(bf16[256,2304]{1,0:T(8,128)(2,1)S(1)} %add_convert_fusion.3.refs_0_), channel_id=1, source_target_pairs={{0,2},{1,3},{2,0},{3,1},{4,6},{5,7},{6,4},{7,5},{8,10},{9,11},{10,... | collective-permute-start | bytes 3538952 | tf_op jit(solution)/shard_map/ppermute | solution.py:555
  661.0 89.1 %collective-permute-start.53 = (f32[256,2304]{1,0:T(8,128)}, f32[256,2304]{1,0:T(8,128)}, u32[]{:S(2)}, u32[]{:S(2)}) collective-permute-start(f32[256,2304]{1,0:T(8,128)} %shard_map.395.refs_1_), channel_id=1, source_target_pairs={{0,1},{1,0},{2,3},{3,2},{4,5},{5,4},{6,7},{7,6},{8,9},{9,8},{10,11... | collective-permute-start | bytes 7077896 | tf_op jit(solution)/shard_map/ppermute | solution.py:555
  694.0 45.2 %collective-permute-start.58 = (bf16[256,2304]{1,0:T(8,128)(2,1)}, bf16[256,2304]{1,0:T(8,128)(2,1)}, u32[]{:S(2)}, u32[]{:S(2)}) collective-permute-start(bf16[256,2304]{1,0:T(8,128)(2,1)} %get-tuple-element.424), channel_id=1, source_target_pairs={{0,1},{1,0},{2,3},{3,2},{4,5},{5,4},{6,7},{7,6},{8,9},{9,8},{10,11... | collective-permute-start | bytes 3538952 | tf_op jit(solution)/shard_map/ppermute | solution.py:555
  819.2 31.8 %collective-permute-start.63 = (bf16[256,2304]{1,0:T(8,128)(2,1)S(1)}, bf16[256,2304]{1,0:T(8,128)(2,1)S(1)}, u32[]{:S(2)}, u32[]{:S(2)}) collective-permute-start(bf16[256,2304]{1,0:T(8,128)(2,1)S(1)} %add_convert_fusion.refs_0_), channel_id=1, source_target_pairs={{0,2},{1,3},{2,0},{3,1},{4,6},{5,7},{6,4},{7,5},{8,10},{9,11},{10,... | collective-permute-start | bytes 3538952 | tf_op jit(solution)/shard_map/ppermute | solution.py:555
  (115 other events, 2102.1 us)

commit v2 on v1

v2 whole, which is shorter than its diff:
```python
import functools
import jax
import jax.numpy as jnp
from jax import lax
from jax.experimental import pallas as pl
from jax.experimental.pallas import tpu as pltpu
from jax.sharding import PartitionSpec as P

W, C, T = "weight", "context", "tensor"
HD = 32
LANES = 128
bf16, f32 = jnp.bfloat16, jnp.float32
full_precision = lax.Precision.HIGHEST
norm_eps = 1e-06
attention_epsilon = 1e-06
masked_score = -1000000000.0
big = pltpu.CompilerParams(vmem_limit_bytes=58 * 1024 * 1024)


def shape(dims, dtype):
    return jax.ShapeDtypeStruct(dims, dtype)


def mm(a, b, ca=1, cb=0):
    return lax.dot_general(a, b, (((ca,), (cb,)), ((), ())), preferred_element_type=f32)


def two(pair):
    high = pair.astype(bf16)
    rest = (pair - high.astype(f32)).astype(bf16)
    lane = lax.broadcasted_iota(jnp.int32, pair.shape, 1)
    return jnp.where(lane < pair.shape[1] // 2, high.astype(f32), rest.astype(f32)).astype(bf16)


def split(values):
    high = values.astype(bf16)
    return high, (values - high.astype(f32)).astype(bf16)


def mm3(a, b, ca=1, cb=0):
    ah, al = split(a)
    bh, bl = split(b)
    return mm(ah, bh, ca, cb) + mm(ah, bl, ca, cb) + mm(al, bh, ca, cb)


def head_mask(width):
    row = lax.broadcasted_iota(jnp.int32, (width, width), 0) // HD
    col = lax.broadcasted_iota(jnp.int32, (width, width), 1) // HD
    return (row == col).astype(f32)


def head_total(values, mask):
    high, low = split(values)
    low_mask = mask.astype(bf16)
    return mm(high, low_mask) + mm(low, low_mask)


def squeeze_heads(square, mask):
    kept = square * mask
    total = kept[:HD]
    for h in range(1, kept.shape[0] // HD):
        total = total + kept[h * HD : (h + 1) * HD]
    return total


def spread_heads(state, width, mask):
    return jnp.concatenate([state] * (width // HD), axis=0) * mask


def sigmoid(values):
    return 1.0 / (1.0 + jnp.exp(-values))


def row_stats(values):
    center = values - jnp.mean(values, axis=-1, keepdims=True)
    inverse = lax.rsqrt(jnp.mean(center * center, axis=-1, keepdims=True) + norm_eps)
    return center * inverse, inverse


def put(out, rows, values):
    width = values.shape[1]
    out[rows, :width] = values.astype(out.dtype)
    if width < out.shape[1]:
        out[rows, width:] = jnp.zeros((values.shape[0], out.shape[1] - width), out.dtype)


everything = slice(None)


def attn_front(w, x, mods, d2, u2, a_out, q_out, k_out, lat_out):
    n = x.shape[0]
    step = 64

    def norm(i, carry):
        at = pl.ds(pl.multiple_of(i * step, step), step)
        normed, unused = row_stats(x[at, :].astype(f32))
        a_out[at, :] = (normed * (1.0 + mods[1:2, :]) + mods[0:1, :]).astype(bf16)
        return carry

    lax.fori_loop(0, n // step, norm, 0)
    a = a_out[...]
    lat = mm(a, d2[...])
    lat_out[...] = lat
    pair = two(lat)
    width = q_out.shape[1]
    both = mm(a, w[0].take(0))
    q_out[...] = both[:, :width] + mm(pair, u2[0])
    k_out[...] = both[:, width:] + mm(pair, u2[1])


def attn_state(w, a, k, lat, u2, v_out, st_out):
    w[0].take(0)
    v_out[...] = mm(a[...], w[0].columns(0, 0, v_out.shape[1])) + mm(two(lat[...]), u2[2])
    keys = jnp.maximum(k[...], 0.0)
    width = keys.shape[1]
    st_out[:HD, :] = squeeze_heads(mm3(v_out[...], keys, 0, 0), head_mask(width))
    st_out[HD:, :] = jnp.broadcast_to(jnp.sum(keys, axis=0, keepdims=True), (8, width))


def put_partial(low, lat_pair, w, u2, mine, away):
    half = mine.shape[0]
    put(mine, everything, mm(low[:half], w, 1, 1) + mm(lat_pair[:half], u2))
    put(away, everything, mm(low[half:], w, 1, 1) + mm(lat_pair[half:], u2))


def attn_back(w, q, st1, st2, owned, d2, u2, ratio_out, den_out, mixed_out, lat_out, mine, away):
    st = st1[...] + st2[...]
    width = q.shape[1]
    mask = head_mask(width)
    queries = jnp.maximum(q[...], 0.0)
    numer = mm3(queries, spread_heads(st[:HD], width, mask), 1, 1)
    den = head_total(queries * st[HD : HD + 1], mask) + attention_epsilon
    ratio = numer / den
    ratio_out[...] = ratio
    den_out[...] = den
    mixed = (ratio * owned[...]).astype(bf16)
    mixed_out[...] = mixed
    lat = mm(mixed, d2[...])
    lat_out[...] = lat
    w[0].take(0)
    put_partial(mixed, two(lat), w[0].columns(0, width, width), u2[...], mine, away)


def caption_rows(w, own, other, d2, u2, kv_out, lat_out):
    here = own.shape[0]
    depth = d2.shape[0]
    width = u2.shape[2]
    weight = w[0].take(0)
    for i, rows in enumerate((own, other)):
        lat = mm(rows[:, :depth], d2[...])
        if i == 0:
            lat_out[...] = lat
        both = mm(rows[:, :depth], weight)
        for j in range(2):
            out = both[:, j * width : (j + 1) * width] + mm(two(lat), u2[j])
            kv_out[j, i * here : (i + 1) * here, :] = out.astype(bf16)


def lane_groups(width):
    return [(at, min(LANES, width - at)) for at in range(0, width, LANES)]


def only_head(values, j):
    lane = lax.broadcasted_iota(jnp.int32, values.shape, 1) // HD
    return jnp.where(lane == j, values.astype(f32), 0.0).astype(values.dtype)


def cross_fwd(
    w, rows, kv, live, owned, qd2, qu2, cd2, cu2, q_out, mix_out, qlat_out, clat_out, lse_out, part,
):
    width = q_out.shape[1]
    depth = qd2.shape[0]
    w[0].take(0)
    lat = mm(rows[:, :depth], qd2[...])
    qlat_out[...] = lat
    q_out[...] = (mm(rows[:, :depth], w[0].columns(0, 0, width)) + mm(two(lat), qu2[...])).astype(bf16)
    for first, size in lane_groups(width):
        cols = slice(first, first + size)
        query = q_out[:, cols]
        total = None
        for j in range(size // HD):
            scores = mm(query, only_head(kv[0, :, cols], j), 1, 1) * HD ** (-0.5)
            scores = jnp.where(live[...] > 0.0, scores, masked_score)
            top = jnp.max(scores, axis=-1, keepdims=True)
            exps = jnp.exp(scores - top)
            tot = jnp.sum(exps, axis=-1, keepdims=True)
            h = first // HD + j
            lse_out[:, h : h + 1] = top + jnp.log(tot)
            probs = (exps * (1.0 / tot)).astype(bf16)
            term = mm(probs, only_head(kv[1, :, cols], j))
            total = term if total is None else total + term
        mix_out[:, cols] = (total * owned[:, cols]).astype(bf16)
    mix = mix_out[...]
    lat = mm(mix, cd2[...])
    clat_out[...] = lat
    put(part, everything, mm(mix, w[0].columns(0, width, width), 1, 1) + mm(two(lat), cu2[...]))


def edge_rows(where, rows, edge):
    r = jnp.where(where[1] == 0, rows // edge - 1, 0)
    return pl.ds(own_first(r, edge, rows // 2, where[0]), edge)


def ffn_front(w, where, xo, xt, d2, uv, ug, pv, pg, hv, hg, lat_out, ev, eg, u):
    half = xo.shape[0]
    depth = d2.shape[0]
    h = pl.program_id(0)

    @pl.when(h == 0)
    def first():
        u[:half, :] = xo[:, :depth]
        u[half:, :] = xt[:, :depth]
        lat_out[...] = mm(u[...], d2[...])

    both = mm(u[...], w[0].take(h))
    pair = two(lat_out[...])
    hh = uv.shape[2]
    at = edge_rows(where, u.shape[0], ev.shape[1])
    for i, (up, pre, hid, edge) in enumerate(((uv, pv, hv, ev), (ug, pg, hg, eg))):
        s = both[:, i * hh : (i + 1) * hh] + mm(pair, up[0])
        pre[0] = s
        hid[0] = (s * sigmoid(s)).astype(bf16)
        edge[0] = hid[0, at, :]


def fill_grid(buf, rows, halo, b, c):
    half = rows.shape[0] // 2
    edge = halo.shape[0]
    buf[pl.ds(pl.multiple_of(edge + b * half, edge), half), :] = rows[:half, :].astype(f32)
    buf[pl.ds(pl.multiple_of(edge + (1 - b) * half, edge), half), :] = rows[half:, :].astype(f32)
    zero = jnp.zeros(halo.shape, f32)
    got = halo.astype(f32)
    buf[:edge, :] = jnp.where(c == 0, zero, got)
    buf[buf.shape[0] - edge :, :] = jnp.where(c == 0, got, zero)


def conv_row(buf, taps, r, edge, flip):
    sums = []
    rows = [buf[pl.ds(pl.multiple_of((r + i) * edge, edge), edge), :] for i in range(3)]
    for j in range(3):
        total = None
        for i in range(3):
            k = (2 - i) * 3 + 2 - j if flip else i * 3 + j
            term = rows[i] * taps[k : k + 1, :]
            total = term if total is None else total + term
        sums.append(total)
    cell = lax.broadcasted_iota(jnp.int32, sums[0].shape, 0)
    left = jnp.where(cell == 0, 0.0, pltpu.roll(sums[0], 1, 0))
    right = jnp.where(cell == edge - 1, 0.0, pltpu.roll(sums[2], edge - 1, 0))
    return left + sums[1] + right


def own_first(r, edge, half, b):
    per = half // edge
    return pl.multiple_of(jnp.where(r // per == b, 0, half) + (r % per) * edge, edge)


def ffn_mid(
    w, where, hv, hg, halo_v, halo_g, taps, cot, gate, d2, u2,
    gated_out, gcv_out, gcg_out, gffn_out, gl_out, lat_out, down_out, edge_out, mine, away, bv, bg, gg, acc,
):
    h = pl.program_id(0)
    b, c = where[0], where[1]
    n = hv.shape[1]
    half = n // 2
    edge = halo_v.shape[1]

    @pl.when(h == 0)
    def first():
        gffn_out[...] = (gate[...] * cot[...].astype(f32)).astype(bf16)
        gl_out[...] = mm(gffn_out[...], u2[...], 1, 1)

    fill_grid(bv, hv[0], halo_v[0], b, c)
    fill_grid(bg, hg[0], halo_g[0], b, c)
    weight = w[0].take(h)
    gg[...] = mm(gffn_out[...], weight) + mm(two(gl_out[...]), d2[0], 1, 1)

    def row(r, carry):
        v = conv_row(bv, taps[0, 0], r, edge, False)
        g = conv_row(bg, taps[0, 1], r, edge, False)
        sig = sigmoid(g)
        act = g * sig
        at = pl.ds(own_first(r, edge, half, b), edge)
        gated_out[0, at, :] = (v * act).astype(bf16)
        grad = gg[at, :]
        gcv_out[0, at, :] = (grad * act).astype(bf16)
        gcg_out[0, at, :] = (grad * v * (sig * (1.0 + g * (1.0 - sig)))).astype(bf16)
        return carry

    lax.fori_loop(0, n // edge, row, 0)
    at = edge_rows(where, n, edge)
    edge_out[0, 0] = gcv_out[0, at, :]
    edge_out[0, 1] = gcg_out[0, at, :]
    gated = gated_out[0]
    down_out[0] = mm(two(gl_out[...]), gated, 0, 0)
    part = mm(gated, weight, 1, 1)
    lat = mm(gated, d2[0])

    @pl.when(h == 0)
    def start():
        acc[...] = part
        lat_out[...] = lat

    @pl.when(h == 1)
    def end():
        total = lat_out[...] + lat
        lat_out[...] = total
        full = acc[...] + part + mm(two(total), u2[...])
        put(mine, everything, full[:half])
        put(away, everything, full[half:])


def ffn_back(
    w, where, gcv, gcg, halo, taps, pv, pg, lat, d2, uv, ug,
    gpv_out, gpg_out, up_out, gl_out, mine, away, bv, bg, acc,
):
    h = pl.program_id(0)
    b, c = where[0], where[1]
    n = gcv.shape[1]
    half = n // 2
    edge = halo.shape[2]
    fill_grid(bv, gcv[0], halo[0, 0], b, c)
    fill_grid(bg, gcg[0], halo[0, 1], b, c)

    def row(r, carry):
        at = pl.ds(own_first(r, edge, half, b), edge)
        for i, (buf, pre, out) in enumerate(((bv, pv, gpv_out), (bg, pg, gpg_out))):
            grad = conv_row(buf, taps[0, i], r, edge, True)
            s = pre[0, at, :]
            sig = sigmoid(s)
            out[0, at, :] = (grad * (sig * (1.0 + s * (1.0 - sig)))).astype(bf16)
        return carry

    lax.fori_loop(0, n // edge, row, 0)
    gpv, gpg = gpv_out[0], gpg_out[0]
    part = mm(jnp.concatenate([gpv, gpg], axis=1), w[0].take(h), 1, 1)
    gl = mm(gpv, uv[0], 1, 1) + mm(gpg, ug[0], 1, 1)
    pair = two(lat[...])
    up_out[0, 0] = mm(pair, gpv, 0, 0)
    up_out[0, 1] = mm(pair, gpg, 0, 0)

    @pl.when(h == 0)
    def start():
        acc[...] = part
        gl_out[...] = gl

    @pl.when(h == 1)
    def end():
        total = gl_out[...] + gl
        gl_out[...] = total
        full = acc[...] + part + mm(two(total), d2[...], 1, 1)
        put(mine, everything, full[:half])
        put(away, everything, full[half:])


def cross_bwd(
    w, go, gt, kv, live, owned, qd2, qu2, cd2, cu2, qo, qt, lo, lt,
    gq_out, gkv_out, qgl_out, cgl_out, mine, away, gm, gqs,
):
    half = go.shape[0]
    width = qo.shape[1]
    w[0].take(0)
    depth = cu2.shape[1]
    weight = w[0].columns(0, width, width)
    scale = HD ** (-0.5)
    for i, (rows, query, lse) in enumerate(((go, qo, lo), (gt, qt, lt))):
        at = slice(i * half, (i + 1) * half)
        gl = mm(rows[:, :depth], cu2[...], 1, 1)
        cgl_out[at, :] = gl
        grad = mm(rows[:, :depth], weight) + mm(two(gl), cd2[...], 1, 1)
        gm[...] = (grad * owned[...]).astype(bf16)
        for first, size in lane_groups(width):
            cols = slice(first, first + size)
            q_all, g_all = query[:, cols], gm[:, cols]
            grad_q, grad_k, grad_v = 0.0, 0.0, 0.0
            for j in range(size // HD):
                key, val = only_head(kv[0, :, cols], j), only_head(kv[1, :, cols], j)
                h = first // HD + j
                scores = mm(q_all, key, 1, 1) * scale
                scores = jnp.where(live[...] > 0.0, scores, masked_score)
                probs = jnp.exp(scores - lse[:, h : h + 1])
                grad_p = mm(g_all, val, 1, 1)
                grad_v = grad_v + mm(probs.astype(bf16), only_head(g_all, j), 0, 0)
                inner = jnp.sum(probs * grad_p, axis=-1, keepdims=True)
                grad_s = (probs * (grad_p - inner)).astype(bf16)
                grad_q = grad_q + mm(grad_s, key)
                grad_k = grad_k + mm(grad_s, only_head(q_all, j), 0, 0)
            gqs[at, cols] = grad_q
            for side, new in ((0, grad_k * scale), (1, grad_v)):
                gkv_out[side, :, cols] = new if i == 0 else gkv_out[side, :, cols] + new
    gq = (gqs[...] * scale).astype(bf16)
    gq_out[...] = gq
    gl = mm(gq, qu2[...], 1, 1)
    qgl_out[...] = gl
    pair = two(gl)
    weight = w[0].columns(0, 0, width)
    put(mine, everything, mm(gq[:half], weight, 1, 1) + mm(pair[:half], qd2[...], 1, 1))
    put(away, everything, mm(gq[half:], weight, 1, 1) + mm(pair[half:], qd2[...], 1, 1))


def linear_bwd(
    w, go, gt, q, st1, st2, ratio, den, owned, d2, u2, gq_out, gl_out, st_out, gh,
):
    half = go.shape[0]
    width = q.shape[1]
    depth = u2.shape[1]
    w[0].take(0)
    weight = w[0].columns(0, width, width)
    for i, rows in enumerate((go, gt)):
        at = pl.ds(i * half, half)
        gl = mm(rows[:, :depth], u2[...], 1, 1)
        gl_out[at, :] = gl
        gh[at, :] = (mm(rows[:, :depth], weight) + mm(two(gl), d2[...], 1, 1)) * owned[...]
    st = st1[...] + st2[...]
    mask = head_mask(width)
    grad = gh[...]
    inverse = 1.0 / den[...]
    numer = grad * inverse
    grad_den = -head_total(grad * ratio[...], mask) * inverse
    raw = q[...]
    queries = jnp.maximum(raw, 0.0)
    grad_q = mm3(numer, spread_heads(st[:HD], width, mask)) + grad_den * st[HD : HD + 1]
    gq_out[...] = jnp.where(raw > 0.0, grad_q, 0.0).astype(bf16)
    st_out[:HD, :] = squeeze_heads(mm3(numer, queries, 0, 0), mask)
    total = jnp.sum(grad_den * queries, axis=0, keepdims=True)
    st_out[HD:, :] = jnp.broadcast_to(total, (8, width))


def linear_end(
    w, gq, k, v, st1, st2, d2, u2, gk_out, gv_out, gl_out, mine, away,
):
    width = k.shape[1]
    half = mine.shape[0]
    st = st1[...] + st2[...]
    mask = head_mask(width)
    wide = spread_heads(st[:HD], width, mask)
    raw = k[...]
    grad_k = mm3(v[...], wide) + st[HD : HD + 1]
    gk_out[...] = jnp.where(raw > 0.0, grad_k, 0.0).astype(bf16)
    gv_out[...] = mm3(jnp.maximum(raw, 0.0), wide, 1, 1).astype(bf16)
    grads = (gq, gk_out, gv_out)
    gl = sum(mm(g[...], u2[i], 1, 1) for i, g in enumerate(grads))
    gl_out[...] = gl
    pair = two(gl)
    w[0].take(0)
    w[0].take(1)
    weights = [w[0].columns(j, first, width) for j, first in ((0, 0), (0, width), (1, 0))]

    def part(rows):
        total = mm(pair[rows], d2[...], 1, 1)
        for g, weight in zip(grads, weights):
            total = total + mm(g[rows, :], weight, 1, 1)
        return total

    put(mine, everything, part(slice(0, half)))
    put(away, everything, part(slice(half, 2 * half)))


def in_steps(rows, body, step=32):
    def one(i, carry):
        body(pl.ds(pl.multiple_of(i * step, step), step))
        return carry

    lax.fori_loop(0, rows // step, one, 0)


def slope_of_norm(values, grad):
    normed, inverse = row_stats(values)
    return inverse * (
        grad
        - jnp.mean(grad, axis=-1, keepdims=True)
        - normed * jnp.mean(grad * normed, axis=-1, keepdims=True)
    )


def total_of(low, got, at, width):
    return low[at, :width].astype(f32) + got[at, :width].astype(f32)


def end_attn(low, got, x, mods, after_out, own_out):
    def body(at):
        after = x[at, :].astype(f32) + mods[2:3, :] * total_of(low, got, at, x.shape[1])
        after_out[at, :] = after
        put(own_out, at, after)

    in_steps(x.shape[0], body)


def end_cross(low, got, before, mods, after_out, own_out):
    def body(at):
        after = before[at, :] + total_of(low, got, at, before.shape[1])
        after_out[at, :] = after
        normed, unused = row_stats(after)
        put(own_out, at, normed * (1.0 + mods[4:5, :]) + mods[3:4, :])

    in_steps(before.shape[0], body)


def end_output(low, got, before, mods, out):
    def body(at):
        put(out, at, before[at, :] + mods[5:6, :] * total_of(low, got, at, before.shape[1]))

    in_steps(before.shape[0], body)


def end_ffn_back(low, got, after, cot, mods, grad_out, own_out):
    def body(at):
        grad = total_of(low, got, at, after.shape[1]) * (1.0 + mods[4:5, :])
        grad = cot[at, :].astype(f32) + slope_of_norm(after[at, :], grad)
        grad_out[at, :] = grad
        put(own_out, at, grad)

    in_steps(after.shape[0], body)


def end_cross_back(low, got, before, mods, grad_out, own_out):
    def body(at):
        grad = before[at, :] + total_of(low, got, at, before.shape[1])
        grad_out[at, :] = grad
        put(own_out, at, mods[2:3, :] * grad)

    in_steps(before.shape[0], body)


def end_attn_back(low, got, before, x, mods, out):
    def body(at):
        grad = total_of(low, got, at, before.shape[1]) * (1.0 + mods[1:2, :])
        put(out, at, before[at, :] + slope_of_norm(x[at, :].astype(f32), grad))

    in_steps(before.shape[0], body)


def place_rows(where, own, other, out):
    width = out.shape[2]
    out[where[0]] = own[:, :width]
    out[1 - where[0]] = other[:, :width]


def fold(both):
    half = both.shape[0] // 2
    return both[:half] + both[half:]


def turned(v, b):
    half = v.shape[1] // 2
    return jnp.where(b == 0, v, jnp.concatenate([v[:, half:], v[:, :half]], axis=1))


def thin_sum(latent, *rows):
    high = latent.astype(bf16).astype(f32)
    both = jnp.concatenate([high, latent - high], axis=0).astype(bf16)
    total, at = None, 0
    for values in rows:
        size = values.shape[0]
        term = mm(both[:, at : at + size], values[...])
        total = term if total is None else total + term
        at += size
    return fold(total)


def outer_sum(latent, *rows):
    total, at = None, 0
    pair = two(latent)
    for values in rows:
        size = values.shape[0]
        term = mm(pair[at : at + size], values[...], 0, 0)
        total = term if total is None else total + term
        at += size
    return fold(total)


def set_segments(out, segments, width):
    for i, v in enumerate(segments):
        put(out.at[:, i * width : (i + 1) * width], everything, v)


def pack_first(where, point, up, l0, l1, l2, l3, sums):
    pieces = [point[0], point[1]] + [up[h, p] for p in range(2) for h in range(2)]
    n = l0.shape[0]
    first = sums.shape[1] - 4 * n
    set_segments(sums, [fold(v) for v in pieces], first // 6)
    for i, v in enumerate((l0, l1, l2, l3)):
        sums[:, first + i * n : first + (i + 1) * n] = turned(v[...].T[: sums.shape[0]], where[0])


def to_blocks(home, first, table):
    blocks = home.shape[0]
    size = table.shape[1] // blocks
    rows = table.shape[0]
    for i in range(blocks):
        home[i, first : first + rows, :size] = table[:, i * size : (i + 1) * size]


def set_mark(where, home, first):
    home[:, first:, :] = jnp.zeros((home.shape[0], home.shape[1] - first, home.shape[2]), f32) + where[2].astype(f32)


def second_sums(
    where, sums, gco, gct, fo, ft, gffn, mixo, mixt, cgl, qlat, gq, qgl, gkv, ggot, klat, ku2,
    home_out, projs, out, home,
):
    n, depth = gffn.shape
    b = where[0]
    first = sums.shape[2] - 4 * n
    parts = []
    for i in range(4):
        at = slice(first + i * n, first + (i + 1) * n)
        parts.append(turned(sums[0, :, at] + sums[1, :, at] + sums[2, :, at] + sums[3, :, at], b))
    projs[...] = parts[0]
    rows = parts[0].shape[0]
    home[...] = jnp.zeros(home.shape, f32)
    to_blocks(home, 0, thin_sum(parts[1], gco, gct)[:, :depth])
    to_blocks(home, rows, thin_sum(parts[2], gffn))
    to_blocks(home, 2 * rows, thin_sum(parts[3], fo, ft)[:, :depth])
    pad, hh = first // 6, home.shape[2] * home.shape[0] // 8
    size = home.shape[2]
    for j in range(3):
        for i in range(home.shape[0]):
            t, h, at = i * size // (2 * hh), i * size % (2 * hh) // hh, i * size % hh
            at += (2 * j + h) * pad
            home[i, (3 + j) * rows : (4 + j) * rows, :] = sums[t, :, at : at + size]
    set_mark(where, home, 6 * rows)
    home_out[...] = home[...].astype(home_out.dtype)
    here = ggot.shape[1]
    gk = (gkv[0, :here, :] + ggot[0]).astype(bf16)
    gv = (gkv[1, :here, :] + ggot[1]).astype(bf16)
    segments = [outer_sum(cgl[...], mixo, mixt), outer_sum(qlat[...], gq)]
    segments += [outer_sum(klat[...], gk), outer_sum(klat[...], gv)]
    pad = -(-gq.shape[1] // LANES) * LANES
    set_segments(out, segments, pad)
    rank = out.shape[0]
    out[:, 4 * pad : 4 * pad + n] = turned(qgl[...].T[:rank], b)
    kvgl = mm(gk, ku2[0], 1, 1) + mm(gv, ku2[1], 1, 1)
    put(out.at[:, 4 * pad + n :], everything, kvgl.T[:rank])


def third_sums(where, before, pgl, mixed, qlat, gq, gk, gv, qgl, out):
    first = before.shape[1]
    out[:, :first] = before[...]
    segments = [outer_sum(pgl[...], mixed)] + [outer_sum(qlat[...], g) for g in (gq, gk, gv)]
    pad = -(-gq.shape[1] // LANES) * LANES
    set_segments(out.at[:, first : first + 4 * pad], segments, pad)
    out[:, first + 4 * pad :] = turned(qgl[...].T[: out.shape[0]], where[0])


def last_sums(ranges, where, sums, projs, gao, gat, xo, xt, cap, a, home_out, home):
    n, depth = a.shape
    b = where[0]
    text = -(-cap.shape[0] // LANES) * LANES
    pad = (sums.shape[2] - 2 * n - text) // 8
    second = 4 * pad + n + text
    rows = projs.shape[0]

    def summed(first, size):
        return sum(sums[t, :, first : first + size] for t in range(sums.shape[0]))

    def heads(first):
        parts = [sums[t, :, first + s * HD : first + (s + m) * HD] for t, (s, m) in enumerate(ranges)]
        return jnp.concatenate(parts, axis=1)

    tables = [
        thin_sum(turned(summed(4 * pad, n), b), xo, xt)[:, :depth],
        thin_sum(summed(4 * pad + n, cap.shape[0]), cap)[:, :depth],
        thin_sum(projs[...], gao, gat)[:, :depth],
    ]
    tables += [heads(j * pad) for j in range(4)] + [heads(second + j * pad) for j in range(4)]
    tables.append(thin_sum(turned(summed(second + 4 * pad, n), b), a))
    for j, table in enumerate(tables):
        to_blocks(home, j * rows, table)
    set_mark(where, home, len(tables) * rows)
    home_out[...] = home[...].astype(home_out.dtype)


def adapter_tables(got, out):
    last = got.shape[1] - 1
    for i in range(out.shape[0]):
        total = None
        for s in range(got.shape[0]):
            values = got[s].astype(f32)
            term = jnp.where(values[last:, :1] == float(i), values, 0.0)
            total = term if total is None else total + term
        out[i] = total


def ring_order(n):
    return list(range(0, n, 2)) + list(range(n - 1 - n % 2, 0, -2))


def ring_pairs(n):
    order = ring_order(n)
    return [(order[i], order[(i + 1) % n]) for i in range(n)]


def ring_source(n, step):
    z = lax.axis_index(W)
    place = jnp.where(z % 2 == 0, z // 2, n - 1 - z // 2)
    from_place = (place - step + n) % n
    return jnp.where(2 * from_place < n, 2 * from_place, 2 * (n - 1 - from_place) + 1)


def swap_pairs(n, distance):
    return [(i, i ^ distance) for i in range(n)]


def across(values, axis, distance=1):
    return lax.ppermute(values, axis, swap_pairs(lax.axis_size(axis), distance))


class Stream:
    def __init__(self, makers, order):
        self.n = lax.axis_size(W)
        self.makers, self.order = makers, list(order)
        self.own, self.got, self.crossed = {}, {}, {}
        self.flying, self.crossing = [], []

    def launch(self):
        while not self.flying and self.order:
            name, step = self.order[0]
            if step == 1:
                self.own[name] = self.makers[name]()
                moving = self.own[name][0]
            elif (name, step - 1) in self.got:
                moving = self.got[name, step - 1]
            else:
                break
            self.order.pop(0)
            self.flying.append((name, step, lax.ppermute(moving, W, ring_pairs(self.n))))

    def fence(self, values):
        done = [self.flying.pop(0)] if self.flying else []
        crossed, self.crossing = self.crossing, []
        leaves, tree = jax.tree.flatten((values, [d[2] for d in done], [d[2] for d in crossed]))
        values, arrived, over = jax.tree.unflatten(tree, lax.optimization_barrier(leaves))
        for d, v in zip(crossed, over):
            self.crossed[d[0], d[1]] = v
        for d, v in zip(done, arrived):
            self.got[d[0], d[1]] = v
            self.crossing.append((d[0], d[1], across(v, C)))
        self.launch()
        return values

    def fences(self, count, values):
        for i in range(count * (self.n - 1) // 3):
            values = self.fence(values)
        return values

    def ready(self, names, values):
        while not all((name, self.n - 1) in self.crossed for name in names):
            values = self.fence(values)
        return values

    def pieces(self, name):
        steps = range(1, self.n)
        mine = [self.own[name][0]] + [self.got[name, s] for s in steps]
        other = [self.own[name][1]] + [self.crossed[name, s] for s in steps]
        rows = mine[0].shape[0]
        if rows % 16 == 0:
            return mine + other
        c = lax.axis_index(C)
        buf = jnp.zeros((2, self.n * rows, mine[0].shape[1]), bf16)
        for s in range(self.n):
            at = ring_source(self.n, s) * rows
            buf = lax.dynamic_update_slice(buf, mine[s][None], (c, at, 0))
            buf = lax.dynamic_update_slice(buf, other[s][None], (1 - c, at, 0))
        return [buf]


class Weight:
    def __init__(self, meta, pieces, buf, sems, halves):
        self.meta, self.pieces, self.buf, self.sems, self.halves = meta, pieces, buf, sems, halves

    def copies(self, j, pieces):
        rows = pieces[0].shape[0]
        return [
            pltpu.make_async_copy(
                piece,
                self.buf.at[j, pl.ds(pl.multiple_of(self.meta[1 + k] * rows, rows), rows), :],
                self.sems.at[j, k],
            )
            for k, piece in enumerate(pieces)
        ]

    def start(self):
        count = len(self.pieces) // 2
        for j, half in enumerate(self.halves):
            if not count:
                pltpu.make_async_copy(self.pieces[0].at[half], self.buf.at[j], self.sems.at[j, 0]).start()
                continue

            @pl.when(self.meta[0] == half)
            def mine():
                for copy in self.copies(j, self.pieces[:count]):
                    copy.start()

            @pl.when(self.meta[0] != half)
            def other():
                for copy in self.copies(j, self.pieces[count:]):
                    copy.start()

    def take(self, j):
        count = len(self.pieces) // 2
        if not count:
            pltpu.make_async_copy(self.pieces[0].at[0], self.buf.at[j], self.sems.at[j, 0]).wait()
        else:
            for copy in self.copies(j, self.pieces[:count]):
                copy.wait()
        return self.buf[j]

    def columns(self, j, first, size):
        return self.buf[j, :, first : first + size]


def per_step(a):
    zeros = (0,) * (a.ndim - 1)
    return pl.BlockSpec((1,) + tuple(a.shape[1:]), lambda h: (h,) + zeros)


def row_block(a):
    return pl.BlockSpec((a.shape[0] // 4, a.shape[1]), lambda i: (i, 0))


def both_blocks(a):
    return pl.BlockSpec((2, a.shape[1] // 4, a.shape[2]), lambda i: (0, i, 0))


def all_of(a):
    zeros = (0,) * len(a.shape)
    return pl.BlockSpec(tuple(a.shape), lambda *g: zeros)


def scalars(a):
    return pl.BlockSpec(memory_space=pltpu.SMEM)


def anywhere(a):
    return pl.BlockSpec(memory_space=pl.ANY)


def run(kernel, ins, outs, scratch=(), steps=1, weights=(), meta=None):
    args, specs = [], []
    if weights:
        args.append(meta)
        specs.append(scalars(meta))
    counts, extra = [], []
    for pieces, halves in weights:
        counts.append((len(pieces), halves))
        args += pieces
        specs += [anywhere(p) for p in pieces]
        rows = pieces[0].shape[0] * len(pieces) // 2 if len(pieces) > 1 else pieces[0].shape[1]
        extra.append(pltpu.VMEM((len(halves), rows, pieces[0].shape[-1]), bf16))
        extra.append(pltpu.SemaphoreType.DMA((len(halves), max(len(pieces) // 2, 1))))
    first = len(args)
    for item in ins:
        a, spec = item if isinstance(item, tuple) else (item, all_of)
        args.append(a)
        specs.append(spec(a))
    shapes, out_specs = [], []
    for item in outs:
        dims, dtype, spec = item if len(item) == 3 else item + (all_of,)
        shapes.append(shape(dims, dtype))
        out_specs.append(spec(shapes[-1]))

    def body(*refs):
        if not weights:
            return kernel(*refs)
        at, loaders = 1, []
        tail = refs[len(refs) - len(extra) :]
        for i, (count, halves) in enumerate(counts):
            loaders.append(Weight(refs[0], refs[at : at + count], tail[2 * i], tail[2 * i + 1], halves))
            at += count

        @pl.when(pl.program_id(0) == 0)
        def begin():
            for loader in loaders:
                loader.start()

        kernel(loaders, *refs[first : len(refs) - len(extra)])

    return pl.pallas_call(
        body,
        grid=(steps,),
        in_specs=specs,
        out_specs=out_specs,
        out_shape=shapes,
        scratch_shapes=list(scratch) + extra,
        compiler_params=big,
    )(*args)


def twice(table, axis):
    return jnp.concatenate([table, table], axis=axis)


def slot_layout(groups, rank, heads):
    per, left = heads // groups, heads % groups
    slots = per + (1 if left else 0)
    own_start = rank * per + jnp.minimum(rank, left)
    own_count = per + jnp.where(rank < left, 1, 0)
    first = jnp.minimum(own_start, heads - slots)
    slot = first + jnp.arange(slots, dtype=jnp.int32)
    owned = ((slot >= own_start) & (slot < own_start + own_count)).astype(f32)
    return slots, first, owned


def slot_ranges(groups, heads):
    per, left = heads // groups, heads % groups
    slots = per + (1 if left else 0)
    out = []
    for rank in range(groups):
        own_start = rank * per + min(rank, left)
        count = per + (1 if rank < left else 0)
        out.append((own_start - min(own_start, heads - slots), count))
    return out


def shards(
    tokens, caption, caption_lengths, adapter_index, modulation, cotangent,
    qkv_weight, proj_weight, cross_q_weight, cross_kv_weight, cross_out_weight,
    inverted_weight, depth_weight, point_weight,
    qkv_down, qkv_up, proj_down, proj_up, query_down, query_up, kv_down, kv_up,
    cross_down, cross_up, inverted_down, inverted_up, point_down, point_up,
):
    grid_rows, grid_cols, D = tokens.shape[1:]
    n = grid_rows * grid_cols
    half = n // 2
    heads = D // HD
    groups = lax.axis_size(T)
    rank = lax.axis_index(T)
    c = lax.axis_index(C)
    b = rank % 2
    adapters, R = qkv_up.shape[:2]
    slots, slot_first, owned = slot_layout(groups, rank, heads)
    width = slots * HD
    col = slot_first * HD
    owned = jnp.repeat(owned, HD)[None]
    hid = inverted_weight.shape[2]
    hh = hid // 2
    hid_first = rank * hid
    index = adapter_index[0]
    where = jnp.stack([b, c, index]).astype(jnp.int32)

    def cut(table, start, size, axis):
        return lax.dynamic_slice_in_dim(table, start, size, axis)

    def pick(table):
        return lax.dynamic_index_in_dim(table, index, 0, keepdims=False)

    def own_rows(rows):
        own = cut(rows, b * half, half, 0)
        return own, jnp.concatenate([own, cut(rows, (1 - b) * half, half, 0)])

    late = {}
    def pair_of(first, second):
        return [jnp.where(c == 0, first, second), jnp.where(c == 0, second, first)]

    def taken(table, middle, start, size):
        return lax.dynamic_slice(table, (0, middle, start), (table.shape[0], 1, size))[:, 0]

    def beside(*values):
        return jnp.concatenate(values, axis=1)

    def hidden_columns(i):
        return beside(taken(inverted_weight, 0, i * hh, hh), taken(inverted_weight, 1, i * hh, hh))

    def both(table, start):
        return beside(taken(table, 0, start, width), taken(table, 1, start, width))

    makers = dict(
        ab=lambda: pair_of(
            both(qkv_weight, col), beside(taken(qkv_weight, 2, col, width), cut(proj_weight, col, width, 0).T)
        ),
        cd=lambda: pair_of(
            both(cross_kv_weight, late["col"]),
            beside(cut(cross_q_weight, late["col"], width, 1), cut(cross_out_weight, late["col"], width, 0).T),
        ),
        vg=lambda: [hidden_columns(late["c"]), hidden_columns(1 - late["c"])],
        p=lambda: [cut(point_weight, late["c"] * hh, hh, 0).T, cut(point_weight, (1 - late["c"]) * hh, hh, 0).T],
    )
    size = lax.axis_size(W)
    order = [(name, step) for name in ("ab", "cd", "vg", "p") for step in range(1, size)]
    stream = Stream(makers, order)
    fences = stream.fences

    stream.launch()
    mods = modulation[0]
    low_tokens = tokens.reshape(n, D)
    x_low, x_rows = own_rows(low_tokens)
    qd2, qu2 = twice(pick(qkv_down), 1), twice(cut(pick(qkv_up), col, width, 2), 0).transpose(1, 0, 2)
    pd2, pu2 = twice(cut(pick(proj_down), col, width, 0), 1), twice(pick(proj_up), 0)
    text_here = caption.shape[1]
    text_rows = -(-text_here // 16) * 16
    padded = -(-D // LANES) * LANES
    cap = jnp.pad(caption[0], ((0, text_rows - text_here), (0, padded - D)))
    cap_other = across(cap, C)
    late.update(col=col, c=c)

    def later(values):
        late["col"], late["c"], values = fences(1, (late["col"], late["c"], values))
        return values

    tables = [query_down, query_up, kv_down, kv_up, cross_down, cross_up]
    tables_f = [inverted_down, inverted_up, point_down, point_up, depth_weight]
    tables, tables_f, cap, cap_other, cotangent = later((tables, tables_f, cap, cap_other, cotangent))
    query_down, query_up, kv_down, kv_up, cross_down, cross_up = tables
    cd2 = twice(cut(pick(cross_down), col, width, 0), 1)
    cu2 = twice(pick(cross_up), 0)
    xd2, xu2 = twice(pick(query_down), 1), twice(cut(pick(query_up), col, width, 1), 0)
    kd2, ku2 = twice(pick(kv_down), 1), twice(cut(pick(kv_up), col, width, 2), 0).transpose(1, 0, 2)
    tables_f, cotangent = later((tables_f, cotangent))
    inverted_down, inverted_up, point_down, point_up, depth_weight = tables_f
    fd2, fu2 = twice(pick(inverted_down), 1), twice(cut(pick(inverted_up), hid_first, hid, 2), 0)
    fu2 = fu2.reshape(2 * R, 2, 2, hh).transpose(1, 2, 0, 3)
    od2 = twice(cut(pick(point_down), hid_first, hid, 0), 1).reshape(2, hh, 2 * R)
    ou2 = twice(pick(point_up), 0)
    taps = depth_weight.astype(f32).reshape(9, 2, 2, hh).transpose(2, 1, 0, 3)
    cot_low, cot = own_rows(cotangent.reshape(n, D))
    places = jnp.arange(text_rows)
    live = jnp.concatenate([c * text_here + places, (1 - c) * text_here + places])
    live = (live < caption_lengths[0]) & (jnp.concatenate([places, places]) < text_here)
    live = live.astype(f32)[None]
    tables = [cd2, cu2, xd2, xu2, kd2, ku2, fd2, fu2, od2, ou2, taps, cot_low, cot, live]
    x_rows, tables = later((x_rows, tables))
    cd2, cu2, xd2, xu2, kd2, ku2, fd2, fu2, od2, ou2, taps, cot_low, cot, live = tables
    x_rows = stream.ready(["ab"], x_rows)

    w_ab = stream.pieces("ab")
    meta = jnp.stack([c] + [ring_source(size, s) for s in range(size)]).astype(jnp.int32)
    rows_bf = ((n, D), bf16)
    thin = ((n, 2 * R), f32)
    wide = ((n, width), f32)
    wide_bf = ((n, width), bf16)
    pair = [((half, padded), f32), ((half, padded), bf16)]
    ended = [((half, D), f32, row_block), ((half, padded), bf16, row_block)]

    def finish_rows(kernel, arrays, outs):
        return run(kernel, [(v, row_block) for v in arrays] + [mods], outs, steps=4)

    state_of = ((HD + 8, width), f32)
    attn_in, q_raw, k_raw, qkv_lat = run(
        attn_front, [x_rows, mods, qd2, qu2], [rows_bf, wide, wide, thin], weights=[(w_ab, (0,))], meta=meta,
    )
    v_raw, st_own = run(
        attn_state, [attn_in, k_raw, qkv_lat, qu2], [wide, state_of], weights=[(w_ab, (1,))], meta=meta,
    )
    st_own, st_other = fences(1, (st_own, across(st_own, C)))
    ratio, denom, mixed, proj_lat, mine, away = run(
        attn_back, [q_raw, st_own, st_other, owned, pd2, pu2], [wide, wide, wide_bf, thin] + pair,
        weights=[(w_ab, (1,))], meta=meta,
    )

    def exchanged(mine, away, pace=lambda low: low):
        low, distance = (mine + across(away, T).astype(f32)).astype(bf16), 2
        while True:
            low = pace(low)
            got = across(low, T, distance)
            distance *= 2
            if distance >= groups:
                return low, got
            low = (low.astype(f32) + got.astype(f32)).astype(bf16)

    def while_streaming(mine, away):
        return fences(1, exchanged(mine, away))

    mine, away = fences(1, (mine, away))
    low, got = while_streaming(mine, away)
    after_attn, cross_own = finish_rows(end_attn, [low, got, x_low], ended)
    cross_other = across(cross_own, T)

    cap, cross_own, cross_other, after_attn = stream.ready(["cd"], (cap, cross_own, cross_other, after_attn))
    w_cd = stream.pieces("cd")
    kv_all, kv_lat = run(
        caption_rows, [cap, cap_other, kd2, ku2], [((2, 2 * text_rows, width), bf16), ((text_rows, 2 * R), f32)],
        weights=[(w_cd, (0,))], meta=meta,
    )
    kv_all, cross_own, cross_other = fences(1, (kv_all, cross_own, cross_other))
    half_bf, half_thin = ((half, width), bf16), ((half, 2 * R), f32)

    def cross_part(rows, kv, dtype):
        return run(
            cross_fwd,
            [rows, kv, live, owned, xd2, xu2, cd2, cu2],
            [half_bf, half_bf, half_thin, half_thin, ((half, LANES), f32), ((half, padded), dtype)],
            weights=[(w_cd, (1,))], meta=meta,
        )

    *cross_t, away = cross_part(cross_other, kv_all, bf16)
    away, cross_tied, kv_tied = lax.optimization_barrier((away, cross_own, kv_all))
    *cross_o, mine = cross_part(cross_tied, kv_tied, f32)
    mine, away = fences(1, (mine, away))
    query, mix, query_lat, cross_lat, lse = zip(cross_o, cross_t)
    low, got = while_streaming(mine, away)
    after_cross, ffn_own = finish_rows(end_cross, [low, got, after_attn], ended)
    ffn_other = across(ffn_own, T)

    query_lat, cross_lat = jnp.concatenate(query_lat), jnp.concatenate(cross_lat)

    ffn_own, ffn_other, after_cross = stream.ready(["vg"], fences(1, (ffn_own, ffn_other, after_cross)))
    w_vg = stream.pieces("vg")
    hid_f, hid_bf = ((2, n, hh), f32, per_step), ((2, n, hh), bf16, per_step)
    edge_of = ((2, grid_cols, hh), bf16, per_step)
    pre_v, pre_g, hid_v, hid_g, inv_lat, edge_v, edge_g = run(
        ffn_front, [(where, scalars), ffn_own, ffn_other, fd2, (fu2[0], per_step), (fu2[1], per_step)],
        [hid_f, hid_f, hid_bf, hid_bf, thin, edge_of, edge_of], [pltpu.VMEM((n, D), bf16)], 2,
        weights=[(w_vg, (0, 1))], meta=meta,
    )
    hid_v, edge_v, edge_g = fences(1, (hid_v, edge_v, edge_g))
    halo_v, halo_g = across(edge_v, C), across(edge_g, C)
    hid_v, halo_v, halo_g = stream.ready(["p"], (hid_v, halo_v, halo_g))
    w_p = stream.pieces("p")
    grid_buf = pltpu.VMEM((n + 2 * grid_cols, hh), f32)
    row_acc = pltpu.VMEM((n, D), f32)
    gated, gcv, gcg, grad_ffn, point_gl, point_lat, point_down_g, edge, mine, away = run(
        ffn_mid,
        [
            (where, scalars), (hid_v, per_step), (hid_g, per_step), (halo_v, per_step), (halo_g, per_step), (taps, per_step),
            cot, mods[5:6], (od2, per_step), ou2,
        ],
        [hid_bf, hid_bf, hid_bf, rows_bf, thin, thin, ((2, 2 * R, hh), f32, per_step)]
        + [((2, 2, grid_cols, hh), bf16, per_step)] + pair,
        [grid_buf, grid_buf, pltpu.VMEM((n, hh), f32), row_acc],
        2,
        weights=[(w_p, (0, 1))], meta=meta,
    )
    halo = across(edge, C)
    tied = []

    def after_halo(low):
        low, *tied[:] = lax.optimization_barrier((low, halo, gcv, gcg))
        return low

    out_low, out_got = exchanged(mine, away, after_halo)
    halo, gcv, gcg = tied

    gpv, gpg, inv_up_g, inv_gl, mine, away = run(
        ffn_back,
        [
            (where, scalars), (gcv, per_step), (gcg, per_step), (halo, per_step), (taps, per_step),
            (pre_v, per_step), (pre_g, per_step), inv_lat, fd2,
            (fu2[0], per_step), (fu2[1], per_step),
        ],
        [hid_bf, hid_bf, ((2, 2, 2 * R, hh), f32, per_step), thin] + pair,
        [grid_buf, grid_buf, row_acc],
        2,
        weights=[(w_vg, (0, 1))], meta=meta,
    )
    part_r = R // groups
    blocks = size * lax.axis_size(C)
    ranges = slot_ranges(groups, heads)

    def swapped(sent):
        return lax.all_to_all(sent.reshape(groups, part_r, sent.shape[1]), T, 0, 0, tiled=True)

    def sent_home(values):
        got = lax.all_to_all(values, (W, C), 0, 0, tiled=True)
        return run(adapter_tables, [got], [((adapters,) + got.shape[1:], f32)])[0]

    def up_to_tiles(size):
        return -(-size // LANES) * LANES

    def table_rows(table, i, size):
        return table[:, i * part_r : (i + 1) * part_r, : size // blocks]

    def down_rows(table, i, size):
        return table_rows(table, i, size).transpose(0, 2, 1)

    def together(*values):
        return lax.optimization_barrier(values)

    def during(mine, away, inputs, work):
        held = []

        def pace(low):
            low, tied = together(low, inputs)
            held[:] = [tied]
            return low

        low, got = exchanged(mine, away, pace)
        return together(low, got, work(*held[0]))

    def first_work(out_low, out_got, after_cross, inv_up_g, point_down_g, lats):
        (output,) = finish_rows(end_output, [out_low, out_got, after_cross], [((half, padded), f32, row_block)])
        (sums,) = run(
            pack_first, [(where, scalars), point_down_g, inv_up_g, *lats], [((R, 6 * up_to_tiles(hh) + 4 * n), f32)],
        )
        return output, sums

    mine, away, out_low, out_got = together(mine, away, out_low, out_got)
    low, got, (output, sums_f) = during(
        mine, away,
        (out_low, out_got, after_cross, inv_up_g, point_down_g, (proj_lat, cross_lat, point_lat, inv_gl)),
        first_work,
    )
    grad_cross, gc_own = finish_rows(end_ffn_back, [low, got, after_cross, cot_low], ended)
    gc_other = across(gc_own, T)

    gc_own, gc_other, output, sums_f = together(gc_own, gc_other, output, sums_f)
    output_other = across(output, T)
    sums_f = swapped(sums_f)
    grad_query, gkv, query_gl, cross_gl, mine, away = run(
        cross_bwd,
        [
            gc_own, gc_other, kv_all, live, owned,
            xd2, xu2, cd2, cu2, *query, *lse,
        ],
        [wide_bf, ((2, 2 * text_rows, width), f32), thin, thin] + pair,
        [pltpu.VMEM((half, width), bf16), pltpu.VMEM((n, width), f32)],
        weights=[(w_cd, (1,))], meta=meta,
    )
    mine, away, output_other, sums_f, gkv = together(mine, away, output_other, sums_f, gkv)
    gkv_got = across(gkv[:, text_rows:], C)

    def in_order(own, other):
        (rows,) = run(
            place_rows, [(where, scalars), (own, row_block), (other, row_block)],
            [((2, half, D), f32, both_blocks)], steps=4,
        )
        return rows.reshape(tokens.shape)

    seg = up_to_tiles(width)

    seg = up_to_tiles(width)
    home_dims = (blocks, 8 * part_r, 4 * 2 * hh // blocks)
    last_dims = (blocks, 16 * part_r, D // blocks)

    def second_work(output, output_other, sums, cross_gl, grad_query, query_gl):
        return [in_order(output, output_other)] + list(run(
            second_sums,
            [
                (where, scalars), sums, gc_own, gc_other, ffn_own, ffn_other, grad_ffn, *mix, cross_gl,
                query_lat, grad_query, query_gl, gkv, gkv_got, kv_lat, ku2,
            ],
            [(home_dims, bf16), ((part_r, n), f32), ((R, 4 * seg + n + up_to_tiles(text_rows)), f32)],
            [pltpu.VMEM(home_dims, f32)],
        ))

    low, got, (output, home, proj_s, sums_c) = during(
        mine, away, (output, output_other, sums_f, cross_gl, grad_query, query_gl), second_work
    )
    grad_after, ga_own = finish_rows(end_cross_back, [low, got, grad_cross], ended)
    ga_other = across(ga_own, T)

    grad_q, proj_gl, sg_own = run(
        linear_bwd,
        [ga_own, ga_other, q_raw, st_own, st_other, ratio, denom, owned, pd2, pu2],
        [wide_bf, thin, state_of],
        [pltpu.VMEM((n, width), f32)],
        weights=[(w_ab, (1,))], meta=meta,
    )
    sg_other = across(sg_own, C)
    grad_k, grad_v, qkv_gl, mine, away = run(
        linear_end,
        [grad_q, k_raw, v_raw, sg_own, sg_other, qd2, qu2],
        [wide_bf, wide_bf, thin] + pair,
        weights=[(w_ab, (0, 1))], meta=meta,
    )

    def third_work(home, sums_c, proj_gl, qkv_gl, grad_q, grad_k, grad_v):
        home = lax.all_to_all(home, (W, C), 0, 0, tiled=True)
        return run(
            third_sums, [(where, scalars), sums_c, proj_gl, mixed, qkv_lat, grad_q, grad_k, grad_v, qkv_gl],
            [((R, sums_c.shape[1] + 4 * seg + n), f32)],
        )[0], run(adapter_tables, [home], [((adapters,) + home.shape[1:], f32)])[0]

    low, got, (sums, tables) = during(
        mine, away, (home, sums_c, proj_gl, qkv_gl, grad_q, grad_k, grad_v), third_work
    )
    sums = swapped(sums)
    (input_grad,) = finish_rows(end_attn_back, [low, got, grad_after, x_low], [((half, padded), f32, row_block)])
    input_grad, sums = together(input_grad, sums)
    input_other = across(input_grad, T)
    (last,) = run(
        functools.partial(last_sums, ranges),
        [(where, scalars), sums, proj_s, ga_own, ga_other, cross_own, cross_other, cap, attn_in],
        [(last_dims, bf16)],
        [pltpu.VMEM(last_dims, f32)],
    )
    last = sent_home(last)

    def rows_of(i):
        return table_rows(last, i, D)

    return (
        output,
        in_order(input_grad, input_other),
        down_rows(last, 11, D),
        jnp.stack([rows_of(8), rows_of(9), rows_of(10)], axis=2),
        down_rows(last, 7, D),
        rows_of(2),
        down_rows(last, 0, D),
        rows_of(4),
        down_rows(last, 1, D),
        jnp.stack([rows_of(5), rows_of(6)], axis=2),
        down_rows(last, 3, D),
        table_rows(tables, 0, D),
        down_rows(tables, 2, D),
        jnp.stack([table_rows(tables, i, 8 * hh) for i in (4, 5)], axis=2),
        down_rows(tables, 3, 8 * hh),
        table_rows(tables, 1, D),
    )


def solution(mesh):
    down = P(None, (W, C), T)
    up3 = P(None, T, (W, C))
    up4 = P(None, T, None, (W, C))
    rows = P(W, C)
    return jax.shard_map(
        shards,
        mesh=mesh,
        in_specs=(
            rows, rows, P(W), P(W), P(W), rows,
            P(W), P(None, W), P(W), P(W), P(None, W),
            P(W, None, T), P(None, None, None, T), P(T, W),
        )
        + (P(),) * 14,
        out_specs=(
            rows, rows, down, up4, down, up3, down, up3, down, up4, down, up3, down, up4, down, up3,
        ),
        check_vma=False,
    )
```

time: 891 us -> 748 us (0.84)
  waiting for transfers between devices: 393 us -> 291 us
  starting transfers between devices: 102 us -> 74.8 us
  Pallas kernels: 234 us -> 261 us
  other arithmetic: 45.1 us -> 27.8 us
  matrix products: 16.2 us -> 0 us
    ppermute x45 -> x37, waiting for transfers between devices: 257 us -> 178 us  [across(): return lax.ppermute(values, axis, swap_pairs(lax.axis_size(axis), distance))]
    pallas_call x18 -> x26, Pallas kernels: 234 us -> 261 us  [run(): pl.pallas_call(body, grid=(steps,), in_specs=specs, out_specs=out_specs,...]
    dynamic_slice x0 -> x2, local copies, waits for them, and re-layouts: none -> 24.8 us  [taken(): lax.dynamic_slice(table, (0, middle, start), (table.shape[0], 1, size))]
    all_to_all x6 -> x4, waiting for transfers between devices: 35.9 us -> 19.3 us  [the longest x1 9.44 us: sent_home(): got = lax.all_to_all(values, (W, C), 0, 0, tiled=True)]
    dot_general x25 -> x0, matrix products: 16.2 us -> none  [the longest x23 14.4 us: mm(): lax.dot_general(a, b, (((ca,), (cb,)), ((), ())), preferred_element_type=...]
    ppermute x21 -> x12, starting transfers between devices: 46.2 us -> 31.8 us  [launch(): lax.ppermute(moving, W, ring_pairs(self.n))]
    unnamed x172 -> x126, local copies, waits for them, and re-layouts: 24.6 us -> 13.2 us
    all_to_all x6 -> x4, starting transfers between devices: 21.1 us -> 14.1 us  [the longest x2 6.92 us: swapped(): lax.all_to_all(sent.reshape(groups, part_r, sent.shape[1]), T, 0, 0, tile...]
  transfers between devices with their start and end apart: 72 -> 53, of which waited for: 44 -> 35; matrix products, arithmetic and copies ran while one was open for 14% -> 12% of each run, Pallas kernels for 12% -> 24%
where the time goes in v2:
time: 748 us; the launch traced here: 742 us
  waiting for transfers between devices  291 us (39%)
  Pallas kernels  261 us (35%)
  local copies, waits for them, and re-layouts  85 us (11%)
  starting transfers between devices  74.8 us (10%)
  other arithmetic  27.8 us (4%)
    pallas_call x26, Pallas kernels, run(): pl.pallas_call(body, grid=(steps,), in_specs=specs, out_specs=out_specs,...  261 us
    ppermute x37, waiting for transfers between devices, across(): return lax.ppermute(values, axis, swap_pairs(lax.axis_size(axis), distance))  178 us
    ppermute x12, waiting for transfers between devices, launch(): lax.ppermute(moving, W, ring_pairs(self.n))  94.3 us
    ppermute x12, starting transfers between devices, launch(): lax.ppermute(moving, W, ring_pairs(self.n))  31.8 us
    ppermute x37, starting transfers between devices, across(): return lax.ppermute(values, axis, swap_pairs(lax.axis_size(axis), distance))  28.9 us
    dynamic_slice x2, local copies, waits for them, and re-layouts, taken(): lax.dynamic_slice(table, (0, middle, start), (table.shape[0], 1, size))  24.8 us
  transfers between devices with their start and end apart: 53, of which 35 were waited for; matrix products, arithmetic and copies ran while one was open for 12% of the time, Pallas kernels for 24%

profile of v2, /device:TPU:0, one launch (start us, length us, event | category | flops | bytes accessed | tf_op | source)
XLA Modules:
  0.0 742.5 jit_solution(10103471889749282905)
XLA Ops:
  19.4 11.6 %collective-permute-done.refs_10_ = bf16[160,2304]{1,0:T(8,128)(2,1)} collective-permute-done((bf16[160,2304]{1,0:T(8,128)(2,1)}, bf16[160,2304]{1,0:T(8,128)(2,1)}, u32[]{:S(2)}, u32[]{:S(2)}) %collective-permute-start) | collective-permute-done | bytes 737312 | tf_op jit(solution)/shard_map/ppermute | solution.py:706
  31.0 8.7 %collective-permute-done.1.refs_2_ = bf16[560,1152]{1,0:T(8,128)(2,1)} collective-permute-done((bf16[560,1152]{1,0:T(8,128)(2,1)}, bf16[560,1152]{1,0:T(8,128)(2,1)}, u32[]{:S(2)}, u32[]{:S(2)}) %collective-permute-start.1) | collective-permute-done | bytes 1290272 | tf_op jit(solution)/shard_map/ppermute | solution.py:727
  51.6 17.7 %collective-permute-done.3.refs_6_ = bf16[560,1152]{1,0:T(8,128)(2,1)} collective-permute-done((bf16[560,1152]{1,0:T(8,128)(2,1)}, bf16[560,1152]{1,0:T(8,128)(2,1)}, u32[]{:S(2)}, u32[]{:S(2)}) %collective-permute-start.3) | collective-permute-done | bytes 1290272 | tf_op jit(solution)/shard_map/ppermute | solution.py:706
  82.6 7.4 %constant_dynamic-slice_fusion.13 = (bf16[560,1,576]{2,1,0:T(2,128)(2,1)S(1)}, bf16[560,1,576]{2,1,0:T(2,128)(2,1)S(1)}) fusion(bf16[560,2,2240]{2,1,0:T(2,128)(2,1)} %param.37, s32[]{:T(128)S(6)} %select_n.167), kind=kLoop, calls=%fused_computation.94 | loop fusion | bytes 2580484 | tf_op jit(solution)/shard_map/dynamic_slice | solution.py:957
  106.3 22.5 %collective-permute-done.6.refs_2_ = bf16[560,1152]{1,0:T(8,128)(2,1)} collective-permute-done((bf16[560,1152]{1,0:T(8,128)(2,1)S(1)}, bf16[560,1152]{1,0:T(8,128)(2,1)}, u32[]{:S(2)}, u32[]{:S(2)}) %collective-permute-start.6) | collective-permute-done | bytes 1290272 | tf_op jit(solution)/shard_map/ppermute | solution.py:727
  138.8 12.1 %shard_map.387 = (bf16[512,2240]{1,0:T(8,128)(2,1)}, f32[512,576]{1,0:T(8,128)}, f32[512,576]{1,0:T(8,128)}, f32[512,32]{1,0:T(8,128)}) custom-call(s32[5]{0:T(128)} %stack.60.refs_0_, bf16[560,1152]{1,0:T(8,128)(2,1)} %get-tuple-element.512.refs_1_, bf16[560,1152]{1,0:T(8,128)(2,1)} %collective-permute-done.1.refs_2_, ...), custom_call_target="tpu_custom_call" | custom-call | tf_op jit(solution)/shard_map/pallas_call | solution.py:879
  150.9 10.2 %shard_map.388 = (f32[512,576]{1,0:T(8,128)}, f32[40,576]{1,0:T(8,128)}) custom-call(s32[5]{0:T(128)} %stack.60.refs_0_, bf16[560,1152]{1,0:T(8,128)(2,1)} %get-tuple-element.512.refs_1_, bf16[560,1152]{1,0:T(8,128)(2,1)} %collective-permute-done.1.refs_2_, bf16[560,1152]{1,0:T(8,128)(2,1)} %collective-permute-done.2.refs_3_, ...), custom_call_target="tpu_custom_call" | custom-call | tf_op jit(solution)/shard_map/pallas_call | solution.py:879
  171.7 9.0 %shard_map.389 = (f32[512,576]{1,0:T(8,128)}, f32[512,576]{1,0:T(8,128)}, bf16[512,576]{1,0:T(8,128)(2,1)}, f32[512,32]{1,0:T(8,128)}, f32[256,2304]{1,0:T(8,128)}, /*index=5*/bf16[256,2304]{1,0:T(8,128)(2,1)}) custom-call(s32[5]{0:T(128)} %stack.60.refs_0_, bf16[560,1152]{1,0:T(8,128)(2,1)} %get-tuple-element.512.refs_1_, ...), custom_call_target="tpu_custom_call" | custom-call | tf_op jit(solution)/shard_map/pallas_call | solution.py:879
  180.7 11.8 %collective-permute-done.12.refs_7_ = bf16[560,1152]{1,0:T(8,128)(2,1)S(1)} collective-permute-done((bf16[560,1152]{1,0:T(8,128)(2,1)}, bf16[560,1152]{1,0:T(8,128)(2,1)S(1)}, u32[]{:S(2)}, u32[]{:S(2)}) %collective-permute-start.12) | collective-permute-done | bytes 1290272 | tf_op jit(solution)/shard_map/ppermute | solution.py:706
  192.6 17.4 %constant_dynamic-slice_fusion.1 = (bf16[560,1,700]{2,1,0:T(2,128)(2,1)}, bf16[560,1,700]{2,1,0:T(2,128)(2,1)S(1)}, bf16[560,1,700]{2,1,0:T(2,128)(2,1)S(1)}, bf16[560,1,700]{2,1,0:T(2,128)(2,1)}) fusion(bf16[560,2,1400]{2,1,0:T(2,128)(2,1)S(1)} %copy-done.8, s32[]{:T(128)S(6)} %select_n.181, s32[]{:T(128)S(6)} %select_n.180), kind=kLoop, calls=%fused_computation.82 | loop fusion | bytes 6272008 | tf_op jit(solution)/shard_map/dynamic_slice | solution.py:957
  214.1 33.5 %collective-permute-done.15.refs_2_ = bf16[560,1400]{1,0:T(8,128)(2,1)} collective-permute-done((bf16[560,1400]{1,0:T(8,128)(2,1)S(1)}, bf16[560,1400]{1,0:T(8,128)(2,1)}, u32[]{:S(2)}, u32[]{:S(2)}) %collective-permute-start.15) | collective-permute-done | bytes 1568032 | tf_op jit(solution)/shard_map/ppermute | solution.py:727
  256.9 7.8 %shard_map.390 = (bf16[2,320,576]{2,1,0:T(8,128)(2,1)}, f32[160,32]{1,0:T(8,128)}) custom-call(s32[5]{0:T(128)} %stack.60.refs_0_, bf16[560,1152]{1,0:T(8,128)(2,1)} %copy-done.3, bf16[560,1152]{1,0:T(8,128)(2,1)} %collective-permute-done.6.refs_2_, bf16[560,1152]{1,0:T(8,128)(2,1)} %collective-permute-done.9.refs_3_, ...), custom_call_target="tpu_custom_call" | custom-call | tf_op jit(solution)/shard_map/pallas_call | solution.py:879
  264.8 19.3 %collective-permute-done.19.refs_6_ = bf16[560,1400]{1,0:T(8,128)(2,1)S(1)} collective-permute-done((bf16[560,1400]{1,0:T(8,128)(2,1)}, bf16[560,1400]{1,0:T(8,128)(2,1)S(1)}, u32[]{:S(2)}, u32[]{:S(2)}) %collective-permute-start.19) | collective-permute-done | bytes 1568032 | tf_op jit(solution)/shard_map/ppermute | solution.py:706
  290.8 13.7 %shard_map.392 = (bf16[256,576]{1,0:T(8,128)(2,1)}, bf16[256,576]{1,0:T(8,128)(2,1)}, f32[256,32]{1,0:T(8,128)}, f32[256,32]{1,0:T(8,128)}, f32[256,128]{1,0:T(8,128)}, /*index=5*/bf16[256,2304]{1,0:T(8,128)(2,1)}) custom-call(s32[5]{0:T(128)} %stack.60.refs_0_, bf16[560,1152]{1,0:T(8,128)(2,1)} %copy-done.3, ...), custom_call_target="tpu_custom_call" | custom-call | tf_op jit(solution)/shard_map/pallas_call | solution.py:879
  304.5 14.6 %shard_map.393 = (bf16[256,576]{1,0:T(8,128)(2,1)}, bf16[256,576]{1,0:T(8,128)(2,1)}, f32[256,32]{1,0:T(8,128)}, f32[256,32]{1,0:T(8,128)}, f32[256,128]{1,0:T(8,128)}, /*index=5*/f32[256,2304]{1,0:T(8,128)}) custom-call(s32[5]{0:T(128)} %stack.60.refs_0_, bf16[560,1152]{1,0:T(8,128)(2,1)} %copy-done.3, bf16[560,1152]{1,0:T(8,128)(2,1)} %collective-permute-done.6.refs_2_, ...), custom_call_target="tpu_custom_call" | custom-call | tf_op jit(solution)/shard_map/pallas_call | solution.py:879
  331.9 18.4 %collective-permute-done.24.refs_2_ = bf16[560,700]{1,0:T(8,128)(2,1)S(1)} collective-permute-done((bf16[560,700]{1,0:T(8,128)(2,1)S(1)}, bf16[560,700]{1,0:T(8,128)(2,1)S(1)}, u32[]{:S(2)}, u32[]{:S(2)}) %collective-permute-start.24) | collective-permute-done | bytes 784032 | tf_op jit(solution)/shard_map/ppermute | solution.py:727
  350.3 8.1 %collective-permute-done.25.refs_8_ = bf16[560,1400]{1,0:T(8,128)(2,1)S(1)} collective-permute-done((bf16[560,1400]{1,0:T(8,128)(2,1)}, bf16[560,1400]{1,0:T(8,128)(2,1)S(1)}, u32[]{:S(2)}, u32[]{:S(2)}) %collective-permute-start.25) | collective-permute-done | bytes 1568032 | tf_op jit(solution)/shard_map/ppermute | solution.py:706
  370.4 16.6 %collective-permute-done.28.refs_6_ = bf16[560,700]{1,0:T(8,128)(2,1)S(1)} collective-permute-done((bf16[560,700]{1,0:T(8,128)(2,1)S(1)}, bf16[560,700]{1,0:T(8,128)(2,1)S(1)}, u32[]{:S(2)}, u32[]{:S(2)}) %collective-permute-start.28) | collective-permute-done | bytes 784032 | tf_op jit(solution)/shard_map/ppermute | solution.py:706
  399.6 17.6 %shard_map.395 = (f32[2,512,700]{2,1,0:T(8,128)}, f32[2,512,700]{2,1,0:T(8,128)}, bf16[2,512,700]{2,1,0:T(8,128)(2,1)}, bf16[2,512,700]{2,1,0:T(8,128)(2,1)}, f3...) custom-call(s32[5]{0:T(128)} %stack.60.refs_0_, bf16[560,1400]{1,0:T(8,128)(2,1)} %copy-done.9, ...), custom_call_target="tpu_custom_call" | custom-call | tf_op jit(solution)/shard_map/pallas_call | solution.py:879
  423.2 17.4 %collective-permute-done.31.refs_12_ = bf16[2,32,700]{2,1,0:T(8,128)(2,1)S(1)} collective-permute-done((bf16[2,32,700]{2,1,0:T(8,128)(2,1)}, bf16[2,32,700]{2,1,0:T(8,128)(2,1)S(1)}, u32[]{:S(2)}, u32[]{:S(2)}) %collective-permute-start.31) | collective-permute-done | bytes 89632 | tf_op jit(solution)/shard_map/ppermute | solution.py:706
  442.6 27.9 %shard_map.396 = (bf16[2,512,700]{2,1,0:T(8,128)(2,1)}, bf16[2,512,700]{2,1,0:T(8,128)(2,1)}, bf16[2,512,700]{2,1,0:T(8,128)(2,1)}, bf16[512,2240]{1,0:T(8,128)(...) custom-call(s32[5]{0:T(128)} %stack.60.refs_0_, ...), custom_call_target="tpu_custom_call" | custom-call | tf_op jit(solution)/shard_map/pallas_call | solution.py:879
  478.7 24.6 %shard_map.397 = (bf16[2,512,700]{2,1,0:T(8,128)(2,1)}, bf16[2,512,700]{2,1,0:T(8,128)(2,1)}, f32[2,2,32,700]{3,2,1,0:T(8,128)}, f32[512,32]{1,0:T(8,128)}, f32[...) custom-call(s32[5]{0:T(128)} %stack.60.refs_0_, bf16[560,1400]{1,0:T(8,128)(2,1)} %copy-done.9, ...), custom_call_target="tpu_custom_call" | custom-call | tf_op jit(solution)/shard_map/pallas_call | solution.py:879
  520.1 19.9 %collective-permute-done.38.refs_1_ = bf16[256,2304]{1,0:T(8,128)(2,1)} collective-permute-done((bf16[256,2304]{1,0:T(8,128)(2,1)}, bf16[256,2304]{1,0:T(8,128)(2,1)}, u32[]{:S(2)}, u32[]{:S(2)}) %collective-permute-start.38) | collective-permute-done | bytes 1179680 | tf_op jit(solution)/shard_map/ppermute | solution.py:706
  539.9 6.4 shard_map.400
  554.0 27.7 %shard_map.401 = (bf16[512,576]{1,0:T(8,128)(2,1)}, f32[2,320,576]{2,1,0:T(8,128)}, f32[512,32]{1,0:T(8,128)}, f32[512,32]{1,0:T(8,128)}, f32[256,2304]{1,0:T(8,128)}, /*index=5*/bf16[256,2304]{1,0:T(8,128)(2,1)}) custom-call(s32[5]{0:T(128)} %stack.60.refs_0_, bf16[560,1152]{1,0:T(8,128)(2,1)} %copy-done.3, ...), custom_call_target="tpu_custom_call" | custom-call | tf_op jit(solution)/shard_map/pallas_call | solution.py:879
  597.3 12.8 %collective-permute-done.43.refs_14_ = f32[2,160,576]{2,1,0:T(8,128)} collective-permute-done((f32[2,160,576]{2,1,0:T(8,128)}, f32[2,160,576]{2,1,0:T(8,128)}, u32[]{:S(2)}, u32[]{:S(2)}) %collective-permute-start.43) | collective-permute-done | bytes 737312 | tf_op jit(solution)/shard_map/ppermute | solution.py:706
  610.1 6.8 shard_map.403
  627.2 14.0 %shard_map.405 = (bf16[512,576]{1,0:T(8,128)(2,1)}, f32[512,32]{1,0:T(8,128)}, f32[40,576]{1,0:T(8,128)}) custom-call(s32[5]{0:T(128)} %stack.60.refs_0_, bf16[560,1152]{1,0:T(8,128)(2,1)} %get-tuple-element.512.refs_1_, bf16[560,1152]{1,0:T(8,128)(2,1)} %collective-permute-done.1.refs_2_, bf16[560,1152]{1,0:T(8,128)(2,1)} %collective-permute-done.2.refs_3_, ...), custom_call_target="tpu_custom_call" | custom-call | tf_op jit(solution)/shard_map/pallas_call | solution.py:879
  647.1 15.3 %shard_map.406 = (bf16[512,576]{1,0:T(8,128)(2,1)}, bf16[512,576]{1,0:T(8,128)(2,1)}, f32[512,32]{1,0:T(8,128)}, f32[256,2304]{1,0:T(8,128)}, bf16[256,2304]{1,0:T(8,128)(2,1)}) custom-call(s32[5]{0:T(128)} %stack.60.refs_0_, bf16[560,1152]{1,0:T(8,128)(2,1)} %get-tuple-element.512.refs_1_, bf16[560,1152]{1,0:T(8,128)(2,1)} %collective-permute-done.1.refs_2_, ...), custom_call_target="tpu_custom_call" | custom-call | tf_op jit(solution)/shard_map/pallas_call | solution.py:879
  674.7 8.5 %all-to-all-done.1.refs_0_ = bf16[8,32,700]{2,1,0:T(8,128)(2,1)S(1)} async-done(((bf16[8,32,700]{2,1,0:T(8,128)(2,1)}), bf16[8,32,700]{2,1,0:T(8,128)(2,1)S(1)}, u32[]{:S(2)}, u32[]{:S(2)}) %all-to-all-start.1) | async-done | bytes 358432 | tf_op jit(solution)/shard_map/all_to_all | solution.py:1258
  686.5 9.0 %collective-permute-done.47.refs_1_ = bf16[256,2304]{1,0:T(8,128)(2,1)S(1)} collective-permute-done((bf16[256,2304]{1,0:T(8,128)(2,1)S(1)}, bf16[256,2304]{1,0:T(8,128)(2,1)S(1)}, u32[]{:S(2)}, u32[]{:S(2)}) %collective-permute-start.47) | collective-permute-done | bytes 1179680 | tf_op jit(solution)/shard_map/ppermute | solution.py:706
  720.8 9.4 %all-to-all-done.3.refs_0_ = bf16[8,64,280]{2,1,0:T(8,128)(2,1)S(1)} async-done(((bf16[8,64,280]{2,1,0:T(8,128)(2,1)}), bf16[8,64,280]{2,1,0:T(8,128)(2,1)S(1)}, u32[]{:S(2)}, u32[]{:S(2)}) %all-to-all-start.3) | async-done | bytes 286752 | tf_op jit(solution)/shard_map/all_to_all | solution.py:1154
  (316 shorter events, 261.8 us)
Async XLA Ops:
  7.7 31.9 %collective-permute-start.1 = (bf16[560,1152]{1,0:T(8,128)(2,1)}, bf16[560,1152]{1,0:T(8,128)(2,1)}, u32[]{:S(2)}, u32[]{:S(2)}) collective-permute-start(bf16[560,1152]{1,0:T(8,128)(2,1)} %get-tuple-element.512.refs_1_), channel_id=1, source_target_pairs={{0,16},{16,24},{24,8},{8,0},{1,17},{17,25},{25,9},{9,1},{2,18},{18... | collective-permute-start | bytes 3870728 | tf_op jit(solution)/shard_map/ppermute | solution.py:727
  39.7 29.6 %collective-permute-start.3 = (bf16[560,1152]{1,0:T(8,128)(2,1)}, bf16[560,1152]{1,0:T(8,128)(2,1)}, u32[]{:S(2)}, u32[]{:S(2)}) collective-permute-start(bf16[560,1152]{1,0:T(8,128)(2,1)} %collective-permute-done.1.refs_2_), channel_id=1, source_target_pairs={{0,4},{4,0},{1,5},{5,1},{2,6},{6,2},{3,7},{7,3},{8,12},{12,8},{9,1... | collective-permute-start | bytes 3870728 | tf_op jit(solution)/shard_map/ppermute | solution.py:706
  41.2 30.1 %collective-permute-start.2 = (bf16[560,1152]{1,0:T(8,128)(2,1)}, bf16[560,1152]{1,0:T(8,128)(2,1)}, u32[]{:S(2)}, u32[]{:S(2)}) collective-permute-start(bf16[560,1152]{1,0:T(8,128)(2,1)} %collective-permute-done.1.refs_2_), channel_id=1, source_target_pairs={{0,16},{16,24},{24,8},{8,0},{1,17},{17,25},{25,9},{9,1},{2,18},{18... | collective-permute-start | bytes 3870728 | tf_op jit(solution)/shard_map/ppermute | solution.py:727
  71.3 28.6 %collective-permute-start.5 = (bf16[560,1152]{1,0:T(8,128)(2,1)}, bf16[560,1152]{1,0:T(8,128)(2,1)}, u32[]{:S(2)}, u32[]{:S(2)}) collective-permute-start(bf16[560,1152]{1,0:T(8,128)(2,1)} %collective-permute-done.2.refs_3_), channel_id=1, source_target_pairs={{0,4},{4,0},{1,5},{5,1},{2,6},{6,2},{3,7},{7,3},{8,12},{12,8},{9,1... | collective-permute-start | bytes 3870728 | tf_op jit(solution)/shard_map/ppermute | solution.py:706
  71.8 33.0 %collective-permute-start.4 = (bf16[560,1152]{1,0:T(8,128)(2,1)}, bf16[560,1152]{1,0:T(8,128)(2,1)}, u32[]{:S(2)}, u32[]{:S(2)}) collective-permute-start(bf16[560,1152]{1,0:T(8,128)(2,1)} %collective-permute-done.2.refs_3_), channel_id=1, source_target_pairs={{0,16},{16,24},{24,8},{8,0},{1,17},{17,25},{25,9},{9,1},{2,18},{18... | collective-permute-start | bytes 3870728 | tf_op jit(solution)/shard_map/ppermute | solution.py:727
  94.1 34.8 %collective-permute-start.6 = (bf16[560,1152]{1,0:T(8,128)(2,1)S(1)}, bf16[560,1152]{1,0:T(8,128)(2,1)}, u32[]{:S(2)}, u32[]{:S(2)}) collective-permute-start(bf16[560,1152]{1,0:T(8,128)(2,1)S(1)} %get-tuple-element.510.refs_1_), channel_id=1, source_target_pairs={{0,16},{16,24},{24,8},{8,0},{1,17},{17,25},{25,9},{9,1},{2,18},{18... | collective-permute-start | bytes 3870728 | tf_op jit(solution)/shard_map/ppermute | solution.py:727
  104.8 24.0 %collective-permute-start.7 = (bf16[560,1152]{1,0:T(8,128)(2,1)}, bf16[560,1152]{1,0:T(8,128)(2,1)S(1)}, u32[]{:S(2)}, u32[]{:S(2)}) collective-permute-start(bf16[560,1152]{1,0:T(8,128)(2,1)} %collective-permute-done.4.refs_4_), channel_id=1, source_target_pairs={{0,4},{4,0},{1,5},{5,1},{2,6},{6,2},{3,7},{7,3},{8,12},{12,8},{9,1... | collective-permute-start | bytes 3870728 | tf_op jit(solution)/shard_map/ppermute | solution.py:706
  128.8 38.3 %collective-permute-start.10 = (bf16[560,1152]{1,0:T(8,128)(2,1)}, bf16[560,1152]{1,0:T(8,128)(2,1)S(1)}, u32[]{:S(2)}, u32[]{:S(2)}) collective-permute-start(bf16[560,1152]{1,0:T(8,128)(2,1)} %collective-permute-done.6.refs_2_), channel_id=1, source_target_pairs={{0,4},{4,0},{1,5},{5,1},{2,6},{6,2},{3,7},{7,3},{8,12},{12,8},{9,1... | collective-permute-start | bytes 3870728 | tf_op jit(solution)/shard_map/ppermute | solution.py:706
  130.3 36.8 %collective-permute-start.9 = (bf16[560,1152]{1,0:T(8,128)(2,1)}, bf16[560,1152]{1,0:T(8,128)(2,1)}, u32[]{:S(2)}, u32[]{:S(2)}) collective-permute-start(bf16[560,1152]{1,0:T(8,128)(2,1)} %collective-permute-done.6.refs_2_), channel_id=1, source_target_pairs={{0,16},{16,24},{24,8},{8,0},{1,17},{17,25},{25,9},{9,1},{2,18},{18... | collective-permute-start | bytes 3870728 | tf_op jit(solution)/shard_map/ppermute | solution.py:727
  167.2 25.4 %collective-permute-start.12 = (bf16[560,1152]{1,0:T(8,128)(2,1)}, bf16[560,1152]{1,0:T(8,128)(2,1)S(1)}, u32[]{:S(2)}, u32[]{:S(2)}) collective-permute-start(bf16[560,1152]{1,0:T(8,128)(2,1)} %collective-permute-done.9.refs_3_), channel_id=1, source_target_pairs={{0,4},{4,0},{1,5},{5,1},{2,6},{6,2},{3,7},{7,3},{8,12},{12,8},{9,1... | collective-permute-start | bytes 3870728 | tf_op jit(solution)/shard_map/ppermute | solution.py:706
  167.8 24.8 %collective-permute-start.11 = (bf16[560,1152]{1,0:T(8,128)(2,1)}, bf16[560,1152]{1,0:T(8,128)(2,1)}, u32[]{:S(2)}, u32[]{:S(2)}) collective-permute-start(bf16[560,1152]{1,0:T(8,128)(2,1)} %collective-permute-done.9.refs_3_), channel_id=1, source_target_pairs={{0,16},{16,24},{24,8},{8,0},{1,17},{17,25},{25,9},{9,1},{2,18},{18... | collective-permute-start | bytes 3870728 | tf_op jit(solution)/shard_map/ppermute | solution.py:727
  210.7 37.0 %collective-permute-start.15 = (bf16[560,1400]{1,0:T(8,128)(2,1)S(1)}, bf16[560,1400]{1,0:T(8,128)(2,1)}, u32[]{:S(2)}, u32[]{:S(2)}) collective-permute-start(bf16[560,1400]{1,0:T(8,128)(2,1)S(1)} %pad_maximum_fusion.2.refs_1_), channel_id=1, source_target_pairs={{0,16},{16,24},{24,8},{8,0},{1,17},{17,25},{25,9},{9,1},{2,18},{18... | collective-permute-start | bytes 4704008 | tf_op jit(solution)/shard_map/ppermute | solution.py:727
  211.7 36.0 %collective-permute-start.16 = (bf16[560,1152]{1,0:T(8,128)(2,1)}, bf16[560,1152]{1,0:T(8,128)(2,1)S(1)}, u32[]{:S(2)}, u32[]{:S(2)}) collective-permute-start(bf16[560,1152]{1,0:T(8,128)(2,1)} %collective-permute-done.11.refs_4_), channel_id=1, source_target_pairs={{0,4},{4,0},{1,5},{5,1},{2,6},{6,2},{3,7},{7,3},{8,12},{12,8},{9,1... | collective-permute-start | bytes 3870728 | tf_op jit(solution)/shard_map/ppermute | solution.py:706
  213.5 34.2 %collective-permute-start.14 = (bf16[256,2304]{1,0:T(8,128)(2,1)S(1)}, bf16[256,2304]{1,0:T(8,128)(2,1)S(1)}, u32[]{:S(2)}, u32[]{:S(2)}) collective-permute-start(bf16[256,2304]{1,0:T(8,128)(2,1)S(1)} %add_convert_fusion.5.refs_0_), channel_id=1, source_target_pairs={{0,2},{1,3},{2,0},{3,1},{4,6},{5,7},{6,4},{7,5},{8,10},{9,11},{10,... | collective-permute-start | bytes 3538952 | tf_op jit(solution)/shard_map/ppermute | solution.py:706
  247.7 36.3 %collective-permute-start.19 = (bf16[560,1400]{1,0:T(8,128)(2,1)}, bf16[560,1400]{1,0:T(8,128)(2,1)S(1)}, u32[]{:S(2)}, u32[]{:S(2)}) collective-permute-start(bf16[560,1400]{1,0:T(8,128)(2,1)} %collective-permute-done.15.refs_2_), channel_id=1, source_target_pairs={{0,4},{4,0},{1,5},{5,1},{2,6},{6,2},{3,7},{7,3},{8,12},{12,8},{9,1... | collective-permute-start | bytes 4704008 | tf_op jit(solution)/shard_map/ppermute | solution.py:706
  248.5 36.3 %collective-permute-start.18 = (bf16[560,1400]{1,0:T(8,128)(2,1)}, bf16[560,1400]{1,0:T(8,128)(2,1)}, u32[]{:S(2)}, u32[]{:S(2)}) collective-permute-start(bf16[560,1400]{1,0:T(8,128)(2,1)} %collective-permute-done.15.refs_2_), channel_id=1, source_target_pairs={{0,16},{16,24},{24,8},{8,0},{1,17},{17,25},{25,9},{9,1},{2,18},{18... | collective-permute-start | bytes 4704008 | tf_op jit(solution)/shard_map/ppermute | solution.py:727
  284.8 35.2 %collective-permute-start.21 = (bf16[560,1400]{1,0:T(8,128)(2,1)}, bf16[560,1400]{1,0:T(8,128)(2,1)}, u32[]{:S(2)}, u32[]{:S(2)}) collective-permute-start(bf16[560,1400]{1,0:T(8,128)(2,1)} %collective-permute-done.18.refs_3_), channel_id=1, source_target_pairs={{0,4},{4,0},{1,5},{5,1},{2,6},{6,2},{3,7},{7,3},{8,12},{12,8},{9,1... | collective-permute-start | bytes 4704008 | tf_op jit(solution)/shard_map/ppermute | solution.py:706
  285.9 35.4 %collective-permute-start.20 = (bf16[560,1400]{1,0:T(8,128)(2,1)}, bf16[560,1400]{1,0:T(8,128)(2,1)}, u32[]{:S(2)}, u32[]{:S(2)}) collective-permute-start(bf16[560,1400]{1,0:T(8,128)(2,1)} %collective-permute-done.18.refs_3_), channel_id=1, source_target_pairs={{0,16},{16,24},{24,8},{8,0},{1,17},{17,25},{25,9},{9,1},{2,18},{18... | collective-permute-start | bytes 4704008 | tf_op jit(solution)/shard_map/ppermute | solution.py:727
  321.3 37.1 %collective-permute-start.25 = (bf16[560,1400]{1,0:T(8,128)(2,1)}, bf16[560,1400]{1,0:T(8,128)(2,1)S(1)}, u32[]{:S(2)}, u32[]{:S(2)}) collective-permute-start(bf16[560,1400]{1,0:T(8,128)(2,1)} %collective-permute-done.20.refs_4_), channel_id=1, source_target_pairs={{0,4},{4,0},{1,5},{5,1},{2,6},{6,2},{3,7},{7,3},{8,12},{12,8},{9,1... | collective-permute-start | bytes 4704008 | tf_op jit(solution)/shard_map/ppermute | solution.py:706
  326.1 32.3 %collective-permute-start.23 = (bf16[256,2304]{1,0:T(8,128)(2,1)S(1)}, bf16[256,2304]{1,0:T(8,128)(2,1)S(1)}, u32[]{:S(2)}, u32[]{:S(2)}) collective-permute-start(bf16[256,2304]{1,0:T(8,128)(2,1)S(1)} %add_convert_fusion.4.refs_0_), channel_id=1, source_target_pairs={{0,2},{1,3},{2,0},{3,1},{4,6},{5,7},{6,4},{7,5},{8,10},{9,11},{10,... | collective-permute-start | bytes 3538952 | tf_op jit(solution)/shard_map/ppermute | solution.py:706
  365.4 23.7 %collective-permute-start.26 = (bf16[256,2304]{1,0:T(8,128)(2,1)}, bf16[256,2304]{1,0:T(8,128)(2,1)S(1)}, u32[]{:S(2)}, u32[]{:S(2)}) collective-permute-start(bf16[256,2304]{1,0:T(8,128)(2,1)} %get-tuple-element.318.refs_10_.refs_4_), channel_id=1, source_target_pairs={{0,1},{1,0},{2,3},{3,2},{4,5},{5,4},{6,7},{7,6},{8,9},{9,8},{10,11... | collective-permute-start | bytes 3538952 | tf_op jit(solution)/shard_map/ppermute | solution.py:706
  389.1 28.2 %collective-permute-start.30 = (bf16[560,700]{1,0:T(8,128)(2,1)}, bf16[560,700]{1,0:T(8,128)(2,1)}, u32[]{:S(2)}, u32[]{:S(2)}) collective-permute-start(bf16[560,700]{1,0:T(8,128)(2,1)} %collective-permute-done.27.refs_3_), channel_id=1, source_target_pairs={{0,4},{4,0},{1,5},{5,1},{2,6},{6,2},{3,7},{7,3},{8,12},{12,8},{9,1... | collective-permute-start | bytes 2352008 | tf_op jit(solution)/shard_map/ppermute | solution.py:706
  389.6 27.7 %collective-permute-start.29 = (bf16[560,700]{1,0:T(8,128)(2,1)}, bf16[560,700]{1,0:T(8,128)(2,1)}, u32[]{:S(2)}, u32[]{:S(2)}) collective-permute-start(bf16[560,700]{1,0:T(8,128)(2,1)} %collective-permute-done.27.refs_3_), channel_id=1, source_target_pairs={{0,16},{16,24},{24,8},{8,0},{1,17},{17,25},{25,9},{9,1},{2,18},{18... | collective-permute-start | bytes 2352008 | tf_op jit(solution)/shard_map/ppermute | solution.py:727
  417.3 24.3 %collective-permute-start.33 = (bf16[560,700]{1,0:T(8,128)(2,1)}, bf16[560,700]{1,0:T(8,128)(2,1)S(1)}, u32[]{:S(2)}, u32[]{:S(2)}) collective-permute-start(bf16[560,700]{1,0:T(8,128)(2,1)} %collective-permute-done.29.refs_4_), channel_id=1, source_target_pairs={{0,4},{4,0},{1,5},{5,1},{2,6},{6,2},{3,7},{7,3},{8,12},{12,8},{9,1... | collective-permute-start | bytes 2352008 | tf_op jit(solution)/shard_map/ppermute | solution.py:706
  419.4 22.2 %collective-permute-start.32 = (bf16[2,32,700]{2,1,0:T(8,128)(2,1)}, bf16[2,32,700]{2,1,0:T(8,128)(2,1)S(1)}, u32[]{:S(2)}, u32[]{:S(2)}) collective-permute-start(bf16[2,32,700]{2,1,0:T(8,128)(2,1)} %get-tuple-element.330), channel_id=1, source_target_pairs={{0,4},{4,0},{1,5},{5,1},{2,6},{6,2},{3,7},{7,3},{8,12},{12,8},{9,1... | collective-permute-start | bytes 268808 | tf_op jit(solution)/shard_map/ppermute | solution.py:706
  478.1 27.5 %collective-permute-start.36 = (bf16[256,2304]{1,0:T(8,128)(2,1)S(1)}, bf16[256,2304]{1,0:T(8,128)(2,1)S(1)}, u32[]{:S(2)}, u32[]{:S(2)}) collective-permute-start(bf16[256,2304]{1,0:T(8,128)(2,1)S(1)} %add_convert_fusion.3.refs_0_), channel_id=1, source_target_pairs={{0,2},{1,3},{2,0},{3,1},{4,6},{5,7},{6,4},{7,5},{8,10},{9,11},{10,... | collective-permute-start | bytes 3538952 | tf_op jit(solution)/shard_map/ppermute | solution.py:706
  511.6 28.3 %collective-permute-start.38 = (bf16[256,2304]{1,0:T(8,128)(2,1)}, bf16[256,2304]{1,0:T(8,128)(2,1)}, u32[]{:S(2)}, u32[]{:S(2)}) collective-permute-start(bf16[256,2304]{1,0:T(8,128)(2,1)} %add_convert_fusion.2.refs_0_), channel_id=1, source_target_pairs={{0,2},{1,3},{2,0},{3,1},{4,6},{5,7},{6,4},{7,5},{8,10},{9,11},{10,... | collective-permute-start | bytes 3538952 | tf_op jit(solution)/shard_map/ppermute | solution.py:706
  549.5 32.2 %collective-permute-start.40 = (f32[256,2304]{1,0:T(8,128)S(1)}, f32[256,2304]{1,0:T(8,128)}, u32[]{:S(2)}, u32[]{:S(2)}) collective-permute-start(f32[256,2304]{1,0:T(8,128)S(1)} %copy-done.11), channel_id=1, source_target_pairs={{0,1},{1,0},{2,3},{3,2},{4,5},{5,4},{6,7},{7,6},{8,9},{9,8},{10,11... | collective-permute-start | bytes 7077896 | tf_op jit(solution)/shard_map/ppermute | solution.py:706
  550.5 31.2 %all-to-all-start = ((f32[4,4,6656]{2,1,0:T(4,128)}), f32[4,4,6656]{2,1,0:T(4,128)S(1)}, u32[]{:S(2)}, u32[]{:S(2)}) async-start(f32[4,4,6656]{2,1,0:T(4,128)} %reshape.121), calls=%async_computation | async-start | bytes 851968 | tf_op jit(solution)/shard_map/all_to_all | solution.py:1151
  586.8 30.1 %collective-permute-start.42 = (bf16[256,2304]{1,0:T(8,128)(2,1)S(1)}, bf16[256,2304]{1,0:T(8,128)(2,1)S(1)}, u32[]{:S(2)}, u32[]{:S(2)}) collective-permute-start(bf16[256,2304]{1,0:T(8,128)(2,1)S(1)} %add_convert_fusion.1.refs_0_), channel_id=1, source_target_pairs={{0,2},{1,3},{2,0},{3,1},{4,6},{5,7},{6,4},{7,5},{8,10},{9,11},{10,... | collective-permute-start | bytes 3538952 | tf_op jit(solution)/shard_map/ppermute | solution.py:706
  667.4 28.1 %collective-permute-start.47 = (bf16[256,2304]{1,0:T(8,128)(2,1)S(1)}, bf16[256,2304]{1,0:T(8,128)(2,1)S(1)}, u32[]{:S(2)}, u32[]{:S(2)}) collective-permute-start(bf16[256,2304]{1,0:T(8,128)(2,1)S(1)} %add_convert_fusion.refs_0_), channel_id=1, source_target_pairs={{0,2},{1,3},{2,0},{3,1},{4,6},{5,7},{6,4},{7,5},{8,10},{9,11},{10,... | collective-permute-start | bytes 3538952 | tf_op jit(solution)/shard_map/ppermute | solution.py:706
  708.7 28.3 %collective-permute-start.48 = (f32[256,2304]{1,0:T(8,128)}, f32[256,2304]{1,0:T(8,128)}, u32[]{:S(2)}, u32[]{:S(2)}) collective-permute-start(f32[256,2304]{1,0:T(8,128)} %shard_map.409.refs_1_), channel_id=1, source_target_pairs={{0,1},{1,0},{2,3},{3,2},{4,5},{5,4},{6,7},{7,6},{8,9},{9,8},{10,11... | collective-permute-start | bytes 7077896 | tf_op jit(solution)/shard_map/ppermute | solution.py:706
  (80 other events, 974.4 us)

commit v3 on v2

--- a/solution.py
+++ b/solution.py
@@ -43,28 +43,45 @@
     return mm(ah, bh, ca, cb) + mm(ah, bl, ca, cb) + mm(al, bh, ca, cb)
 
 
+def head_blocks(width):
+    return [slice(at, min(at + 2 * LANES, width)) for at in range(0, width, 2 * LANES)]
+
+
 def head_mask(width):
     row = lax.broadcasted_iota(jnp.int32, (width, width), 0) // HD
     col = lax.broadcasted_iota(jnp.int32, (width, width), 1) // HD
     return (row == col).astype(f32)
 
 
-def head_total(values, mask):
-    high, low = split(values)
-    low_mask = mask.astype(bf16)
-    return mm(high, low_mask) + mm(low, low_mask)
-
-
-def squeeze_heads(square, mask):
-    kept = square * mask
-    total = kept[:HD]
-    for h in range(1, kept.shape[0] // HD):
-        total = total + kept[h * HD : (h + 1) * HD]
-    return total
-
-
-def spread_heads(state, width, mask):
-    return jnp.concatenate([state] * (width // HD), axis=0) * mask
+def by_blocks(one, *arrays):
+    parts = [one(*[v[:, cols] for v in arrays]) for cols in head_blocks(arrays[0].shape[1])]
+    return jnp.concatenate(parts, axis=1)
+
+
+def head_total(values):
+    def one(v):
+        high, low = split(v)
+        mask = head_mask(v.shape[1]).astype(bf16)
+        return mm(high, mask) + mm(low, mask)
+
+    return by_blocks(one, values)
+
+
+def head_outer(a, b):
+    def one(x, y):
+        kept = mm3(x, y, 0, 0) * head_mask(x.shape[1])
+        return sum(kept[h * HD : (h + 1) * HD] for h in range(kept.shape[0] // HD))
+
+    return by_blocks(one, a, b)
+
+
+def head_product(values, state, over):
+    def one(v, s):
+        size = v.shape[1]
+        wide = jnp.concatenate([s] * (size // HD), axis=0) * head_mask(size)
+        return mm3(v, wide, 1, over)
+
+    return by_blocks(one, values, state)
 
 
 def sigmoid(values):
@@ -113,7 +130,7 @@
     v_out[...] = mm(a[...], w[0].columns(0, 0, v_out.shape[1])) + mm(two(lat[...]), u2[2])
     keys = jnp.maximum(k[...], 0.0)
     width = keys.shape[1]
-    st_out[:HD, :] = squeeze_heads(mm3(v_out[...], keys, 0, 0), head_mask(width))
+    st_out[:HD, :] = head_outer(v_out[...], keys)
     st_out[HD:, :] = jnp.broadcast_to(jnp.sum(keys, axis=0, keepdims=True), (8, width))
 
 
@@ -126,10 +143,9 @@
 def attn_back(w, q, st1, st2, owned, d2, u2, ratio_out, den_out, mixed_out, lat_out, mine, away):
     st = st1[...] + st2[...]
     width = q.shape[1]
-    mask = head_mask(width)
     queries = jnp.maximum(q[...], 0.0)
-    numer = mm3(queries, spread_heads(st[:HD], width, mask), 1, 1)
-    den = head_total(queries * st[HD : HD + 1], mask) + attention_epsilon
+    numer = head_product(queries, st[:HD], 1)
+    den = head_total(queries * st[HD : HD + 1]) + attention_epsilon
     ratio = numer / den
     ratio_out[...] = ratio
     den_out[...] = den
@@ -166,7 +182,7 @@
 
 
 def cross_fwd(
-    w, rows, kv, live, owned, qd2, qu2, cd2, cu2, q_out, mix_out, qlat_out, clat_out, lse_out, part,
+    w, rows, kv, live, owned, qd2, qu2, cd2, cu2, q_out, mix_out, qlat_out, clat_out, lse_out, part, logs,
 ):
     width = q_out.shape[1]
     depth = qd2.shape[0]
@@ -185,11 +201,12 @@
             exps = jnp.exp(scores - top)
             tot = jnp.sum(exps, axis=-1, keepdims=True)
             h = first // HD + j
-            lse_out[:, h : h + 1] = top + jnp.log(tot)
+            logs[:, h : h + 1] = top + jnp.log(tot)
             probs = (exps * (1.0 / tot)).astype(bf16)
             term = mm(probs, only_head(kv[1, :, cols], j))
             total = term if total is None else total + term
         mix_out[:, cols] = (total * owned[:, cols]).astype(bf16)
+    lse_out[...] = logs[...].T
     mix = mix_out[...]
     lat = mm(mix, cd2[...])
     clat_out[...] = lat
@@ -201,19 +218,17 @@
     return pl.ds(own_first(r, edge, rows // 2, where[0]), edge)
 
 
-def ffn_front(w, where, xo, xt, d2, uv, ug, pv, pg, hv, hg, lat_out, ev, eg, u):
+def ffn_front(h, w, where, xo, xt, d2, uv, ug, *refs):
     half = xo.shape[0]
     depth = d2.shape[0]
-    h = pl.program_id(0)
-
-    @pl.when(h == 0)
-    def first():
-        u[:half, :] = xo[:, :depth]
-        u[half:, :] = xt[:, :depth]
-        lat_out[...] = mm(u[...], d2[...])
-
-    both = mm(u[...], w[0].take(h))
-    pair = two(lat_out[...])
+    pv, pg, hv, hg, ev, eg = refs[:6] if h == 0 else refs[-7:-1]
+    u = refs[-1]
+    u[:half, :] = xo[:, :depth]
+    u[half:, :] = xt[:, :depth]
+    if h == 0:
+        refs[6][...] = mm(u[...], d2[...])
+    pair = two(refs[6][...] if h == 0 else refs[0][...])
+    both = mm(u[...], w[0].take(0))
     hh = uv.shape[2]
     at = edge_rows(where, u.shape[0], ev.shape[1])
     for i, (up, pre, hid, edge) in enumerate(((uv, pv, hv, ev), (ug, pg, hg, eg))):
@@ -376,15 +391,15 @@
             for j in range(size // HD):
                 key, val = only_head(kv[0, :, cols], j), only_head(kv[1, :, cols], j)
                 h = first // HD + j
-                scores = mm(q_all, key, 1, 1) * scale
+                scores = mm(key, q_all, 1, 1) * scale
                 scores = jnp.where(live[...] > 0.0, scores, masked_score)
-                probs = jnp.exp(scores - lse[:, h : h + 1])
-                grad_p = mm(g_all, val, 1, 1)
-                grad_v = grad_v + mm(probs.astype(bf16), only_head(g_all, j), 0, 0)
-                inner = jnp.sum(probs * grad_p, axis=-1, keepdims=True)
+                probs = jnp.exp(scores - lse[h : h + 1, :])
+                grad_p = mm(val, g_all, 1, 1)
+                grad_v = grad_v + mm(probs.astype(bf16), only_head(g_all, j))
+                inner = jnp.sum(probs * grad_p, axis=0, keepdims=True)
                 grad_s = (probs * (grad_p - inner)).astype(bf16)
-                grad_q = grad_q + mm(grad_s, key)
-                grad_k = grad_k + mm(grad_s, only_head(q_all, j), 0, 0)
+                grad_q = grad_q + mm(grad_s, key, 0, 0)
+                grad_k = grad_k + mm(grad_s, only_head(q_all, j))
             gqs[at, cols] = grad_q
             for side, new in ((0, grad_k * scale), (1, grad_v)):
                 gkv_out[side, :, cols] = new if i == 0 else gkv_out[side, :, cols] + new
@@ -393,9 +408,9 @@
     gl = mm(gq, qu2[...], 1, 1)
     qgl_out[...] = gl
     pair = two(gl)
-    weight = w[0].columns(0, 0, width)
-    put(mine, everything, mm(gq[:half], weight, 1, 1) + mm(pair[:half], qd2[...], 1, 1))
-    put(away, everything, mm(gq[half:], weight, 1, 1) + mm(pair[half:], qd2[...], 1, 1))
+    total = mm(gq, w[0].columns(0, 0, width), 1, 1) + mm(pair, qd2[...], 1, 1)
+    put(mine, everything, total[:half])
+    put(away, everything, total[half:])
 
 
 def linear_bwd(
@@ -412,16 +427,15 @@
         gl_out[at, :] = gl
         gh[at, :] = (mm(rows[:, :depth], weight) + mm(two(gl), d2[...], 1, 1)) * owned[...]
     st = st1[...] + st2[...]
-    mask = head_mask(width)
     grad = gh[...]
     inverse = 1.0 / den[...]
     numer = grad * inverse
-    grad_den = -head_total(grad * ratio[...], mask) * inverse
+    grad_den = -head_total(grad * ratio[...]) * inverse
     raw = q[...]
     queries = jnp.maximum(raw, 0.0)
-    grad_q = mm3(numer, spread_heads(st[:HD], width, mask)) + grad_den * st[HD : HD + 1]
+    grad_q = head_product(numer, st[:HD], 0) + grad_den * st[HD : HD + 1]
     gq_out[...] = jnp.where(raw > 0.0, grad_q, 0.0).astype(bf16)
-    st_out[:HD, :] = squeeze_heads(mm3(numer, queries, 0, 0), mask)
+    st_out[:HD, :] = head_outer(numer, queries)
     total = jnp.sum(grad_den * queries, axis=0, keepdims=True)
     st_out[HD:, :] = jnp.broadcast_to(total, (8, width))
 
@@ -432,31 +446,24 @@
     width = k.shape[1]
     half = mine.shape[0]
     st = st1[...] + st2[...]
-    mask = head_mask(width)
-    wide = spread_heads(st[:HD], width, mask)
     raw = k[...]
-    grad_k = mm3(v[...], wide) + st[HD : HD + 1]
+    grad_k = head_product(v[...], st[:HD], 0) + st[HD : HD + 1]
     gk_out[...] = jnp.where(raw > 0.0, grad_k, 0.0).astype(bf16)
-    gv_out[...] = mm3(jnp.maximum(raw, 0.0), wide, 1, 1).astype(bf16)
+    gv_out[...] = head_product(jnp.maximum(raw, 0.0), st[:HD], 1).astype(bf16)
     grads = (gq, gk_out, gv_out)
     gl = sum(mm(g[...], u2[i], 1, 1) for i, g in enumerate(grads))
     gl_out[...] = gl
     pair = two(gl)
     w[0].take(0)
     w[0].take(1)
-    weights = [w[0].columns(j, first, width) for j, first in ((0, 0), (0, width), (1, 0))]
-
-    def part(rows):
-        total = mm(pair[rows], d2[...], 1, 1)
-        for g, weight in zip(grads, weights):
-            total = total + mm(g[rows, :], weight, 1, 1)
-        return total
-
-    put(mine, everything, part(slice(0, half)))
-    put(away, everything, part(slice(half, 2 * half)))
-
-
-def in_steps(rows, body, step=32):
+    both = jnp.concatenate([gq[...], gk_out[...]], axis=1)
+    total = mm(both, w[0].columns(0, 0, 2 * width), 1, 1) + mm(gv_out[...], w[0].columns(1, 0, width), 1, 1)
+    total = total + mm(pair, d2[...], 1, 1)
+    put(mine, everything, total[:half])
+    put(away, everything, total[half:])
+
+
+def in_steps(rows, body, step=64):
     def one(i, carry):
         body(pl.ds(pl.multiple_of(i * step, step), step))
         return carry
@@ -707,9 +714,9 @@
 
 
 class Stream:
-    def __init__(self, makers, order):
+    def __init__(self, order):
         self.n = lax.axis_size(W)
-        self.makers, self.order = makers, list(order)
+        self.order = list(order)
         self.own, self.got, self.crossed = {}, {}, {}
         self.flying, self.crossing = [], []
 
@@ -717,7 +724,6 @@
         while not self.flying and self.order:
             name, step = self.order[0]
             if step == 1:
-                self.own[name] = self.makers[name]()
                 moving = self.own[name][0]
             elif (name, step - 1) in self.got:
                 moving = self.got[name, step - 1]
@@ -815,6 +821,14 @@
     return pl.BlockSpec((1,) + tuple(a.shape[1:]), lambda h: (h,) + zeros)
 
 
+def half_block(i):
+    def spec(a):
+        zeros = (0,) * (len(a.shape) - 1)
+        return pl.BlockSpec((1,) + tuple(a.shape[1:]), lambda *g: (i,) + zeros)
+
+    return spec
+
+
 def row_block(a):
     return pl.BlockSpec((a.shape[0] // 4, a.shape[1]), lambda i: (i, 0))
 
@@ -836,7 +850,7 @@
     return pl.BlockSpec(memory_space=pl.ANY)
 
 
-def run(kernel, ins, outs, scratch=(), steps=1, weights=(), meta=None):
+def run(kernel, ins, outs, scratch=(), steps=1, weights=(), meta=None, same=()):
     args, specs = [], []
     if weights:
         args.append(meta)
@@ -882,6 +896,7 @@
         in_specs=specs,
         out_specs=out_specs,
         out_shape=shapes,
+        input_output_aliases={first + i: j for i, j in same},
         scratch_shapes=list(scratch) + extra,
         compiler_params=big,
     )(*args)
@@ -949,7 +964,6 @@
         own = cut(rows, b * half, half, 0)
         return own, jnp.concatenate([own, cut(rows, (1 - b) * half, half, 0)])
 
-    late = {}
     def pair_of(first, second):
         return [jnp.where(c == 0, first, second), jnp.where(c == 0, second, first)]
 
@@ -959,28 +973,19 @@
     def beside(*values):
         return jnp.concatenate(values, axis=1)
 
-    def hidden_columns(i):
-        return beside(taken(inverted_weight, 0, i * hh, hh), taken(inverted_weight, 1, i * hh, hh))
-
-    def both(table, start):
-        return beside(taken(table, 0, start, width), taken(table, 1, start, width))
-
-    makers = dict(
-        ab=lambda: pair_of(
-            both(qkv_weight, col), beside(taken(qkv_weight, 2, col, width), cut(proj_weight, col, width, 0).T)
-        ),
-        cd=lambda: pair_of(
-            both(cross_kv_weight, late["col"]),
-            beside(cut(cross_q_weight, late["col"], width, 1), cut(cross_out_weight, late["col"], width, 0).T),
-        ),
-        vg=lambda: [hidden_columns(late["c"]), hidden_columns(1 - late["c"])],
-        p=lambda: [cut(point_weight, late["c"] * hh, hh, 0).T, cut(point_weight, (1 - late["c"]) * hh, hh, 0).T],
-    )
+    def both(table, start, size=width):
+        return beside(taken(table, 0, start, size), taken(table, 1, start, size))
+
     size = lax.axis_size(W)
     order = [(name, step) for name in ("ab", "cd", "vg", "p") for step in range(1, size)]
-    stream = Stream(makers, order)
+    stream = Stream(order)
     fences = stream.fences
 
+    side_qk = both(qkv_weight, col)
+    side_vo = beside(taken(qkv_weight, 2, col, width), cut(proj_weight, col, width, 0).T)
+    stream.own["ab"] = [jnp.where(c == 0, side_qk, side_vo), None]
+    c_late, caption, stream.own["ab"][0] = lax.optimization_barrier((c, caption, stream.own["ab"][0]))
+    stream.own["ab"][1] = jnp.where(c_late == 0, side_vo, side_qk)
     stream.launch()
     mods = modulation[0]
     low_tokens = tokens.reshape(n, D)
@@ -992,21 +997,27 @@
     padded = -(-D // LANES) * LANES
     cap = jnp.pad(caption[0], ((0, text_rows - text_here), (0, padded - D)))
     cap_other = across(cap, C)
-    late.update(col=col, c=c)
-
-    def later(values):
-        late["col"], late["c"], values = fences(1, (late["col"], late["c"], values))
-        return values
-
     tables = [query_down, query_up, kv_down, kv_up, cross_down, cross_up]
     tables_f = [inverted_down, inverted_up, point_down, point_up, depth_weight]
-    tables, tables_f, cap, cap_other, cotangent = later((tables, tables_f, cap, cap_other, cotangent))
+    raw = [cross_kv_weight, cross_q_weight, cross_out_weight]
+    raw_f = [inverted_weight, point_weight]
+    raw, raw_f, tables, tables_f, cap, cap_other, cotangent = fences(
+        1, (raw, raw_f, tables, tables_f, cap, cap_other, cotangent)
+    )
+    pair_cd = pair_of(both(raw[0], col), beside(cut(raw[1], col, width, 1), cut(raw[2], col, width, 0).T))
     query_down, query_up, kv_down, kv_up, cross_down, cross_up = tables
     cd2 = twice(cut(pick(cross_down), col, width, 0), 1)
     cu2 = twice(pick(cross_up), 0)
     xd2, xu2 = twice(pick(query_down), 1), twice(cut(pick(query_up), col, width, 1), 0)
     kd2, ku2 = twice(pick(kv_down), 1), twice(cut(pick(kv_up), col, width, 2), 0).transpose(1, 0, 2)
-    tables_f, cotangent = later((tables_f, cotangent))
+    front = [x_low, x_rows, qd2, qu2, pd2, pu2]
+    pair_cd, raw_f, tables_f, cotangent, front = fences(1, (pair_cd, raw_f, tables_f, cotangent, front))
+    stream.own["cd"] = pair_cd
+    x_low, x_rows, qd2, qu2, pd2, pu2 = front
+    pair_vg = [both(raw_f[0], i * hh, hh) for i in (c, 1 - c)]
+    pair_p = [cut(raw_f[1], i * hh, hh, 0).T for i in (c, 1 - c)]
+    pair_vg, pair_p, tables_f, cotangent = fences(1, (pair_vg, pair_p, tables_f, cotangent))
+    stream.own.update(vg=pair_vg, p=pair_p)
     inverted_down, inverted_up, point_down, point_up, depth_weight = tables_f
     fd2, fu2 = twice(pick(inverted_down), 1), twice(cut(pick(inverted_up), hid_first, hid, 2), 0)
     fu2 = fu2.reshape(2 * R, 2, 2, hh).transpose(1, 2, 0, 3)
@@ -1018,10 +1029,9 @@
     live = jnp.concatenate([c * text_here + places, (1 - c) * text_here + places])
     live = (live < caption_lengths[0]) & (jnp.concatenate([places, places]) < text_here)
     live = live.astype(f32)[None]
-    tables = [cd2, cu2, xd2, xu2, kd2, ku2, fd2, fu2, od2, ou2, taps, cot_low, cot, live]
-    x_rows, tables = later((x_rows, tables))
-    cd2, cu2, xd2, xu2, kd2, ku2, fd2, fu2, od2, ou2, taps, cot_low, cot, live = tables
-    x_rows = stream.ready(["ab"], x_rows)
+    tables = [cd2, cu2, xd2, xu2, kd2, ku2, fd2, fu2[0], fu2[1], od2, ou2, taps, cot_low, cot, live]
+    x_rows, tables = stream.ready(["ab"], (x_rows, tables))
+    cd2, cu2, xd2, xu2, kd2, ku2, fd2, fuv, fug, od2, ou2, taps, cot_low, cot, live = tables
 
     w_ab = stream.pieces("ab")
     meta = jnp.stack([c] + [ring_source(size, s) for s in range(size)]).astype(jnp.int32)
@@ -1029,7 +1039,7 @@
     thin = ((n, 2 * R), f32)
     wide = ((n, width), f32)
     wide_bf = ((n, width), bf16)
-    pair = [((half, padded), f32), ((half, padded), bf16)]
+    pair = [((half, padded), bf16)] * 2
     ended = [((half, D), f32, row_block), ((half, padded), bf16, row_block)]
 
     def finish_rows(kernel, arrays, outs):
@@ -1049,7 +1059,7 @@
     )
 
     def exchanged(mine, away, pace=lambda low: low):
-        low, distance = (mine + across(away, T).astype(f32)).astype(bf16), 2
+        low, distance = (mine.astype(f32) + across(away, T).astype(f32)).astype(bf16), 2
         while True:
             low = pace(low)
             got = across(low, T, distance)
@@ -1075,35 +1085,46 @@
     kv_all, cross_own, cross_other = fences(1, (kv_all, cross_own, cross_other))
     half_bf, half_thin = ((half, width), bf16), ((half, 2 * R), f32)
 
-    def cross_part(rows, kv, dtype):
+    def cross_part(rows, kv):
         return run(
             cross_fwd,
             [rows, kv, live, owned, xd2, xu2, cd2, cu2],
-            [half_bf, half_bf, half_thin, half_thin, ((half, LANES), f32), ((half, padded), dtype)],
+            [half_bf, half_bf, half_thin, half_thin, ((LANES, half), f32), ((half, padded), bf16)],
+            [pltpu.VMEM((half, LANES), f32)],
             weights=[(w_cd, (1,))], meta=meta,
         )
 
-    *cross_t, away = cross_part(cross_other, kv_all, bf16)
+    *cross_t, away = cross_part(cross_other, kv_all)
     away, cross_tied, kv_tied = lax.optimization_barrier((away, cross_own, kv_all))
-    *cross_o, mine = cross_part(cross_tied, kv_tied, f32)
+    *cross_o, mine = cross_part(cross_tied, kv_tied)
     mine, away = fences(1, (mine, away))
     query, mix, query_lat, cross_lat, lse = zip(cross_o, cross_t)
     low, got = while_streaming(mine, away)
     after_cross, ffn_own = finish_rows(end_cross, [low, got, after_attn], ended)
+    ffn_own, after_cross = fences(1, (ffn_own, after_cross))
     ffn_other = across(ffn_own, T)
 
     query_lat, cross_lat = jnp.concatenate(query_lat), jnp.concatenate(cross_lat)
 
-    ffn_own, ffn_other, after_cross = stream.ready(["vg"], fences(1, (ffn_own, ffn_other, after_cross)))
+    ffn_own, ffn_other, after_cross = stream.ready(["vg"], (ffn_own, ffn_other, after_cross))
     w_vg = stream.pieces("vg")
-    hid_f, hid_bf = ((2, n, hh), f32, per_step), ((2, n, hh), bf16, per_step)
-    edge_of = ((2, grid_cols, hh), bf16, per_step)
-    pre_v, pre_g, hid_v, hid_g, inv_lat, edge_v, edge_g = run(
-        ffn_front, [(where, scalars), ffn_own, ffn_other, fd2, (fu2[0], per_step), (fu2[1], per_step)],
-        [hid_f, hid_f, hid_bf, hid_bf, thin, edge_of, edge_of], [pltpu.VMEM((n, D), bf16)], 2,
-        weights=[(w_vg, (0, 1))], meta=meta,
-    )
-    hid_v, edge_v, edge_g = fences(1, (hid_v, edge_v, edge_g))
+    hid_bf = ((2, n, hh), bf16, per_step)
+
+    def ffn_part(h, more, same):
+        outs = [((2, n, hh), f32)] * 2 + [((2, n, hh), bf16)] * 2 + [((2, grid_cols, hh), bf16)] * 2
+        return run(
+            functools.partial(ffn_front, h),
+            [(where, scalars), ffn_own, ffn_other, fd2, (fuv, half_block(h)), (fug, half_block(h))] + more,
+            [out + (half_block(h),) for out in outs] + [thin][h:],
+            [pltpu.VMEM((n, D), bf16)],
+            weights=[(w_vg, (h,))], meta=meta, same=same,
+        )
+
+    *started, inv_lat = ffn_part(0, [], ())
+    ffn_own, started, inv_lat = fences(1, (ffn_own, started, inv_lat))
+    pre_v, pre_g, hid_v, hid_g, edge_v, edge_g = ffn_part(
+        1, [inv_lat] + [(v, anywhere) for v in started], [(7 + i, i) for i in range(6)]
+    )
     halo_v, halo_g = across(edge_v, C), across(edge_g, C)
     hid_v, halo_v, halo_g = stream.ready(["p"], (hid_v, halo_v, halo_g))
     w_p = stream.pieces("p")
@@ -1136,7 +1157,7 @@
         [
             (where, scalars), (gcv, per_step), (gcg, per_step), (halo, per_step), (taps, per_step),
             (pre_v, per_step), (pre_g, per_step), inv_lat, fd2,
-            (fu2[0], per_step), (fu2[1], per_step),
+            (fuv, per_step), (fug, per_step),
         ],
         [hid_bf, hid_bf, ((2, 2, 2 * R, hh), f32, per_step), thin] + pair,
         [grid_buf, grid_buf, row_acc],
@@ -1149,10 +1170,6 @@
 
     def swapped(sent):
         return lax.all_to_all(sent.reshape(groups, part_r, sent.shape[1]), T, 0, 0, tiled=True)
-
-    def sent_home(values):
-        got = lax.all_to_all(values, (W, C), 0, 0, tiled=True)
-        return run(adapter_tables, [got], [((adapters,) + got.shape[1:], f32)])[0]
 
     def up_to_tiles(size):
         return -(-size // LANES) * LANES
@@ -1199,7 +1216,7 @@
     grad_query, gkv, query_gl, cross_gl, mine, away = run(
         cross_bwd,
         [
-            gc_own, gc_other, kv_all, live, owned,
+            gc_own, gc_other, kv_all, live.T, owned,
             xd2, xu2, cd2, cu2, *query, *lse,
         ],
         [wide_bf, ((2, 2 * text_rows, width), f32), thin, thin] + pair,
@@ -1256,17 +1273,16 @@
 
     def third_work(home, sums_c, proj_gl, qkv_gl, grad_q, grad_k, grad_v):
         home = lax.all_to_all(home, (W, C), 0, 0, tiled=True)
-        return run(
+        (sums,) = run(
             third_sums, [(where, scalars), sums_c, proj_gl, mixed, qkv_lat, grad_q, grad_k, grad_v, qkv_gl],
             [((R, sums_c.shape[1] + 4 * seg + n), f32)],
-        )[0], run(adapter_tables, [home], [((adapters,) + home.shape[1:], f32)])[0]
+        )
+        return swapped(sums), run(adapter_tables, [home], [((adapters,) + home.shape[1:], f32)])[0]
 
     low, got, (sums, tables) = during(
         mine, away, (home, sums_c, proj_gl, qkv_gl, grad_q, grad_k, grad_v), third_work
     )
-    sums = swapped(sums)
     (input_grad,) = finish_rows(end_attn_back, [low, got, grad_after, x_low], [((half, padded), f32, row_block)])
-    input_grad, sums = together(input_grad, sums)
     input_other = across(input_grad, T)
     (last,) = run(
         functools.partial(last_sums, ranges),
@@ -1274,14 +1290,17 @@
         [(last_dims, bf16)],
         [pltpu.VMEM(last_dims, f32)],
     )
-    last = sent_home(last)
+    last = lax.all_to_all(last, (W, C), 0, 0, tiled=True)
+    input_grad = in_order(input_grad, input_other)
+    last, input_grad = together(last, input_grad)
+    (last,) = run(adapter_tables, [last], [((adapters,) + last.shape[1:], f32)])
 
     def rows_of(i):
         return table_rows(last, i, D)
 
     return (
         output,
-        in_order(input_grad, input_other),
+        input_grad,
         down_rows(last, 11, D),
         jnp.stack([rows_of(8), rows_of(9), rows_of(10)], axis=2),
         down_rows(last, 7, D),

time: 748 us -> 711 us (0.951)
  waiting for transfers between devices: 291 us -> 276 us
  local copies, waits for them, and re-layouts: 85 us -> 70.6 us
  starting transfers between devices: 74.8 us -> 64 us
    ppermute x37, waiting for transfers between devices: 178 us -> 103 us  [across(): return lax.ppermute(values, axis, swap_pairs(lax.axis_size(axis), distance))]
    ppermute x12, waiting for transfers between devices: 94.3 us -> 152 us  [launch(): lax.ppermute(moving, W, ring_pairs(self.n))]
    dynamic_slice x2 -> x0, local copies, waits for them, and re-layouts: 24.8 us -> none  [taken(): lax.dynamic_slice(table, (0, middle, start), (table.shape[0], 1, size))]
    ppermute x12, starting transfers between devices: 31.8 us -> 20.3 us  [launch(): lax.ppermute(moving, W, ring_pairs(self.n))]
    all_to_all x2, waiting for transfers between devices: 1.39 us -> 10.5 us  [swapped(): lax.all_to_all(sent.reshape(groups, part_r, sent.shape[1]), T, 0, 0, tile...]
    pallas_call x26 -> x27, Pallas kernels: 261 us -> 256 us  [run(): pl.pallas_call(body, grid=(steps,), in_specs=specs, out_specs=out_specs,...]
  transfers between devices with their start and end apart: 53 -> 53, of which waited for: 35 -> 39; matrix products, arithmetic and copies ran while one was open for 12% -> 11% of each run, Pallas kernels for 24% -> 26%
where the time goes in v3:
time: 711 us; the launch traced here: 702 us
  waiting for transfers between devices  276 us (39%)
  Pallas kernels  256 us (36%)
  local copies, waits for them, and re-layouts  70.6 us (10%)
  starting transfers between devices  64 us (9%)
  other arithmetic  33.2 us (5%)
    pallas_call x27, Pallas kernels, run(): pl.pallas_call(body, grid=(steps,), in_specs=specs, out_specs=out_specs,...  256 us
    ppermute x12, waiting for transfers between devices, launch(): lax.ppermute(moving, W, ring_pairs(self.n))  152 us
    ppermute x37, waiting for transfers between devices, across(): return lax.ppermute(values, axis, swap_pairs(lax.axis_size(axis), distance))  103 us
    ppermute x37, starting transfers between devices, across(): return lax.ppermute(values, axis, swap_pairs(lax.axis_size(axis), distance))  28.4 us
    ppermute x12, starting transfers between devices, launch(): lax.ppermute(moving, W, ring_pairs(self.n))  20.3 us
  transfers between devices with their start and end apart: 53, of which 39 were waited for; matrix products, arithmetic and copies ran while one was open for 11% of the time, Pallas kernels for 26%

profile of v3, /device:TPU:0, one launch (start us, length us, event | category | flops | bytes accessed | tf_op | source)
XLA Modules:
  0.0 702.2 jit_solution(3523060390033351162)
XLA Ops:
  28.6 5.6 collective-permute-done.refs_10_
  34.3 8.7 %collective-permute-done.1.refs_2_ = bf16[560,1152]{1,0:T(8,128)(2,1)} collective-permute-done((bf16[560,1152]{1,0:T(8,128)(2,1)}, bf16[560,1152]{1,0:T(8,128)(2,1)}, u32[]{:S(2)}, u32[]{:S(2)}) %collective-permute-start.1) | collective-permute-done | bytes 1290272 | tf_op jit(solution)/shard_map/ppermute | solution.py:733
  63.3 10.1 %collective-permute-done.2.refs_3_ = bf16[560,1152]{1,0:T(8,128)(2,1)S(1)} collective-permute-done((bf16[560,1152]{1,0:T(8,128)(2,1)}, bf16[560,1152]{1,0:T(8,128)(2,1)S(1)}, u32[]{:S(2)}, u32[]{:S(2)}) %collective-permute-start.2) | collective-permute-done | bytes 1290272 | tf_op jit(solution)/shard_map/ppermute | solution.py:733
  88.0 18.9 %collective-permute-done.4.refs_4_ = bf16[560,1152]{1,0:T(8,128)(2,1)} collective-permute-done((bf16[560,1152]{1,0:T(8,128)(2,1)S(1)}, bf16[560,1152]{1,0:T(8,128)(2,1)}, u32[]{:S(2)}, u32[]{:S(2)}) %collective-permute-start.4) | collective-permute-done | bytes 1290272 | tf_op jit(solution)/shard_map/ppermute | solution.py:733
  118.5 12.7 %collective-permute-done.6.refs_2_ = bf16[560,1152]{1,0:T(8,128)(2,1)} collective-permute-done((bf16[560,1152]{1,0:T(8,128)(2,1)}, bf16[560,1152]{1,0:T(8,128)(2,1)}, u32[]{:S(2)}, u32[]{:S(2)}) %collective-permute-start.6) | collective-permute-done | bytes 1290272 | tf_op jit(solution)/shard_map/ppermute | solution.py:733
  143.3 12.1 %shard_map.387 = (bf16[512,2240]{1,0:T(8,128)(2,1)}, f32[512,576]{1,0:T(8,128)}, f32[512,576]{1,0:T(8,128)}, f32[512,32]{1,0:T(8,128)}) custom-call(s32[5]{0:T(128)} %stack.60.refs_0_, bf16[560,1152]{1,0:T(8,128)(2,1)} %broadcast_select_fusion.3.refs_1_, bf16[560,1152]{1,0:T(8,128)(2,1)} %collective-permute-done.1.refs_2_, bf16[560,1152]{1,0:T(8,128)(2,1)} %copy-done.2, ...), custom_call_target="tpu_custom_call" | custom-call | tf_op jit(solution)/shard_map/pallas_call | solution.py:893
  155.4 8.4 %shard_map.388 = (f32[512,576]{1,0:T(8,128)}, f32[40,576]{1,0:T(8,128)}) custom-call(s32[5]{0:T(128)} %stack.60.refs_0_, bf16[560,1152]{1,0:T(8,128)(2,1)} %broadcast_select_fusion.3.refs_1_, bf16[560,1152]{1,0:T(8,128)(2,1)} %collective-permute-done.1.refs_2_, bf16[560,1152]{1,0:T(8,128)(2,1)} %copy-done.2, ...), custom_call_target="tpu_custom_call" | custom-call | tf_op jit(solution)/shard_map/pallas_call | solution.py:893
  174.4 8.5 %shard_map.389 = (f32[512,576]{1,0:T(8,128)}, f32[512,576]{1,0:T(8,128)}, bf16[512,576]{1,0:T(8,128)(2,1)}, f32[512,32]{1,0:T(8,128)}, bf16[256,2304]{1,0:T(8,128)(2,1)}, /*index=5*/bf16[256,2304]{1,0:T(8,128)(2,1)}) custom-call(s32[5]{0:T(128)} %stack.60.refs_0_, bf16[560,1152]{1,0:T(8,128)(2,1)} %broadcast_select_fusion.3.refs_1_, ...), custom_call_target="tpu_custom_call" | custom-call | tf_op jit(solution)/shard_map/pallas_call | solution.py:893
  182.9 10.5 %collective-permute-done.11.refs_4_ = bf16[560,1152]{1,0:T(8,128)(2,1)} collective-permute-done((bf16[560,1152]{1,0:T(8,128)(2,1)}, bf16[560,1152]{1,0:T(8,128)(2,1)}, u32[]{:S(2)}, u32[]{:S(2)}) %collective-permute-start.11) | collective-permute-done | bytes 1290272 | tf_op jit(solution)/shard_map/ppermute | solution.py:733
  201.0 31.6 %collective-permute-done.15.refs_2_ = bf16[560,1400]{1,0:T(8,128)(2,1)} collective-permute-done((bf16[560,1400]{1,0:T(8,128)(2,1)S(1)}, bf16[560,1400]{1,0:T(8,128)(2,1)}, u32[]{:S(2)}, u32[]{:S(2)}) %collective-permute-start.15) | collective-permute-done | bytes 1568032 | tf_op jit(solution)/shard_map/ppermute | solution.py:733
  240.9 7.8 %shard_map.390 = (bf16[2,320,576]{2,1,0:T(8,128)(2,1)}, f32[160,32]{1,0:T(8,128)}) custom-call(s32[5]{0:T(128)} %stack.60.refs_0_, bf16[560,1152]{1,0:T(8,128)(2,1)} %get-tuple-element.281.refs_1_, bf16[560,1152]{1,0:T(8,128)(2,1)} %collective-permute-done.6.refs_2_, bf16[560,1152]{1,0:T(8,128)(2,1)} %collective-permute-done.9.refs_3_, ...), custom_call_target="tpu_custom_call" | custom-call | tf_op jit(solution)/shard_map/pallas_call | solution.py:893
  248.7 20.3 %collective-permute-done.18.refs_3_ = bf16[560,1400]{1,0:T(8,128)(2,1)S(1)} collective-permute-done((bf16[560,1400]{1,0:T(8,128)(2,1)}, bf16[560,1400]{1,0:T(8,128)(2,1)S(1)}, u32[]{:S(2)}, u32[]{:S(2)}) %collective-permute-start.18) | collective-permute-done | bytes 1568032 | tf_op jit(solution)/shard_map/ppermute | solution.py:733
  275.4 13.7 %shard_map.392 = (bf16[256,576]{1,0:T(8,128)(2,1)}, bf16[256,576]{1,0:T(8,128)(2,1)}, f32[256,32]{1,0:T(8,128)}, f32[256,32]{1,0:T(8,128)}, f32[128,256]{1,0:T(8,128)}, /*index=5*/bf16[256,2304]{1,0:T(8,128)(2,1)}) custom-call(s32[5]{0:T(128)} %stack.60.refs_0_, bf16[560,1152]{1,0:T(8,128)(2,1)} %get-tuple-element.281.refs_1_, ...), custom_call_target="tpu_custom_call" | custom-call | tf_op jit(solution)/shard_map/pallas_call | solution.py:893
  289.2 14.2 %shard_map.393 = (bf16[256,576]{1,0:T(8,128)(2,1)}, bf16[256,576]{1,0:T(8,128)(2,1)}, f32[256,32]{1,0:T(8,128)}, f32[256,32]{1,0:T(8,128)}, f32[128,256]{1,0:T(8,128)}, /*index=5*/bf16[256,2304]{1,0:T(8,128)(2,1)}) custom-call(s32[5]{0:T(128)} %stack.60.refs_0_, bf16[560,1152]{1,0:T(8,128)(2,1)} %get-tuple-element.281.refs_1_, ...), custom_call_target="tpu_custom_call" | custom-call | tf_op jit(solution)/shard_map/pallas_call | solution.py:893
  313.3 19.4 %collective-permute-done.24.refs_2_ = bf16[560,700]{1,0:T(8,128)(2,1)} collective-permute-done((bf16[560,700]{1,0:T(8,128)(2,1)S(1)}, bf16[560,700]{1,0:T(8,128)(2,1)}, u32[]{:S(2)}, u32[]{:S(2)}) %collective-permute-start.24) | collective-permute-done | bytes 784032 | tf_op jit(solution)/shard_map/ppermute | solution.py:733
  332.8 10.7 %collective-permute-done.25.refs_8_ = bf16[560,1400]{1,0:T(8,128)(2,1)S(1)} collective-permute-done((bf16[560,1400]{1,0:T(8,128)(2,1)S(1)}, bf16[560,1400]{1,0:T(8,128)(2,1)S(1)}, u32[]{:S(2)}, u32[]{:S(2)}) %collective-permute-start.25) | collective-permute-done | bytes 1568032 | tf_op jit(solution)/shard_map/ppermute | solution.py:713
  352.4 13.1 %collective-permute-done.26.refs_3_ = bf16[560,700]{1,0:T(8,128)(2,1)S(1)} collective-permute-done((bf16[560,700]{1,0:T(8,128)(2,1)}, bf16[560,700]{1,0:T(8,128)(2,1)S(1)}, u32[]{:S(2)}, u32[]{:S(2)}) %collective-permute-start.26) | collective-permute-done | bytes 784032 | tf_op jit(solution)/shard_map/ppermute | solution.py:733
  372.0 11.7 %shard_map.395 = (f32[2,512,700]{2,1,0:T(8,128)}, f32[2,512,700]{2,1,0:T(8,128)}, bf16[2,512,700]{2,1,0:T(8,128)(2,1)}, bf16[2,512,700]{2,1,0:T(8,128)(2,1)}, bf...) custom-call(s32[5]{0:T(128)} %stack.60.refs_0_, ...), custom_call_target="tpu_custom_call" | custom-call | tf_op jit(solution)/shard_map/pallas_call | solution.py:893
  390.7 12.1 %shard_map.396 = (f32[2,512,700]{2,1,0:T(8,128)}, f32[2,512,700]{2,1,0:T(8,128)}, bf16[2,512,700]{2,1,0:T(8,128)(2,1)}, bf16[2,512,700]{2,1,0:T(8,128)(2,1)}, bf...) custom-call(s32[5]{0:T(128)} %stack.60.refs_0_, ...), custom_call_target="tpu_custom_call", output_to_operand_aliasing={{0}: (16, {}), {1}: (17, {}), {2}: (18, {}), {3}: (19, {}),... | custom-call | tf_op jit(solution)/shard_map/pallas_call | solution.py:893
  407.1 6.3 collective-permute-done.31.refs_12_
  415.4 27.7 %shard_map.397 = (bf16[2,512,700]{2,1,0:T(8,128)(2,1)}, bf16[2,512,700]{2,1,0:T(8,128)(2,1)}, bf16[2,512,700]{2,1,0:T(8,128)(2,1)}, bf16[512,2240]{1,0:T(8,128)(...) custom-call(s32[5]{0:T(128)} %stack.60.refs_0_, ...), custom_call_target="tpu_custom_call" | custom-call | tf_op jit(solution)/shard_map/pallas_call | solution.py:893
  451.5 24.1 %shard_map.398 = (bf16[2,512,700]{2,1,0:T(8,128)(2,1)}, bf16[2,512,700]{2,1,0:T(8,128)(2,1)}, f32[2,2,32,700]{3,2,1,0:T(8,128)}, f32[512,32]{1,0:T(8,128)}, bf16...) custom-call(s32[5]{0:T(128)} %stack.60.refs_0_, bf16[560,1400]{1,0:T(8,128)(2,1)} %get-tuple-element.331.refs_1_, ...), custom_call_target="tpu_custom_call" | custom-call | tf_op jit(solution)/shard_map/pallas_call | solution.py:893
  492.4 18.7 %collective-permute-done.38.refs_1_ = bf16[256,2304]{1,0:T(8,128)(2,1)} collective-permute-done((bf16[256,2304]{1,0:T(8,128)(2,1)S(1)}, bf16[256,2304]{1,0:T(8,128)(2,1)}, u32[]{:S(2)}, u32[]{:S(2)}) %collective-permute-start.38) | collective-permute-done | bytes 1179680 | tf_op jit(solution)/shard_map/ppermute | solution.py:713
  511.1 5.9 shard_map.401
  527.6 26.3 %shard_map.402 = (bf16[512,576]{1,0:T(8,128)(2,1)}, f32[2,320,576]{2,1,0:T(8,128)}, f32[512,32]{1,0:T(8,128)}, f32[512,32]{1,0:T(8,128)}, bf16[256,2304]{1,0:T(8,128)(2,1)}, /*index=5*/bf16[256,2304]{1,0:T(8,128)(2,1)}) custom-call(s32[5]{0:T(128)} %stack.60.refs_0_, bf16[560,1152]{1,0:T(8,128)(2,1)} %get-tuple-element.281.refs_1_, ...), custom_call_target="tpu_custom_call" | custom-call | tf_op jit(solution)/shard_map/pallas_call | solution.py:893
  568.8 13.1 %collective-permute-done.43.refs_14_ = f32[2,160,576]{2,1,0:T(8,128)S(1)} collective-permute-done((f32[2,160,576]{2,1,0:T(8,128)}, f32[2,160,576]{2,1,0:T(8,128)S(1)}, u32[]{:S(2)}, u32[]{:S(2)}) %collective-permute-start.43) | collective-permute-done | bytes 737312 | tf_op jit(solution)/shard_map/ppermute | solution.py:713
  582.8 6.8 shard_map.404
  598.8 11.0 %shard_map.406 = (bf16[512,576]{1,0:T(8,128)(2,1)}, f32[512,32]{1,0:T(8,128)}, f32[40,576]{1,0:T(8,128)}) custom-call(s32[5]{0:T(128)} %stack.60.refs_0_, bf16[560,1152]{1,0:T(8,128)(2,1)} %broadcast_select_fusion.3.refs_1_, bf16[560,1152]{1,0:T(8,128)(2,1)} %collective-permute-done.1.refs_2_, bf16[560,1152]{1,0:T(8,128)(2,1)} %copy-done.2, ...), custom_call_target="tpu_custom_call" | custom-call | tf_op jit(solution)/shard_map/pallas_call | solution.py:893
  615.6 13.9 %shard_map.407 = (bf16[512,576]{1,0:T(8,128)(2,1)}, bf16[512,576]{1,0:T(8,128)(2,1)}, f32[512,32]{1,0:T(8,128)}, bf16[256,2304]{1,0:T(8,128)(2,1)}, bf16[256,2304]{1,0:T(8,128)(2,1)}) custom-call(s32[5]{0:T(128)} %stack.60.refs_0_, bf16[560,1152]{1,0:T(8,128)(2,1)} %broadcast_select_fusion.3.refs_1_, bf16[560,1152]{1,0:T(8,128)(2,1)} %collective-permute-done.1.refs_2_, ...), custom_call_target="tpu_custom_call" | custom-call | tf_op jit(solution)/shard_map/pallas_call | solution.py:893
  643.7 6.5 all-to-all-done.2.refs_0_
  656.1 10.5 %all-to-all-done.1.refs_1_ = f32[4,4,6400]{2,1,0:T(4,128)S(1)} async-done(((f32[4,4,6400]{2,1,0:T(4,128)}), f32[4,4,6400]{2,1,0:T(4,128)S(1)}, u32[]{:S(2)}, u32[]{:S(2)}) %all-to-all-start.1) | async-done | bytes 409632 | tf_op jit(solution)/shard_map/all_to_all | solution.py:1172
  667.7 5.6 shard_map.411.refs_1_
  (317 shorter events, 272.5 us)
Async XLA Ops:
  11.0 31.9 %collective-permute-start.1 = (bf16[560,1152]{1,0:T(8,128)(2,1)}, bf16[560,1152]{1,0:T(8,128)(2,1)}, u32[]{:S(2)}, u32[]{:S(2)}) collective-permute-start(bf16[560,1152]{1,0:T(8,128)(2,1)} %broadcast_select_fusion.3.refs_1_), channel_id=1, source_target_pairs={{0,16},{16,24},{24,8},{8,0},{1,17},{17,25},{25,9},{9,1},{2,18},{18... | collective-permute-start | bytes 3870728 | tf_op jit(solution)/shard_map/ppermute | solution.py:733
  43.0 30.4 %collective-permute-start.2 = (bf16[560,1152]{1,0:T(8,128)(2,1)}, bf16[560,1152]{1,0:T(8,128)(2,1)S(1)}, u32[]{:S(2)}, u32[]{:S(2)}) collective-permute-start(bf16[560,1152]{1,0:T(8,128)(2,1)} %collective-permute-done.1.refs_2_), channel_id=1, source_target_pairs={{0,16},{16,24},{24,8},{8,0},{1,17},{17,25},{25,9},{9,1},{2,18},{18... | collective-permute-start | bytes 3870728 | tf_op jit(solution)/shard_map/ppermute | solution.py:733
  46.4 29.1 %collective-permute-start.3 = (bf16[560,1152]{1,0:T(8,128)(2,1)}, bf16[560,1152]{1,0:T(8,128)(2,1)S(1)}, u32[]{:S(2)}, u32[]{:S(2)}) collective-permute-start(bf16[560,1152]{1,0:T(8,128)(2,1)} %collective-permute-done.1.refs_2_), channel_id=1, source_target_pairs={{0,4},{4,0},{1,5},{5,1},{2,6},{6,2},{3,7},{7,3},{8,12},{12,8},{9,1... | collective-permute-start | bytes 3870728 | tf_op jit(solution)/shard_map/ppermute | solution.py:713
  75.5 31.4 %collective-permute-start.4 = (bf16[560,1152]{1,0:T(8,128)(2,1)S(1)}, bf16[560,1152]{1,0:T(8,128)(2,1)}, u32[]{:S(2)}, u32[]{:S(2)}) collective-permute-start(bf16[560,1152]{1,0:T(8,128)(2,1)S(1)} %collective-permute-done.2.refs_3_), channel_id=1, source_target_pairs={{0,16},{16,24},{24,8},{8,0},{1,17},{17,25},{25,9},{9,1},{2,18},{18... | collective-permute-start | bytes 3870728 | tf_op jit(solution)/shard_map/ppermute | solution.py:733
  76.7 30.2 %collective-permute-start.5 = (bf16[560,1152]{1,0:T(8,128)(2,1)S(1)}, bf16[560,1152]{1,0:T(8,128)(2,1)S(1)}, u32[]{:S(2)}, u32[]{:S(2)}) collective-permute-start(bf16[560,1152]{1,0:T(8,128)(2,1)S(1)} %collective-permute-done.2.refs_3_), channel_id=1, source_target_pairs={{0,4},{4,0},{1,5},{5,1},{2,6},{6,2},{3,7},{7,3},{8,12},{12,8},{9,1... | collective-permute-start | bytes 3870728 | tf_op jit(solution)/shard_map/ppermute | solution.py:713
  80.2 51.1 %collective-permute-start.6 = (bf16[560,1152]{1,0:T(8,128)(2,1)}, bf16[560,1152]{1,0:T(8,128)(2,1)}, u32[]{:S(2)}, u32[]{:S(2)}) collective-permute-start(bf16[560,1152]{1,0:T(8,128)(2,1)} %get-tuple-element.281.refs_1_), channel_id=1, source_target_pairs={{0,16},{16,24},{24,8},{8,0},{1,17},{17,25},{25,9},{9,1},{2,18},{18... | collective-permute-start | bytes 3870728 | tf_op jit(solution)/shard_map/ppermute | solution.py:733
  108.0 27.6 %collective-permute-start.7 = (bf16[560,1152]{1,0:T(8,128)(2,1)}, bf16[560,1152]{1,0:T(8,128)(2,1)}, u32[]{:S(2)}, u32[]{:S(2)}) collective-permute-start(bf16[560,1152]{1,0:T(8,128)(2,1)} %collective-permute-done.4.refs_4_), channel_id=1, source_target_pairs={{0,4},{4,0},{1,5},{5,1},{2,6},{6,2},{3,7},{7,3},{8,12},{12,8},{9,1... | collective-permute-start | bytes 3870728 | tf_op jit(solution)/shard_map/ppermute | solution.py:713
  135.5 34.4 %collective-permute-start.10 = (bf16[560,1152]{1,0:T(8,128)(2,1)}, bf16[560,1152]{1,0:T(8,128)(2,1)S(1)}, u32[]{:S(2)}, u32[]{:S(2)}) collective-permute-start(bf16[560,1152]{1,0:T(8,128)(2,1)} %collective-permute-done.6.refs_2_), channel_id=1, source_target_pairs={{0,4},{4,0},{1,5},{5,1},{2,6},{6,2},{3,7},{7,3},{8,12},{12,8},{9,1... | collective-permute-start | bytes 3870728 | tf_op jit(solution)/shard_map/ppermute | solution.py:713
  137.0 32.9 %collective-permute-start.9 = (bf16[560,1152]{1,0:T(8,128)(2,1)}, bf16[560,1152]{1,0:T(8,128)(2,1)}, u32[]{:S(2)}, u32[]{:S(2)}) collective-permute-start(bf16[560,1152]{1,0:T(8,128)(2,1)} %collective-permute-done.6.refs_2_), channel_id=1, source_target_pairs={{0,16},{16,24},{24,8},{8,0},{1,17},{17,25},{25,9},{9,1},{2,18},{18... | collective-permute-start | bytes 3870728 | tf_op jit(solution)/shard_map/ppermute | solution.py:733
  169.9 23.5 %collective-permute-start.11 = (bf16[560,1152]{1,0:T(8,128)(2,1)}, bf16[560,1152]{1,0:T(8,128)(2,1)}, u32[]{:S(2)}, u32[]{:S(2)}) collective-permute-start(bf16[560,1152]{1,0:T(8,128)(2,1)} %collective-permute-done.9.refs_3_), channel_id=1, source_target_pairs={{0,16},{16,24},{24,8},{8,0},{1,17},{17,25},{25,9},{9,1},{2,18},{18... | collective-permute-start | bytes 3870728 | tf_op jit(solution)/shard_map/ppermute | solution.py:733
  172.3 23.4 %collective-permute-start.12 = (bf16[560,1152]{1,0:T(8,128)(2,1)}, bf16[560,1152]{1,0:T(8,128)(2,1)}, u32[]{:S(2)}, u32[]{:S(2)}) collective-permute-start(bf16[560,1152]{1,0:T(8,128)(2,1)} %collective-permute-done.9.refs_3_), channel_id=1, source_target_pairs={{0,4},{4,0},{1,5},{5,1},{2,6},{6,2},{3,7},{7,3},{8,12},{12,8},{9,1... | collective-permute-start | bytes 3870728 | tf_op jit(solution)/shard_map/ppermute | solution.py:713
  195.7 37.0 %collective-permute-start.15 = (bf16[560,1400]{1,0:T(8,128)(2,1)S(1)}, bf16[560,1400]{1,0:T(8,128)(2,1)}, u32[]{:S(2)}, u32[]{:S(2)}) collective-permute-start(bf16[560,1400]{1,0:T(8,128)(2,1)S(1)} %copy-done.5), channel_id=1, source_target_pairs={{0,16},{16,24},{24,8},{8,0},{1,17},{17,25},{25,9},{9,1},{2,18},{18... | collective-permute-start | bytes 4704008 | tf_op jit(solution)/shard_map/ppermute | solution.py:733
  196.1 36.6 %collective-permute-start.16 = (bf16[560,1152]{1,0:T(8,128)(2,1)}, bf16[560,1152]{1,0:T(8,128)(2,1)S(1)}, u32[]{:S(2)}, u32[]{:S(2)}) collective-permute-start(bf16[560,1152]{1,0:T(8,128)(2,1)} %collective-permute-done.11.refs_4_), channel_id=1, source_target_pairs={{0,4},{4,0},{1,5},{5,1},{2,6},{6,2},{3,7},{7,3},{8,12},{12,8},{9,1... | collective-permute-start | bytes 3870728 | tf_op jit(solution)/shard_map/ppermute | solution.py:713
  200.3 32.4 %collective-permute-start.14 = (bf16[256,2304]{1,0:T(8,128)(2,1)S(1)}, bf16[256,2304]{1,0:T(8,128)(2,1)S(1)}, u32[]{:S(2)}, u32[]{:S(2)}) collective-permute-start(bf16[256,2304]{1,0:T(8,128)(2,1)S(1)} %add_convert_fusion.5.refs_0_), channel_id=1, source_target_pairs={{0,2},{1,3},{2,0},{3,1},{4,6},{5,7},{6,4},{7,5},{8,10},{9,11},{10,... | collective-permute-start | bytes 3538952 | tf_op jit(solution)/shard_map/ppermute | solution.py:713
  232.7 36.4 %collective-permute-start.18 = (bf16[560,1400]{1,0:T(8,128)(2,1)}, bf16[560,1400]{1,0:T(8,128)(2,1)S(1)}, u32[]{:S(2)}, u32[]{:S(2)}) collective-permute-start(bf16[560,1400]{1,0:T(8,128)(2,1)} %collective-permute-done.15.refs_2_), channel_id=1, source_target_pairs={{0,16},{16,24},{24,8},{8,0},{1,17},{17,25},{25,9},{9,1},{2,18},{18... | collective-permute-start | bytes 4704008 | tf_op jit(solution)/shard_map/ppermute | solution.py:733
  234.1 36.1 %collective-permute-start.19 = (bf16[560,1400]{1,0:T(8,128)(2,1)}, bf16[560,1400]{1,0:T(8,128)(2,1)}, u32[]{:S(2)}, u32[]{:S(2)}) collective-permute-start(bf16[560,1400]{1,0:T(8,128)(2,1)} %collective-permute-done.15.refs_2_), channel_id=1, source_target_pairs={{0,4},{4,0},{1,5},{5,1},{2,6},{6,2},{3,7},{7,3},{8,12},{12,8},{9,1... | collective-permute-start | bytes 4704008 | tf_op jit(solution)/shard_map/ppermute | solution.py:713
  270.2 35.1 %collective-permute-start.20 = (bf16[560,1400]{1,0:T(8,128)(2,1)S(1)}, bf16[560,1400]{1,0:T(8,128)(2,1)S(1)}, u32[]{:S(2)}, u32[]{:S(2)}) collective-permute-start(bf16[560,1400]{1,0:T(8,128)(2,1)S(1)} %collective-permute-done.18.refs_3_), channel_id=1, source_target_pairs={{0,16},{16,24},{24,8},{8,0},{1,17},{17,25},{25,9},{9,1},{2,18},{18... | collective-permute-start | bytes 4704008 | tf_op jit(solution)/shard_map/ppermute | solution.py:733
  271.5 35.0 %collective-permute-start.21 = (bf16[560,1400]{1,0:T(8,128)(2,1)S(1)}, bf16[560,1400]{1,0:T(8,128)(2,1)}, u32[]{:S(2)}, u32[]{:S(2)}) collective-permute-start(bf16[560,1400]{1,0:T(8,128)(2,1)S(1)} %collective-permute-done.18.refs_3_), channel_id=1, source_target_pairs={{0,4},{4,0},{1,5},{5,1},{2,6},{6,2},{3,7},{7,3},{8,12},{12,8},{9,1... | collective-permute-start | bytes 4704008 | tf_op jit(solution)/shard_map/ppermute | solution.py:713
  306.6 36.9 %collective-permute-start.25 = (bf16[560,1400]{1,0:T(8,128)(2,1)S(1)}, bf16[560,1400]{1,0:T(8,128)(2,1)S(1)}, u32[]{:S(2)}, u32[]{:S(2)}) collective-permute-start(bf16[560,1400]{1,0:T(8,128)(2,1)S(1)} %collective-permute-done.20.refs_4_), channel_id=1, source_target_pairs={{0,4},{4,0},{1,5},{5,1},{2,6},{6,2},{3,7},{7,3},{8,12},{12,8},{9,1... | collective-permute-start | bytes 4704008 | tf_op jit(solution)/shard_map/ppermute | solution.py:713
  311.0 32.5 %collective-permute-start.23 = (bf16[256,2304]{1,0:T(8,128)(2,1)S(1)}, bf16[256,2304]{1,0:T(8,128)(2,1)S(1)}, u32[]{:S(2)}, u32[]{:S(2)}) collective-permute-start(bf16[256,2304]{1,0:T(8,128)(2,1)S(1)} %add_convert_fusion.4.refs_0_), channel_id=1, source_target_pairs={{0,2},{1,3},{2,0},{3,1},{4,6},{5,7},{6,4},{7,5},{8,10},{9,11},{10,... | collective-permute-start | bytes 3538952 | tf_op jit(solution)/shard_map/ppermute | solution.py:713
  311.8 21.0 %collective-permute-start.24 = (bf16[560,700]{1,0:T(8,128)(2,1)S(1)}, bf16[560,700]{1,0:T(8,128)(2,1)}, u32[]{:S(2)}, u32[]{:S(2)}) collective-permute-start(bf16[560,700]{1,0:T(8,128)(2,1)S(1)} %copy-done.27), channel_id=1, source_target_pairs={{0,16},{16,24},{24,8},{8,0},{1,17},{17,25},{25,9},{9,1},{2,18},{18... | collective-permute-start | bytes 2352008 | tf_op jit(solution)/shard_map/ppermute | solution.py:733
  344.6 20.9 %collective-permute-start.26 = (bf16[560,700]{1,0:T(8,128)(2,1)}, bf16[560,700]{1,0:T(8,128)(2,1)S(1)}, u32[]{:S(2)}, u32[]{:S(2)}) collective-permute-start(bf16[560,700]{1,0:T(8,128)(2,1)} %collective-permute-done.24.refs_2_), channel_id=1, source_target_pairs={{0,16},{16,24},{24,8},{8,0},{1,17},{17,25},{25,9},{9,1},{2,18},{18... | collective-permute-start | bytes 2352008 | tf_op jit(solution)/shard_map/ppermute | solution.py:733
  346.1 20.6 %collective-permute-start.27 = (bf16[560,700]{1,0:T(8,128)(2,1)}, bf16[560,700]{1,0:T(8,128)(2,1)S(1)}, u32[]{:S(2)}, u32[]{:S(2)}) collective-permute-start(bf16[560,700]{1,0:T(8,128)(2,1)} %collective-permute-done.24.refs_2_), channel_id=1, source_target_pairs={{0,4},{4,0},{1,5},{5,1},{2,6},{6,2},{3,7},{7,3},{8,12},{12,8},{9,1... | collective-permute-start | bytes 2352008 | tf_op jit(solution)/shard_map/ppermute | solution.py:713
  366.8 21.6 %collective-permute-start.29 = (bf16[560,700]{1,0:T(8,128)(2,1)S(1)}, bf16[560,700]{1,0:T(8,128)(2,1)}, u32[]{:S(2)}, u32[]{:S(2)}) collective-permute-start(bf16[560,700]{1,0:T(8,128)(2,1)S(1)} %collective-permute-done.26.refs_3_), channel_id=1, source_target_pairs={{0,16},{16,24},{24,8},{8,0},{1,17},{17,25},{25,9},{9,1},{2,18},{18... | collective-permute-start | bytes 2352008 | tf_op jit(solution)/shard_map/ppermute | solution.py:733
  368.2 21.4 %collective-permute-start.30 = (bf16[560,700]{1,0:T(8,128)(2,1)S(1)}, bf16[560,700]{1,0:T(8,128)(2,1)}, u32[]{:S(2)}, u32[]{:S(2)}) collective-permute-start(bf16[560,700]{1,0:T(8,128)(2,1)S(1)} %collective-permute-done.26.refs_3_), channel_id=1, source_target_pairs={{0,4},{4,0},{1,5},{5,1},{2,6},{6,2},{3,7},{7,3},{8,12},{12,8},{9,1... | collective-permute-start | bytes 2352008 | tf_op jit(solution)/shard_map/ppermute | solution.py:713
  389.6 24.9 %collective-permute-start.33 = (bf16[560,700]{1,0:T(8,128)(2,1)}, bf16[560,700]{1,0:T(8,128)(2,1)S(1)}, u32[]{:S(2)}, u32[]{:S(2)}) collective-permute-start(bf16[560,700]{1,0:T(8,128)(2,1)} %collective-permute-done.29.refs_4_), channel_id=1, source_target_pairs={{0,4},{4,0},{1,5},{5,1},{2,6},{6,2},{3,7},{7,3},{8,12},{12,8},{9,1... | collective-permute-start | bytes 2352008 | tf_op jit(solution)/shard_map/ppermute | solution.py:713
  450.8 27.5 %collective-permute-start.36 = (bf16[256,2304]{1,0:T(8,128)(2,1)S(1)}, bf16[256,2304]{1,0:T(8,128)(2,1)S(1)}, u32[]{:S(2)}, u32[]{:S(2)}) collective-permute-start(bf16[256,2304]{1,0:T(8,128)(2,1)S(1)} %add_convert_fusion.3.refs_0_), channel_id=1, source_target_pairs={{0,2},{1,3},{2,0},{3,1},{4,6},{5,7},{6,4},{7,5},{8,10},{9,11},{10,... | collective-permute-start | bytes 3538952 | tf_op jit(solution)/shard_map/ppermute | solution.py:713
  482.9 28.2 %collective-permute-start.38 = (bf16[256,2304]{1,0:T(8,128)(2,1)S(1)}, bf16[256,2304]{1,0:T(8,128)(2,1)}, u32[]{:S(2)}, u32[]{:S(2)}) collective-permute-start(bf16[256,2304]{1,0:T(8,128)(2,1)S(1)} %add_convert_fusion.2.refs_0_), channel_id=1, source_target_pairs={{0,2},{1,3},{2,0},{3,1},{4,6},{5,7},{6,4},{7,5},{8,10},{9,11},{10,... | collective-permute-start | bytes 3538952 | tf_op jit(solution)/shard_map/ppermute | solution.py:713
  520.2 33.8 %collective-permute-start.40 = (f32[256,2304]{1,0:T(8,128)S(1)}, f32[256,2304]{1,0:T(8,128)}, u32[]{:S(2)}, u32[]{:S(2)}) collective-permute-start(f32[256,2304]{1,0:T(8,128)S(1)} %copy-done.14), channel_id=1, source_target_pairs={{0,1},{1,0},{2,3},{3,2},{4,5},{5,4},{6,7},{7,6},{8,9},{9,8},{10,11... | collective-permute-start | bytes 7077896 | tf_op jit(solution)/shard_map/ppermute | solution.py:713
  522.5 31.5 %all-to-all-start = ((f32[4,4,6656]{2,1,0:T(4,128)}), f32[4,4,6656]{2,1,0:T(4,128)}, u32[]{:S(2)}, u32[]{:S(2)}) async-start(f32[4,4,6656]{2,1,0:T(4,128)} %reshape.121), calls=%async_computation | async-start | bytes 851968 | tf_op jit(solution)/shard_map/all_to_all | solution.py:1172
  558.8 30.9 %collective-permute-start.42 = (bf16[256,2304]{1,0:T(8,128)(2,1)S(1)}, bf16[256,2304]{1,0:T(8,128)(2,1)}, u32[]{:S(2)}, u32[]{:S(2)}) collective-permute-start(bf16[256,2304]{1,0:T(8,128)(2,1)S(1)} %add_convert_fusion.1.refs_0_), channel_id=1, source_target_pairs={{0,2},{1,3},{2,0},{3,1},{4,6},{5,7},{6,4},{7,5},{8,10},{9,11},{10,... | collective-permute-start | bytes 3538952 | tf_op jit(solution)/shard_map/ppermute | solution.py:713
  634.2 32.5 %collective-permute-start.47 = (bf16[256,2304]{1,0:T(8,128)(2,1)S(1)}, bf16[256,2304]{1,0:T(8,128)(2,1)S(1)}, u32[]{:S(2)}, u32[]{:S(2)}) collective-permute-start(bf16[256,2304]{1,0:T(8,128)(2,1)S(1)} %add_convert_fusion.refs_0_), channel_id=1, source_target_pairs={{0,2},{1,3},{2,0},{3,1},{4,6},{5,7},{6,4},{7,5},{8,10},{9,11},{10,... | collective-permute-start | bytes 3538952 | tf_op jit(solution)/shard_map/ppermute | solution.py:713
  (80 other events, 915.6 us)

commit v4 on v3

--- a/solution.py
+++ b/solution.py
@@ -581,13 +581,22 @@
         put(out.at[:, i * width : (i + 1) * width], everything, v)
 
 
+def set_ranks(out, first, pad, values):
+    rows = out.shape[1]
+    for t in range(out.shape[0]):
+        put(out.at[t, :, first : first + pad], everything, values[t * rows : (t + 1) * rows])
+
+
 def pack_first(where, point, up, l0, l1, l2, l3, sums):
     pieces = [point[0], point[1]] + [up[h, p] for p in range(2) for h in range(2)]
     n = l0.shape[0]
-    first = sums.shape[1] - 4 * n
-    set_segments(sums, [fold(v) for v in pieces], first // 6)
+    rank = sums.shape[0] * sums.shape[1]
+    first = sums.shape[2] - 4 * n
+    pad = first // 6
+    for i, v in enumerate(pieces):
+        set_ranks(sums, i * pad, pad, fold(v))
     for i, v in enumerate((l0, l1, l2, l3)):
-        sums[:, first + i * n : first + (i + 1) * n] = turned(v[...].T[: sums.shape[0]], where[0])
+        set_ranks(sums, first + i * n, n, turned(v[...].T[:rank], where[0]))
 
 
 def to_blocks(home, first, table):
@@ -642,12 +651,13 @@
 
 
 def third_sums(where, before, pgl, mixed, qlat, gq, gk, gv, qgl, out):
-    first = before.shape[1]
-    out[:, :first] = before[...]
+    rank, first = before.shape
+    set_ranks(out, 0, first, before[...])
     segments = [outer_sum(pgl[...], mixed)] + [outer_sum(qlat[...], g) for g in (gq, gk, gv)]
     pad = -(-gq.shape[1] // LANES) * LANES
-    set_segments(out.at[:, first : first + 4 * pad], segments, pad)
-    out[:, first + 4 * pad :] = turned(qgl[...].T[: out.shape[0]], where[0])
+    for i, v in enumerate(segments):
+        set_ranks(out, first + i * pad, pad, v)
+    set_ranks(out, first + 4 * pad, qgl.shape[0], turned(qgl[...].T[:rank], where[0]))
 
 
 def last_sums(ranges, where, sums, projs, gao, gat, xo, xt, cap, a, home_out, home):
@@ -721,9 +731,9 @@
         self.flying, self.crossing = [], []
 
     def launch(self):
-        while not self.flying and self.order:
+        while self.order and (not self.flying or len(self.flying) < 2 and self.order[0][1] == 1):
             name, step = self.order[0]
-            if step == 1:
+            if step == 1 and name in self.own:
                 moving = self.own[name][0]
             elif (name, step - 1) in self.got:
                 moving = self.got[name, step - 1]
@@ -732,9 +742,10 @@
             self.order.pop(0)
             self.flying.append((name, step, lax.ppermute(moving, W, ring_pairs(self.n))))
 
-    def fence(self, values):
-        done = [self.flying.pop(0)] if self.flying else []
-        crossed, self.crossing = self.crossing, []
+    def fence(self, values, take=1, cross=None):
+        done, self.flying = self.flying[:take], self.flying[take:]
+        count = len(self.crossing) if cross is None else cross
+        crossed, self.crossing = self.crossing[:count], self.crossing[count:]
         leaves, tree = jax.tree.flatten((values, [d[2] for d in done], [d[2] for d in crossed]))
         values, arrived, over = jax.tree.unflatten(tree, lax.optimization_barrier(leaves))
         for d, v in zip(crossed, over):
@@ -1010,10 +1021,10 @@
     cu2 = twice(pick(cross_up), 0)
     xd2, xu2 = twice(pick(query_down), 1), twice(cut(pick(query_up), col, width, 1), 0)
     kd2, ku2 = twice(pick(kv_down), 1), twice(cut(pick(kv_up), col, width, 2), 0).transpose(1, 0, 2)
-    front = [x_low, x_rows, qd2, qu2, pd2, pu2]
+    front = [x_low, x_rows, qd2, qu2, pd2, pu2, stream.own["ab"][1]]
     pair_cd, raw_f, tables_f, cotangent, front = fences(1, (pair_cd, raw_f, tables_f, cotangent, front))
     stream.own["cd"] = pair_cd
-    x_low, x_rows, qd2, qu2, pd2, pu2 = front
+    x_low, x_rows, qd2, qu2, pd2, pu2, stream.own["ab"][1] = front
     pair_vg = [both(raw_f[0], i * hh, hh) for i in (c, 1 - c)]
     pair_p = [cut(raw_f[1], i * hh, hh, 0).T for i in (c, 1 - c)]
     pair_vg, pair_p, tables_f, cotangent = fences(1, (pair_vg, pair_p, tables_f, cotangent))
@@ -1069,10 +1080,10 @@
             low = (low.astype(f32) + got.astype(f32)).astype(bf16)
 
     def while_streaming(mine, away):
-        return fences(1, exchanged(mine, away))
+        return exchanged(mine, away)
 
     mine, away = fences(1, (mine, away))
-    low, got = while_streaming(mine, away)
+    low, got = fences(1, while_streaming(mine, away))
     after_attn, cross_own = finish_rows(end_attn, [low, got, x_low], ended)
     cross_other = across(cross_own, T)
 
@@ -1100,8 +1111,9 @@
     mine, away = fences(1, (mine, away))
     query, mix, query_lat, cross_lat, lse = zip(cross_o, cross_t)
     low, got = while_streaming(mine, away)
+    low, got = stream.fence((stream.fence(low, 1, 0), got), 0, 1)
     after_cross, ffn_own = finish_rows(end_cross, [low, got, after_attn], ended)
-    ffn_own, after_cross = fences(1, (ffn_own, after_cross))
+    ffn_own, after_cross = stream.fence((ffn_own, after_cross), 1, 1)
     ffn_other = across(ffn_own, T)
 
     query_lat, cross_lat = jnp.concatenate(query_lat), jnp.concatenate(cross_lat)
@@ -1121,7 +1133,7 @@
         )
 
     *started, inv_lat = ffn_part(0, [], ())
-    ffn_own, started, inv_lat = fences(1, (ffn_own, started, inv_lat))
+    ffn_own, started, inv_lat = stream.fence((ffn_own, started, inv_lat), 1, 1)
     pre_v, pre_g, hid_v, hid_g, edge_v, edge_g = ffn_part(
         1, [inv_lat] + [(v, anywhere) for v in started], [(7 + i, i) for i in range(6)]
     )
@@ -1169,7 +1181,7 @@
     ranges = slot_ranges(groups, heads)
 
     def swapped(sent):
-        return lax.all_to_all(sent.reshape(groups, part_r, sent.shape[1]), T, 0, 0, tiled=True)
+        return lax.all_to_all(sent, T, 0, 0, tiled=True)
 
     def up_to_tiles(size):
         return -(-size // LANES) * LANES
@@ -1197,7 +1209,7 @@
     def first_work(out_low, out_got, after_cross, inv_up_g, point_down_g, lats):
         (output,) = finish_rows(end_output, [out_low, out_got, after_cross], [((half, padded), f32, row_block)])
         (sums,) = run(
-            pack_first, [(where, scalars), point_down_g, inv_up_g, *lats], [((R, 6 * up_to_tiles(hh) + 4 * n), f32)],
+            pack_first, [(where, scalars), point_down_g, inv_up_g, *lats], [((groups, part_r, 6 * up_to_tiles(hh) + 4 * n), f32)],
         )
         return output, sums
 
@@ -1275,7 +1287,7 @@
         home = lax.all_to_all(home, (W, C), 0, 0, tiled=True)
         (sums,) = run(
             third_sums, [(where, scalars), sums_c, proj_gl, mixed, qkv_lat, grad_q, grad_k, grad_v, qkv_gl],
-            [((R, sums_c.shape[1] + 4 * seg + n), f32)],
+            [((groups, part_r, sums_c.shape[1] + 4 * seg + n), f32)],
         )
         return swapped(sums), run(adapter_tables, [home], [((adapters,) + home.shape[1:], f32)])[0]
 

time: 711 us -> 704 us (level)
    ppermute x12, waiting for transfers between devices: 152 us -> 140 us  [launch(): lax.ppermute(moving, W, ring_pairs(self.n))]
    ppermute x37, waiting for transfers between devices: 103 us -> 113 us  [across(): return lax.ppermute(values, axis, swap_pairs(lax.axis_size(axis), distance))]
  transfers between devices with their start and end apart: 53 -> 53, of which waited for: 39 -> 38; matrix products, arithmetic and copies ran while one was open for 11% -> 10% of each run, Pallas kernels for 26% -> 26%
where the time goes in v4:
time: 704 us; the launch traced here: 695 us
  waiting for transfers between devices  275 us (39%)
  Pallas kernels  256 us (36%)
  local copies, waits for them, and re-layouts  67.3 us (10%)
  starting transfers between devices  60.3 us (9%)
  other arithmetic  33.5 us (5%)
    pallas_call x27, Pallas kernels, run(): pl.pallas_call(body, grid=(steps,), in_specs=specs, out_specs=out_specs,...  256 us
    ppermute x12, waiting for transfers between devices, launch(): lax.ppermute(moving, W, ring_pairs(self.n))  140 us
    ppermute x37, waiting for transfers between devices, across(): return lax.ppermute(values, axis, swap_pairs(lax.axis_size(axis), distance))  113 us
    ppermute x12, starting transfers between devices, launch(): lax.ppermute(moving, W, ring_pairs(self.n))  23 us
    ppermute x37, starting transfers between devices, across(): return lax.ppermute(values, axis, swap_pairs(lax.axis_size(axis), distance))  22.4 us
    unnamed x120, local copies, waits for them, and re-layouts  14.2 us
  transfers between devices with their start and end apart: 53, of which 38 were waited for; matrix products, arithmetic and copies ran while one was open for 10% of the time, Pallas kernels for 26%

profile of v4, /device:TPU:0, one launch (start us, length us, event | category | flops | bytes accessed | tf_op | source)
XLA Modules:
  0.0 694.9 jit_solution(10056487933133913072)
XLA Ops:
  34.2 8.7 %collective-permute-done.1.refs_2_ = bf16[560,1152]{1,0:T(8,128)(2,1)} collective-permute-done((bf16[560,1152]{1,0:T(8,128)(2,1)}, bf16[560,1152]{1,0:T(8,128)(2,1)}, u32[]{:S(2)}, u32[]{:S(2)}) %collective-permute-start.1) | collective-permute-done | bytes 1290272 | tf_op jit(solution)/shard_map/ppermute | solution.py:743
  62.6 10.8 %collective-permute-done.2.refs_3_ = bf16[560,1152]{1,0:T(8,128)(2,1)S(1)} collective-permute-done((bf16[560,1152]{1,0:T(8,128)(2,1)}, bf16[560,1152]{1,0:T(8,128)(2,1)S(1)}, u32[]{:S(2)}, u32[]{:S(2)}) %collective-permute-start.2) | collective-permute-done | bytes 1290272 | tf_op jit(solution)/shard_map/ppermute | solution.py:743
  87.9 18.9 %collective-permute-done.4.refs_4_ = bf16[560,1152]{1,0:T(8,128)(2,1)} collective-permute-done((bf16[560,1152]{1,0:T(8,128)(2,1)S(1)}, bf16[560,1152]{1,0:T(8,128)(2,1)}, u32[]{:S(2)}, u32[]{:S(2)}) %collective-permute-start.4) | collective-permute-done | bytes 1290272 | tf_op jit(solution)/shard_map/ppermute | solution.py:743
  118.6 12.7 %collective-permute-done.6.refs_2_ = bf16[560,1152]{1,0:T(8,128)(2,1)} collective-permute-done((bf16[560,1152]{1,0:T(8,128)(2,1)}, bf16[560,1152]{1,0:T(8,128)(2,1)}, u32[]{:S(2)}, u32[]{:S(2)}) %collective-permute-start.6) | collective-permute-done | bytes 1290272 | tf_op jit(solution)/shard_map/ppermute | solution.py:743
  139.7 12.1 %shard_map.387 = (bf16[512,2240]{1,0:T(8,128)(2,1)}, f32[512,576]{1,0:T(8,128)}, f32[512,576]{1,0:T(8,128)}, f32[512,32]{1,0:T(8,128)}) custom-call(s32[5]{0:T(128)} %stack.60.refs_0_, bf16[560,1152]{1,0:T(8,128)(2,1)} %broadcast_select_fusion.3.refs_1_, bf16[560,1152]{1,0:T(8,128)(2,1)} %collective-permute-done.1.refs_2_, bf16[560,1152]{1,0:T(8,128)(2,1)} %copy-done.2, ...), custom_call_target="tpu_custom_call" | custom-call | tf_op jit(solution)/shard_map/pallas_call | solution.py:904
  151.8 8.4 %shard_map.388 = (f32[512,576]{1,0:T(8,128)}, f32[40,576]{1,0:T(8,128)}) custom-call(s32[5]{0:T(128)} %stack.60.refs_0_, bf16[560,1152]{1,0:T(8,128)(2,1)} %broadcast_select_fusion.3.refs_1_, bf16[560,1152]{1,0:T(8,128)(2,1)} %collective-permute-done.1.refs_2_, bf16[560,1152]{1,0:T(8,128)(2,1)} %copy-done.2, ...), custom_call_target="tpu_custom_call" | custom-call | tf_op jit(solution)/shard_map/pallas_call | solution.py:904
  170.5 8.5 %shard_map.389 = (f32[512,576]{1,0:T(8,128)}, f32[512,576]{1,0:T(8,128)}, bf16[512,576]{1,0:T(8,128)(2,1)}, f32[512,32]{1,0:T(8,128)}, bf16[256,2304]{1,0:T(8,128)(2,1)}, /*index=5*/bf16[256,2304]{1,0:T(8,128)(2,1)}) custom-call(s32[5]{0:T(128)} %stack.60.refs_0_, bf16[560,1152]{1,0:T(8,128)(2,1)} %broadcast_select_fusion.3.refs_1_, ...), custom_call_target="tpu_custom_call" | custom-call | tf_op jit(solution)/shard_map/pallas_call | solution.py:904
  179.0 12.1 %collective-permute-done.11.refs_4_ = bf16[560,1152]{1,0:T(8,128)(2,1)} collective-permute-done((bf16[560,1152]{1,0:T(8,128)(2,1)}, bf16[560,1152]{1,0:T(8,128)(2,1)}, u32[]{:S(2)}, u32[]{:S(2)}) %collective-permute-start.11) | collective-permute-done | bytes 1290272 | tf_op jit(solution)/shard_map/ppermute | solution.py:743
  197.6 31.6 %collective-permute-done.15.refs_2_ = bf16[560,1400]{1,0:T(8,128)(2,1)} collective-permute-done((bf16[560,1400]{1,0:T(8,128)(2,1)S(1)}, bf16[560,1400]{1,0:T(8,128)(2,1)}, u32[]{:S(2)}, u32[]{:S(2)}) %collective-permute-start.15) | collective-permute-done | bytes 1568032 | tf_op jit(solution)/shard_map/ppermute | solution.py:743
  238.0 7.8 %shard_map.390 = (bf16[2,320,576]{2,1,0:T(8,128)(2,1)}, f32[160,32]{1,0:T(8,128)}) custom-call(s32[5]{0:T(128)} %stack.60.refs_0_, bf16[560,1152]{1,0:T(8,128)(2,1)} %get-tuple-element.284.refs_1_, bf16[560,1152]{1,0:T(8,128)(2,1)} %collective-permute-done.6.refs_2_, bf16[560,1152]{1,0:T(8,128)(2,1)} %collective-permute-done.9.refs_3_, ...), custom_call_target="tpu_custom_call" | custom-call | tf_op jit(solution)/shard_map/pallas_call | solution.py:904
  245.8 20.6 %collective-permute-done.18.refs_3_ = bf16[560,1400]{1,0:T(8,128)(2,1)S(1)} collective-permute-done((bf16[560,1400]{1,0:T(8,128)(2,1)}, bf16[560,1400]{1,0:T(8,128)(2,1)S(1)}, u32[]{:S(2)}, u32[]{:S(2)}) %collective-permute-start.18) | collective-permute-done | bytes 1568032 | tf_op jit(solution)/shard_map/ppermute | solution.py:743
  272.4 13.7 %shard_map.392 = (bf16[256,576]{1,0:T(8,128)(2,1)}, bf16[256,576]{1,0:T(8,128)(2,1)}, f32[256,32]{1,0:T(8,128)}, f32[256,32]{1,0:T(8,128)}, f32[128,256]{1,0:T(8,128)}, /*index=5*/bf16[256,2304]{1,0:T(8,128)(2,1)}) custom-call(s32[5]{0:T(128)} %stack.60.refs_0_, bf16[560,1152]{1,0:T(8,128)(2,1)} %get-tuple-element.284.refs_1_, ...), custom_call_target="tpu_custom_call" | custom-call | tf_op jit(solution)/shard_map/pallas_call | solution.py:904
  286.1 14.3 %shard_map.393 = (bf16[256,576]{1,0:T(8,128)(2,1)}, bf16[256,576]{1,0:T(8,128)(2,1)}, f32[256,32]{1,0:T(8,128)}, f32[256,32]{1,0:T(8,128)}, f32[128,256]{1,0:T(8,128)}, /*index=5*/bf16[256,2304]{1,0:T(8,128)(2,1)}) custom-call(s32[5]{0:T(128)} %stack.60.refs_0_, bf16[560,1152]{1,0:T(8,128)(2,1)} %get-tuple-element.284.refs_1_, ...), custom_call_target="tpu_custom_call" | custom-call | tf_op jit(solution)/shard_map/pallas_call | solution.py:904
  309.5 16.5 %collective-permute-done.23.refs_2_ = bf16[560,700]{1,0:T(8,128)(2,1)} collective-permute-done((bf16[560,700]{1,0:T(8,128)(2,1)S(1)}, bf16[560,700]{1,0:T(8,128)(2,1)}, u32[]{:S(2)}, u32[]{:S(2)}) %collective-permute-start.23) | collective-permute-done | bytes 784032 | tf_op jit(solution)/shard_map/ppermute | solution.py:743
  328.9 14.3 %collective-permute-done.25.refs_8_ = bf16[560,1400]{1,0:T(8,128)(2,1)S(1)} collective-permute-done((bf16[560,1400]{1,0:T(8,128)(2,1)S(1)}, bf16[560,1400]{1,0:T(8,128)(2,1)S(1)}, u32[]{:S(2)}, u32[]{:S(2)}) %collective-permute-start.25) | collective-permute-done | bytes 1568032 | tf_op jit(solution)/shard_map/ppermute | solution.py:723
  349.4 11.5 %collective-permute-done.27.refs_6_ = bf16[560,700]{1,0:T(8,128)(2,1)S(1)} collective-permute-done((bf16[560,700]{1,0:T(8,128)(2,1)}, bf16[560,700]{1,0:T(8,128)(2,1)S(1)}, u32[]{:S(2)}, u32[]{:S(2)}) %collective-permute-start.27) | collective-permute-done | bytes 784032 | tf_op jit(solution)/shard_map/ppermute | solution.py:723
  366.5 11.7 %shard_map.395 = (f32[2,512,700]{2,1,0:T(8,128)}, f32[2,512,700]{2,1,0:T(8,128)}, bf16[2,512,700]{2,1,0:T(8,128)(2,1)}, bf16[2,512,700]{2,1,0:T(8,128)(2,1)}, bf...) custom-call(s32[5]{0:T(128)} %stack.60.refs_0_, ...), custom_call_target="tpu_custom_call" | custom-call | tf_op jit(solution)/shard_map/pallas_call | solution.py:904
  385.3 12.1 %shard_map.396 = (f32[2,512,700]{2,1,0:T(8,128)}, f32[2,512,700]{2,1,0:T(8,128)}, bf16[2,512,700]{2,1,0:T(8,128)(2,1)}, bf16[2,512,700]{2,1,0:T(8,128)(2,1)}, bf...) custom-call(s32[5]{0:T(128)} %stack.60.refs_0_, ...), custom_call_target="tpu_custom_call", output_to_operand_aliasing={{0}: (16, {}), {1}: (17, {}), {2}: (18, {}), {3}: (19, {}),... | custom-call | tf_op jit(solution)/shard_map/pallas_call | solution.py:904
  401.8 6.6 collective-permute-done.31.refs_12_
  410.4 27.7 %shard_map.397 = (bf16[2,512,700]{2,1,0:T(8,128)(2,1)}, bf16[2,512,700]{2,1,0:T(8,128)(2,1)}, bf16[2,512,700]{2,1,0:T(8,128)(2,1)}, bf16[512,2240]{1,0:T(8,128)(...) custom-call(s32[5]{0:T(128)} %stack.60.refs_0_, ...), custom_call_target="tpu_custom_call" | custom-call | tf_op jit(solution)/shard_map/pallas_call | solution.py:904
  446.5 24.1 %shard_map.398 = (bf16[2,512,700]{2,1,0:T(8,128)(2,1)}, bf16[2,512,700]{2,1,0:T(8,128)(2,1)}, f32[2,2,32,700]{3,2,1,0:T(8,128)}, f32[512,32]{1,0:T(8,128)}, bf16...) custom-call(s32[5]{0:T(128)} %stack.60.refs_0_, bf16[560,1400]{1,0:T(8,128)(2,1)} %get-tuple-element.334.refs_1_, ...), custom_call_target="tpu_custom_call" | custom-call | tf_op jit(solution)/shard_map/pallas_call | solution.py:904
  487.4 18.7 %collective-permute-done.38.refs_1_ = bf16[256,2304]{1,0:T(8,128)(2,1)} collective-permute-done((bf16[256,2304]{1,0:T(8,128)(2,1)S(1)}, bf16[256,2304]{1,0:T(8,128)(2,1)}, u32[]{:S(2)}, u32[]{:S(2)}) %collective-permute-start.38) | collective-permute-done | bytes 1179680 | tf_op jit(solution)/shard_map/ppermute | solution.py:723
  506.1 5.9 shard_map.401
  520.4 26.3 %shard_map.402 = (bf16[512,576]{1,0:T(8,128)(2,1)}, f32[2,320,576]{2,1,0:T(8,128)}, f32[512,32]{1,0:T(8,128)}, f32[512,32]{1,0:T(8,128)}, bf16[256,2304]{1,0:T(8,128)(2,1)}, /*index=5*/bf16[256,2304]{1,0:T(8,128)(2,1)}) custom-call(s32[5]{0:T(128)} %stack.60.refs_0_, bf16[560,1152]{1,0:T(8,128)(2,1)} %get-tuple-element.284.refs_1_, ...), custom_call_target="tpu_custom_call" | custom-call | tf_op jit(solution)/shard_map/pallas_call | solution.py:904
  561.0 13.7 %collective-permute-done.43.refs_14_ = f32[2,160,576]{2,1,0:T(8,128)S(1)} collective-permute-done((f32[2,160,576]{2,1,0:T(8,128)}, f32[2,160,576]{2,1,0:T(8,128)S(1)}, u32[]{:S(2)}, u32[]{:S(2)}) %collective-permute-start.43) | collective-permute-done | bytes 737312 | tf_op jit(solution)/shard_map/ppermute | solution.py:723
  575.6 6.8 shard_map.404
  591.5 11.0 %shard_map.406 = (bf16[512,576]{1,0:T(8,128)(2,1)}, f32[512,32]{1,0:T(8,128)}, f32[40,576]{1,0:T(8,128)}) custom-call(s32[5]{0:T(128)} %stack.60.refs_0_, bf16[560,1152]{1,0:T(8,128)(2,1)} %broadcast_select_fusion.3.refs_1_, bf16[560,1152]{1,0:T(8,128)(2,1)} %collective-permute-done.1.refs_2_, bf16[560,1152]{1,0:T(8,128)(2,1)} %copy-done.2, ...), custom_call_target="tpu_custom_call" | custom-call | tf_op jit(solution)/shard_map/pallas_call | solution.py:904
  608.4 13.9 %shard_map.407 = (bf16[512,576]{1,0:T(8,128)(2,1)}, bf16[512,576]{1,0:T(8,128)(2,1)}, f32[512,32]{1,0:T(8,128)}, bf16[256,2304]{1,0:T(8,128)(2,1)}, bf16[256,2304]{1,0:T(8,128)(2,1)}) custom-call(s32[5]{0:T(128)} %stack.60.refs_0_, bf16[560,1152]{1,0:T(8,128)(2,1)} %broadcast_select_fusion.3.refs_1_, bf16[560,1152]{1,0:T(8,128)(2,1)} %collective-permute-done.1.refs_2_, ...), custom_call_target="tpu_custom_call" | custom-call | tf_op jit(solution)/shard_map/pallas_call | solution.py:904
  634.3 8.6 %all-to-all-done.2.refs_0_ = bf16[8,32,700]{2,1,0:T(8,128)(2,1)S(1)} async-done(((bf16[8,32,700]{2,1,0:T(8,128)(2,1)}), bf16[8,32,700]{2,1,0:T(8,128)(2,1)S(1)}, u32[]{:S(2)}, u32[]{:S(2)}) %all-to-all-start.2) | async-done | bytes 358432 | tf_op jit(solution)/shard_map/all_to_all | solution.py:1287
  648.9 10.5 %all-to-all-done.1.refs_1_ = f32[4,4,6400]{2,1,0:T(4,128)S(1)} async-done(((f32[4,4,6400]{2,1,0:T(4,128)}), f32[4,4,6400]{2,1,0:T(4,128)S(1)}, u32[]{:S(2)}, u32[]{:S(2)}) %all-to-all-start.1) | async-done | bytes 409632 | tf_op jit(solution)/shard_map/all_to_all | solution.py:1184
  660.5 5.6 shard_map.411.refs_1_
  666.1 5.5 shard_map.410
  (313 shorter events, 260.8 us)
Async XLA Ops:
  11.0 31.9 %collective-permute-start.1 = (bf16[560,1152]{1,0:T(8,128)(2,1)}, bf16[560,1152]{1,0:T(8,128)(2,1)}, u32[]{:S(2)}, u32[]{:S(2)}) collective-permute-start(bf16[560,1152]{1,0:T(8,128)(2,1)} %broadcast_select_fusion.3.refs_1_), channel_id=1, source_target_pairs={{0,16},{16,24},{24,8},{8,0},{1,17},{17,25},{25,9},{9,1},{2,18},{18... | collective-permute-start | bytes 3870728 | tf_op jit(solution)/shard_map/ppermute | solution.py:743
  43.0 30.4 %collective-permute-start.2 = (bf16[560,1152]{1,0:T(8,128)(2,1)}, bf16[560,1152]{1,0:T(8,128)(2,1)S(1)}, u32[]{:S(2)}, u32[]{:S(2)}) collective-permute-start(bf16[560,1152]{1,0:T(8,128)(2,1)} %collective-permute-done.1.refs_2_), channel_id=1, source_target_pairs={{0,16},{16,24},{24,8},{8,0},{1,17},{17,25},{25,9},{9,1},{2,18},{18... | collective-permute-start | bytes 3870728 | tf_op jit(solution)/shard_map/ppermute | solution.py:743
  46.4 29.1 %collective-permute-start.3 = (bf16[560,1152]{1,0:T(8,128)(2,1)}, bf16[560,1152]{1,0:T(8,128)(2,1)S(1)}, u32[]{:S(2)}, u32[]{:S(2)}) collective-permute-start(bf16[560,1152]{1,0:T(8,128)(2,1)} %collective-permute-done.1.refs_2_), channel_id=1, source_target_pairs={{0,4},{4,0},{1,5},{5,1},{2,6},{6,2},{3,7},{7,3},{8,12},{12,8},{9,1... | collective-permute-start | bytes 3870728 | tf_op jit(solution)/shard_map/ppermute | solution.py:723
  75.5 31.4 %collective-permute-start.4 = (bf16[560,1152]{1,0:T(8,128)(2,1)S(1)}, bf16[560,1152]{1,0:T(8,128)(2,1)}, u32[]{:S(2)}, u32[]{:S(2)}) collective-permute-start(bf16[560,1152]{1,0:T(8,128)(2,1)S(1)} %collective-permute-done.2.refs_3_), channel_id=1, source_target_pairs={{0,16},{16,24},{24,8},{8,0},{1,17},{17,25},{25,9},{9,1},{2,18},{18... | collective-permute-start | bytes 3870728 | tf_op jit(solution)/shard_map/ppermute | solution.py:743
  76.7 30.2 %collective-permute-start.5 = (bf16[560,1152]{1,0:T(8,128)(2,1)S(1)}, bf16[560,1152]{1,0:T(8,128)(2,1)S(1)}, u32[]{:S(2)}, u32[]{:S(2)}) collective-permute-start(bf16[560,1152]{1,0:T(8,128)(2,1)S(1)} %collective-permute-done.2.refs_3_), channel_id=1, source_target_pairs={{0,4},{4,0},{1,5},{5,1},{2,6},{6,2},{3,7},{7,3},{8,12},{12,8},{9,1... | collective-permute-start | bytes 3870728 | tf_op jit(solution)/shard_map/ppermute | solution.py:723
  80.2 51.1 %collective-permute-start.6 = (bf16[560,1152]{1,0:T(8,128)(2,1)}, bf16[560,1152]{1,0:T(8,128)(2,1)}, u32[]{:S(2)}, u32[]{:S(2)}) collective-permute-start(bf16[560,1152]{1,0:T(8,128)(2,1)} %get-tuple-element.284.refs_1_), channel_id=1, source_target_pairs={{0,16},{16,24},{24,8},{8,0},{1,17},{17,25},{25,9},{9,1},{2,18},{18... | collective-permute-start | bytes 3870728 | tf_op jit(solution)/shard_map/ppermute | solution.py:743
  108.0 27.6 %collective-permute-start.7 = (bf16[560,1152]{1,0:T(8,128)(2,1)}, bf16[560,1152]{1,0:T(8,128)(2,1)}, u32[]{:S(2)}, u32[]{:S(2)}) collective-permute-start(bf16[560,1152]{1,0:T(8,128)(2,1)} %collective-permute-done.4.refs_4_), channel_id=1, source_target_pairs={{0,4},{4,0},{1,5},{5,1},{2,6},{6,2},{3,7},{7,3},{8,12},{12,8},{9,1... | collective-permute-start | bytes 3870728 | tf_op jit(solution)/shard_map/ppermute | solution.py:723
  135.6 30.6 %collective-permute-start.10 = (bf16[560,1152]{1,0:T(8,128)(2,1)}, bf16[560,1152]{1,0:T(8,128)(2,1)S(1)}, u32[]{:S(2)}, u32[]{:S(2)}) collective-permute-start(bf16[560,1152]{1,0:T(8,128)(2,1)} %collective-permute-done.6.refs_2_), channel_id=1, source_target_pairs={{0,4},{4,0},{1,5},{5,1},{2,6},{6,2},{3,7},{7,3},{8,12},{12,8},{9,1... | collective-permute-start | bytes 3870728 | tf_op jit(solution)/shard_map/ppermute | solution.py:723
  137.1 29.1 %collective-permute-start.9 = (bf16[560,1152]{1,0:T(8,128)(2,1)}, bf16[560,1152]{1,0:T(8,128)(2,1)}, u32[]{:S(2)}, u32[]{:S(2)}) collective-permute-start(bf16[560,1152]{1,0:T(8,128)(2,1)} %collective-permute-done.6.refs_2_), channel_id=1, source_target_pairs={{0,16},{16,24},{24,8},{8,0},{1,17},{17,25},{25,9},{9,1},{2,18},{18... | collective-permute-start | bytes 3870728 | tf_op jit(solution)/shard_map/ppermute | solution.py:743
  166.2 24.8 %collective-permute-start.11 = (bf16[560,1152]{1,0:T(8,128)(2,1)}, bf16[560,1152]{1,0:T(8,128)(2,1)}, u32[]{:S(2)}, u32[]{:S(2)}) collective-permute-start(bf16[560,1152]{1,0:T(8,128)(2,1)} %collective-permute-done.9.refs_3_), channel_id=1, source_target_pairs={{0,16},{16,24},{24,8},{8,0},{1,17},{17,25},{25,9},{9,1},{2,18},{18... | collective-permute-start | bytes 3870728 | tf_op jit(solution)/shard_map/ppermute | solution.py:743
  168.4 23.8 %collective-permute-start.12 = (bf16[560,1152]{1,0:T(8,128)(2,1)}, bf16[560,1152]{1,0:T(8,128)(2,1)}, u32[]{:S(2)}, u32[]{:S(2)}) collective-permute-start(bf16[560,1152]{1,0:T(8,128)(2,1)} %collective-permute-done.9.refs_3_), channel_id=1, source_target_pairs={{0,4},{4,0},{1,5},{5,1},{2,6},{6,2},{3,7},{7,3},{8,12},{12,8},{9,1... | collective-permute-start | bytes 3870728 | tf_op jit(solution)/shard_map/ppermute | solution.py:723
  192.2 37.0 %collective-permute-start.15 = (bf16[560,1400]{1,0:T(8,128)(2,1)S(1)}, bf16[560,1400]{1,0:T(8,128)(2,1)}, u32[]{:S(2)}, u32[]{:S(2)}) collective-permute-start(bf16[560,1400]{1,0:T(8,128)(2,1)S(1)} %copy-done.5), channel_id=1, source_target_pairs={{0,16},{16,24},{24,8},{8,0},{1,17},{17,25},{25,9},{9,1},{2,18},{18... | collective-permute-start | bytes 4704008 | tf_op jit(solution)/shard_map/ppermute | solution.py:743
  193.8 35.4 %collective-permute-start.16 = (bf16[560,1152]{1,0:T(8,128)(2,1)}, bf16[560,1152]{1,0:T(8,128)(2,1)S(1)}, u32[]{:S(2)}, u32[]{:S(2)}) collective-permute-start(bf16[560,1152]{1,0:T(8,128)(2,1)} %collective-permute-done.11.refs_4_), channel_id=1, source_target_pairs={{0,4},{4,0},{1,5},{5,1},{2,6},{6,2},{3,7},{7,3},{8,12},{12,8},{9,1... | collective-permute-start | bytes 3870728 | tf_op jit(solution)/shard_map/ppermute | solution.py:723
  196.8 32.4 %collective-permute-start.14 = (bf16[256,2304]{1,0:T(8,128)(2,1)S(1)}, bf16[256,2304]{1,0:T(8,128)(2,1)S(1)}, u32[]{:S(2)}, u32[]{:S(2)}) collective-permute-start(bf16[256,2304]{1,0:T(8,128)(2,1)S(1)} %add_convert_fusion.5.refs_0_), channel_id=1, source_target_pairs={{0,2},{1,3},{2,0},{3,1},{4,6},{5,7},{6,4},{7,5},{8,10},{9,11},{10,... | collective-permute-start | bytes 3538952 | tf_op jit(solution)/shard_map/ppermute | solution.py:723
  229.3 37.2 %collective-permute-start.18 = (bf16[560,1400]{1,0:T(8,128)(2,1)}, bf16[560,1400]{1,0:T(8,128)(2,1)S(1)}, u32[]{:S(2)}, u32[]{:S(2)}) collective-permute-start(bf16[560,1400]{1,0:T(8,128)(2,1)} %collective-permute-done.15.refs_2_), channel_id=1, source_target_pairs={{0,16},{16,24},{24,8},{8,0},{1,17},{17,25},{25,9},{9,1},{2,18},{18... | collective-permute-start | bytes 4704008 | tf_op jit(solution)/shard_map/ppermute | solution.py:743
  231.8 36.1 %collective-permute-start.19 = (bf16[560,1400]{1,0:T(8,128)(2,1)}, bf16[560,1400]{1,0:T(8,128)(2,1)}, u32[]{:S(2)}, u32[]{:S(2)}) collective-permute-start(bf16[560,1400]{1,0:T(8,128)(2,1)} %collective-permute-done.15.refs_2_), channel_id=1, source_target_pairs={{0,4},{4,0},{1,5},{5,1},{2,6},{6,2},{3,7},{7,3},{8,12},{12,8},{9,1... | collective-permute-start | bytes 4704008 | tf_op jit(solution)/shard_map/ppermute | solution.py:723
  267.9 35.1 %collective-permute-start.20 = (bf16[560,1400]{1,0:T(8,128)(2,1)S(1)}, bf16[560,1400]{1,0:T(8,128)(2,1)S(1)}, u32[]{:S(2)}, u32[]{:S(2)}) collective-permute-start(bf16[560,1400]{1,0:T(8,128)(2,1)S(1)} %collective-permute-done.18.refs_3_), channel_id=1, source_target_pairs={{0,16},{16,24},{24,8},{8,0},{1,17},{17,25},{25,9},{9,1},{2,18},{18... | collective-permute-start | bytes 4704008 | tf_op jit(solution)/shard_map/ppermute | solution.py:743
  269.2 35.0 %collective-permute-start.21 = (bf16[560,1400]{1,0:T(8,128)(2,1)S(1)}, bf16[560,1400]{1,0:T(8,128)(2,1)}, u32[]{:S(2)}, u32[]{:S(2)}) collective-permute-start(bf16[560,1400]{1,0:T(8,128)(2,1)S(1)} %collective-permute-done.18.refs_3_), channel_id=1, source_target_pairs={{0,4},{4,0},{1,5},{5,1},{2,6},{6,2},{3,7},{7,3},{8,12},{12,8},{9,1... | collective-permute-start | bytes 4704008 | tf_op jit(solution)/shard_map/ppermute | solution.py:723
  304.3 21.6 %collective-permute-start.23 = (bf16[560,700]{1,0:T(8,128)(2,1)S(1)}, bf16[560,700]{1,0:T(8,128)(2,1)}, u32[]{:S(2)}, u32[]{:S(2)}) collective-permute-start(bf16[560,700]{1,0:T(8,128)(2,1)S(1)} %copy-done.25), channel_id=1, source_target_pairs={{0,16},{16,24},{24,8},{8,0},{1,17},{17,25},{25,9},{9,1},{2,18},{18... | collective-permute-start | bytes 2352008 | tf_op jit(solution)/shard_map/ppermute | solution.py:743
  305.9 37.3 %collective-permute-start.25 = (bf16[560,1400]{1,0:T(8,128)(2,1)S(1)}, bf16[560,1400]{1,0:T(8,128)(2,1)S(1)}, u32[]{:S(2)}, u32[]{:S(2)}) collective-permute-start(bf16[560,1400]{1,0:T(8,128)(2,1)S(1)} %collective-permute-done.20.refs_4_), channel_id=1, source_target_pairs={{0,4},{4,0},{1,5},{5,1},{2,6},{6,2},{3,7},{7,3},{8,12},{12,8},{9,1... | collective-permute-start | bytes 4704008 | tf_op jit(solution)/shard_map/ppermute | solution.py:723
  308.7 34.5 %collective-permute-start.24 = (bf16[256,2304]{1,0:T(8,128)(2,1)S(1)}, bf16[256,2304]{1,0:T(8,128)(2,1)S(1)}, u32[]{:S(2)}, u32[]{:S(2)}) collective-permute-start(bf16[256,2304]{1,0:T(8,128)(2,1)S(1)} %add_convert_fusion.4.refs_0_), channel_id=1, source_target_pairs={{0,2},{1,3},{2,0},{3,1},{4,6},{5,7},{6,4},{7,5},{8,10},{9,11},{10,... | collective-permute-start | bytes 3538952 | tf_op jit(solution)/shard_map/ppermute | solution.py:723
  325.9 23.5 %collective-permute-start.26 = (bf16[560,700]{1,0:T(8,128)(2,1)}, bf16[560,700]{1,0:T(8,128)(2,1)}, u32[]{:S(2)}, u32[]{:S(2)}) collective-permute-start(bf16[560,700]{1,0:T(8,128)(2,1)} %collective-permute-done.23.refs_2_), channel_id=1, source_target_pairs={{0,16},{16,24},{24,8},{8,0},{1,17},{17,25},{25,9},{9,1},{2,18},{18... | collective-permute-start | bytes 2352008 | tf_op jit(solution)/shard_map/ppermute | solution.py:743
  328.4 32.5 %collective-permute-start.27 = (bf16[560,700]{1,0:T(8,128)(2,1)}, bf16[560,700]{1,0:T(8,128)(2,1)S(1)}, u32[]{:S(2)}, u32[]{:S(2)}) collective-permute-start(bf16[560,700]{1,0:T(8,128)(2,1)} %collective-permute-done.23.refs_2_), channel_id=1, source_target_pairs={{0,4},{4,0},{1,5},{5,1},{2,6},{6,2},{3,7},{7,3},{8,12},{12,8},{9,1... | collective-permute-start | bytes 2352008 | tf_op jit(solution)/shard_map/ppermute | solution.py:723
  361.9 21.7 %collective-permute-start.29 = (bf16[560,700]{1,0:T(8,128)(2,1)}, bf16[560,700]{1,0:T(8,128)(2,1)S(1)}, u32[]{:S(2)}, u32[]{:S(2)}) collective-permute-start(bf16[560,700]{1,0:T(8,128)(2,1)} %collective-permute-done.26.refs_3_), channel_id=1, source_target_pairs={{0,16},{16,24},{24,8},{8,0},{1,17},{17,25},{25,9},{9,1},{2,18},{18... | collective-permute-start | bytes 2352008 | tf_op jit(solution)/shard_map/ppermute | solution.py:743
  363.3 21.5 %collective-permute-start.30 = (bf16[560,700]{1,0:T(8,128)(2,1)}, bf16[560,700]{1,0:T(8,128)(2,1)S(1)}, u32[]{:S(2)}, u32[]{:S(2)}) collective-permute-start(bf16[560,700]{1,0:T(8,128)(2,1)} %collective-permute-done.26.refs_3_), channel_id=1, source_target_pairs={{0,4},{4,0},{1,5},{5,1},{2,6},{6,2},{3,7},{7,3},{8,12},{12,8},{9,1... | collective-permute-start | bytes 2352008 | tf_op jit(solution)/shard_map/ppermute | solution.py:723
  384.8 24.7 %collective-permute-start.33 = (bf16[560,700]{1,0:T(8,128)(2,1)S(1)}, bf16[560,700]{1,0:T(8,128)(2,1)S(1)}, u32[]{:S(2)}, u32[]{:S(2)}) collective-permute-start(bf16[560,700]{1,0:T(8,128)(2,1)S(1)} %collective-permute-done.29.refs_4_), channel_id=1, source_target_pairs={{0,4},{4,0},{1,5},{5,1},{2,6},{6,2},{3,7},{7,3},{8,12},{12,8},{9,1... | collective-permute-start | bytes 2352008 | tf_op jit(solution)/shard_map/ppermute | solution.py:723
  445.8 27.5 %collective-permute-start.36 = (bf16[256,2304]{1,0:T(8,128)(2,1)S(1)}, bf16[256,2304]{1,0:T(8,128)(2,1)S(1)}, u32[]{:S(2)}, u32[]{:S(2)}) collective-permute-start(bf16[256,2304]{1,0:T(8,128)(2,1)S(1)} %add_convert_fusion.3.refs_0_), channel_id=1, source_target_pairs={{0,2},{1,3},{2,0},{3,1},{4,6},{5,7},{6,4},{7,5},{8,10},{9,11},{10,... | collective-permute-start | bytes 3538952 | tf_op jit(solution)/shard_map/ppermute | solution.py:723
  477.9 28.2 %collective-permute-start.38 = (bf16[256,2304]{1,0:T(8,128)(2,1)S(1)}, bf16[256,2304]{1,0:T(8,128)(2,1)}, u32[]{:S(2)}, u32[]{:S(2)}) collective-permute-start(bf16[256,2304]{1,0:T(8,128)(2,1)S(1)} %add_convert_fusion.2.refs_0_), channel_id=1, source_target_pairs={{0,2},{1,3},{2,0},{3,1},{4,6},{5,7},{6,4},{7,5},{8,10},{9,11},{10,... | collective-permute-start | bytes 3538952 | tf_op jit(solution)/shard_map/ppermute | solution.py:723
  515.1 31.6 %collective-permute-start.40 = (f32[256,2304]{1,0:T(8,128)S(1)}, f32[256,2304]{1,0:T(8,128)}, u32[]{:S(2)}, u32[]{:S(2)}) collective-permute-start(f32[256,2304]{1,0:T(8,128)S(1)} %copy-done.14), channel_id=1, source_target_pairs={{0,1},{1,0},{2,3},{3,2},{4,5},{5,4},{6,7},{7,6},{8,9},{9,8},{10,11... | collective-permute-start | bytes 7077896 | tf_op jit(solution)/shard_map/ppermute | solution.py:723
  515.2 31.5 %all-to-all-start = ((f32[4,4,6656]{2,1,0:T(4,128)}), f32[4,4,6656]{2,1,0:T(4,128)}, u32[]{:S(2)}, u32[]{:S(2)}) async-start(f32[4,4,6656]{2,1,0:T(4,128)} %shard_map.400), calls=%async_computation | async-start | bytes 851968 | tf_op jit(solution)/shard_map/all_to_all | solution.py:1184
  551.5 30.9 %collective-permute-start.42 = (bf16[256,2304]{1,0:T(8,128)(2,1)S(1)}, bf16[256,2304]{1,0:T(8,128)(2,1)}, u32[]{:S(2)}, u32[]{:S(2)}) collective-permute-start(bf16[256,2304]{1,0:T(8,128)(2,1)S(1)} %add_convert_fusion.1.refs_0_), channel_id=1, source_target_pairs={{0,2},{1,3},{2,0},{3,1},{4,6},{5,7},{6,4},{7,5},{8,10},{9,11},{10,... | collective-permute-start | bytes 3538952 | tf_op jit(solution)/shard_map/ppermute | solution.py:723
  626.9 32.5 %collective-permute-start.47 = (bf16[256,2304]{1,0:T(8,128)(2,1)S(1)}, bf16[256,2304]{1,0:T(8,128)(2,1)S(1)}, u32[]{:S(2)}, u32[]{:S(2)}) collective-permute-start(bf16[256,2304]{1,0:T(8,128)(2,1)S(1)} %add_convert_fusion.refs_0_), channel_id=1, source_target_pairs={{0,2},{1,3},{2,0},{3,1},{4,6},{5,7},{6,4},{7,5},{8,10},{9,11},{10,... | collective-permute-start | bytes 3538952 | tf_op jit(solution)/shard_map/ppermute | solution.py:723
  (79 other events, 881.3 us)

commit v5 on v4

--- a/solution.py
+++ b/solution.py
@@ -14,6 +14,7 @@
 norm_eps = 1e-06
 attention_epsilon = 1e-06
 masked_score = -1000000000.0
+LOG2E = 1.4426950408889634
 big = pltpu.CompilerParams(vmem_limit_bytes=58 * 1024 * 1024)
 
 
@@ -177,8 +178,8 @@
 
 
 def only_head(values, j):
-    lane = lax.broadcasted_iota(jnp.int32, values.shape, 1) // HD
-    return jnp.where(lane == j, values.astype(f32), 0.0).astype(values.dtype)
+    lane = lax.broadcasted_iota(jnp.int32, (1, values.shape[1]), 1) // HD
+    return values * (lane == j).astype(f32).astype(values.dtype)
 
 
 def cross_fwd(
@@ -378,6 +379,7 @@
     depth = cu2.shape[1]
     weight = w[0].columns(0, width, width)
     scale = HD ** (-0.5)
+    hidden_text = jnp.where(live[...] > 0.0, 0.0, masked_score)
     for i, (rows, query, lse) in enumerate(((go, qo, lo), (gt, qt, lt))):
         at = slice(i * half, (i + 1) * half)
         gl = mm(rows[:, :depth], cu2[...], 1, 1)
@@ -391,9 +393,8 @@
             for j in range(size // HD):
                 key, val = only_head(kv[0, :, cols], j), only_head(kv[1, :, cols], j)
                 h = first // HD + j
-                scores = mm(key, q_all, 1, 1) * scale
-                scores = jnp.where(live[...] > 0.0, scores, masked_score)
-                probs = jnp.exp(scores - lse[h : h + 1, :])
+                scores = mm(key, q_all, 1, 1) * (scale * LOG2E) + hidden_text
+                probs = jnp.exp2(scores - lse[h : h + 1, :] * LOG2E)
                 grad_p = mm(val, g_all, 1, 1)
                 grad_v = grad_v + mm(probs.astype(bf16), only_head(g_all, j))
                 inner = jnp.sum(probs * grad_p, axis=0, keepdims=True)
@@ -841,11 +842,11 @@
 
 
 def row_block(a):
-    return pl.BlockSpec((a.shape[0] // 4, a.shape[1]), lambda i: (i, 0))
+    return pl.BlockSpec((a.shape[0] // 2, a.shape[1]), lambda i: (i, 0))
 
 
 def both_blocks(a):
-    return pl.BlockSpec((2, a.shape[1] // 4, a.shape[2]), lambda i: (0, i, 0))
+    return pl.BlockSpec((2, a.shape[1] // 2, a.shape[2]), lambda i: (0, i, 0))
 
 
 def all_of(a):
@@ -992,11 +993,13 @@
     stream = Stream(order)
     fences = stream.fences
 
-    side_qk = both(qkv_weight, col)
-    side_vo = beside(taken(qkv_weight, 2, col, width), cut(proj_weight, col, width, 0).T)
-    stream.own["ab"] = [jnp.where(c == 0, side_qk, side_vo), None]
+    def front_side(c):
+        key, out = taken(qkv_weight, 1, col, width), cut(proj_weight, col, width, 0).T
+        return beside(taken(qkv_weight, 2 * c, col, width), jnp.where(c == 0, key, out))
+
+    stream.own["ab"] = [front_side(c), None]
     c_late, caption, stream.own["ab"][0] = lax.optimization_barrier((c, caption, stream.own["ab"][0]))
-    stream.own["ab"][1] = jnp.where(c_late == 0, side_vo, side_qk)
+    stream.own["ab"][1] = front_side(1 - c_late)
     stream.launch()
     mods = modulation[0]
     low_tokens = tokens.reshape(n, D)
@@ -1054,7 +1057,7 @@
     ended = [((half, D), f32, row_block), ((half, padded), bf16, row_block)]
 
     def finish_rows(kernel, arrays, outs):
-        return run(kernel, [(v, row_block) for v in arrays] + [mods], outs, steps=4)
+        return run(kernel, [(v, row_block) for v in arrays] + [mods], outs, steps=2)
 
     state_of = ((HD + 8, width), f32)
     attn_in, q_raw, k_raw, qkv_lat = run(
@@ -1241,7 +1244,7 @@
     def in_order(own, other):
         (rows,) = run(
             place_rows, [(where, scalars), (own, row_block), (other, row_block)],
-            [((2, half, D), f32, both_blocks)], steps=4,
+            [((2, half, D), f32, both_blocks)], steps=2,
         )
         return rows.reshape(tokens.shape)
 

time: 704 us -> 696 us (0.989)
  transfers between devices with their start and end apart: 53 -> 53, of which waited for: 38 -> 37; matrix products, arithmetic and copies ran while one was open for 10% -> 11% of each run, Pallas kernels for 26% -> 26%
where the time goes in v5:
time: 696 us; the launch traced here: 688 us
  waiting for transfers between devices  275 us (40%)
  Pallas kernels  249 us (36%)
  local copies, waits for them, and re-layouts  64.7 us (9%)
  starting transfers between devices  61.1 us (9%)
  other arithmetic  35 us (5%)
    pallas_call x27, Pallas kernels, run(): pl.pallas_call(body, grid=(steps,), in_specs=specs, out_specs=out_specs,...  249 us
    ppermute x12, waiting for transfers between devices, launch(): lax.ppermute(moving, W, ring_pairs(self.n))  137 us
    ppermute x37, waiting for transfers between devices, across(): return lax.ppermute(values, axis, swap_pairs(lax.axis_size(axis), distance))  113 us
    ppermute x37, starting transfers between devices, across(): return lax.ppermute(values, axis, swap_pairs(lax.axis_size(axis), distance))  23.1 us
    ppermute x12, starting transfers between devices, launch(): lax.ppermute(moving, W, ring_pairs(self.n))  23.1 us
    unnamed x120, local copies, waits for them, and re-layouts  14.2 us
  transfers between devices with their start and end apart: 53, of which 37 were waited for; matrix products, arithmetic and copies ran while one was open for 11% of the time, Pallas kernels for 26%

profile of v5, /device:TPU:0, one launch (start us, length us, event | category | flops | bytes accessed | tf_op | source)
XLA Modules:
  0.0 687.7 jit_solution(2362674062427411010)
XLA Ops:
  31.9 5.9 collective-permute-done.1.refs_2_
  57.4 10.7 %collective-permute-done.2.refs_3_ = bf16[560,1152]{1,0:T(8,128)(2,1)S(1)} collective-permute-done((bf16[560,1152]{1,0:T(8,128)(2,1)}, bf16[560,1152]{1,0:T(8,128)(2,1)S(1)}, u32[]{:S(2)}, u32[]{:S(2)}) %collective-permute-start.2) | collective-permute-done | bytes 1290272 | tf_op jit(solution)/shard_map/ppermute | solution.py:744
  82.8 18.9 %collective-permute-done.4.refs_4_ = bf16[560,1152]{1,0:T(8,128)(2,1)} collective-permute-done((bf16[560,1152]{1,0:T(8,128)(2,1)S(1)}, bf16[560,1152]{1,0:T(8,128)(2,1)}, u32[]{:S(2)}, u32[]{:S(2)}) %collective-permute-start.4) | collective-permute-done | bytes 1290272 | tf_op jit(solution)/shard_map/ppermute | solution.py:744
  113.4 12.7 %collective-permute-done.6.refs_2_ = bf16[560,1152]{1,0:T(8,128)(2,1)} collective-permute-done((bf16[560,1152]{1,0:T(8,128)(2,1)}, bf16[560,1152]{1,0:T(8,128)(2,1)}, u32[]{:S(2)}, u32[]{:S(2)}) %collective-permute-start.6) | collective-permute-done | bytes 1290272 | tf_op jit(solution)/shard_map/ppermute | solution.py:744
  134.4 12.1 %shard_map.387 = (bf16[512,2240]{1,0:T(8,128)(2,1)}, f32[512,576]{1,0:T(8,128)}, f32[512,576]{1,0:T(8,128)}, f32[512,32]{1,0:T(8,128)}) custom-call(s32[5]{0:T(128)} %stack.60.refs_0_, bf16[560,1152]{1,0:T(8,128)(2,1)} %pad_maximum_fusion.4.refs_1_, bf16[560,1152]{1,0:T(8,128)(2,1)} %collective-permute-done.1.refs_2_, bf16[560,1152]{1,0:T(8,128)(2,1)} %copy-done.2, ...), custom_call_target="tpu_custom_call" | custom-call | tf_op jit(solution)/shard_map/pallas_call | solution.py:905
  146.5 8.4 %shard_map.388 = (f32[512,576]{1,0:T(8,128)}, f32[40,576]{1,0:T(8,128)}) custom-call(s32[5]{0:T(128)} %stack.60.refs_0_, bf16[560,1152]{1,0:T(8,128)(2,1)} %pad_maximum_fusion.4.refs_1_, bf16[560,1152]{1,0:T(8,128)(2,1)} %collective-permute-done.1.refs_2_, bf16[560,1152]{1,0:T(8,128)(2,1)} %copy-done.2, bf16[560,1152]{1,0:T(8,128)(2,1)} %collective-permute-done.4.refs_4_, ...), custom_call_target="tpu_custom_call" | custom-call | tf_op jit(solution)/shard_map/pallas_call | solution.py:905
  155.5 5.4 collective-permute-done.8.refs_11_.refs_13_
  165.2 8.5 %shard_map.389 = (f32[512,576]{1,0:T(8,128)}, f32[512,576]{1,0:T(8,128)}, bf16[512,576]{1,0:T(8,128)(2,1)}, f32[512,32]{1,0:T(8,128)}, bf16[256,2304]{1,0:T(8,128)(2,1)}, /*index=5*/bf16[256,2304]{1,0:T(8,128)(2,1)}) custom-call(s32[5]{0:T(128)} %stack.60.refs_0_, bf16[560,1152]{1,0:T(8,128)(2,1)} %pad_maximum_fusion.4.refs_1_, ...), custom_call_target="tpu_custom_call" | custom-call | tf_op jit(solution)/shard_map/pallas_call | solution.py:905
  173.7 12.1 %collective-permute-done.11.refs_4_ = bf16[560,1152]{1,0:T(8,128)(2,1)} collective-permute-done((bf16[560,1152]{1,0:T(8,128)(2,1)}, bf16[560,1152]{1,0:T(8,128)(2,1)}, u32[]{:S(2)}, u32[]{:S(2)}) %collective-permute-start.11) | collective-permute-done | bytes 1290272 | tf_op jit(solution)/shard_map/ppermute | solution.py:744
  192.5 31.5 %collective-permute-done.15.refs_2_ = bf16[560,1400]{1,0:T(8,128)(2,1)} collective-permute-done((bf16[560,1400]{1,0:T(8,128)(2,1)S(1)}, bf16[560,1400]{1,0:T(8,128)(2,1)}, u32[]{:S(2)}, u32[]{:S(2)}) %collective-permute-start.15) | collective-permute-done | bytes 1568032 | tf_op jit(solution)/shard_map/ppermute | solution.py:744
  232.0 7.8 %shard_map.390 = (bf16[2,320,576]{2,1,0:T(8,128)(2,1)}, f32[160,32]{1,0:T(8,128)}) custom-call(s32[5]{0:T(128)} %stack.60.refs_0_, bf16[560,1152]{1,0:T(8,128)(2,1)} %get-tuple-element.284.refs_1_, bf16[560,1152]{1,0:T(8,128)(2,1)} %collective-permute-done.6.refs_2_, bf16[560,1152]{1,0:T(8,128)(2,1)} %collective-permute-done.9.refs_3_, ...), custom_call_target="tpu_custom_call" | custom-call | tf_op jit(solution)/shard_map/pallas_call | solution.py:905
  239.8 21.4 %collective-permute-done.18.refs_3_ = bf16[560,1400]{1,0:T(8,128)(2,1)S(1)} collective-permute-done((bf16[560,1400]{1,0:T(8,128)(2,1)}, bf16[560,1400]{1,0:T(8,128)(2,1)S(1)}, u32[]{:S(2)}, u32[]{:S(2)}) %collective-permute-start.18) | collective-permute-done | bytes 1568032 | tf_op jit(solution)/shard_map/ppermute | solution.py:744
  267.2 13.7 %shard_map.392 = (bf16[256,576]{1,0:T(8,128)(2,1)}, bf16[256,576]{1,0:T(8,128)(2,1)}, f32[256,32]{1,0:T(8,128)}, f32[256,32]{1,0:T(8,128)}, f32[128,256]{1,0:T(8,128)}, /*index=5*/bf16[256,2304]{1,0:T(8,128)(2,1)}) custom-call(s32[5]{0:T(128)} %stack.60.refs_0_, bf16[560,1152]{1,0:T(8,128)(2,1)} %get-tuple-element.284.refs_1_, ...), custom_call_target="tpu_custom_call" | custom-call | tf_op jit(solution)/shard_map/pallas_call | solution.py:905
  280.9 14.3 %shard_map.393 = (bf16[256,576]{1,0:T(8,128)(2,1)}, bf16[256,576]{1,0:T(8,128)(2,1)}, f32[256,32]{1,0:T(8,128)}, f32[256,32]{1,0:T(8,128)}, f32[128,256]{1,0:T(8,128)}, /*index=5*/bf16[256,2304]{1,0:T(8,128)(2,1)}) custom-call(s32[5]{0:T(128)} %stack.60.refs_0_, bf16[560,1152]{1,0:T(8,128)(2,1)} %get-tuple-element.284.refs_1_, ...), custom_call_target="tpu_custom_call" | custom-call | tf_op jit(solution)/shard_map/pallas_call | solution.py:905
  304.4 16.3 %collective-permute-done.23.refs_2_ = bf16[560,700]{1,0:T(8,128)(2,1)} collective-permute-done((bf16[560,700]{1,0:T(8,128)(2,1)S(1)}, bf16[560,700]{1,0:T(8,128)(2,1)}, u32[]{:S(2)}, u32[]{:S(2)}) %collective-permute-start.23) | collective-permute-done | bytes 784032 | tf_op jit(solution)/shard_map/ppermute | solution.py:744
  323.7 14.3 %collective-permute-done.25.refs_8_ = bf16[560,1400]{1,0:T(8,128)(2,1)S(1)} collective-permute-done((bf16[560,1400]{1,0:T(8,128)(2,1)S(1)}, bf16[560,1400]{1,0:T(8,128)(2,1)S(1)}, u32[]{:S(2)}, u32[]{:S(2)}) %collective-permute-start.25) | collective-permute-done | bytes 1568032 | tf_op jit(solution)/shard_map/ppermute | solution.py:724
  343.6 12.1 %collective-permute-done.27.refs_6_ = bf16[560,700]{1,0:T(8,128)(2,1)S(1)} collective-permute-done((bf16[560,700]{1,0:T(8,128)(2,1)}, bf16[560,700]{1,0:T(8,128)(2,1)S(1)}, u32[]{:S(2)}, u32[]{:S(2)}) %collective-permute-start.27) | collective-permute-done | bytes 784032 | tf_op jit(solution)/shard_map/ppermute | solution.py:724
  361.3 11.7 %shard_map.395 = (f32[2,512,700]{2,1,0:T(8,128)}, f32[2,512,700]{2,1,0:T(8,128)}, bf16[2,512,700]{2,1,0:T(8,128)(2,1)}, bf16[2,512,700]{2,1,0:T(8,128)(2,1)}, bf...) custom-call(s32[5]{0:T(128)} %stack.60.refs_0_, ...), custom_call_target="tpu_custom_call" | custom-call | tf_op jit(solution)/shard_map/pallas_call | solution.py:905
  380.1 12.1 %shard_map.396 = (f32[2,512,700]{2,1,0:T(8,128)}, f32[2,512,700]{2,1,0:T(8,128)}, bf16[2,512,700]{2,1,0:T(8,128)(2,1)}, bf16[2,512,700]{2,1,0:T(8,128)(2,1)}, bf...) custom-call(s32[5]{0:T(128)} %stack.60.refs_0_, ...), custom_call_target="tpu_custom_call", output_to_operand_aliasing={{0}: (16, {}), {1}: (17, {}), {2}: (18, {}), {3}: (19, {}),... | custom-call | tf_op jit(solution)/shard_map/pallas_call | solution.py:905
  396.5 6.6 collective-permute-done.31.refs_12_
  405.2 27.7 %shard_map.397 = (bf16[2,512,700]{2,1,0:T(8,128)(2,1)}, bf16[2,512,700]{2,1,0:T(8,128)(2,1)}, bf16[2,512,700]{2,1,0:T(8,128)(2,1)}, bf16[512,2240]{1,0:T(8,128)(...) custom-call(s32[5]{0:T(128)} %stack.60.refs_0_, ...), custom_call_target="tpu_custom_call" | custom-call | tf_op jit(solution)/shard_map/pallas_call | solution.py:905
  441.4 24.1 %shard_map.398 = (bf16[2,512,700]{2,1,0:T(8,128)(2,1)}, bf16[2,512,700]{2,1,0:T(8,128)(2,1)}, f32[2,2,32,700]{3,2,1,0:T(8,128)}, f32[512,32]{1,0:T(8,128)}, bf16...) custom-call(s32[5]{0:T(128)} %stack.60.refs_0_, bf16[560,1400]{1,0:T(8,128)(2,1)} %get-tuple-element.334.refs_1_, ...), custom_call_target="tpu_custom_call" | custom-call | tf_op jit(solution)/shard_map/pallas_call | solution.py:905
  481.4 19.5 %collective-permute-done.38.refs_1_ = bf16[256,2304]{1,0:T(8,128)(2,1)} collective-permute-done((bf16[256,2304]{1,0:T(8,128)(2,1)S(1)}, bf16[256,2304]{1,0:T(8,128)(2,1)}, u32[]{:S(2)}, u32[]{:S(2)}) %collective-permute-start.38) | collective-permute-done | bytes 1179680 | tf_op jit(solution)/shard_map/ppermute | solution.py:724
  500.9 5.4 shard_map.401
  514.7 26.1 %shard_map.402 = (bf16[512,576]{1,0:T(8,128)(2,1)}, f32[2,320,576]{2,1,0:T(8,128)}, f32[512,32]{1,0:T(8,128)}, f32[512,32]{1,0:T(8,128)}, bf16[256,2304]{1,0:T(8,128)(2,1)}, /*index=5*/bf16[256,2304]{1,0:T(8,128)(2,1)}) custom-call(s32[5]{0:T(128)} %stack.60.refs_0_, bf16[560,1152]{1,0:T(8,128)(2,1)} %get-tuple-element.284.refs_1_, ...), custom_call_target="tpu_custom_call" | custom-call | tf_op jit(solution)/shard_map/pallas_call | solution.py:905
  554.1 14.7 %collective-permute-done.43.refs_14_ = f32[2,160,576]{2,1,0:T(8,128)S(1)} collective-permute-done((f32[2,160,576]{2,1,0:T(8,128)}, f32[2,160,576]{2,1,0:T(8,128)S(1)}, u32[]{:S(2)}, u32[]{:S(2)}) %collective-permute-start.43) | collective-permute-done | bytes 737312 | tf_op jit(solution)/shard_map/ppermute | solution.py:724
  569.7 6.8 shard_map.404
  584.8 11.0 %shard_map.406 = (bf16[512,576]{1,0:T(8,128)(2,1)}, f32[512,32]{1,0:T(8,128)}, f32[40,576]{1,0:T(8,128)}) custom-call(s32[5]{0:T(128)} %stack.60.refs_0_, bf16[560,1152]{1,0:T(8,128)(2,1)} %pad_maximum_fusion.4.refs_1_, bf16[560,1152]{1,0:T(8,128)(2,1)} %collective-permute-done.1.refs_2_, bf16[560,1152]{1,0:T(8,128)(2,1)} %copy-done.2, ...), custom_call_target="tpu_custom_call" | custom-call | tf_op jit(solution)/shard_map/pallas_call | solution.py:905
  601.6 13.9 %shard_map.407 = (bf16[512,576]{1,0:T(8,128)(2,1)}, bf16[512,576]{1,0:T(8,128)(2,1)}, f32[512,32]{1,0:T(8,128)}, bf16[256,2304]{1,0:T(8,128)(2,1)}, bf16[256,2304]{1,0:T(8,128)(2,1)}) custom-call(s32[5]{0:T(128)} %stack.60.refs_0_, bf16[560,1152]{1,0:T(8,128)(2,1)} %pad_maximum_fusion.4.refs_1_, bf16[560,1152]{1,0:T(8,128)(2,1)} %collective-permute-done.1.refs_2_, ...), custom_call_target="tpu_custom_call" | custom-call | tf_op jit(solution)/shard_map/pallas_call | solution.py:905
  627.6 8.6 %all-to-all-done.2.refs_0_ = bf16[8,32,700]{2,1,0:T(8,128)(2,1)S(1)} async-done(((bf16[8,32,700]{2,1,0:T(8,128)(2,1)}), bf16[8,32,700]{2,1,0:T(8,128)(2,1)S(1)}, u32[]{:S(2)}, u32[]{:S(2)}) %all-to-all-start.2) | async-done | bytes 358432 | tf_op jit(solution)/shard_map/all_to_all | solution.py:1290
  642.1 10.5 %all-to-all-done.1.refs_1_ = f32[4,4,6400]{2,1,0:T(4,128)S(1)} async-done(((f32[4,4,6400]{2,1,0:T(4,128)}), f32[4,4,6400]{2,1,0:T(4,128)S(1)}, u32[]{:S(2)}, u32[]{:S(2)}) %all-to-all-start.1) | async-done | bytes 409632 | tf_op jit(solution)/shard_map/all_to_all | solution.py:1187
  658.9 5.5 shard_map.410
  (315 shorter events, 254.5 us)
Async XLA Ops:
  5.8 31.9 %collective-permute-start.1 = (bf16[560,1152]{1,0:T(8,128)(2,1)}, bf16[560,1152]{1,0:T(8,128)(2,1)}, u32[]{:S(2)}, u32[]{:S(2)}) collective-permute-start(bf16[560,1152]{1,0:T(8,128)(2,1)} %pad_maximum_fusion.4.refs_1_), channel_id=1, source_target_pairs={{0,16},{16,24},{24,8},{8,0},{1,17},{17,25},{25,9},{9,1},{2,18},{18... | collective-permute-start | bytes 3870728 | tf_op jit(solution)/shard_map/ppermute | solution.py:744
  37.8 30.4 %collective-permute-start.2 = (bf16[560,1152]{1,0:T(8,128)(2,1)}, bf16[560,1152]{1,0:T(8,128)(2,1)S(1)}, u32[]{:S(2)}, u32[]{:S(2)}) collective-permute-start(bf16[560,1152]{1,0:T(8,128)(2,1)} %collective-permute-done.1.refs_2_), channel_id=1, source_target_pairs={{0,16},{16,24},{24,8},{8,0},{1,17},{17,25},{25,9},{9,1},{2,18},{18... | collective-permute-start | bytes 3870728 | tf_op jit(solution)/shard_map/ppermute | solution.py:744
  41.1 29.1 %collective-permute-start.3 = (bf16[560,1152]{1,0:T(8,128)(2,1)}, bf16[560,1152]{1,0:T(8,128)(2,1)S(1)}, u32[]{:S(2)}, u32[]{:S(2)}) collective-permute-start(bf16[560,1152]{1,0:T(8,128)(2,1)} %collective-permute-done.1.refs_2_), channel_id=1, source_target_pairs={{0,4},{4,0},{1,5},{5,1},{2,6},{6,2},{3,7},{7,3},{8,12},{12,8},{9,1... | collective-permute-start | bytes 3870728 | tf_op jit(solution)/shard_map/ppermute | solution.py:724
  70.3 31.4 %collective-permute-start.4 = (bf16[560,1152]{1,0:T(8,128)(2,1)S(1)}, bf16[560,1152]{1,0:T(8,128)(2,1)}, u32[]{:S(2)}, u32[]{:S(2)}) collective-permute-start(bf16[560,1152]{1,0:T(8,128)(2,1)S(1)} %collective-permute-done.2.refs_3_), channel_id=1, source_target_pairs={{0,16},{16,24},{24,8},{8,0},{1,17},{17,25},{25,9},{9,1},{2,18},{18... | collective-permute-start | bytes 3870728 | tf_op jit(solution)/shard_map/ppermute | solution.py:744
  71.5 30.2 %collective-permute-start.5 = (bf16[560,1152]{1,0:T(8,128)(2,1)S(1)}, bf16[560,1152]{1,0:T(8,128)(2,1)S(1)}, u32[]{:S(2)}, u32[]{:S(2)}) collective-permute-start(bf16[560,1152]{1,0:T(8,128)(2,1)S(1)} %collective-permute-done.2.refs_3_), channel_id=1, source_target_pairs={{0,4},{4,0},{1,5},{5,1},{2,6},{6,2},{3,7},{7,3},{8,12},{12,8},{9,1... | collective-permute-start | bytes 3870728 | tf_op jit(solution)/shard_map/ppermute | solution.py:724
  75.0 51.1 %collective-permute-start.6 = (bf16[560,1152]{1,0:T(8,128)(2,1)}, bf16[560,1152]{1,0:T(8,128)(2,1)}, u32[]{:S(2)}, u32[]{:S(2)}) collective-permute-start(bf16[560,1152]{1,0:T(8,128)(2,1)} %get-tuple-element.284.refs_1_), channel_id=1, source_target_pairs={{0,16},{16,24},{24,8},{8,0},{1,17},{17,25},{25,9},{9,1},{2,18},{18... | collective-permute-start | bytes 3870728 | tf_op jit(solution)/shard_map/ppermute | solution.py:744
  102.8 27.6 %collective-permute-start.7 = (bf16[560,1152]{1,0:T(8,128)(2,1)}, bf16[560,1152]{1,0:T(8,128)(2,1)}, u32[]{:S(2)}, u32[]{:S(2)}) collective-permute-start(bf16[560,1152]{1,0:T(8,128)(2,1)} %collective-permute-done.4.refs_4_), channel_id=1, source_target_pairs={{0,4},{4,0},{1,5},{5,1},{2,6},{6,2},{3,7},{7,3},{8,12},{12,8},{9,1... | collective-permute-start | bytes 3870728 | tf_op jit(solution)/shard_map/ppermute | solution.py:724
  130.4 30.5 %collective-permute-start.10 = (bf16[560,1152]{1,0:T(8,128)(2,1)}, bf16[560,1152]{1,0:T(8,128)(2,1)S(1)}, u32[]{:S(2)}, u32[]{:S(2)}) collective-permute-start(bf16[560,1152]{1,0:T(8,128)(2,1)} %collective-permute-done.6.refs_2_), channel_id=1, source_target_pairs={{0,4},{4,0},{1,5},{5,1},{2,6},{6,2},{3,7},{7,3},{8,12},{12,8},{9,1... | collective-permute-start | bytes 3870728 | tf_op jit(solution)/shard_map/ppermute | solution.py:724
  131.8 29.0 %collective-permute-start.9 = (bf16[560,1152]{1,0:T(8,128)(2,1)}, bf16[560,1152]{1,0:T(8,128)(2,1)}, u32[]{:S(2)}, u32[]{:S(2)}) collective-permute-start(bf16[560,1152]{1,0:T(8,128)(2,1)} %collective-permute-done.6.refs_2_), channel_id=1, source_target_pairs={{0,16},{16,24},{24,8},{8,0},{1,17},{17,25},{25,9},{9,1},{2,18},{18... | collective-permute-start | bytes 3870728 | tf_op jit(solution)/shard_map/ppermute | solution.py:744
  160.9 24.9 %collective-permute-start.11 = (bf16[560,1152]{1,0:T(8,128)(2,1)}, bf16[560,1152]{1,0:T(8,128)(2,1)}, u32[]{:S(2)}, u32[]{:S(2)}) collective-permute-start(bf16[560,1152]{1,0:T(8,128)(2,1)} %collective-permute-done.9.refs_3_), channel_id=1, source_target_pairs={{0,16},{16,24},{24,8},{8,0},{1,17},{17,25},{25,9},{9,1},{2,18},{18... | collective-permute-start | bytes 3870728 | tf_op jit(solution)/shard_map/ppermute | solution.py:744
  163.1 23.8 %collective-permute-start.12 = (bf16[560,1152]{1,0:T(8,128)(2,1)}, bf16[560,1152]{1,0:T(8,128)(2,1)}, u32[]{:S(2)}, u32[]{:S(2)}) collective-permute-start(bf16[560,1152]{1,0:T(8,128)(2,1)} %collective-permute-done.9.refs_3_), channel_id=1, source_target_pairs={{0,4},{4,0},{1,5},{5,1},{2,6},{6,2},{3,7},{7,3},{8,12},{12,8},{9,1... | collective-permute-start | bytes 3870728 | tf_op jit(solution)/shard_map/ppermute | solution.py:724
  187.0 37.0 %collective-permute-start.15 = (bf16[560,1400]{1,0:T(8,128)(2,1)S(1)}, bf16[560,1400]{1,0:T(8,128)(2,1)}, u32[]{:S(2)}, u32[]{:S(2)}) collective-permute-start(bf16[560,1400]{1,0:T(8,128)(2,1)S(1)} %copy-done.5), channel_id=1, source_target_pairs={{0,16},{16,24},{24,8},{8,0},{1,17},{17,25},{25,9},{9,1},{2,18},{18... | collective-permute-start | bytes 4704008 | tf_op jit(solution)/shard_map/ppermute | solution.py:744
  188.5 35.4 %collective-permute-start.16 = (bf16[560,1152]{1,0:T(8,128)(2,1)}, bf16[560,1152]{1,0:T(8,128)(2,1)S(1)}, u32[]{:S(2)}, u32[]{:S(2)}) collective-permute-start(bf16[560,1152]{1,0:T(8,128)(2,1)} %collective-permute-done.11.refs_4_), channel_id=1, source_target_pairs={{0,4},{4,0},{1,5},{5,1},{2,6},{6,2},{3,7},{7,3},{8,12},{12,8},{9,1... | collective-permute-start | bytes 3870728 | tf_op jit(solution)/shard_map/ppermute | solution.py:724
  191.6 32.4 %collective-permute-start.14 = (bf16[256,2304]{1,0:T(8,128)(2,1)S(1)}, bf16[256,2304]{1,0:T(8,128)(2,1)S(1)}, u32[]{:S(2)}, u32[]{:S(2)}) collective-permute-start(bf16[256,2304]{1,0:T(8,128)(2,1)S(1)} %add_convert_fusion.5.refs_0_), channel_id=1, source_target_pairs={{0,2},{1,3},{2,0},{3,1},{4,6},{5,7},{6,4},{7,5},{8,10},{9,11},{10,... | collective-permute-start | bytes 3538952 | tf_op jit(solution)/shard_map/ppermute | solution.py:724
  224.0 37.2 %collective-permute-start.18 = (bf16[560,1400]{1,0:T(8,128)(2,1)}, bf16[560,1400]{1,0:T(8,128)(2,1)S(1)}, u32[]{:S(2)}, u32[]{:S(2)}) collective-permute-start(bf16[560,1400]{1,0:T(8,128)(2,1)} %collective-permute-done.15.refs_2_), channel_id=1, source_target_pairs={{0,16},{16,24},{24,8},{8,0},{1,17},{17,25},{25,9},{9,1},{2,18},{18... | collective-permute-start | bytes 4704008 | tf_op jit(solution)/shard_map/ppermute | solution.py:744
  226.5 36.1 %collective-permute-start.19 = (bf16[560,1400]{1,0:T(8,128)(2,1)}, bf16[560,1400]{1,0:T(8,128)(2,1)}, u32[]{:S(2)}, u32[]{:S(2)}) collective-permute-start(bf16[560,1400]{1,0:T(8,128)(2,1)} %collective-permute-done.15.refs_2_), channel_id=1, source_target_pairs={{0,4},{4,0},{1,5},{5,1},{2,6},{6,2},{3,7},{7,3},{8,12},{12,8},{9,1... | collective-permute-start | bytes 4704008 | tf_op jit(solution)/shard_map/ppermute | solution.py:724
  262.7 35.1 %collective-permute-start.20 = (bf16[560,1400]{1,0:T(8,128)(2,1)S(1)}, bf16[560,1400]{1,0:T(8,128)(2,1)S(1)}, u32[]{:S(2)}, u32[]{:S(2)}) collective-permute-start(bf16[560,1400]{1,0:T(8,128)(2,1)S(1)} %collective-permute-done.18.refs_3_), channel_id=1, source_target_pairs={{0,16},{16,24},{24,8},{8,0},{1,17},{17,25},{25,9},{9,1},{2,18},{18... | collective-permute-start | bytes 4704008 | tf_op jit(solution)/shard_map/ppermute | solution.py:744
  264.0 35.0 %collective-permute-start.21 = (bf16[560,1400]{1,0:T(8,128)(2,1)S(1)}, bf16[560,1400]{1,0:T(8,128)(2,1)}, u32[]{:S(2)}, u32[]{:S(2)}) collective-permute-start(bf16[560,1400]{1,0:T(8,128)(2,1)S(1)} %collective-permute-done.18.refs_3_), channel_id=1, source_target_pairs={{0,4},{4,0},{1,5},{5,1},{2,6},{6,2},{3,7},{7,3},{8,12},{12,8},{9,1... | collective-permute-start | bytes 4704008 | tf_op jit(solution)/shard_map/ppermute | solution.py:724
  299.0 21.6 %collective-permute-start.23 = (bf16[560,700]{1,0:T(8,128)(2,1)S(1)}, bf16[560,700]{1,0:T(8,128)(2,1)}, u32[]{:S(2)}, u32[]{:S(2)}) collective-permute-start(bf16[560,700]{1,0:T(8,128)(2,1)S(1)} %copy-done.25), channel_id=1, source_target_pairs={{0,16},{16,24},{24,8},{8,0},{1,17},{17,25},{25,9},{9,1},{2,18},{18... | collective-permute-start | bytes 2352008 | tf_op jit(solution)/shard_map/ppermute | solution.py:744
  300.7 37.3 %collective-permute-start.25 = (bf16[560,1400]{1,0:T(8,128)(2,1)S(1)}, bf16[560,1400]{1,0:T(8,128)(2,1)S(1)}, u32[]{:S(2)}, u32[]{:S(2)}) collective-permute-start(bf16[560,1400]{1,0:T(8,128)(2,1)S(1)} %collective-permute-done.20.refs_4_), channel_id=1, source_target_pairs={{0,4},{4,0},{1,5},{5,1},{2,6},{6,2},{3,7},{7,3},{8,12},{12,8},{9,1... | collective-permute-start | bytes 4704008 | tf_op jit(solution)/shard_map/ppermute | solution.py:724
  303.5 34.5 %collective-permute-start.24 = (bf16[256,2304]{1,0:T(8,128)(2,1)S(1)}, bf16[256,2304]{1,0:T(8,128)(2,1)S(1)}, u32[]{:S(2)}, u32[]{:S(2)}) collective-permute-start(bf16[256,2304]{1,0:T(8,128)(2,1)S(1)} %add_convert_fusion.4.refs_0_), channel_id=1, source_target_pairs={{0,2},{1,3},{2,0},{3,1},{4,6},{5,7},{6,4},{7,5},{8,10},{9,11},{10,... | collective-permute-start | bytes 3538952 | tf_op jit(solution)/shard_map/ppermute | solution.py:724
  320.7 22.9 %collective-permute-start.26 = (bf16[560,700]{1,0:T(8,128)(2,1)}, bf16[560,700]{1,0:T(8,128)(2,1)}, u32[]{:S(2)}, u32[]{:S(2)}) collective-permute-start(bf16[560,700]{1,0:T(8,128)(2,1)} %collective-permute-done.23.refs_2_), channel_id=1, source_target_pairs={{0,16},{16,24},{24,8},{8,0},{1,17},{17,25},{25,9},{9,1},{2,18},{18... | collective-permute-start | bytes 2352008 | tf_op jit(solution)/shard_map/ppermute | solution.py:744
  323.2 32.5 %collective-permute-start.27 = (bf16[560,700]{1,0:T(8,128)(2,1)}, bf16[560,700]{1,0:T(8,128)(2,1)S(1)}, u32[]{:S(2)}, u32[]{:S(2)}) collective-permute-start(bf16[560,700]{1,0:T(8,128)(2,1)} %collective-permute-done.23.refs_2_), channel_id=1, source_target_pairs={{0,4},{4,0},{1,5},{5,1},{2,6},{6,2},{3,7},{7,3},{8,12},{12,8},{9,1... | collective-permute-start | bytes 2352008 | tf_op jit(solution)/shard_map/ppermute | solution.py:724
  356.6 21.7 %collective-permute-start.29 = (bf16[560,700]{1,0:T(8,128)(2,1)}, bf16[560,700]{1,0:T(8,128)(2,1)S(1)}, u32[]{:S(2)}, u32[]{:S(2)}) collective-permute-start(bf16[560,700]{1,0:T(8,128)(2,1)} %collective-permute-done.26.refs_3_), channel_id=1, source_target_pairs={{0,16},{16,24},{24,8},{8,0},{1,17},{17,25},{25,9},{9,1},{2,18},{18... | collective-permute-start | bytes 2352008 | tf_op jit(solution)/shard_map/ppermute | solution.py:744
  358.1 21.5 %collective-permute-start.30 = (bf16[560,700]{1,0:T(8,128)(2,1)}, bf16[560,700]{1,0:T(8,128)(2,1)S(1)}, u32[]{:S(2)}, u32[]{:S(2)}) collective-permute-start(bf16[560,700]{1,0:T(8,128)(2,1)} %collective-permute-done.26.refs_3_), channel_id=1, source_target_pairs={{0,4},{4,0},{1,5},{5,1},{2,6},{6,2},{3,7},{7,3},{8,12},{12,8},{9,1... | collective-permute-start | bytes 2352008 | tf_op jit(solution)/shard_map/ppermute | solution.py:724
  379.6 24.7 %collective-permute-start.33 = (bf16[560,700]{1,0:T(8,128)(2,1)S(1)}, bf16[560,700]{1,0:T(8,128)(2,1)S(1)}, u32[]{:S(2)}, u32[]{:S(2)}) collective-permute-start(bf16[560,700]{1,0:T(8,128)(2,1)S(1)} %collective-permute-done.29.refs_4_), channel_id=1, source_target_pairs={{0,4},{4,0},{1,5},{5,1},{2,6},{6,2},{3,7},{7,3},{8,12},{12,8},{9,1... | collective-permute-start | bytes 2352008 | tf_op jit(solution)/shard_map/ppermute | solution.py:724
  440.6 27.5 %collective-permute-start.36 = (bf16[256,2304]{1,0:T(8,128)(2,1)S(1)}, bf16[256,2304]{1,0:T(8,128)(2,1)S(1)}, u32[]{:S(2)}, u32[]{:S(2)}) collective-permute-start(bf16[256,2304]{1,0:T(8,128)(2,1)S(1)} %add_convert_fusion.3.refs_0_), channel_id=1, source_target_pairs={{0,2},{1,3},{2,0},{3,1},{4,6},{5,7},{6,4},{7,5},{8,10},{9,11},{10,... | collective-permute-start | bytes 3538952 | tf_op jit(solution)/shard_map/ppermute | solution.py:724
  472.7 28.2 %collective-permute-start.38 = (bf16[256,2304]{1,0:T(8,128)(2,1)S(1)}, bf16[256,2304]{1,0:T(8,128)(2,1)}, u32[]{:S(2)}, u32[]{:S(2)}) collective-permute-start(bf16[256,2304]{1,0:T(8,128)(2,1)S(1)} %add_convert_fusion.2.refs_0_), channel_id=1, source_target_pairs={{0,2},{1,3},{2,0},{3,1},{4,6},{5,7},{6,4},{7,5},{8,10},{9,11},{10,... | collective-permute-start | bytes 3538952 | tf_op jit(solution)/shard_map/ppermute | solution.py:724
  509.4 31.4 %collective-permute-start.40 = (f32[256,2304]{1,0:T(8,128)S(1)}, f32[256,2304]{1,0:T(8,128)}, u32[]{:S(2)}, u32[]{:S(2)}) collective-permute-start(f32[256,2304]{1,0:T(8,128)S(1)} %copy-done.14), channel_id=1, source_target_pairs={{0,1},{1,0},{2,3},{3,2},{4,5},{5,4},{6,7},{7,6},{8,9},{9,8},{10,11... | collective-permute-start | bytes 7077896 | tf_op jit(solution)/shard_map/ppermute | solution.py:724
  509.5 31.3 %all-to-all-start = ((f32[4,4,6656]{2,1,0:T(4,128)}), f32[4,4,6656]{2,1,0:T(4,128)}, u32[]{:S(2)}, u32[]{:S(2)}) async-start(f32[4,4,6656]{2,1,0:T(4,128)} %shard_map.400), calls=%async_computation | async-start | bytes 851968 | tf_op jit(solution)/shard_map/all_to_all | solution.py:1187
  545.6 30.9 %collective-permute-start.42 = (bf16[256,2304]{1,0:T(8,128)(2,1)S(1)}, bf16[256,2304]{1,0:T(8,128)(2,1)}, u32[]{:S(2)}, u32[]{:S(2)}) collective-permute-start(bf16[256,2304]{1,0:T(8,128)(2,1)S(1)} %add_convert_fusion.1.refs_0_), channel_id=1, source_target_pairs={{0,2},{1,3},{2,0},{3,1},{4,6},{5,7},{6,4},{7,5},{8,10},{9,11},{10,... | collective-permute-start | bytes 3538952 | tf_op jit(solution)/shard_map/ppermute | solution.py:724
  620.2 32.5 %collective-permute-start.47 = (bf16[256,2304]{1,0:T(8,128)(2,1)S(1)}, bf16[256,2304]{1,0:T(8,128)(2,1)S(1)}, u32[]{:S(2)}, u32[]{:S(2)}) collective-permute-start(bf16[256,2304]{1,0:T(8,128)(2,1)S(1)} %add_convert_fusion.refs_0_), channel_id=1, source_target_pairs={{0,2},{1,3},{2,0},{3,1},{4,6},{5,7},{6,4},{7,5},{8,10},{9,11},{10,... | collective-permute-start | bytes 3538952 | tf_op jit(solution)/shard_map/ppermute | solution.py:724
  (79 other events, 874.3 us)

commit v6 on v5

--- a/solution.py
+++ b/solution.py
@@ -608,8 +608,8 @@
         home[i, first : first + rows, :size] = table[:, i * size : (i + 1) * size]
 
 
-def set_mark(where, home, first):
-    home[:, first:, :] = jnp.zeros((home.shape[0], home.shape[1] - first, home.shape[2]), f32) + where[2].astype(f32)
+def set_mark(where, home, last):
+    home[:, :, last:] = jnp.zeros((home.shape[0], home.shape[1], 1), f32) + where[2].astype(f32)
 
 
 def second_sums(
@@ -629,14 +629,14 @@
     to_blocks(home, 0, thin_sum(parts[1], gco, gct)[:, :depth])
     to_blocks(home, rows, thin_sum(parts[2], gffn))
     to_blocks(home, 2 * rows, thin_sum(parts[3], fo, ft)[:, :depth])
-    pad, hh = first // 6, home.shape[2] * home.shape[0] // 8
-    size = home.shape[2]
+    size = home.shape[2] - 1
+    pad, hh = first // 6, size * home.shape[0] // 8
     for j in range(3):
         for i in range(home.shape[0]):
             t, h, at = i * size // (2 * hh), i * size % (2 * hh) // hh, i * size % hh
             at += (2 * j + h) * pad
-            home[i, (3 + j) * rows : (4 + j) * rows, :] = sums[t, :, at : at + size]
-    set_mark(where, home, 6 * rows)
+            home[i, (3 + j) * rows : (4 + j) * rows, :size] = sums[t, :, at : at + size]
+    set_mark(where, home, size)
     home_out[...] = home[...].astype(home_out.dtype)
     here = ggot.shape[1]
     gk = (gkv[0, :here, :] + ggot[0]).astype(bf16)
@@ -670,11 +670,11 @@
     rows = projs.shape[0]
 
     def summed(first, size):
-        return sum(sums[t, :, first : first + size] for t in range(sums.shape[0]))
+        return sum(sums[t, :, first : first + size].astype(f32) for t in range(sums.shape[0]))
 
     def heads(first):
         parts = [sums[t, :, first + s * HD : first + (s + m) * HD] for t, (s, m) in enumerate(ranges)]
-        return jnp.concatenate(parts, axis=1)
+        return jnp.concatenate([v.astype(f32) for v in parts], axis=1)
 
     tables = [
         thin_sum(turned(summed(4 * pad, n), b), xo, xt)[:, :depth],
@@ -685,17 +685,17 @@
     tables.append(thin_sum(turned(summed(second + 4 * pad, n), b), a))
     for j, table in enumerate(tables):
         to_blocks(home, j * rows, table)
-    set_mark(where, home, len(tables) * rows)
+    set_mark(where, home, home.shape[2] - 1)
     home_out[...] = home[...].astype(home_out.dtype)
 
 
 def adapter_tables(got, out):
-    last = got.shape[1] - 1
+    last = got.shape[2] - 1
     for i in range(out.shape[0]):
         total = None
         for s in range(got.shape[0]):
             values = got[s].astype(f32)
-            term = jnp.where(values[last:, :1] == float(i), values, 0.0)
+            term = jnp.where(values[:1, last:] == float(i), values, 0.0)
             total = term if total is None else total + term
         out[i] = total
 
@@ -1251,8 +1251,8 @@
     seg = up_to_tiles(width)
 
     seg = up_to_tiles(width)
-    home_dims = (blocks, 8 * part_r, 4 * 2 * hh // blocks)
-    last_dims = (blocks, 16 * part_r, D // blocks)
+    home_dims = (blocks, 8 * part_r, 4 * 2 * hh // blocks + 1)
+    last_dims = (blocks, 12 * part_r, D // blocks + 1)
 
     def second_work(output, output_other, sums, cross_gl, grad_query, query_gl):
         return [in_order(output, output_other)] + list(run(
@@ -1292,7 +1292,7 @@
             third_sums, [(where, scalars), sums_c, proj_gl, mixed, qkv_lat, grad_q, grad_k, grad_v, qkv_gl],
             [((groups, part_r, sums_c.shape[1] + 4 * seg + n), f32)],
         )
-        return swapped(sums), run(adapter_tables, [home], [((adapters,) + home.shape[1:], f32)])[0]
+        return swapped(sums.astype(bf16)), run(adapter_tables, [home], [((adapters,) + home.shape[1:], f32)])[0]
 
     low, got, (sums, tables) = during(
         mine, away, (home, sums_c, proj_gl, qkv_gl, grad_q, grad_k, grad_v), third_work

time: 696 us -> 691 us (level)
    unnamed x120 -> x118, local copies, waits for them, and re-layouts: 14.2 us -> 12.8 us
where the time goes in v6:
time: 691 us; the launch traced here: 683 us
  waiting for transfers between devices  270 us (39%)
  Pallas kernels  249 us (36%)
  local copies, waits for them, and re-layouts  63.3 us (9%)
  starting transfers between devices  60.9 us (9%)
  other arithmetic  36.7 us (5%)
    pallas_call x27, Pallas kernels, run(): pl.pallas_call(body, grid=(steps,), in_specs=specs, out_specs=out_specs,...  249 us
    ppermute x12, waiting for transfers between devices, launch(): lax.ppermute(moving, W, ring_pairs(self.n))  137 us
    ppermute x37, waiting for transfers between devices, across(): return lax.ppermute(values, axis, swap_pairs(lax.axis_size(axis), distance))  113 us
    ppermute x12, starting transfers between devices, launch(): lax.ppermute(moving, W, ring_pairs(self.n))  23.1 us
    ppermute x37, starting transfers between devices, across(): return lax.ppermute(values, axis, swap_pairs(lax.axis_size(axis), distance))  23 us
  transfers between devices with their start and end apart: 53, of which 37 were waited for; matrix products, arithmetic and copies ran while one was open for 11% of the time, Pallas kernels for 26%

profile of v6, /device:TPU:0, one launch (start us, length us, event | category | flops | bytes accessed | tf_op | source)
XLA Modules:
  0.0 682.9 jit_solution(12478458867552015405)
XLA Ops:
  31.8 5.9 collective-permute-done.1.refs_2_
  57.5 10.7 %collective-permute-done.2.refs_3_ = bf16[560,1152]{1,0:T(8,128)(2,1)S(1)} collective-permute-done((bf16[560,1152]{1,0:T(8,128)(2,1)}, bf16[560,1152]{1,0:T(8,128)(2,1)S(1)}, u32[]{:S(2)}, u32[]{:S(2)}) %collective-permute-start.2) | collective-permute-done | bytes 1290272 | tf_op jit(solution)/shard_map/ppermute | solution.py:744
  82.8 18.9 %collective-permute-done.4.refs_4_ = bf16[560,1152]{1,0:T(8,128)(2,1)} collective-permute-done((bf16[560,1152]{1,0:T(8,128)(2,1)S(1)}, bf16[560,1152]{1,0:T(8,128)(2,1)}, u32[]{:S(2)}, u32[]{:S(2)}) %collective-permute-start.4) | collective-permute-done | bytes 1290272 | tf_op jit(solution)/shard_map/ppermute | solution.py:744
  113.3 12.7 %collective-permute-done.6.refs_2_ = bf16[560,1152]{1,0:T(8,128)(2,1)} collective-permute-done((bf16[560,1152]{1,0:T(8,128)(2,1)}, bf16[560,1152]{1,0:T(8,128)(2,1)}, u32[]{:S(2)}, u32[]{:S(2)}) %collective-permute-start.6) | collective-permute-done | bytes 1290272 | tf_op jit(solution)/shard_map/ppermute | solution.py:744
  134.5 12.1 %shard_map.387 = (bf16[512,2240]{1,0:T(8,128)(2,1)}, f32[512,576]{1,0:T(8,128)}, f32[512,576]{1,0:T(8,128)}, f32[512,32]{1,0:T(8,128)}) custom-call(s32[5]{0:T(128)} %stack.60.refs_0_, bf16[560,1152]{1,0:T(8,128)(2,1)} %pad_maximum_fusion.4.refs_1_, bf16[560,1152]{1,0:T(8,128)(2,1)} %collective-permute-done.1.refs_2_, bf16[560,1152]{1,0:T(8,128)(2,1)} %copy-done.2, ...), custom_call_target="tpu_custom_call" | custom-call | tf_op jit(solution)/shard_map/pallas_call | solution.py:905
  146.6 8.4 %shard_map.388 = (f32[512,576]{1,0:T(8,128)}, f32[40,576]{1,0:T(8,128)}) custom-call(s32[5]{0:T(128)} %stack.60.refs_0_, bf16[560,1152]{1,0:T(8,128)(2,1)} %pad_maximum_fusion.4.refs_1_, bf16[560,1152]{1,0:T(8,128)(2,1)} %collective-permute-done.1.refs_2_, bf16[560,1152]{1,0:T(8,128)(2,1)} %copy-done.2, bf16[560,1152]{1,0:T(8,128)(2,1)} %collective-permute-done.4.refs_4_, ...), custom_call_target="tpu_custom_call" | custom-call | tf_op jit(solution)/shard_map/pallas_call | solution.py:905
  155.6 5.4 collective-permute-done.8.refs_11_.refs_13_
  165.3 8.5 %shard_map.389 = (f32[512,576]{1,0:T(8,128)}, f32[512,576]{1,0:T(8,128)}, bf16[512,576]{1,0:T(8,128)(2,1)}, f32[512,32]{1,0:T(8,128)}, bf16[256,2304]{1,0:T(8,128)(2,1)}, /*index=5*/bf16[256,2304]{1,0:T(8,128)(2,1)}) custom-call(s32[5]{0:T(128)} %stack.60.refs_0_, bf16[560,1152]{1,0:T(8,128)(2,1)} %pad_maximum_fusion.4.refs_1_, ...), custom_call_target="tpu_custom_call" | custom-call | tf_op jit(solution)/shard_map/pallas_call | solution.py:905
  173.8 12.1 %collective-permute-done.11.refs_4_ = bf16[560,1152]{1,0:T(8,128)(2,1)} collective-permute-done((bf16[560,1152]{1,0:T(8,128)(2,1)}, bf16[560,1152]{1,0:T(8,128)(2,1)}, u32[]{:S(2)}, u32[]{:S(2)}) %collective-permute-start.11) | collective-permute-done | bytes 1290272 | tf_op jit(solution)/shard_map/ppermute | solution.py:744
  192.6 31.5 %collective-permute-done.15.refs_2_ = bf16[560,1400]{1,0:T(8,128)(2,1)} collective-permute-done((bf16[560,1400]{1,0:T(8,128)(2,1)S(1)}, bf16[560,1400]{1,0:T(8,128)(2,1)}, u32[]{:S(2)}, u32[]{:S(2)}) %collective-permute-start.15) | collective-permute-done | bytes 1568032 | tf_op jit(solution)/shard_map/ppermute | solution.py:744
  232.1 7.8 %shard_map.390 = (bf16[2,320,576]{2,1,0:T(8,128)(2,1)}, f32[160,32]{1,0:T(8,128)}) custom-call(s32[5]{0:T(128)} %stack.60.refs_0_, bf16[560,1152]{1,0:T(8,128)(2,1)} %get-tuple-element.284.refs_1_, bf16[560,1152]{1,0:T(8,128)(2,1)} %collective-permute-done.6.refs_2_, bf16[560,1152]{1,0:T(8,128)(2,1)} %collective-permute-done.9.refs_3_, ...), custom_call_target="tpu_custom_call" | custom-call | tf_op jit(solution)/shard_map/pallas_call | solution.py:905
  239.9 21.4 %collective-permute-done.18.refs_3_ = bf16[560,1400]{1,0:T(8,128)(2,1)S(1)} collective-permute-done((bf16[560,1400]{1,0:T(8,128)(2,1)}, bf16[560,1400]{1,0:T(8,128)(2,1)S(1)}, u32[]{:S(2)}, u32[]{:S(2)}) %collective-permute-start.18) | collective-permute-done | bytes 1568032 | tf_op jit(solution)/shard_map/ppermute | solution.py:744
  267.3 13.7 %shard_map.392 = (bf16[256,576]{1,0:T(8,128)(2,1)}, bf16[256,576]{1,0:T(8,128)(2,1)}, f32[256,32]{1,0:T(8,128)}, f32[256,32]{1,0:T(8,128)}, f32[128,256]{1,0:T(8,128)}, /*index=5*/bf16[256,2304]{1,0:T(8,128)(2,1)}) custom-call(s32[5]{0:T(128)} %stack.60.refs_0_, bf16[560,1152]{1,0:T(8,128)(2,1)} %get-tuple-element.284.refs_1_, ...), custom_call_target="tpu_custom_call" | custom-call | tf_op jit(solution)/shard_map/pallas_call | solution.py:905
  281.0 14.3 %shard_map.393 = (bf16[256,576]{1,0:T(8,128)(2,1)}, bf16[256,576]{1,0:T(8,128)(2,1)}, f32[256,32]{1,0:T(8,128)}, f32[256,32]{1,0:T(8,128)}, f32[128,256]{1,0:T(8,128)}, /*index=5*/bf16[256,2304]{1,0:T(8,128)(2,1)}) custom-call(s32[5]{0:T(128)} %stack.60.refs_0_, bf16[560,1152]{1,0:T(8,128)(2,1)} %get-tuple-element.284.refs_1_, ...), custom_call_target="tpu_custom_call" | custom-call | tf_op jit(solution)/shard_map/pallas_call | solution.py:905
  304.5 16.3 %collective-permute-done.23.refs_2_ = bf16[560,700]{1,0:T(8,128)(2,1)} collective-permute-done((bf16[560,700]{1,0:T(8,128)(2,1)S(1)}, bf16[560,700]{1,0:T(8,128)(2,1)}, u32[]{:S(2)}, u32[]{:S(2)}) %collective-permute-start.23) | collective-permute-done | bytes 784032 | tf_op jit(solution)/shard_map/ppermute | solution.py:744
  323.8 14.3 %collective-permute-done.25.refs_8_ = bf16[560,1400]{1,0:T(8,128)(2,1)S(1)} collective-permute-done((bf16[560,1400]{1,0:T(8,128)(2,1)S(1)}, bf16[560,1400]{1,0:T(8,128)(2,1)S(1)}, u32[]{:S(2)}, u32[]{:S(2)}) %collective-permute-start.25) | collective-permute-done | bytes 1568032 | tf_op jit(solution)/shard_map/ppermute | solution.py:724
  343.7 12.1 %collective-permute-done.27.refs_6_ = bf16[560,700]{1,0:T(8,128)(2,1)S(1)} collective-permute-done((bf16[560,700]{1,0:T(8,128)(2,1)}, bf16[560,700]{1,0:T(8,128)(2,1)S(1)}, u32[]{:S(2)}, u32[]{:S(2)}) %collective-permute-start.27) | collective-permute-done | bytes 784032 | tf_op jit(solution)/shard_map/ppermute | solution.py:724
  361.4 11.7 %shard_map.395 = (f32[2,512,700]{2,1,0:T(8,128)}, f32[2,512,700]{2,1,0:T(8,128)}, bf16[2,512,700]{2,1,0:T(8,128)(2,1)}, bf16[2,512,700]{2,1,0:T(8,128)(2,1)}, bf...) custom-call(s32[5]{0:T(128)} %stack.60.refs_0_, ...), custom_call_target="tpu_custom_call" | custom-call | tf_op jit(solution)/shard_map/pallas_call | solution.py:905
  380.2 12.1 %shard_map.396 = (f32[2,512,700]{2,1,0:T(8,128)}, f32[2,512,700]{2,1,0:T(8,128)}, bf16[2,512,700]{2,1,0:T(8,128)(2,1)}, bf16[2,512,700]{2,1,0:T(8,128)(2,1)}, bf...) custom-call(s32[5]{0:T(128)} %stack.60.refs_0_, ...), custom_call_target="tpu_custom_call", output_to_operand_aliasing={{0}: (16, {}), {1}: (17, {}), {2}: (18, {}), {3}: (19, {}),... | custom-call | tf_op jit(solution)/shard_map/pallas_call | solution.py:905
  396.6 6.6 collective-permute-done.31.refs_12_
  405.3 27.7 %shard_map.397 = (bf16[2,512,700]{2,1,0:T(8,128)(2,1)}, bf16[2,512,700]{2,1,0:T(8,128)(2,1)}, bf16[2,512,700]{2,1,0:T(8,128)(2,1)}, bf16[512,2240]{1,0:T(8,128)(...) custom-call(s32[5]{0:T(128)} %stack.60.refs_0_, ...), custom_call_target="tpu_custom_call" | custom-call | tf_op jit(solution)/shard_map/pallas_call | solution.py:905
  441.6 24.1 %shard_map.398 = (bf16[2,512,700]{2,1,0:T(8,128)(2,1)}, bf16[2,512,700]{2,1,0:T(8,128)(2,1)}, f32[2,2,32,700]{3,2,1,0:T(8,128)}, f32[512,32]{1,0:T(8,128)}, bf16...) custom-call(s32[5]{0:T(128)} %stack.60.refs_0_, bf16[560,1400]{1,0:T(8,128)(2,1)} %get-tuple-element.334.refs_1_, ...), custom_call_target="tpu_custom_call" | custom-call | tf_op jit(solution)/shard_map/pallas_call | solution.py:905
  481.5 19.5 %collective-permute-done.38.refs_1_ = bf16[256,2304]{1,0:T(8,128)(2,1)} collective-permute-done((bf16[256,2304]{1,0:T(8,128)(2,1)S(1)}, bf16[256,2304]{1,0:T(8,128)(2,1)}, u32[]{:S(2)}, u32[]{:S(2)}) %collective-permute-start.38) | collective-permute-done | bytes 1179680 | tf_op jit(solution)/shard_map/ppermute | solution.py:724
  501.0 5.4 shard_map.401
  514.8 26.1 %shard_map.402 = (bf16[512,576]{1,0:T(8,128)(2,1)}, f32[2,320,576]{2,1,0:T(8,128)}, f32[512,32]{1,0:T(8,128)}, f32[512,32]{1,0:T(8,128)}, bf16[256,2304]{1,0:T(8,128)(2,1)}, /*index=5*/bf16[256,2304]{1,0:T(8,128)(2,1)}) custom-call(s32[5]{0:T(128)} %stack.60.refs_0_, bf16[560,1152]{1,0:T(8,128)(2,1)} %get-tuple-element.284.refs_1_, ...), custom_call_target="tpu_custom_call" | custom-call | tf_op jit(solution)/shard_map/pallas_call | solution.py:905
  554.2 14.7 %collective-permute-done.43.refs_14_ = f32[2,160,576]{2,1,0:T(8,128)S(1)} collective-permute-done((f32[2,160,576]{2,1,0:T(8,128)}, f32[2,160,576]{2,1,0:T(8,128)S(1)}, u32[]{:S(2)}, u32[]{:S(2)}) %collective-permute-start.43) | collective-permute-done | bytes 737312 | tf_op jit(solution)/shard_map/ppermute | solution.py:724
  569.8 6.8 shard_map.404
  584.9 11.0 %shard_map.406 = (bf16[512,576]{1,0:T(8,128)(2,1)}, f32[512,32]{1,0:T(8,128)}, f32[40,576]{1,0:T(8,128)}) custom-call(s32[5]{0:T(128)} %stack.60.refs_0_, bf16[560,1152]{1,0:T(8,128)(2,1)} %pad_maximum_fusion.4.refs_1_, bf16[560,1152]{1,0:T(8,128)(2,1)} %collective-permute-done.1.refs_2_, bf16[560,1152]{1,0:T(8,128)(2,1)} %copy-done.2, ...), custom_call_target="tpu_custom_call" | custom-call | tf_op jit(solution)/shard_map/pallas_call | solution.py:905
  601.8 13.8 %shard_map.407 = (bf16[512,576]{1,0:T(8,128)(2,1)}, bf16[512,576]{1,0:T(8,128)(2,1)}, f32[512,32]{1,0:T(8,128)}, bf16[256,2304]{1,0:T(8,128)(2,1)}, bf16[256,2304]{1,0:T(8,128)(2,1)}) custom-call(s32[5]{0:T(128)} %stack.60.refs_0_, bf16[560,1152]{1,0:T(8,128)(2,1)} %pad_maximum_fusion.4.refs_1_, bf16[560,1152]{1,0:T(8,128)(2,1)} %collective-permute-done.1.refs_2_, ...), custom_call_target="tpu_custom_call" | custom-call | tf_op jit(solution)/shard_map/pallas_call | solution.py:905
  629.4 6.8 all-to-all-done.2.refs_0_
  642.3 8.3 %all-to-all-done.1.refs_1_ = bf16[4,4,6400]{2,1,0:T(4,128)(2,1)S(1)} async-done(((bf16[4,4,6400]{2,1,0:T(4,128)(2,1)}), bf16[4,4,6400]{2,1,0:T(4,128)(2,1)S(1)}, u32[]{:S(2)}, u32[]{:S(2)}) %all-to-all-start.1) | async-done | bytes 204832 | tf_op jit(solution)/shard_map/all_to_all | solution.py:1187
  656.8 5.4 shard_map.410
  (314 shorter events, 253.6 us)
Async XLA Ops:
  5.8 31.9 %collective-permute-start.1 = (bf16[560,1152]{1,0:T(8,128)(2,1)}, bf16[560,1152]{1,0:T(8,128)(2,1)}, u32[]{:S(2)}, u32[]{:S(2)}) collective-permute-start(bf16[560,1152]{1,0:T(8,128)(2,1)} %pad_maximum_fusion.4.refs_1_), channel_id=1, source_target_pairs={{0,16},{16,24},{24,8},{8,0},{1,17},{17,25},{25,9},{9,1},{2,18},{18... | collective-permute-start | bytes 3870728 | tf_op jit(solution)/shard_map/ppermute | solution.py:744
  37.8 30.4 %collective-permute-start.2 = (bf16[560,1152]{1,0:T(8,128)(2,1)}, bf16[560,1152]{1,0:T(8,128)(2,1)S(1)}, u32[]{:S(2)}, u32[]{:S(2)}) collective-permute-start(bf16[560,1152]{1,0:T(8,128)(2,1)} %collective-permute-done.1.refs_2_), channel_id=1, source_target_pairs={{0,16},{16,24},{24,8},{8,0},{1,17},{17,25},{25,9},{9,1},{2,18},{18... | collective-permute-start | bytes 3870728 | tf_op jit(solution)/shard_map/ppermute | solution.py:744
  41.1 29.1 %collective-permute-start.3 = (bf16[560,1152]{1,0:T(8,128)(2,1)}, bf16[560,1152]{1,0:T(8,128)(2,1)S(1)}, u32[]{:S(2)}, u32[]{:S(2)}) collective-permute-start(bf16[560,1152]{1,0:T(8,128)(2,1)} %collective-permute-done.1.refs_2_), channel_id=1, source_target_pairs={{0,4},{4,0},{1,5},{5,1},{2,6},{6,2},{3,7},{7,3},{8,12},{12,8},{9,1... | collective-permute-start | bytes 3870728 | tf_op jit(solution)/shard_map/ppermute | solution.py:724
  70.3 31.4 %collective-permute-start.4 = (bf16[560,1152]{1,0:T(8,128)(2,1)S(1)}, bf16[560,1152]{1,0:T(8,128)(2,1)}, u32[]{:S(2)}, u32[]{:S(2)}) collective-permute-start(bf16[560,1152]{1,0:T(8,128)(2,1)S(1)} %collective-permute-done.2.refs_3_), channel_id=1, source_target_pairs={{0,16},{16,24},{24,8},{8,0},{1,17},{17,25},{25,9},{9,1},{2,18},{18... | collective-permute-start | bytes 3870728 | tf_op jit(solution)/shard_map/ppermute | solution.py:744
  71.5 30.2 %collective-permute-start.5 = (bf16[560,1152]{1,0:T(8,128)(2,1)S(1)}, bf16[560,1152]{1,0:T(8,128)(2,1)S(1)}, u32[]{:S(2)}, u32[]{:S(2)}) collective-permute-start(bf16[560,1152]{1,0:T(8,128)(2,1)S(1)} %collective-permute-done.2.refs_3_), channel_id=1, source_target_pairs={{0,4},{4,0},{1,5},{5,1},{2,6},{6,2},{3,7},{7,3},{8,12},{12,8},{9,1... | collective-permute-start | bytes 3870728 | tf_op jit(solution)/shard_map/ppermute | solution.py:724
  75.0 51.1 %collective-permute-start.6 = (bf16[560,1152]{1,0:T(8,128)(2,1)}, bf16[560,1152]{1,0:T(8,128)(2,1)}, u32[]{:S(2)}, u32[]{:S(2)}) collective-permute-start(bf16[560,1152]{1,0:T(8,128)(2,1)} %get-tuple-element.284.refs_1_), channel_id=1, source_target_pairs={{0,16},{16,24},{24,8},{8,0},{1,17},{17,25},{25,9},{9,1},{2,18},{18... | collective-permute-start | bytes 3870728 | tf_op jit(solution)/shard_map/ppermute | solution.py:744
  102.8 27.6 %collective-permute-start.7 = (bf16[560,1152]{1,0:T(8,128)(2,1)}, bf16[560,1152]{1,0:T(8,128)(2,1)}, u32[]{:S(2)}, u32[]{:S(2)}) collective-permute-start(bf16[560,1152]{1,0:T(8,128)(2,1)} %collective-permute-done.4.refs_4_), channel_id=1, source_target_pairs={{0,4},{4,0},{1,5},{5,1},{2,6},{6,2},{3,7},{7,3},{8,12},{12,8},{9,1... | collective-permute-start | bytes 3870728 | tf_op jit(solution)/shard_map/ppermute | solution.py:724
  130.4 30.6 %collective-permute-start.10 = (bf16[560,1152]{1,0:T(8,128)(2,1)}, bf16[560,1152]{1,0:T(8,128)(2,1)S(1)}, u32[]{:S(2)}, u32[]{:S(2)}) collective-permute-start(bf16[560,1152]{1,0:T(8,128)(2,1)} %collective-permute-done.6.refs_2_), channel_id=1, source_target_pairs={{0,4},{4,0},{1,5},{5,1},{2,6},{6,2},{3,7},{7,3},{8,12},{12,8},{9,1... | collective-permute-start | bytes 3870728 | tf_op jit(solution)/shard_map/ppermute | solution.py:724
  131.9 29.1 %collective-permute-start.9 = (bf16[560,1152]{1,0:T(8,128)(2,1)}, bf16[560,1152]{1,0:T(8,128)(2,1)}, u32[]{:S(2)}, u32[]{:S(2)}) collective-permute-start(bf16[560,1152]{1,0:T(8,128)(2,1)} %collective-permute-done.6.refs_2_), channel_id=1, source_target_pairs={{0,16},{16,24},{24,8},{8,0},{1,17},{17,25},{25,9},{9,1},{2,18},{18... | collective-permute-start | bytes 3870728 | tf_op jit(solution)/shard_map/ppermute | solution.py:744
  161.0 24.9 %collective-permute-start.11 = (bf16[560,1152]{1,0:T(8,128)(2,1)}, bf16[560,1152]{1,0:T(8,128)(2,1)}, u32[]{:S(2)}, u32[]{:S(2)}) collective-permute-start(bf16[560,1152]{1,0:T(8,128)(2,1)} %collective-permute-done.9.refs_3_), channel_id=1, source_target_pairs={{0,16},{16,24},{24,8},{8,0},{1,17},{17,25},{25,9},{9,1},{2,18},{18... | collective-permute-start | bytes 3870728 | tf_op jit(solution)/shard_map/ppermute | solution.py:744
  163.3 23.8 %collective-permute-start.12 = (bf16[560,1152]{1,0:T(8,128)(2,1)}, bf16[560,1152]{1,0:T(8,128)(2,1)}, u32[]{:S(2)}, u32[]{:S(2)}) collective-permute-start(bf16[560,1152]{1,0:T(8,128)(2,1)} %collective-permute-done.9.refs_3_), channel_id=1, source_target_pairs={{0,4},{4,0},{1,5},{5,1},{2,6},{6,2},{3,7},{7,3},{8,12},{12,8},{9,1... | collective-permute-start | bytes 3870728 | tf_op jit(solution)/shard_map/ppermute | solution.py:724
  187.1 37.0 %collective-permute-start.15 = (bf16[560,1400]{1,0:T(8,128)(2,1)S(1)}, bf16[560,1400]{1,0:T(8,128)(2,1)}, u32[]{:S(2)}, u32[]{:S(2)}) collective-permute-start(bf16[560,1400]{1,0:T(8,128)(2,1)S(1)} %copy-done.5), channel_id=1, source_target_pairs={{0,16},{16,24},{24,8},{8,0},{1,17},{17,25},{25,9},{9,1},{2,18},{18... | collective-permute-start | bytes 4704008 | tf_op jit(solution)/shard_map/ppermute | solution.py:744
  188.6 35.4 %collective-permute-start.16 = (bf16[560,1152]{1,0:T(8,128)(2,1)}, bf16[560,1152]{1,0:T(8,128)(2,1)S(1)}, u32[]{:S(2)}, u32[]{:S(2)}) collective-permute-start(bf16[560,1152]{1,0:T(8,128)(2,1)} %collective-permute-done.11.refs_4_), channel_id=1, source_target_pairs={{0,4},{4,0},{1,5},{5,1},{2,6},{6,2},{3,7},{7,3},{8,12},{12,8},{9,1... | collective-permute-start | bytes 3870728 | tf_op jit(solution)/shard_map/ppermute | solution.py:724
  191.7 32.4 %collective-permute-start.14 = (bf16[256,2304]{1,0:T(8,128)(2,1)S(1)}, bf16[256,2304]{1,0:T(8,128)(2,1)S(1)}, u32[]{:S(2)}, u32[]{:S(2)}) collective-permute-start(bf16[256,2304]{1,0:T(8,128)(2,1)S(1)} %add_convert_fusion.5.refs_0_), channel_id=1, source_target_pairs={{0,2},{1,3},{2,0},{3,1},{4,6},{5,7},{6,4},{7,5},{8,10},{9,11},{10,... | collective-permute-start | bytes 3538952 | tf_op jit(solution)/shard_map/ppermute | solution.py:724
  224.1 37.2 %collective-permute-start.18 = (bf16[560,1400]{1,0:T(8,128)(2,1)}, bf16[560,1400]{1,0:T(8,128)(2,1)S(1)}, u32[]{:S(2)}, u32[]{:S(2)}) collective-permute-start(bf16[560,1400]{1,0:T(8,128)(2,1)} %collective-permute-done.15.refs_2_), channel_id=1, source_target_pairs={{0,16},{16,24},{24,8},{8,0},{1,17},{17,25},{25,9},{9,1},{2,18},{18... | collective-permute-start | bytes 4704008 | tf_op jit(solution)/shard_map/ppermute | solution.py:744
  226.6 36.1 %collective-permute-start.19 = (bf16[560,1400]{1,0:T(8,128)(2,1)}, bf16[560,1400]{1,0:T(8,128)(2,1)}, u32[]{:S(2)}, u32[]{:S(2)}) collective-permute-start(bf16[560,1400]{1,0:T(8,128)(2,1)} %collective-permute-done.15.refs_2_), channel_id=1, source_target_pairs={{0,4},{4,0},{1,5},{5,1},{2,6},{6,2},{3,7},{7,3},{8,12},{12,8},{9,1... | collective-permute-start | bytes 4704008 | tf_op jit(solution)/shard_map/ppermute | solution.py:724
  262.8 35.1 %collective-permute-start.20 = (bf16[560,1400]{1,0:T(8,128)(2,1)S(1)}, bf16[560,1400]{1,0:T(8,128)(2,1)S(1)}, u32[]{:S(2)}, u32[]{:S(2)}) collective-permute-start(bf16[560,1400]{1,0:T(8,128)(2,1)S(1)} %collective-permute-done.18.refs_3_), channel_id=1, source_target_pairs={{0,16},{16,24},{24,8},{8,0},{1,17},{17,25},{25,9},{9,1},{2,18},{18... | collective-permute-start | bytes 4704008 | tf_op jit(solution)/shard_map/ppermute | solution.py:744
  264.1 35.0 %collective-permute-start.21 = (bf16[560,1400]{1,0:T(8,128)(2,1)S(1)}, bf16[560,1400]{1,0:T(8,128)(2,1)}, u32[]{:S(2)}, u32[]{:S(2)}) collective-permute-start(bf16[560,1400]{1,0:T(8,128)(2,1)S(1)} %collective-permute-done.18.refs_3_), channel_id=1, source_target_pairs={{0,4},{4,0},{1,5},{5,1},{2,6},{6,2},{3,7},{7,3},{8,12},{12,8},{9,1... | collective-permute-start | bytes 4704008 | tf_op jit(solution)/shard_map/ppermute | solution.py:724
  299.1 21.6 %collective-permute-start.23 = (bf16[560,700]{1,0:T(8,128)(2,1)S(1)}, bf16[560,700]{1,0:T(8,128)(2,1)}, u32[]{:S(2)}, u32[]{:S(2)}) collective-permute-start(bf16[560,700]{1,0:T(8,128)(2,1)S(1)} %copy-done.25), channel_id=1, source_target_pairs={{0,16},{16,24},{24,8},{8,0},{1,17},{17,25},{25,9},{9,1},{2,18},{18... | collective-permute-start | bytes 2352008 | tf_op jit(solution)/shard_map/ppermute | solution.py:744
  300.8 37.3 %collective-permute-start.25 = (bf16[560,1400]{1,0:T(8,128)(2,1)S(1)}, bf16[560,1400]{1,0:T(8,128)(2,1)S(1)}, u32[]{:S(2)}, u32[]{:S(2)}) collective-permute-start(bf16[560,1400]{1,0:T(8,128)(2,1)S(1)} %collective-permute-done.20.refs_4_), channel_id=1, source_target_pairs={{0,4},{4,0},{1,5},{5,1},{2,6},{6,2},{3,7},{7,3},{8,12},{12,8},{9,1... | collective-permute-start | bytes 4704008 | tf_op jit(solution)/shard_map/ppermute | solution.py:724
  303.6 34.5 %collective-permute-start.24 = (bf16[256,2304]{1,0:T(8,128)(2,1)S(1)}, bf16[256,2304]{1,0:T(8,128)(2,1)S(1)}, u32[]{:S(2)}, u32[]{:S(2)}) collective-permute-start(bf16[256,2304]{1,0:T(8,128)(2,1)S(1)} %add_convert_fusion.4.refs_0_), channel_id=1, source_target_pairs={{0,2},{1,3},{2,0},{3,1},{4,6},{5,7},{6,4},{7,5},{8,10},{9,11},{10,... | collective-permute-start | bytes 3538952 | tf_op jit(solution)/shard_map/ppermute | solution.py:724
  320.8 22.9 %collective-permute-start.26 = (bf16[560,700]{1,0:T(8,128)(2,1)}, bf16[560,700]{1,0:T(8,128)(2,1)}, u32[]{:S(2)}, u32[]{:S(2)}) collective-permute-start(bf16[560,700]{1,0:T(8,128)(2,1)} %collective-permute-done.23.refs_2_), channel_id=1, source_target_pairs={{0,16},{16,24},{24,8},{8,0},{1,17},{17,25},{25,9},{9,1},{2,18},{18... | collective-permute-start | bytes 2352008 | tf_op jit(solution)/shard_map/ppermute | solution.py:744
  323.3 32.5 %collective-permute-start.27 = (bf16[560,700]{1,0:T(8,128)(2,1)}, bf16[560,700]{1,0:T(8,128)(2,1)S(1)}, u32[]{:S(2)}, u32[]{:S(2)}) collective-permute-start(bf16[560,700]{1,0:T(8,128)(2,1)} %collective-permute-done.23.refs_2_), channel_id=1, source_target_pairs={{0,4},{4,0},{1,5},{5,1},{2,6},{6,2},{3,7},{7,3},{8,12},{12,8},{9,1... | collective-permute-start | bytes 2352008 | tf_op jit(solution)/shard_map/ppermute | solution.py:724
  356.7 21.7 %collective-permute-start.29 = (bf16[560,700]{1,0:T(8,128)(2,1)}, bf16[560,700]{1,0:T(8,128)(2,1)S(1)}, u32[]{:S(2)}, u32[]{:S(2)}) collective-permute-start(bf16[560,700]{1,0:T(8,128)(2,1)} %collective-permute-done.26.refs_3_), channel_id=1, source_target_pairs={{0,16},{16,24},{24,8},{8,0},{1,17},{17,25},{25,9},{9,1},{2,18},{18... | collective-permute-start | bytes 2352008 | tf_op jit(solution)/shard_map/ppermute | solution.py:744
  358.2 21.5 %collective-permute-start.30 = (bf16[560,700]{1,0:T(8,128)(2,1)}, bf16[560,700]{1,0:T(8,128)(2,1)S(1)}, u32[]{:S(2)}, u32[]{:S(2)}) collective-permute-start(bf16[560,700]{1,0:T(8,128)(2,1)} %collective-permute-done.26.refs_3_), channel_id=1, source_target_pairs={{0,4},{4,0},{1,5},{5,1},{2,6},{6,2},{3,7},{7,3},{8,12},{12,8},{9,1... | collective-permute-start | bytes 2352008 | tf_op jit(solution)/shard_map/ppermute | solution.py:724
  379.7 24.7 %collective-permute-start.33 = (bf16[560,700]{1,0:T(8,128)(2,1)S(1)}, bf16[560,700]{1,0:T(8,128)(2,1)S(1)}, u32[]{:S(2)}, u32[]{:S(2)}) collective-permute-start(bf16[560,700]{1,0:T(8,128)(2,1)S(1)} %collective-permute-done.29.refs_4_), channel_id=1, source_target_pairs={{0,4},{4,0},{1,5},{5,1},{2,6},{6,2},{3,7},{7,3},{8,12},{12,8},{9,1... | collective-permute-start | bytes 2352008 | tf_op jit(solution)/shard_map/ppermute | solution.py:724
  440.7 27.5 %collective-permute-start.36 = (bf16[256,2304]{1,0:T(8,128)(2,1)S(1)}, bf16[256,2304]{1,0:T(8,128)(2,1)S(1)}, u32[]{:S(2)}, u32[]{:S(2)}) collective-permute-start(bf16[256,2304]{1,0:T(8,128)(2,1)S(1)} %add_convert_fusion.3.refs_0_), channel_id=1, source_target_pairs={{0,2},{1,3},{2,0},{3,1},{4,6},{5,7},{6,4},{7,5},{8,10},{9,11},{10,... | collective-permute-start | bytes 3538952 | tf_op jit(solution)/shard_map/ppermute | solution.py:724
  472.8 28.2 %collective-permute-start.38 = (bf16[256,2304]{1,0:T(8,128)(2,1)S(1)}, bf16[256,2304]{1,0:T(8,128)(2,1)}, u32[]{:S(2)}, u32[]{:S(2)}) collective-permute-start(bf16[256,2304]{1,0:T(8,128)(2,1)S(1)} %add_convert_fusion.2.refs_0_), channel_id=1, source_target_pairs={{0,2},{1,3},{2,0},{3,1},{4,6},{5,7},{6,4},{7,5},{8,10},{9,11},{10,... | collective-permute-start | bytes 3538952 | tf_op jit(solution)/shard_map/ppermute | solution.py:724
  509.5 31.4 %collective-permute-start.40 = (f32[256,2304]{1,0:T(8,128)S(1)}, f32[256,2304]{1,0:T(8,128)}, u32[]{:S(2)}, u32[]{:S(2)}) collective-permute-start(f32[256,2304]{1,0:T(8,128)S(1)} %copy-done.14), channel_id=1, source_target_pairs={{0,1},{1,0},{2,3},{3,2},{4,5},{5,4},{6,7},{7,6},{8,9},{9,8},{10,11... | collective-permute-start | bytes 7077896 | tf_op jit(solution)/shard_map/ppermute | solution.py:724
  509.6 31.3 %all-to-all-start = ((f32[4,4,6656]{2,1,0:T(4,128)}), f32[4,4,6656]{2,1,0:T(4,128)}, u32[]{:S(2)}, u32[]{:S(2)}) async-start(f32[4,4,6656]{2,1,0:T(4,128)} %shard_map.400), calls=%async_computation | async-start | bytes 851968 | tf_op jit(solution)/shard_map/all_to_all | solution.py:1187
  545.7 30.9 %collective-permute-start.42 = (bf16[256,2304]{1,0:T(8,128)(2,1)S(1)}, bf16[256,2304]{1,0:T(8,128)(2,1)}, u32[]{:S(2)}, u32[]{:S(2)}) collective-permute-start(bf16[256,2304]{1,0:T(8,128)(2,1)S(1)} %add_convert_fusion.1.refs_0_), channel_id=1, source_target_pairs={{0,2},{1,3},{2,0},{3,1},{4,6},{5,7},{6,4},{7,5},{8,10},{9,11},{10,... | collective-permute-start | bytes 3538952 | tf_op jit(solution)/shard_map/ppermute | solution.py:724
  620.3 30.3 %collective-permute-start.47 = (bf16[256,2304]{1,0:T(8,128)(2,1)S(1)}, bf16[256,2304]{1,0:T(8,128)(2,1)S(1)}, u32[]{:S(2)}, u32[]{:S(2)}) collective-permute-start(bf16[256,2304]{1,0:T(8,128)(2,1)S(1)} %add_convert_fusion.refs_0_), channel_id=1, source_target_pairs={{0,2},{1,3},{2,0},{3,1},{4,6},{5,7},{6,4},{7,5},{8,10},{9,11},{10,... | collective-permute-start | bytes 3538952 | tf_op jit(solution)/shard_map/ppermute | solution.py:724
  (78 other events, 875.9 us)

commit v7 on v6

--- a/solution.py
+++ b/solution.py
@@ -1239,7 +1239,7 @@
         weights=[(w_cd, (1,))], meta=meta,
     )
     mine, away, output_other, sums_f, gkv = together(mine, away, output_other, sums_f, gkv)
-    gkv_got = across(gkv[:, text_rows:], C)
+    gkv_got = across(gkv[:, text_rows:].astype(bf16), C)
 
     def in_order(own, other):
         (rows,) = run(

time: 691 us -> 690 us (level)
  transfers between devices with their start and end apart: 53 -> 53, of which waited for: 37 -> 38; matrix products, arithmetic and copies ran while one was open for 11% -> 11% of each run, Pallas kernels for 26% -> 26%
where the time goes in v7:
time: 690 us; the launch traced here: 681 us
  waiting for transfers between devices  266 us (39%)
  Pallas kernels  249 us (36%)
  local copies, waits for them, and re-layouts  64.4 us (9%)
  starting transfers between devices  62.3 us (9%)
  other arithmetic  36.7 us (5%)
    pallas_call x27, Pallas kernels, run(): pl.pallas_call(body, grid=(steps,), in_specs=specs, out_specs=out_specs,...  249 us
    ppermute x12, waiting for transfers between devices, launch(): lax.ppermute(moving, W, ring_pairs(self.n))  137 us
    ppermute x37, waiting for transfers between devices, across(): return lax.ppermute(values, axis, swap_pairs(lax.axis_size(axis), distance))  111 us
    ppermute x37, starting transfers between devices, across(): return lax.ppermute(values, axis, swap_pairs(lax.axis_size(axis), distance))  24.4 us
    ppermute x12, starting transfers between devices, launch(): lax.ppermute(moving, W, ring_pairs(self.n))  23.1 us
  transfers between devices with their start and end apart: 53, of which 38 were waited for; matrix products, arithmetic and copies ran while one was open for 11% of the time, Pallas kernels for 26%

profile of v7, /device:TPU:0, one launch (start us, length us, event | category | flops | bytes accessed | tf_op | source)
XLA Modules:
  0.0 681.3 jit_solution(1743060046987962948)
XLA Ops:
  31.8 5.9 collective-permute-done.1.refs_2_
  57.5 10.7 %collective-permute-done.2.refs_3_ = bf16[560,1152]{1,0:T(8,128)(2,1)S(1)} collective-permute-done((bf16[560,1152]{1,0:T(8,128)(2,1)}, bf16[560,1152]{1,0:T(8,128)(2,1)S(1)}, u32[]{:S(2)}, u32[]{:S(2)}) %collective-permute-start.2) | collective-permute-done | bytes 1290272 | tf_op jit(solution)/shard_map/ppermute | solution.py:744
  82.8 18.9 %collective-permute-done.4.refs_4_ = bf16[560,1152]{1,0:T(8,128)(2,1)} collective-permute-done((bf16[560,1152]{1,0:T(8,128)(2,1)S(1)}, bf16[560,1152]{1,0:T(8,128)(2,1)}, u32[]{:S(2)}, u32[]{:S(2)}) %collective-permute-start.4) | collective-permute-done | bytes 1290272 | tf_op jit(solution)/shard_map/ppermute | solution.py:744
  113.3 12.7 %collective-permute-done.6.refs_2_ = bf16[560,1152]{1,0:T(8,128)(2,1)} collective-permute-done((bf16[560,1152]{1,0:T(8,128)(2,1)}, bf16[560,1152]{1,0:T(8,128)(2,1)}, u32[]{:S(2)}, u32[]{:S(2)}) %collective-permute-start.6) | collective-permute-done | bytes 1290272 | tf_op jit(solution)/shard_map/ppermute | solution.py:744
  134.5 12.1 %shard_map.387 = (bf16[512,2240]{1,0:T(8,128)(2,1)}, f32[512,576]{1,0:T(8,128)}, f32[512,576]{1,0:T(8,128)}, f32[512,32]{1,0:T(8,128)}) custom-call(s32[5]{0:T(128)} %stack.60.refs_0_, bf16[560,1152]{1,0:T(8,128)(2,1)} %pad_maximum_fusion.4.refs_1_, bf16[560,1152]{1,0:T(8,128)(2,1)} %collective-permute-done.1.refs_2_, bf16[560,1152]{1,0:T(8,128)(2,1)} %copy-done.2, ...), custom_call_target="tpu_custom_call" | custom-call | tf_op jit(solution)/shard_map/pallas_call | solution.py:905
  146.6 8.4 %shard_map.388 = (f32[512,576]{1,0:T(8,128)}, f32[40,576]{1,0:T(8,128)}) custom-call(s32[5]{0:T(128)} %stack.60.refs_0_, bf16[560,1152]{1,0:T(8,128)(2,1)} %pad_maximum_fusion.4.refs_1_, bf16[560,1152]{1,0:T(8,128)(2,1)} %collective-permute-done.1.refs_2_, bf16[560,1152]{1,0:T(8,128)(2,1)} %copy-done.2, bf16[560,1152]{1,0:T(8,128)(2,1)} %collective-permute-done.4.refs_4_, ...), custom_call_target="tpu_custom_call" | custom-call | tf_op jit(solution)/shard_map/pallas_call | solution.py:905
  155.6 5.4 collective-permute-done.8.refs_11_.refs_13_
  165.3 8.5 %shard_map.389 = (f32[512,576]{1,0:T(8,128)}, f32[512,576]{1,0:T(8,128)}, bf16[512,576]{1,0:T(8,128)(2,1)}, f32[512,32]{1,0:T(8,128)}, bf16[256,2304]{1,0:T(8,128)(2,1)}, /*index=5*/bf16[256,2304]{1,0:T(8,128)(2,1)}) custom-call(s32[5]{0:T(128)} %stack.60.refs_0_, bf16[560,1152]{1,0:T(8,128)(2,1)} %pad_maximum_fusion.4.refs_1_, ...), custom_call_target="tpu_custom_call" | custom-call | tf_op jit(solution)/shard_map/pallas_call | solution.py:905
  173.8 12.1 %collective-permute-done.11.refs_4_ = bf16[560,1152]{1,0:T(8,128)(2,1)} collective-permute-done((bf16[560,1152]{1,0:T(8,128)(2,1)}, bf16[560,1152]{1,0:T(8,128)(2,1)}, u32[]{:S(2)}, u32[]{:S(2)}) %collective-permute-start.11) | collective-permute-done | bytes 1290272 | tf_op jit(solution)/shard_map/ppermute | solution.py:744
  192.6 31.5 %collective-permute-done.15.refs_2_ = bf16[560,1400]{1,0:T(8,128)(2,1)} collective-permute-done((bf16[560,1400]{1,0:T(8,128)(2,1)S(1)}, bf16[560,1400]{1,0:T(8,128)(2,1)}, u32[]{:S(2)}, u32[]{:S(2)}) %collective-permute-start.15) | collective-permute-done | bytes 1568032 | tf_op jit(solution)/shard_map/ppermute | solution.py:744
  232.1 7.8 %shard_map.390 = (bf16[2,320,576]{2,1,0:T(8,128)(2,1)}, f32[160,32]{1,0:T(8,128)}) custom-call(s32[5]{0:T(128)} %stack.60.refs_0_, bf16[560,1152]{1,0:T(8,128)(2,1)} %get-tuple-element.284.refs_1_, bf16[560,1152]{1,0:T(8,128)(2,1)} %collective-permute-done.6.refs_2_, bf16[560,1152]{1,0:T(8,128)(2,1)} %collective-permute-done.9.refs_3_, ...), custom_call_target="tpu_custom_call" | custom-call | tf_op jit(solution)/shard_map/pallas_call | solution.py:905
  239.9 21.4 %collective-permute-done.18.refs_3_ = bf16[560,1400]{1,0:T(8,128)(2,1)S(1)} collective-permute-done((bf16[560,1400]{1,0:T(8,128)(2,1)}, bf16[560,1400]{1,0:T(8,128)(2,1)S(1)}, u32[]{:S(2)}, u32[]{:S(2)}) %collective-permute-start.18) | collective-permute-done | bytes 1568032 | tf_op jit(solution)/shard_map/ppermute | solution.py:744
  267.3 13.7 %shard_map.392 = (bf16[256,576]{1,0:T(8,128)(2,1)}, bf16[256,576]{1,0:T(8,128)(2,1)}, f32[256,32]{1,0:T(8,128)}, f32[256,32]{1,0:T(8,128)}, f32[128,256]{1,0:T(8,128)}, /*index=5*/bf16[256,2304]{1,0:T(8,128)(2,1)}) custom-call(s32[5]{0:T(128)} %stack.60.refs_0_, bf16[560,1152]{1,0:T(8,128)(2,1)} %get-tuple-element.284.refs_1_, ...), custom_call_target="tpu_custom_call" | custom-call | tf_op jit(solution)/shard_map/pallas_call | solution.py:905
  281.0 14.3 %shard_map.393 = (bf16[256,576]{1,0:T(8,128)(2,1)}, bf16[256,576]{1,0:T(8,128)(2,1)}, f32[256,32]{1,0:T(8,128)}, f32[256,32]{1,0:T(8,128)}, f32[128,256]{1,0:T(8,128)}, /*index=5*/bf16[256,2304]{1,0:T(8,128)(2,1)}) custom-call(s32[5]{0:T(128)} %stack.60.refs_0_, bf16[560,1152]{1,0:T(8,128)(2,1)} %get-tuple-element.284.refs_1_, ...), custom_call_target="tpu_custom_call" | custom-call | tf_op jit(solution)/shard_map/pallas_call | solution.py:905
  304.5 16.3 %collective-permute-done.23.refs_2_ = bf16[560,700]{1,0:T(8,128)(2,1)} collective-permute-done((bf16[560,700]{1,0:T(8,128)(2,1)S(1)}, bf16[560,700]{1,0:T(8,128)(2,1)}, u32[]{:S(2)}, u32[]{:S(2)}) %collective-permute-start.23) | collective-permute-done | bytes 784032 | tf_op jit(solution)/shard_map/ppermute | solution.py:744
  323.8 14.3 %collective-permute-done.25.refs_8_ = bf16[560,1400]{1,0:T(8,128)(2,1)S(1)} collective-permute-done((bf16[560,1400]{1,0:T(8,128)(2,1)S(1)}, bf16[560,1400]{1,0:T(8,128)(2,1)S(1)}, u32[]{:S(2)}, u32[]{:S(2)}) %collective-permute-start.25) | collective-permute-done | bytes 1568032 | tf_op jit(solution)/shard_map/ppermute | solution.py:724
  343.7 12.1 %collective-permute-done.27.refs_6_ = bf16[560,700]{1,0:T(8,128)(2,1)S(1)} collective-permute-done((bf16[560,700]{1,0:T(8,128)(2,1)}, bf16[560,700]{1,0:T(8,128)(2,1)S(1)}, u32[]{:S(2)}, u32[]{:S(2)}) %collective-permute-start.27) | collective-permute-done | bytes 784032 | tf_op jit(solution)/shard_map/ppermute | solution.py:724
  361.4 11.7 %shard_map.395 = (f32[2,512,700]{2,1,0:T(8,128)}, f32[2,512,700]{2,1,0:T(8,128)}, bf16[2,512,700]{2,1,0:T(8,128)(2,1)}, bf16[2,512,700]{2,1,0:T(8,128)(2,1)}, bf...) custom-call(s32[5]{0:T(128)} %stack.60.refs_0_, ...), custom_call_target="tpu_custom_call" | custom-call | tf_op jit(solution)/shard_map/pallas_call | solution.py:905
  380.2 12.1 %shard_map.396 = (f32[2,512,700]{2,1,0:T(8,128)}, f32[2,512,700]{2,1,0:T(8,128)}, bf16[2,512,700]{2,1,0:T(8,128)(2,1)}, bf16[2,512,700]{2,1,0:T(8,128)(2,1)}, bf...) custom-call(s32[5]{0:T(128)} %stack.60.refs_0_, ...), custom_call_target="tpu_custom_call", output_to_operand_aliasing={{0}: (16, {}), {1}: (17, {}), {2}: (18, {}), {3}: (19, {}),... | custom-call | tf_op jit(solution)/shard_map/pallas_call | solution.py:905
  396.6 6.6 collective-permute-done.31.refs_12_
  405.3 27.7 %shard_map.397 = (bf16[2,512,700]{2,1,0:T(8,128)(2,1)}, bf16[2,512,700]{2,1,0:T(8,128)(2,1)}, bf16[2,512,700]{2,1,0:T(8,128)(2,1)}, bf16[512,2240]{1,0:T(8,128)(...) custom-call(s32[5]{0:T(128)} %stack.60.refs_0_, ...), custom_call_target="tpu_custom_call" | custom-call | tf_op jit(solution)/shard_map/pallas_call | solution.py:905
  441.6 24.1 %shard_map.398 = (bf16[2,512,700]{2,1,0:T(8,128)(2,1)}, bf16[2,512,700]{2,1,0:T(8,128)(2,1)}, f32[2,2,32,700]{3,2,1,0:T(8,128)}, f32[512,32]{1,0:T(8,128)}, bf16...) custom-call(s32[5]{0:T(128)} %stack.60.refs_0_, bf16[560,1400]{1,0:T(8,128)(2,1)} %get-tuple-element.334.refs_1_, ...), custom_call_target="tpu_custom_call" | custom-call | tf_op jit(solution)/shard_map/pallas_call | solution.py:905
  481.5 19.5 %collective-permute-done.38.refs_1_ = bf16[256,2304]{1,0:T(8,128)(2,1)} collective-permute-done((bf16[256,2304]{1,0:T(8,128)(2,1)S(1)}, bf16[256,2304]{1,0:T(8,128)(2,1)}, u32[]{:S(2)}, u32[]{:S(2)}) %collective-permute-start.38) | collective-permute-done | bytes 1179680 | tf_op jit(solution)/shard_map/ppermute | solution.py:724
  514.8 26.1 %shard_map.402 = (bf16[512,576]{1,0:T(8,128)(2,1)}, f32[2,320,576]{2,1,0:T(8,128)}, f32[512,32]{1,0:T(8,128)}, f32[512,32]{1,0:T(8,128)}, bf16[256,2304]{1,0:T(8,128)(2,1)}, /*index=5*/bf16[256,2304]{1,0:T(8,128)(2,1)}) custom-call(s32[5]{0:T(128)} %stack.60.refs_0_, bf16[560,1152]{1,0:T(8,128)(2,1)} %get-tuple-element.284.refs_1_, ...), custom_call_target="tpu_custom_call" | custom-call | tf_op jit(solution)/shard_map/pallas_call | solution.py:905
  554.4 5.7 collective-permute-done.43.refs_14_
  560.9 6.7 shard_map.404
  567.6 6.4 collective-permute-done.42.refs_1_
  583.3 11.0 %shard_map.406 = (bf16[512,576]{1,0:T(8,128)(2,1)}, f32[512,32]{1,0:T(8,128)}, f32[40,576]{1,0:T(8,128)}) custom-call(s32[5]{0:T(128)} %stack.60.refs_0_, bf16[560,1152]{1,0:T(8,128)(2,1)} %pad_maximum_fusion.4.refs_1_, bf16[560,1152]{1,0:T(8,128)(2,1)} %collective-permute-done.1.refs_2_, bf16[560,1152]{1,0:T(8,128)(2,1)} %copy-done.2, ...), custom_call_target="tpu_custom_call" | custom-call | tf_op jit(solution)/shard_map/pallas_call | solution.py:905
  600.2 13.8 %shard_map.407 = (bf16[512,576]{1,0:T(8,128)(2,1)}, bf16[512,576]{1,0:T(8,128)(2,1)}, f32[512,32]{1,0:T(8,128)}, bf16[256,2304]{1,0:T(8,128)(2,1)}, bf16[256,2304]{1,0:T(8,128)(2,1)}) custom-call(s32[5]{0:T(128)} %stack.60.refs_0_, bf16[560,1152]{1,0:T(8,128)(2,1)} %pad_maximum_fusion.4.refs_1_, bf16[560,1152]{1,0:T(8,128)(2,1)} %collective-permute-done.1.refs_2_, ...), custom_call_target="tpu_custom_call" | custom-call | tf_op jit(solution)/shard_map/pallas_call | solution.py:905
  629.2 6.8 all-to-all-done.2.refs_0_
  642.0 7.0 %all-to-all-done.1.refs_1_ = bf16[4,4,6400]{2,1,0:T(4,128)(2,1)S(1)} async-done(((bf16[4,4,6400]{2,1,0:T(4,128)(2,1)}), bf16[4,4,6400]{2,1,0:T(4,128)(2,1)S(1)}, u32[]{:S(2)}, u32[]{:S(2)}) %all-to-all-start.1) | async-done | bytes 204832 | tf_op jit(solution)/shard_map/all_to_all | solution.py:1187
  655.2 5.4 shard_map.410
  (314 shorter events, 261.5 us)
Async XLA Ops:
  5.8 31.9 %collective-permute-start.1 = (bf16[560,1152]{1,0:T(8,128)(2,1)}, bf16[560,1152]{1,0:T(8,128)(2,1)}, u32[]{:S(2)}, u32[]{:S(2)}) collective-permute-start(bf16[560,1152]{1,0:T(8,128)(2,1)} %pad_maximum_fusion.4.refs_1_), channel_id=1, source_target_pairs={{0,16},{16,24},{24,8},{8,0},{1,17},{17,25},{25,9},{9,1},{2,18},{18... | collective-permute-start | bytes 3870728 | tf_op jit(solution)/shard_map/ppermute | solution.py:744
  37.8 30.4 %collective-permute-start.2 = (bf16[560,1152]{1,0:T(8,128)(2,1)}, bf16[560,1152]{1,0:T(8,128)(2,1)S(1)}, u32[]{:S(2)}, u32[]{:S(2)}) collective-permute-start(bf16[560,1152]{1,0:T(8,128)(2,1)} %collective-permute-done.1.refs_2_), channel_id=1, source_target_pairs={{0,16},{16,24},{24,8},{8,0},{1,17},{17,25},{25,9},{9,1},{2,18},{18... | collective-permute-start | bytes 3870728 | tf_op jit(solution)/shard_map/ppermute | solution.py:744
  41.1 29.1 %collective-permute-start.3 = (bf16[560,1152]{1,0:T(8,128)(2,1)}, bf16[560,1152]{1,0:T(8,128)(2,1)S(1)}, u32[]{:S(2)}, u32[]{:S(2)}) collective-permute-start(bf16[560,1152]{1,0:T(8,128)(2,1)} %collective-permute-done.1.refs_2_), channel_id=1, source_target_pairs={{0,4},{4,0},{1,5},{5,1},{2,6},{6,2},{3,7},{7,3},{8,12},{12,8},{9,1... | collective-permute-start | bytes 3870728 | tf_op jit(solution)/shard_map/ppermute | solution.py:724
  70.3 31.4 %collective-permute-start.4 = (bf16[560,1152]{1,0:T(8,128)(2,1)S(1)}, bf16[560,1152]{1,0:T(8,128)(2,1)}, u32[]{:S(2)}, u32[]{:S(2)}) collective-permute-start(bf16[560,1152]{1,0:T(8,128)(2,1)S(1)} %collective-permute-done.2.refs_3_), channel_id=1, source_target_pairs={{0,16},{16,24},{24,8},{8,0},{1,17},{17,25},{25,9},{9,1},{2,18},{18... | collective-permute-start | bytes 3870728 | tf_op jit(solution)/shard_map/ppermute | solution.py:744
  71.5 30.2 %collective-permute-start.5 = (bf16[560,1152]{1,0:T(8,128)(2,1)S(1)}, bf16[560,1152]{1,0:T(8,128)(2,1)S(1)}, u32[]{:S(2)}, u32[]{:S(2)}) collective-permute-start(bf16[560,1152]{1,0:T(8,128)(2,1)S(1)} %collective-permute-done.2.refs_3_), channel_id=1, source_target_pairs={{0,4},{4,0},{1,5},{5,1},{2,6},{6,2},{3,7},{7,3},{8,12},{12,8},{9,1... | collective-permute-start | bytes 3870728 | tf_op jit(solution)/shard_map/ppermute | solution.py:724
  75.0 51.1 %collective-permute-start.6 = (bf16[560,1152]{1,0:T(8,128)(2,1)}, bf16[560,1152]{1,0:T(8,128)(2,1)}, u32[]{:S(2)}, u32[]{:S(2)}) collective-permute-start(bf16[560,1152]{1,0:T(8,128)(2,1)} %get-tuple-element.284.refs_1_), channel_id=1, source_target_pairs={{0,16},{16,24},{24,8},{8,0},{1,17},{17,25},{25,9},{9,1},{2,18},{18... | collective-permute-start | bytes 3870728 | tf_op jit(solution)/shard_map/ppermute | solution.py:744
  102.8 27.6 %collective-permute-start.7 = (bf16[560,1152]{1,0:T(8,128)(2,1)}, bf16[560,1152]{1,0:T(8,128)(2,1)}, u32[]{:S(2)}, u32[]{:S(2)}) collective-permute-start(bf16[560,1152]{1,0:T(8,128)(2,1)} %collective-permute-done.4.refs_4_), channel_id=1, source_target_pairs={{0,4},{4,0},{1,5},{5,1},{2,6},{6,2},{3,7},{7,3},{8,12},{12,8},{9,1... | collective-permute-start | bytes 3870728 | tf_op jit(solution)/shard_map/ppermute | solution.py:724
  130.4 30.6 %collective-permute-start.10 = (bf16[560,1152]{1,0:T(8,128)(2,1)}, bf16[560,1152]{1,0:T(8,128)(2,1)S(1)}, u32[]{:S(2)}, u32[]{:S(2)}) collective-permute-start(bf16[560,1152]{1,0:T(8,128)(2,1)} %collective-permute-done.6.refs_2_), channel_id=1, source_target_pairs={{0,4},{4,0},{1,5},{5,1},{2,6},{6,2},{3,7},{7,3},{8,12},{12,8},{9,1... | collective-permute-start | bytes 3870728 | tf_op jit(solution)/shard_map/ppermute | solution.py:724
  131.9 29.1 %collective-permute-start.9 = (bf16[560,1152]{1,0:T(8,128)(2,1)}, bf16[560,1152]{1,0:T(8,128)(2,1)}, u32[]{:S(2)}, u32[]{:S(2)}) collective-permute-start(bf16[560,1152]{1,0:T(8,128)(2,1)} %collective-permute-done.6.refs_2_), channel_id=1, source_target_pairs={{0,16},{16,24},{24,8},{8,0},{1,17},{17,25},{25,9},{9,1},{2,18},{18... | collective-permute-start | bytes 3870728 | tf_op jit(solution)/shard_map/ppermute | solution.py:744
  161.0 24.9 %collective-permute-start.11 = (bf16[560,1152]{1,0:T(8,128)(2,1)}, bf16[560,1152]{1,0:T(8,128)(2,1)}, u32[]{:S(2)}, u32[]{:S(2)}) collective-permute-start(bf16[560,1152]{1,0:T(8,128)(2,1)} %collective-permute-done.9.refs_3_), channel_id=1, source_target_pairs={{0,16},{16,24},{24,8},{8,0},{1,17},{17,25},{25,9},{9,1},{2,18},{18... | collective-permute-start | bytes 3870728 | tf_op jit(solution)/shard_map/ppermute | solution.py:744
  163.3 23.8 %collective-permute-start.12 = (bf16[560,1152]{1,0:T(8,128)(2,1)}, bf16[560,1152]{1,0:T(8,128)(2,1)}, u32[]{:S(2)}, u32[]{:S(2)}) collective-permute-start(bf16[560,1152]{1,0:T(8,128)(2,1)} %collective-permute-done.9.refs_3_), channel_id=1, source_target_pairs={{0,4},{4,0},{1,5},{5,1},{2,6},{6,2},{3,7},{7,3},{8,12},{12,8},{9,1... | collective-permute-start | bytes 3870728 | tf_op jit(solution)/shard_map/ppermute | solution.py:724
  187.1 37.0 %collective-permute-start.15 = (bf16[560,1400]{1,0:T(8,128)(2,1)S(1)}, bf16[560,1400]{1,0:T(8,128)(2,1)}, u32[]{:S(2)}, u32[]{:S(2)}) collective-permute-start(bf16[560,1400]{1,0:T(8,128)(2,1)S(1)} %copy-done.5), channel_id=1, source_target_pairs={{0,16},{16,24},{24,8},{8,0},{1,17},{17,25},{25,9},{9,1},{2,18},{18... | collective-permute-start | bytes 4704008 | tf_op jit(solution)/shard_map/ppermute | solution.py:744
  188.6 35.4 %collective-permute-start.16 = (bf16[560,1152]{1,0:T(8,128)(2,1)}, bf16[560,1152]{1,0:T(8,128)(2,1)S(1)}, u32[]{:S(2)}, u32[]{:S(2)}) collective-permute-start(bf16[560,1152]{1,0:T(8,128)(2,1)} %collective-permute-done.11.refs_4_), channel_id=1, source_target_pairs={{0,4},{4,0},{1,5},{5,1},{2,6},{6,2},{3,7},{7,3},{8,12},{12,8},{9,1... | collective-permute-start | bytes 3870728 | tf_op jit(solution)/shard_map/ppermute | solution.py:724
  191.7 32.4 %collective-permute-start.14 = (bf16[256,2304]{1,0:T(8,128)(2,1)S(1)}, bf16[256,2304]{1,0:T(8,128)(2,1)S(1)}, u32[]{:S(2)}, u32[]{:S(2)}) collective-permute-start(bf16[256,2304]{1,0:T(8,128)(2,1)S(1)} %add_convert_fusion.5.refs_0_), channel_id=1, source_target_pairs={{0,2},{1,3},{2,0},{3,1},{4,6},{5,7},{6,4},{7,5},{8,10},{9,11},{10,... | collective-permute-start | bytes 3538952 | tf_op jit(solution)/shard_map/ppermute | solution.py:724
  224.1 37.2 %collective-permute-start.18 = (bf16[560,1400]{1,0:T(8,128)(2,1)}, bf16[560,1400]{1,0:T(8,128)(2,1)S(1)}, u32[]{:S(2)}, u32[]{:S(2)}) collective-permute-start(bf16[560,1400]{1,0:T(8,128)(2,1)} %collective-permute-done.15.refs_2_), channel_id=1, source_target_pairs={{0,16},{16,24},{24,8},{8,0},{1,17},{17,25},{25,9},{9,1},{2,18},{18... | collective-permute-start | bytes 4704008 | tf_op jit(solution)/shard_map/ppermute | solution.py:744
  226.6 36.1 %collective-permute-start.19 = (bf16[560,1400]{1,0:T(8,128)(2,1)}, bf16[560,1400]{1,0:T(8,128)(2,1)}, u32[]{:S(2)}, u32[]{:S(2)}) collective-permute-start(bf16[560,1400]{1,0:T(8,128)(2,1)} %collective-permute-done.15.refs_2_), channel_id=1, source_target_pairs={{0,4},{4,0},{1,5},{5,1},{2,6},{6,2},{3,7},{7,3},{8,12},{12,8},{9,1... | collective-permute-start | bytes 4704008 | tf_op jit(solution)/shard_map/ppermute | solution.py:724
  262.8 35.1 %collective-permute-start.20 = (bf16[560,1400]{1,0:T(8,128)(2,1)S(1)}, bf16[560,1400]{1,0:T(8,128)(2,1)S(1)}, u32[]{:S(2)}, u32[]{:S(2)}) collective-permute-start(bf16[560,1400]{1,0:T(8,128)(2,1)S(1)} %collective-permute-done.18.refs_3_), channel_id=1, source_target_pairs={{0,16},{16,24},{24,8},{8,0},{1,17},{17,25},{25,9},{9,1},{2,18},{18... | collective-permute-start | bytes 4704008 | tf_op jit(solution)/shard_map/ppermute | solution.py:744
  264.1 35.0 %collective-permute-start.21 = (bf16[560,1400]{1,0:T(8,128)(2,1)S(1)}, bf16[560,1400]{1,0:T(8,128)(2,1)}, u32[]{:S(2)}, u32[]{:S(2)}) collective-permute-start(bf16[560,1400]{1,0:T(8,128)(2,1)S(1)} %collective-permute-done.18.refs_3_), channel_id=1, source_target_pairs={{0,4},{4,0},{1,5},{5,1},{2,6},{6,2},{3,7},{7,3},{8,12},{12,8},{9,1... | collective-permute-start | bytes 4704008 | tf_op jit(solution)/shard_map/ppermute | solution.py:724
  299.1 21.6 %collective-permute-start.23 = (bf16[560,700]{1,0:T(8,128)(2,1)S(1)}, bf16[560,700]{1,0:T(8,128)(2,1)}, u32[]{:S(2)}, u32[]{:S(2)}) collective-permute-start(bf16[560,700]{1,0:T(8,128)(2,1)S(1)} %copy-done.24), channel_id=1, source_target_pairs={{0,16},{16,24},{24,8},{8,0},{1,17},{17,25},{25,9},{9,1},{2,18},{18... | collective-permute-start | bytes 2352008 | tf_op jit(solution)/shard_map/ppermute | solution.py:744
  300.8 37.3 %collective-permute-start.25 = (bf16[560,1400]{1,0:T(8,128)(2,1)S(1)}, bf16[560,1400]{1,0:T(8,128)(2,1)S(1)}, u32[]{:S(2)}, u32[]{:S(2)}) collective-permute-start(bf16[560,1400]{1,0:T(8,128)(2,1)S(1)} %collective-permute-done.20.refs_4_), channel_id=1, source_target_pairs={{0,4},{4,0},{1,5},{5,1},{2,6},{6,2},{3,7},{7,3},{8,12},{12,8},{9,1... | collective-permute-start | bytes 4704008 | tf_op jit(solution)/shard_map/ppermute | solution.py:724
  303.6 34.5 %collective-permute-start.24 = (bf16[256,2304]{1,0:T(8,128)(2,1)S(1)}, bf16[256,2304]{1,0:T(8,128)(2,1)S(1)}, u32[]{:S(2)}, u32[]{:S(2)}) collective-permute-start(bf16[256,2304]{1,0:T(8,128)(2,1)S(1)} %add_convert_fusion.4.refs_0_), channel_id=1, source_target_pairs={{0,2},{1,3},{2,0},{3,1},{4,6},{5,7},{6,4},{7,5},{8,10},{9,11},{10,... | collective-permute-start | bytes 3538952 | tf_op jit(solution)/shard_map/ppermute | solution.py:724
  320.8 22.9 %collective-permute-start.26 = (bf16[560,700]{1,0:T(8,128)(2,1)}, bf16[560,700]{1,0:T(8,128)(2,1)}, u32[]{:S(2)}, u32[]{:S(2)}) collective-permute-start(bf16[560,700]{1,0:T(8,128)(2,1)} %collective-permute-done.23.refs_2_), channel_id=1, source_target_pairs={{0,16},{16,24},{24,8},{8,0},{1,17},{17,25},{25,9},{9,1},{2,18},{18... | collective-permute-start | bytes 2352008 | tf_op jit(solution)/shard_map/ppermute | solution.py:744
  323.3 32.5 %collective-permute-start.27 = (bf16[560,700]{1,0:T(8,128)(2,1)}, bf16[560,700]{1,0:T(8,128)(2,1)S(1)}, u32[]{:S(2)}, u32[]{:S(2)}) collective-permute-start(bf16[560,700]{1,0:T(8,128)(2,1)} %collective-permute-done.23.refs_2_), channel_id=1, source_target_pairs={{0,4},{4,0},{1,5},{5,1},{2,6},{6,2},{3,7},{7,3},{8,12},{12,8},{9,1... | collective-permute-start | bytes 2352008 | tf_op jit(solution)/shard_map/ppermute | solution.py:724
  356.7 21.7 %collective-permute-start.29 = (bf16[560,700]{1,0:T(8,128)(2,1)}, bf16[560,700]{1,0:T(8,128)(2,1)S(1)}, u32[]{:S(2)}, u32[]{:S(2)}) collective-permute-start(bf16[560,700]{1,0:T(8,128)(2,1)} %collective-permute-done.26.refs_3_), channel_id=1, source_target_pairs={{0,16},{16,24},{24,8},{8,0},{1,17},{17,25},{25,9},{9,1},{2,18},{18... | collective-permute-start | bytes 2352008 | tf_op jit(solution)/shard_map/ppermute | solution.py:744
  358.2 21.5 %collective-permute-start.30 = (bf16[560,700]{1,0:T(8,128)(2,1)}, bf16[560,700]{1,0:T(8,128)(2,1)S(1)}, u32[]{:S(2)}, u32[]{:S(2)}) collective-permute-start(bf16[560,700]{1,0:T(8,128)(2,1)} %collective-permute-done.26.refs_3_), channel_id=1, source_target_pairs={{0,4},{4,0},{1,5},{5,1},{2,6},{6,2},{3,7},{7,3},{8,12},{12,8},{9,1... | collective-permute-start | bytes 2352008 | tf_op jit(solution)/shard_map/ppermute | solution.py:724
  379.7 24.7 %collective-permute-start.33 = (bf16[560,700]{1,0:T(8,128)(2,1)S(1)}, bf16[560,700]{1,0:T(8,128)(2,1)S(1)}, u32[]{:S(2)}, u32[]{:S(2)}) collective-permute-start(bf16[560,700]{1,0:T(8,128)(2,1)S(1)} %collective-permute-done.29.refs_4_), channel_id=1, source_target_pairs={{0,4},{4,0},{1,5},{5,1},{2,6},{6,2},{3,7},{7,3},{8,12},{12,8},{9,1... | collective-permute-start | bytes 2352008 | tf_op jit(solution)/shard_map/ppermute | solution.py:724
  440.7 27.5 %collective-permute-start.36 = (bf16[256,2304]{1,0:T(8,128)(2,1)S(1)}, bf16[256,2304]{1,0:T(8,128)(2,1)S(1)}, u32[]{:S(2)}, u32[]{:S(2)}) collective-permute-start(bf16[256,2304]{1,0:T(8,128)(2,1)S(1)} %add_convert_fusion.3.refs_0_), channel_id=1, source_target_pairs={{0,2},{1,3},{2,0},{3,1},{4,6},{5,7},{6,4},{7,5},{8,10},{9,11},{10,... | collective-permute-start | bytes 3538952 | tf_op jit(solution)/shard_map/ppermute | solution.py:724
  472.8 28.2 %collective-permute-start.38 = (bf16[256,2304]{1,0:T(8,128)(2,1)S(1)}, bf16[256,2304]{1,0:T(8,128)(2,1)}, u32[]{:S(2)}, u32[]{:S(2)}) collective-permute-start(bf16[256,2304]{1,0:T(8,128)(2,1)S(1)} %add_convert_fusion.2.refs_0_), channel_id=1, source_target_pairs={{0,2},{1,3},{2,0},{3,1},{4,6},{5,7},{6,4},{7,5},{8,10},{9,11},{10,... | collective-permute-start | bytes 3538952 | tf_op jit(solution)/shard_map/ppermute | solution.py:724
  509.5 31.4 %collective-permute-start.40 = (f32[256,2304]{1,0:T(8,128)S(1)}, f32[256,2304]{1,0:T(8,128)}, u32[]{:S(2)}, u32[]{:S(2)}) collective-permute-start(f32[256,2304]{1,0:T(8,128)S(1)} %copy-done.14), channel_id=1, source_target_pairs={{0,1},{1,0},{2,3},{3,2},{4,5},{5,4},{6,7},{7,6},{8,9},{9,8},{10,11... | collective-permute-start | bytes 7077896 | tf_op jit(solution)/shard_map/ppermute | solution.py:724
  509.6 31.3 %all-to-all-start = ((f32[4,4,6656]{2,1,0:T(4,128)}), f32[4,4,6656]{2,1,0:T(4,128)}, u32[]{:S(2)}, u32[]{:S(2)}) async-start(f32[4,4,6656]{2,1,0:T(4,128)} %shard_map.400), calls=%async_computation | async-start | bytes 851968 | tf_op jit(solution)/shard_map/all_to_all | solution.py:1187
  545.7 28.3 %collective-permute-start.42 = (bf16[256,2304]{1,0:T(8,128)(2,1)S(1)}, bf16[256,2304]{1,0:T(8,128)(2,1)S(1)}, u32[]{:S(2)}, u32[]{:S(2)}) collective-permute-start(bf16[256,2304]{1,0:T(8,128)(2,1)S(1)} %add_convert_fusion.1.refs_0_), channel_id=1, source_target_pairs={{0,2},{1,3},{2,0},{3,1},{4,6},{5,7},{6,4},{7,5},{8,10},{9,11},{10,... | collective-permute-start | bytes 3538952 | tf_op jit(solution)/shard_map/ppermute | solution.py:724
  618.7 30.3 %collective-permute-start.47 = (bf16[256,2304]{1,0:T(8,128)(2,1)S(1)}, bf16[256,2304]{1,0:T(8,128)(2,1)S(1)}, u32[]{:S(2)}, u32[]{:S(2)}) collective-permute-start(bf16[256,2304]{1,0:T(8,128)(2,1)S(1)} %add_convert_fusion.refs_0_), channel_id=1, source_target_pairs={{0,2},{1,3},{2,0},{3,1},{4,6},{5,7},{6,4},{7,5},{8,10},{9,11},{10,... | collective-permute-start | bytes 3538952 | tf_op jit(solution)/shard_map/ppermute | solution.py:724
  (78 other events, 871.4 us)
